TPU v7x, 32 devices: a whole 2x2x4 slice. The times are simulated.
32 devices in a mesh: frame: 8 (over z, x), fsdp: 4 (over y, core).
Axes of the slice: x: 2, y: 2, z: 4, core: 2. Of those that a mesh axis runs over, the one named last changes fastest.
Arguments:
- queries: bfloat16 [32, 192, 3072], P(('frame', 'fsdp')), may hold values from -18 to 18
- keys: bfloat16 [32, 192, 3072], P(('frame', 'fsdp')), may hold values from -7 to 7
- values: bfloat16 [32, 192, 3072], P(('frame', 'fsdp')), may hold values from -6 to 6
- residual: bfloat16 [32, 192, 3072], P(('frame', 'fsdp')), may hold values from -6 to 6
- target: bfloat16 [32, 192, 3072], P(('frame', 'fsdp')), may hold values from -6 to 6
- output_weight: bfloat16 [3072, 3072], P('fsdp'), may hold values from -0.109375 to 0.109375
- down_adapter: bfloat16 [8, 64, 3072], P('frame', None, 'fsdp'), may hold values from -0.109375 to 0.109375
- up_adapter: bfloat16 [8, 64, 3072], P('frame', None, 'fsdp'), may hold values from -1.1953125 to 1.1953125
- scene_of_frame: int32 [32], P(('frame', 'fsdp')), may hold values from 0 to 7
- scene_adapter_row: int32 [8], replicated, may hold values from 0 to 7, each once
- valid_token_count: int32 [32], P(('frame', 'fsdp')), may hold values from 1 to 192, 3840 in all
Outputs:
- grad_down: float32 [8, 64, 3072], P('frame', None, 'fsdp')
- grad_up: float32 [8, 64, 3072], P('frame', None, 'fsdp')
- frame_loss: float32 [32], P(('frame', 'fsdp'))
Inputs may be any that keep to these rules, and one draw needn't show every extreme that they name: `scene_adapter_row`: each scene has its own adapter row. `valid_token_count`: some frame has all 192 slots valid.
All inputs are finite; a program needn't handle non-finite values. No bound on the sum of `valid_token_count` on one device may be relied on, other than what follows from the above.
Results may differ from a plain program's by a relative error of at most 0.0053.
Values may be sent and summed in bfloat16 or wider, within the bound.
No kernel may reach another device: no remote copies, remote signals or barrier semaphores. Data moves between devices by JAX's collectives and lax.ppermute only.
A program may use at most 192 MiB of HBM per device.

v0:
```python
import math

import jax
import jax.numpy as jnp
from jax import lax
from jax.sharding import PartitionSpec as P

HEADS = 24


adapter_scale = 2.0


def slot_lookup(scene_ids, scene_adapter_row):
    scene_range = jnp.arange(scene_adapter_row.shape[0], dtype=jnp.int32)
    matches = scene_ids[:, None] == scene_range[None, :]
    return jnp.sum(jnp.where(matches, scene_adapter_row[None, :], 0), axis=1)


def per_device(
    queries,
    keys,
    values,
    residual,
    target,
    output_weight,
    down_adapter,
    up_adapter,
    scene_of_frame,
    scene_adapter_row,
    valid_token_count,
):
    frames, slot_count, model_width = queries.shape
    head_count = HEADS
    head_size = model_width // head_count
    row_count = frames * slot_count
    score_scale = 1.0 / math.sqrt(head_size)
    query_heads = queries.reshape(frames, slot_count, head_count, head_size)
    key_heads = keys.reshape(frames, slot_count, head_count, head_size)
    value_heads = values.reshape(frames, slot_count, head_count, head_size)
    scores = (
        jnp.einsum("fqhd,fkhd->fhqk", query_heads, key_heads, preferred_element_type=jnp.float32)
        * score_scale
    )
    positions = lax.broadcasted_iota(jnp.int32, (frames, slot_count), 1)
    valid_mask = positions < valid_token_count[:, None]
    scores = jnp.where(valid_mask[:, None, None, :], scores, -jnp.inf)
    row_max = jnp.max(scores, axis=-1, keepdims=True)
    exponent = jnp.exp(scores - row_max)
    weights = (exponent / jnp.sum(exponent, axis=-1, keepdims=True)).astype(jnp.bfloat16)
    attended = jnp.einsum(
        "fhqk,fkhd->fqhd", weights, value_heads, preferred_element_type=jnp.float32
    )
    attended = attended.astype(jnp.bfloat16).reshape(frames, slot_count, model_width)
    mixed_flat = attended.reshape(row_count, model_width)
    projected_tokens = jnp.dot(
        mixed_flat,
        lax.all_gather(output_weight, "fsdp", axis=0, tiled=True),
        preferred_element_type=jnp.float32,
    )
    projected_tokens = projected_tokens.reshape(frames, slot_count, model_width)
    column_ids = lax.all_gather(scene_of_frame, "fsdp", axis=0, tiled=True)
    column_slots = slot_lookup(column_ids, scene_adapter_row)
    owner_range = jnp.arange(scene_adapter_row.shape[0], dtype=jnp.int32)
    column_pick = column_slots[:, None] == owner_range[None, :]
    adapter_couple = jnp.stack([down_adapter, up_adapter], axis=1)
    blocks = lax.all_gather(adapter_couple, "frame", axis=0, tiled=True)
    chosen = jnp.einsum(
        "fs,sxrd->fxrd",
        column_pick.astype(jnp.bfloat16),
        blocks,
        preferred_element_type=jnp.float32,
    )
    adapters = lax.all_to_all(
        chosen.astype(jnp.bfloat16), "fsdp", split_axis=0, concat_axis=3, tiled=True
    )
    down_weight_rows = adapters[:, 0]
    up_weight_rows = adapters[:, 1]
    low_rank_state = jnp.einsum(
        "ftd,frd->ftr", attended, down_weight_rows, preferred_element_type=jnp.float32
    ).astype(jnp.bfloat16)
    adapter_output = jnp.einsum(
        "akw,awe->ake", low_rank_state, up_weight_rows, preferred_element_type=jnp.float32
    )
    combined_output = (
        residual.astype(jnp.float32)
        + projected_tokens
        + adapter_scale * adapter_output
        - target.astype(jnp.float32)
    )
    residual_error = jnp.where(
        valid_mask[:, :, None], combined_output, jnp.zeros_like(combined_output)
    )
    token_float = valid_token_count.astype(jnp.float32)
    frame_loss = jnp.sum(residual_error * residual_error, axis=(1, 2)) / (token_float * model_width)
    output_gradient = (2.0 * residual_error / token_float[:, None, None]).astype(jnp.bfloat16)
    up_gradient_terms = adapter_scale * jnp.einsum(
        "ftr,ftd->frd", low_rank_state, output_gradient, preferred_element_type=jnp.float32
    )
    backward_low_rank = (
        adapter_scale
        * jnp.einsum(
            "ftd,frd->ftr", output_gradient, up_weight_rows, preferred_element_type=jnp.float32
        )
    ).astype(jnp.bfloat16)
    down_terms = jnp.einsum(
        "ftr,ftd->frd", backward_low_rank, attended, preferred_element_type=jnp.float32
    )
    grad_terms = jnp.stack([down_terms, up_gradient_terms], axis=1)
    pieces = lax.all_to_all(grad_terms, "fsdp", split_axis=3, concat_axis=0, tiled=True)
    scene_dense = jnp.einsum(
        "fs,fxrd->sxrd", column_pick.astype(jnp.float32), pieces, precision=lax.Precision.HIGHEST
    )
    scene_full = lax.psum(scene_dense, "frame")
    owned_rows = lax.dynamic_slice_in_dim(scene_full, lax.axis_index("frame"), 1, 0)
    return (owned_rows[:, 0], owned_rows[:, 1], frame_loss)


def solution(mesh):
    placed = (
        P(("frame", "fsdp"), None, None),
        P(("frame", "fsdp"), None, None),
        P(("frame", "fsdp"), None, None),
        P(("frame", "fsdp"), None, None),
        P(("frame", "fsdp"), None, None),
        P("fsdp", None),
        P("frame", None, "fsdp"),
        P("frame", None, "fsdp"),
        P(("frame", "fsdp")),
        P(),
        P(("frame", "fsdp")),
    )
    return jax.shard_map(
        per_device,
        mesh=mesh,
        in_specs=placed,
        out_specs=(P("frame", None, "fsdp"), P("frame", None, "fsdp"), P(("frame", "fsdp"))),
        check_vma=False,
    )
```

profile of v0, /device:TPU:0, one launch (start us, length us, event | category | flops | bytes accessed | tf_op | source)
XLA Modules:
  0.0 386.6 jit_solution(14730314297767134358)
XLA Ops:
  7.2 0.0 all-gather.5.cloned.1.call-start
  7.2 1.6 pad_maximum_fusion.1
  8.8 0.0 all-gather.5.cloned.1.call-update
  8.9 0.0 copy-start.6
  8.9 0.0 copy-start
  8.9 0.0 all-gather.3.cloned.1.call-start
  8.9 0.7 all-gather.3.cloned.1.call-update
  9.6 0.0 copy-start.1
  10.4 0.6 dynamic-slice
  11.0 0.8 dynamic-update-slice
  11.8 6.4 %all-reduce = s32[4]{0:T(128)S(1)} all-reduce(s32[4]{0:T(128)S(1)} %dynamic-update-slice), channel_id=1, replica_groups=mesh['frame'=8,'fsdp'=4] {'fsdp'}, use_global_device_ids=true, to_apply=%add | all-reduce | flops 4 | bytes 32
  18.8 0.0 copy-start.2
  18.8 0.2 copy.68
  19.1 0.2 copy.69
  19.3 0.8 copy-done.2
  20.1 0.2 copy.70
  20.3 0.2 select_reduce_fusion
  20.5 0.8 fusion.29
  21.3 4.1 %fusion.55 = (f32[24,192]{1,0:T(8,128)S(1)}, f32[24,192,192]{1,2,0:T(8,128)}) fusion(f32[24,192,192]{1,2,0:T(8,128)S(1)} %fusion.29, pred[192]{0:T(512)(128)(4,1)S(1)} %iota_compare_fusion.2), kind=kOutput, calls=%fused_computation.62 | output fusion | flops 5308607 | bytes 7096512 | tf_op jit(solution)/shard_map/sub | solution.py:49
  25.4 32.3 %all-gather.5.cloned.1.call-done = bf16[8,2,64,768]{3,2,1,0:T(8,128)(2,1)} async-done(((bf16[1,2,64,768]{3,2,1,0:T(8,128)(2,1)}), bf16[8,2,64,768]{3,2,1,0:T(8,128)(2,1)}) %all-gather.5.cloned.1.call-update) | async-done | bytes 1572880 | tf_op jit(solution)/shard_map/all_gather | solution.py:67
  57.7 2.5 fusion.18
  60.2 1.0 copy.58
  61.2 3.5 all-to-all-start
  64.7 0.2 all-reduce.3.cloned.1.call-start
  65.0 4.3 %fusion.17 = bf16[1,192,24,128]{3,1,2,0:T(8,128)(2,1)S(1)} fusion(f32[24,192,192]{1,2,0:T(8,128)} %get-tuple-element.21, f32[24,192]{1,0:T(8,128)S(1)} %get-tuple-element.20, bf16[192,24,128]{2,1,0:T(8,128)(2,1)S(1)} %bitcast.107), kind=kOutput, calls=%fused_computation.27 | convolution fusion | flops 228851712 | bytes 5916672 | tf_op jit(solution)/shard_map/fhqk,fkhd->fqhd/dot_general | solution.py:51
  69.3 0.8 copy.56
  70.1 8.2 %all-to-all-done = bf16[4,2,64,768]{3,2,1,0:T(8,128)(2,1)S(1)} async-done(((bf16[4,2,64,768]{3,2,1,0:T(8,128)(2,1)}), bf16[4,2,64,768]{3,2,1,0:T(8,128)(2,1)S(1)}, u32[]{:S(2)}, u32[]{:S(2)}) %all-to-all-start) | async-done | bytes 786464 | tf_op jit(solution)/shard_map/all_to_all | solution.py:74
  78.3 0.1 copy.67
  78.4 0.5 fusion.38
  78.9 100.8 %all-gather.3.cloned.1.call-done = bf16[3072,3072]{1,0:T(8,128)(2,1)} async-done(((bf16[768,3072]{1,0:T(8,128)(2,1)}), bf16[3072,3072]{1,0:T(8,128)(2,1)}) %all-gather.3.cloned.1.call-update) | async-done | bytes 18874384 | tf_op jit(solution)/shard_map/all_gather | solution.py:58
  179.7 9.1 %fusion.5 = f32[1,192,3072]{2,1,0:T(8,128)S(1)} fusion(bf16[3072,3072]{1,0:T(8,128)(2,1)} %all-gather.3.cloned.1.call-done, bf16[1,192,3072]{2,1,0:T(8,128)(2,1)} %param.14, bf16[24,8,24,128]{3,2,1,0:T(8,128)(2,1)S(1)} %bitcast.109), kind=kOutput, calls=%fused_computation.10 | convolution fusion | flops 3625058304 | bytes 23592960 | tf_op jit(solution)/shard_map/dot_general | solution.py:56
  188.8 1.5 multiply_reduce_fusion
  190.3 1.3 fusion.7
  191.6 3.2 convolution_bitcast_fusion.1
  194.8 2.7 pad_maximum_fusion
  197.5 4.4 %copy.60 = f32[1,2,64,3072]{2,1,0,3:T(2,128)S(1)} copy(f32[1,2,64,3072]{3,2,1,0:T(8,128)} %pad_maximum_fusion) | data formatting | bytes 3145728 | tf_op jit(solution)/shard_map/stack | solution.py:109
  201.9 4.1 %reshape.119 = f32[4,1,98304]{2,1,0:T(1,128)} reshape(f32[3072,1,2,64]{3,2,1,0:T(2,128)S(1)} %bitcast.96) | data formatting | bytes 3145728
  206.0 23.6 %all_to_all.36 = f32[4,1,98304]{2,1,0:T(1,128)S(1)} all-to-all(f32[4,1,98304]{2,1,0:T(1,128)} %reshape.119), channel_id=1, replica_groups=mesh['frame'=8,'fsdp'=4] {'fsdp'}, dimensions={0} | all-to-all | bytes 3145728 | tf_op jit(solution)/shard_map/all_to_all | solution.py:110
  229.6 0.5 broadcast.46
  230.2 6.4 %reduce.5 = f32[4,98304]{1,0:T(4,128)} reduce(f32[4,1,98304]{2,1,0:T(1,128)S(1)} %all_to_all.36, f32[]{:T(128)} %broadcast.46), dimensions={1}, to_apply=%all_to_all.30.reduce_sub_computation | reduce | bytes 3145732 | tf_op jit(solution)/shard_map/all_to_all | solution.py:110
  236.5 3.9 %reshape.120 = f32[3072,1,2,64]{3,2,1,0:T(2,128)S(1)} reshape(f32[4,98304]{1,0:T(4,128)} %reduce.5) | data formatting | bytes 3145728
  240.4 3.1 copy.66
  243.5 4.5 %fusion.12 = f32[8,2,64,768]{3,0,2,1:T(8,128)} fusion(f32[1,2,64,4,768]{4,3,2,1,0:T(4,128)} %copy.66, s32[4]{0:T(128)S(1)} %select_reduce_fusion), kind=kOutput, calls=%fused_computation.22 | convolution fusion | flops 37748768 | bytes 4718608 | tf_op jit(solution)/shard_map/fs,fxrd->sxrd/dot_general | solution.py:111
  248.0 0.0 all-reduce.3.cloned.1.call-update
  248.7 126.7 %all-reduce.3.cloned.1.call-done = f32[8,2,64,768]{3,0,2,1:T(8,128)} async-done(((f32[8,2,64,768]{3,0,2,1:T(8,128)}), f32[8,2,64,768]{3,0,2,1:T(8,128)}) %all-reduce.3.cloned.1.call-update) | async-done | bytes 3145744 | tf_op jit(solution)/shard_map/psum | solution.py:114
  375.4 2.2 dynamic-slice_bitcast_fusion
  377.6 0.7 copy.62
  378.3 0.7 copy.63
  (11 shorter events, 0.0 us)
Async XLA Ops:
  7.2 50.5 %all-gather.5.cloned.1.call-start = ((), (), s32[]{:S(2)}) async-start(), calls=%async_computation.3 | async-start | bytes 1769472 | tf_op jit(solution)/shard_map/all_gather | solution.py:67
  8.9 1.5 copy-start.6
  8.9 9.9 %copy-start = (bf16[1,192,3072]{2,1,0:T(8,128)(2,1)S(1)}, bf16[1,192,3072]{2,1,0:T(8,128)(2,1)}, u32[]{:S(2)}) copy-start(bf16[1,192,3072]{2,1,0:T(8,128)(2,1)} %param.11) | copy-start | bytes 3538948
  8.9 170.8 %all-gather.3.cloned.1.call-start = ((), (), s32[]{:S(2)}) async-start(), calls=%async_computation.2 | async-start | bytes 23592960 | tf_op jit(solution)/shard_map/all_gather | solution.py:58
  9.6 9.4 %copy-start.1 = (bf16[1,192,3072]{2,1,0:T(8,128)(2,1)S(1)}, bf16[1,192,3072]{2,1,0:T(8,128)(2,1)}, u32[]{:S(2)}) copy-start(bf16[1,192,3072]{2,1,0:T(8,128)(2,1)} %param.12) | copy-start | bytes 3538948
  18.8 1.3 copy-start.2
  19.0 1.3 copy-start.5
  61.2 17.1 %all-to-all-start = ((bf16[4,2,64,768]{3,2,1,0:T(8,128)(2,1)}), bf16[4,2,64,768]{3,2,1,0:T(8,128)(2,1)S(1)}, u32[]{:S(2)}, u32[]{:S(2)}) async-start(bf16[4,2,64,768]{3,2,1,0:T(8,128)(2,1)} %copy.58), calls=%async_computation | async-start | bytes 1572864 | tf_op jit(solution)/shard_map/all_to_all | solution.py:74
  64.7 310.7 %all-reduce.3.cloned.1.call-start = ((), (), s32[]{:S(2)}) async-start(), calls=%async_computation.4 | async-start | bytes 6291456 | tf_op jit(solution)/shard_map/psum | solution.py:114
  70.0 109.7 %copy-start.3 = (bf16[1,192,24,128]{3,2,1,0:T(8,128)(2,1)}, bf16[1,192,24,128]{3,2,1,0:T(8,128)(2,1)S(1)}, u32[]{:S(2)}) copy-start(bf16[1,192,24,128]{3,2,1,0:T(8,128)(2,1)S(1)} %copy.56) | copy-start | bytes 3538948
  179.7 9.1 %copy-start.4 = (bf16[1,192,3072]{2,1,0:T(8,128)(2,1)S(1)}, bf16[1,192,3072]{2,1,0:T(8,128)(2,1)}, u32[]{:S(2)}) copy-start(bf16[1,192,3072]{2,1,0:T(8,128)(2,1)} %param.15) | copy-start | bytes 3538948
Sparse Core Ops, SparseCore 0:
  10.8 46.8 all-gather.4
  59.2 120.4 all-gather.2
  248.2 127.1 all-reduce.2
where the time goes:
time: 387 us
  waiting for transfers between devices  269 us (70%)
  blocking collectives  30 us (8%)
  matrix products  27.7 us (7%)
  local copies, waits for them, and re-layouts  24.2 us (6%)
  between operations  17.1 us (4%)
  other arithmetic  15 us (4%)
    psum x1, waiting for transfers between devices, per_device(): scene_full = lax.psum(scene_dense, 'frame')  127 us
    all_gather x1, waiting for transfers between devices, per_device(): lax.all_gather(output_weight, 'fsdp', axis=0, tiled=True)  101 us
    all_gather x1, waiting for transfers between devices, per_device(): blocks = lax.all_gather(adapter_couple, 'frame', axis=0, tiled=True)  32.3 us
    all_to_all x1, blocking collectives, per_device(): lax.all_to_all(grad_terms, 'fsdp', split_axis=3, concat_axis=0, tiled=True)  23.6 us
    unnamed x24, local copies, waits for them, and re-layouts  12.2 us
    dot_general x1, matrix products, per_device(): jnp.dot(mixed_flat, lax.all_gather(output_weight, 'fsdp', axis=0, tiled=T...  9.07 us
    all_to_all x1, waiting for transfers between devices, per_device(): lax.all_to_all(chosen.astype(jnp.bfloat16), 'fsdp', split_axis=0, concat_...  8.23 us
  transfers between devices with their start and end apart: 4, of which 4 were waited for; matrix products, arithmetic and copies ran while one was open for 4% of the time, Pallas kernels for 0%

commit v1 on v0

v1 whole, which is shorter than its diff:
```python
import math

import jax
import jax.numpy as jnp
from jax import lax
from jax.sharding import PartitionSpec as P

HEADS = 24
ADAPTER_SCALE = 2.0
F32 = jnp.float32
BF16 = jnp.bfloat16


def xor_send(value, axis, size, offset):
    return lax.ppermute(value, axis, [(i, i ^ offset) for i in range(size)])


def split_axis(size):
    inner = 1 << ((size.bit_length() - 1) // 2)
    return size // inner, inner


def gather_scenes(block, size):
    outer, inner = split_axis(size)
    first = [block]
    for step in range(1, outer):
        first.append(xor_send(block, "frame", size, step * inner))
    out = [None] * size
    for step in range(outer):
        out[step * inner] = first[step]
    for step in range(1, inner):
        for lead in range(outer):
            out[lead * inner + step] = xor_send(first[lead], "frame", size, step)
    return jnp.stack(out)


def scatter_scenes(dense, size, inner_first):
    outer, inner = split_axis(size)
    near, far = (inner, outer) if inner_first else (outer, inner)
    near_mul, far_mul = (1, inner) if inner_first else (inner, 1)

    def at(f, s):
        return dense[f * far_mul + s * near_mul]

    staged = [at(f, 0) for f in range(far)]
    for step in range(1, near):
        sent = jnp.stack([at(f, step) for f in range(far)]).astype(BF16)
        got = xor_send(sent, "frame", size, step * near_mul)
        staged = [staged[f] + got[f].astype(F32) for f in range(far)]
    total = staged[0]
    for step in range(1, far):
        total = total + xor_send(staged[step].astype(BF16), "frame", size, step * far_mul).astype(F32)
    return total


def attend(queries, keys, values, valid):
    slots, width = queries.shape
    size = width // HEADS
    q = queries.reshape(slots, HEADS, size)
    k = keys.reshape(slots, HEADS, size)
    v = values.reshape(slots, HEADS, size)
    scores = jnp.einsum("qhd,khd->hqk", q, k, preferred_element_type=F32) * (1.0 / math.sqrt(size))
    scores = jnp.where(valid[None, None, :], scores, -jnp.inf)
    peak = jnp.max(scores, axis=-1, keepdims=True)
    exponent = jnp.exp(scores - peak)
    weights = (exponent / jnp.sum(exponent, axis=-1, keepdims=True)).astype(BF16)
    out = jnp.einsum("hqk,khd->qhd", weights, v, preferred_element_type=F32)
    return out.astype(BF16).reshape(slots, width)


def dot(a, b, ca, cb):
    return lax.dot_general(a, b, (((ca,), (cb,)), ((), ())), preferred_element_type=F32)


def make_per_device(frame_size, fsdp_size):
    chips = fsdp_size // 2

    def per_device(
        queries,
        keys,
        values,
        residual,
        target,
        output_weight,
        down_adapter,
        up_adapter,
        scene_of_frame,
        scene_adapter_row,
        valid_token_count,
    ):
        slots, width = queries.shape[1:]
        depth = output_weight.shape[0]
        shard = lax.axis_index("fsdp")
        group = lax.axis_index("frame")
        core = shard % 2
        chip = shard // 2

        weight_near = xor_send(output_weight, "fsdp", fsdp_size, 1)
        blocks = gather_scenes(jnp.concatenate([down_adapter, up_adapter], axis=0), frame_size)
        own_slot = scene_adapter_row[scene_of_frame[0]]
        offsets = [own_slot ^ group]
        for step in range(1, fsdp_size):
            offsets.append(xor_send(own_slot[None], "fsdp", fsdp_size, step)[0] ^ group)

        count = valid_token_count[0]
        valid = jnp.arange(slots, dtype=jnp.int32) < count
        attended = attend(queries[0], keys[0], values[0], valid)

        def partial(columns):
            mine = lax.dynamic_slice_in_dim(columns, core * depth, depth, 1)
            near = lax.dynamic_slice_in_dim(columns, (1 - core) * depth, depth, 1)
            return dot(mine, output_weight, 1, 0) + dot(near, weight_near, 1, 0)

        def chip_columns(which):
            return lax.dynamic_slice_in_dim(attended, which * 2 * depth, 2 * depth, 1)

        received = []
        for step in range(1, chips):
            theirs = xor_send(chip_columns(chip ^ step), "fsdp", fsdp_size, 2 * step)
            received.append(xor_send(partial(theirs).astype(BF16), "fsdp", fsdp_size, 2 * step))
        projected = partial(chip_columns(chip))
        for got in received:
            projected = projected + got.astype(F32)

        chosen = []
        for step in range(fsdp_size):
            pick = lax.dynamic_index_in_dim(blocks, offsets[step], 0, keepdims=False)
            chosen.append(pick if step == 0 else xor_send(pick, "fsdp", fsdp_size, step))
        adapters = jnp.zeros((2, down_adapter.shape[1], width), BF16)
        for step in range(fsdp_size):
            adapters = lax.dynamic_update_slice_in_dim(adapters, chosen[step], (shard ^ step) * depth, 2)
        down, up = adapters[0], adapters[1]

        low = dot(attended, down, 1, 1).astype(BF16)
        combined = (
            residual[0].astype(F32) + projected + ADAPTER_SCALE * dot(low, up, 1, 0) - target[0].astype(F32)
        )
        error = jnp.where(valid[:, None], combined, 0.0)
        tokens = count.astype(F32)
        loss = jnp.sum(error * error) / (tokens * width)
        cotangent = (2.0 * error / tokens).astype(BF16)
        up_terms = ADAPTER_SCALE * dot(low, cotangent, 0, 0)
        back = (ADAPTER_SCALE * dot(cotangent, up, 1, 1)).astype(BF16)
        down_terms = dot(back, attended, 0, 0)
        terms = jnp.concatenate([down_terms, up_terms], axis=0)

        pieces = []
        for step in range(fsdp_size):
            piece = lax.dynamic_slice_in_dim(terms, (shard ^ step) * depth, depth, 1)
            pieces.append(piece if step == 0 else xor_send(piece.astype(BF16), "fsdp", fsdp_size, step).astype(F32))
        dense = []
        for scene in range(frame_size):
            total = jnp.zeros_like(pieces[0])
            for offset, piece in zip(offsets, pieces):
                total = total + jnp.where(offset == scene, piece, 0.0)
            dense.append(total)
        dense = jnp.stack(dense)
        rank = down_adapter.shape[1]
        cut = 2 * rank * 5 // 8
        top = scatter_scenes(dense[:, :cut], frame_size, True)
        bottom = scatter_scenes(dense[:, cut:], frame_size, False)
        owned = jnp.concatenate([top, bottom], axis=0)
        return owned[None, :rank], owned[None, rank:], loss[None]

    return per_device


def solution(mesh):
    rows = P(("frame", "fsdp"), None, None)
    adapter = P("frame", None, "fsdp")
    vector = P(("frame", "fsdp"))
    placed = (rows, rows, rows, rows, rows, P("fsdp", None), adapter, adapter, vector, P(), vector)
    return jax.shard_map(
        make_per_device(mesh.shape["frame"], mesh.shape["fsdp"]),
        mesh=mesh,
        in_specs=placed,
        out_specs=(adapter, adapter, vector),
        check_vma=False,
    )
```

time: 387 us -> 147 us (0.38)
  waiting for transfers between devices: 269 us -> 70.6 us
  blocking collectives: 30 us -> 0 us
  starting transfers between devices: 3.84 us -> 30.6 us
  other arithmetic: 15 us -> 4.09 us
  between operations: 17.1 us -> 6.79 us
  matrix products: 27.7 us -> 18.5 us
  local copies, waits for them, and re-layouts: 24.2 us -> 16.3 us
    all_gather x2 -> x0, waiting for transfers between devices: 133 us -> none  [the longest x1 101 us: per_device(): lax.all_gather(output_weight, 'fsdp', axis=0, tiled=True)]
    psum x1 -> x0, waiting for transfers between devices: 127 us -> none  [per_device(): scene_full = lax.psum(scene_dense, 'frame')]
    ppermute x0 -> x27, waiting for transfers between devices: none -> 70.6 us  [xor_send(): return lax.ppermute(value, axis, [(i, i ^ offset) for i in range(size)])]
    ppermute x0 -> x27, starting transfers between devices: none -> 30.6 us  [xor_send(): return lax.ppermute(value, axis, [(i, i ^ offset) for i in range(size)])]
    all_to_all x1 -> x0, blocking collectives: 23.6 us -> none  [per_device(): lax.all_to_all(grad_terms, 'fsdp', split_axis=3, concat_axis=0, tiled=True)]
    dot_general x9 -> x10, matrix products: 27.7 us -> 18.5 us  [the longest x8 16.6 us: dot(): lax.dot_general(a, b, (((ca,), (cb,)), ((), ())), preferred_element_type=...]
    all_to_all x1 -> x0, waiting for transfers between devices: 8.23 us -> none  [per_device(): lax.all_to_all(chosen.astype(jnp.bfloat16), 'fsdp', split_axis=0, concat_...]
    unnamed x1 -> x0, blocking collectives: 6.38 us -> none
  transfers between devices with their start and end apart: 4 -> 27, of which waited for: 4 -> 12; matrix products, arithmetic and copies ran while one was open for 4% -> 16% of each run, Pallas kernels for 0% -> 0%
where the time goes in v1:
time: 147 us
  waiting for transfers between devices  70.6 us (48%)
  starting transfers between devices  30.6 us (21%)
  matrix products  18.5 us (13%)
  local copies, waits for them, and re-layouts  16.3 us (11%)
  between operations  6.79 us (5%)
  other arithmetic  4.09 us (3%)
    ppermute x27, waiting for transfers between devices, xor_send(): return lax.ppermute(value, axis, [(i, i ^ offset) for i in range(size)])  70.6 us
    ppermute x27, starting transfers between devices, xor_send(): return lax.ppermute(value, axis, [(i, i ^ offset) for i in range(size)])  30.6 us
    dot_general x8, matrix products, dot(): lax.dot_general(a, b, (((ca,), (cb,)), ((), ())), preferred_element_type=...  16.6 us
    unnamed x35, local copies, waits for them, and re-layouts  10.8 us
  transfers between devices with their start and end apart: 27, of which 12 were waited for; matrix products, arithmetic and copies ran while one was open for 16% of the time, Pallas kernels for 0%

profile of v1, /device:TPU:0, one launch (start us, length us, event | category | flops | bytes accessed | tf_op | source)
XLA Modules:
  0.0 146.9 jit_solution(12746220746571543373)
XLA Ops:
  1.8 1.2 dynamic_slice.50
  3.2 2.9 %collective-permute-start.12 = (s32[1]{0:T(128)}, s32[1]{0:T(128)}, u32[]{:S(2)}, u32[]{:S(2)}) collective-permute-start(s32[1]{0:T(128)} %dynamic_slice.50), channel_id=1, source_target_pairs={{0,2},{1,3},{2,0},{3,1},{4,6},{5,7},{6,4},{7,5},{8,10},{9,11},{10,... | collective-permute-start | bytes 20 | tf_op jit(solution)/shard_map/ppermute | solution.py:15
  6.1 0.9 constant_dynamic-update-slice_fusion.1
  7.0 0.9 constant_dynamic-update-slice_fusion
  7.9 1.5 %collective-permute-start.3 = (bf16[2,64,768]{2,1,0:T(8,128)(2,1)S(1)}, bf16[2,64,768]{2,1,0:T(8,128)(2,1)}, u32[]{:S(2)}, u32[]{:S(2)}) collective-permute-start(bf16[2,64,768]{2,1,0:T(8,128)(2,1)S(1)} %constant_dynamic-update-slice_fusion), channel_id=1, source_target_pairs={{0,4},{4,0},{8,12},{12,8},{16,20},{20,16},{24,28},{28,24},{1,5},{5... | collective-permute-start | bytes 589832 | tf_op jit(solution)/shard_map/ppermute | solution.py:15
  10.0 1.6 %copy.25 = bf16[24,8,24,128]{3,2,1,0:T(8,128)(2,1)S(1)} copy(bf16[24,8,24,128]{3,1,2,0:T(8,128)(2,1)} %bitcast.123) | data formatting | bytes 2359296
  12.1 0.8 fusion.15
  12.9 2.0 %fusion.102 = (f32[24,192]{1,0:T(8,128)S(1)}, f32[24,192,192]{1,2,0:T(8,128)S(1)}) fusion(f32[24,192,192]{1,2,0:T(8,128)S(1)} %fusion.15, pred[192]{0:T(512)(128)(4,1)S(1)} %iota_compare_fusion), kind=kOutput, calls=%fused_computation.176 | output fusion | flops 5308607 | bytes 7096512 | tf_op jit(solution)/shard_map/sub | solution.py:65
  14.9 1.1 fusion.13
  16.0 1.0 copy-done.7
  17.4 1.7 %collective-permute-start.4 = (bf16[2,64,768]{2,1,0:T(8,128)(2,1)S(1)}, bf16[2,64,768]{2,1,0:T(8,128)(2,1)}, u32[]{:S(2)}, u32[]{:S(2)}) collective-permute-start(bf16[2,64,768]{2,1,0:T(8,128)(2,1)S(1)} %constant_dynamic-update-slice_fusion), channel_id=1, source_target_pairs={{0,8},{4,12},{8,0},{12,4},{16,24},{20,28},{24,16},{28,20},{1,9},{5... | collective-permute-start | bytes 589832 | tf_op jit(solution)/shard_map/ppermute | solution.py:15
  19.1 2.6 %collective-permute-start.6 = (bf16[2,64,768]{2,1,0:T(8,128)(2,1)S(1)}, bf16[2,64,768]{2,1,0:T(8,128)(2,1)}, u32[]{:S(2)}, u32[]{:S(2)}) collective-permute-start(bf16[2,64,768]{2,1,0:T(8,128)(2,1)S(1)} %constant_dynamic-update-slice_fusion), channel_id=1, source_target_pairs={{0,16},{4,20},{8,24},{12,28},{16,0},{20,4},{24,8},{28,12},{1,17},{... | collective-permute-start | bytes 589832 | tf_op jit(solution)/shard_map/ppermute | solution.py:15
  23.8 1.5 %collective-permute-start.1 = (bf16[192,1536]{1,0:T(8,128)(2,1)S(1)}, bf16[192,1536]{1,0:T(8,128)(2,1)S(1)}, u32[]{:S(2)}, u32[]{:S(2)}) collective-permute-start(bf16[192,1536]{1,0:T(8,128)(2,1)S(1)} %constant_dynamic-slice_fusion), channel_id=1, source_target_pairs={{0,2},{1,3},{2,0},{3,1},{4,6},{5,7},{6,4},{7,5},{8,10},{9,11},{10,... | collective-permute-start | bytes 1769480 | tf_op jit(solution)/shard_map/ppermute | solution.py:15
  25.3 3.2 %collective-permute-done.4 = bf16[2,64,768]{2,1,0:T(8,128)(2,1)} collective-permute-done((bf16[2,64,768]{2,1,0:T(8,128)(2,1)S(1)}, bf16[2,64,768]{2,1,0:T(8,128)(2,1)}, u32[]{:S(2)}, u32[]{:S(2)}) %collective-permute-start.4) | collective-permute-done | bytes 196640 | tf_op jit(solution)/shard_map/ppermute | solution.py:15
  28.8 7.5 %collective-permute-done.6 = bf16[2,64,768]{2,1,0:T(8,128)(2,1)} collective-permute-done((bf16[2,64,768]{2,1,0:T(8,128)(2,1)S(1)}, bf16[2,64,768]{2,1,0:T(8,128)(2,1)}, u32[]{:S(2)}, u32[]{:S(2)}) %collective-permute-start.6) | collective-permute-done | bytes 196640 | tf_op jit(solution)/shard_map/ppermute | solution.py:15
  36.8 1.5 %collective-permute-start.9 = (bf16[2,64,768]{2,1,0:T(8,128)(2,1)}, bf16[2,64,768]{2,1,0:T(8,128)(2,1)S(1)}, u32[]{:S(2)}, u32[]{:S(2)}) collective-permute-start(bf16[2,64,768]{2,1,0:T(8,128)(2,1)} %collective-permute-done.8), channel_id=1, source_target_pairs={{0,4},{4,0},{8,12},{12,8},{16,20},{20,16},{24,28},{28,24},{1,5},{5... | collective-permute-start | bytes 589832 | tf_op jit(solution)/shard_map/ppermute | solution.py:15
  38.3 0.9 bitcast_dynamic-update-slice_fusion.7
  39.3 0.9 bitcast_dynamic-update-slice_fusion.6
  40.3 0.9 bitcast_dynamic-update-slice_fusion.4
  41.2 1.0 collective-permute-done.7
  42.2 0.9 bitcast_dynamic-update-slice_fusion.2
  43.2 1.1 collective-permute-done.9
  44.3 0.9 dynamic-slice_bitcast_fusion
  45.3 3.7 %fusion.59 = f32[192,3072]{1,0:T(8,128)S(1)} fusion(bf16[768,3072]{1,0:T(8,128)(2,1)} %collective-permute-done, bf16[192,1536]{1,0:T(8,128)(2,1)S(1)} %collective-permute-done.1, s32[]{:T(128)S(6)} %select_n.274), kind=kOutput, calls=%fused_computation.106 | convolution fusion | flops 905969664 | bytes 7372804 | tf_op jit(solution)/shard_map/dot_general | solution.py:72
  49.0 2.1 %fusion.6 = bf16[192,3072]{1,0:T(8,128)(2,1)} fusion(f32[192,3072]{1,0:T(8,128)S(1)} %fusion.59, bf16[768,3072]{1,0:T(8,128)(2,1)S(1)} %bitcast.117, bf16[192,1536]{1,0:T(8,128)(2,1)S(1)} %collective-permute-done.1, s32[]{:T(128)S(6)} %select_n.269), kind=kOutput, calls=%fused_computation.12 | convolution fusion | flops 907149312 | bytes 8552452 | tf_op jit(solution)/shard_map/dot_general | solution.py:72
  51.1 1.4 collective-permute-start.2
  52.5 1.2 fusion.63
  55.0 0.8 collective-permute-start.15
  56.0 0.9 bitcast_dynamic-update-slice_fusion
  56.9 0.9 constant_dynamic-update-slice_fusion.4
  57.9 26.4 %collective-permute-done.13 = bf16[2,64,768]{2,1,0:T(8,128)(2,1)S(1)} collective-permute-done((bf16[2,64,768]{2,1,0:T(8,128)(2,1)}, bf16[2,64,768]{2,1,0:T(8,128)(2,1)S(1)}, u32[]{:S(2)}, u32[]{:S(2)}) %collective-permute-start.13) | collective-permute-done | bytes 196640 | tf_op jit(solution)/shard_map/ppermute | solution.py:15
  84.3 3.1 %collective-permute-done.15 = bf16[2,64,768]{2,1,0:T(8,128)(2,1)S(1)} collective-permute-done((bf16[2,64,768]{2,1,0:T(8,128)(2,1)}, bf16[2,64,768]{2,1,0:T(8,128)(2,1)S(1)}, u32[]{:S(2)}, u32[]{:S(2)}) %collective-permute-start.15) | collective-permute-done | bytes 196640 | tf_op jit(solution)/shard_map/ppermute | solution.py:15
  89.4 5.1 %multiply_reduce_fusion = (f32[]{:T(128)}, f32[192,3072]{1,0:T(8,128)S(1)}) fusion(bf16[1,192,3072]{2,1,0:T(8,128)(2,1)S(1)} %copy-done.3, f32[192,3072]{1,0:T(8,128)S(1)} %convolution_multiply_fusion, bf16[192,3072]{1,0:T(8,128)(2,1)} %collective-permute-done.2, f32[192,3072]{1,0:T(8,128)S(1)} %fusion.63, bf16[768,3072]{1,0:T(8,128)(2,1)} %collective-permute-done, ...), kind=kOutput, calls=%fused_computation.23 | convolution fusion | flops 912457728 | bytes 15630856 | tf_op jit(solution)/shard_map/dot_general | solution.py:72
  94.5 1.4 copy-done
  97.0 3.2 %fusion.19 = f32[64,3072]{1,0:T(8,128)S(1)} fusion(bf16[2,64,3072]{2,1,0:T(8,128)(2,1)S(1)} %copy-done.2, bf16[24,24,8,128]{3,2,1,0:T(8,128)(2,1)} %copy-done.7, f32[192,3072]{1,0:T(8,128)} %copy-done, f32[]{:T(128)S(6)} %convert_element_type.142), kind=kOutput, calls=%fused_computation.39 | convolution fusion | flops 152788992 | bytes 4718596 | tf_op jit(solution)/shard_map/dot_general | solution.py:72
  100.7 1.4 collective-permute-start.17
  102.9 5.6 %collective-permute-done.17 = bf16[128,768]{1,0:T(8,128)(2,1)S(1)} collective-permute-done((bf16[128,768]{1,0:T(8,128)(2,1)S(1)}, bf16[128,768]{1,0:T(8,128)(2,1)S(1)}, u32[]{:S(2)}, u32[]{:S(2)}) %collective-permute-start.17) | collective-permute-done | bytes 196640 | tf_op jit(solution)/shard_map/ppermute | solution.py:15
  108.5 2.6 %collective-permute-done.18 = bf16[128,768]{1,0:T(8,128)(2,1)S(1)} collective-permute-done((bf16[128,768]{1,0:T(8,128)(2,1)S(1)}, bf16[128,768]{1,0:T(8,128)(2,1)S(1)}, u32[]{:S(2)}, u32[]{:S(2)}) %collective-permute-start.18) | collective-permute-done | bytes 196640 | tf_op jit(solution)/shard_map/ppermute | solution.py:15
  112.6 2.2 %collective-permute-start.23 = (bf16[2,48,768]{2,1,0:T(8,128)(2,1)S(1)}, bf16[2,48,768]{2,1,0:T(8,128)(2,1)S(1)}, u32[]{:S(2)}, u32[]{:S(2)}) collective-permute-start(bf16[2,48,768]{2,1,0:T(8,128)(2,1)S(1)} %pad_maximum_fusion.4), channel_id=1, source_target_pairs={{0,8},{4,12},{8,0},{12,4},{16,24},{20,28},{24,16},{28,20},{1,9},{5... | collective-permute-start | bytes 442376 | tf_op jit(solution)/shard_map/ppermute | solution.py:15
  114.9 2.6 %collective-permute-start.24 = (bf16[2,48,768]{2,1,0:T(8,128)(2,1)S(1)}, bf16[2,48,768]{2,1,0:T(8,128)(2,1)S(1)}, u32[]{:S(2)}, u32[]{:S(2)}) collective-permute-start(bf16[2,48,768]{2,1,0:T(8,128)(2,1)S(1)} %pad_maximum_fusion.3), channel_id=1, source_target_pairs={{0,16},{4,20},{8,24},{12,28},{16,0},{20,4},{24,8},{28,12},{1,17},{... | collective-permute-start | bytes 442376 | tf_op jit(solution)/shard_map/ppermute | solution.py:15
  117.7 4.1 %collective-permute-done.23 = bf16[2,48,768]{2,1,0:T(8,128)(2,1)S(1)} collective-permute-done((bf16[2,48,768]{2,1,0:T(8,128)(2,1)S(1)}, bf16[2,48,768]{2,1,0:T(8,128)(2,1)S(1)}, u32[]{:S(2)}, u32[]{:S(2)}) %collective-permute-start.23) | collective-permute-done | bytes 147488 | tf_op jit(solution)/shard_map/ppermute | solution.py:15
  121.7 7.2 %collective-permute-done.24 = bf16[2,48,768]{2,1,0:T(8,128)(2,1)S(1)} collective-permute-done((bf16[2,48,768]{2,1,0:T(8,128)(2,1)S(1)}, bf16[2,48,768]{2,1,0:T(8,128)(2,1)S(1)}, u32[]{:S(2)}, u32[]{:S(2)}) %collective-permute-start.24) | collective-permute-done | bytes 147488 | tf_op jit(solution)/shard_map/ppermute | solution.py:15
  128.9 1.6 %collective-permute-start.26 = (bf16[48,768]{1,0:T(8,128)(2,1)S(1)}, bf16[48,768]{1,0:T(8,128)(2,1)S(1)}, u32[]{:S(2)}, u32[]{:S(2)}) collective-permute-start(bf16[48,768]{1,0:T(8,128)(2,1)S(1)} %fusion.86), channel_id=1, source_target_pairs={{0,4},{4,0},{8,12},{12,8},{16,20},{20,16},{24,28},{28,24},{1,5},{5... | collective-permute-start | bytes 221192 | tf_op jit(solution)/shard_map/ppermute | solution.py:15
  130.6 2.9 %collective-permute-start.20 = (bf16[80,768]{1,0:T(8,128)(2,1)S(1)}, bf16[80,768]{1,0:T(8,128)(2,1)S(1)}, u32[]{:S(2)}, u32[]{:S(2)}) collective-permute-start(bf16[80,768]{1,0:T(8,128)(2,1)S(1)} %get-tuple-element.22), channel_id=1, source_target_pairs={{0,8},{4,12},{8,0},{12,4},{16,24},{20,28},{24,16},{28,20},{1,9},{5... | collective-permute-start | bytes 368648 | tf_op jit(solution)/shard_map/ppermute | solution.py:15
  133.5 1.1 collective-permute-start.21
  134.6 1.4 collective-permute-start.22
  136.0 1.5 %collective-permute-done.20 = bf16[80,768]{1,0:T(8,128)(2,1)S(1)} collective-permute-done((bf16[80,768]{1,0:T(8,128)(2,1)S(1)}, bf16[80,768]{1,0:T(8,128)(2,1)S(1)}, u32[]{:S(2)}, u32[]{:S(2)}) %collective-permute-start.20) | collective-permute-done | bytes 122912 | tf_op jit(solution)/shard_map/ppermute | solution.py:15
  137.5 7.4 %collective-permute-done.21 = bf16[80,768]{1,0:T(8,128)(2,1)S(1)} collective-permute-done((bf16[80,768]{1,0:T(8,128)(2,1)S(1)}, bf16[80,768]{1,0:T(8,128)(2,1)S(1)}, u32[]{:S(2)}, u32[]{:S(2)}) %collective-permute-start.21) | collective-permute-done | bytes 122912 | tf_op jit(solution)/shard_map/ppermute | solution.py:15
  (83 shorter events, 9.7 us)
Async XLA Ops:
  0.6 11.0 %copy-start.5 = (bf16[1,192,3072]{2,1,0:T(8,128)(2,1)S(1)}, bf16[1,192,3072]{2,1,0:T(8,128)(2,1)}, u32[]{:S(2)}) copy-start(bf16[1,192,3072]{2,1,0:T(8,128)(2,1)} %param.12) | copy-start | bytes 3538948
  0.6 44.6 %collective-permute-start = (bf16[768,3072]{1,0:T(8,128)(2,1)}, bf16[768,3072]{1,0:T(8,128)(2,1)}, u32[]{:S(2)}, u32[]{:S(2)}) collective-permute-start(bf16[768,3072]{1,0:T(8,128)(2,1)} %param.16), channel_id=1, source_target_pairs={{0,1},{1,0},{2,3},{3,2},{4,5},{5,4},{6,7},{7,6},{8,9},{9,8},{10,11... | collective-permute-start | bytes 14155784 | tf_op jit(solution)/shard_map/ppermute | solution.py:15
  3.1 14.4 %collective-permute-start.10 = (s32[1]{0:T(128)}, s32[1]{0:T(128)}, u32[]{:S(2)}, u32[]{:S(2)}) collective-permute-start(s32[1]{0:T(128)} %dynamic_slice.50), channel_id=1, source_target_pairs={{0,1},{1,0},{2,3},{3,2},{4,5},{5,4},{6,7},{7,6},{8,9},{9,8},{10,11... | collective-permute-start | bytes 20 | tf_op jit(solution)/shard_map/ppermute | solution.py:15
  3.2 15.9 %collective-permute-start.12 = (s32[1]{0:T(128)}, s32[1]{0:T(128)}, u32[]{:S(2)}, u32[]{:S(2)}) collective-permute-start(s32[1]{0:T(128)} %dynamic_slice.50), channel_id=1, source_target_pairs={{0,2},{1,3},{2,0},{3,1},{4,6},{5,7},{6,4},{7,5},{8,10},{9,11},{10,... | collective-permute-start | bytes 20 | tf_op jit(solution)/shard_map/ppermute | solution.py:15
  6.1 15.6 %collective-permute-start.14 = (s32[1]{0:T(128)}, s32[1]{0:T(128)}, u32[]{:S(2)}, u32[]{:S(2)}) collective-permute-start(s32[1]{0:T(128)} %dynamic_slice.50), channel_id=1, source_target_pairs={{0,3},{1,2},{2,1},{3,0},{4,7},{5,6},{6,5},{7,4},{8,11},{9,10},{10,... | collective-permute-start | bytes 20 | tf_op jit(solution)/shard_map/ppermute | solution.py:15
  7.9 15.9 %collective-permute-start.3 = (bf16[2,64,768]{2,1,0:T(8,128)(2,1)S(1)}, bf16[2,64,768]{2,1,0:T(8,128)(2,1)}, u32[]{:S(2)}, u32[]{:S(2)}) collective-permute-start(bf16[2,64,768]{2,1,0:T(8,128)(2,1)S(1)} %constant_dynamic-update-slice_fusion), channel_id=1, source_target_pairs={{0,4},{4,0},{8,12},{12,8},{16,20},{20,16},{24,28},{28,24},{1,5},{5... | collective-permute-start | bytes 589832 | tf_op jit(solution)/shard_map/ppermute | solution.py:15
  10.0 1.8 %copy-start.6 = (bf16[1,192,3072]{2,1,0:T(8,128)(2,1)S(1)}, bf16[1,192,3072]{2,1,0:T(8,128)(2,1)}, u32[]{:S(2)}) copy-start(bf16[1,192,3072]{2,1,0:T(8,128)(2,1)} %param.13) | copy-start | bytes 3538948
  16.0 1.0 copy-start.7
  17.4 11.0 %collective-permute-start.4 = (bf16[2,64,768]{2,1,0:T(8,128)(2,1)S(1)}, bf16[2,64,768]{2,1,0:T(8,128)(2,1)}, u32[]{:S(2)}, u32[]{:S(2)}) collective-permute-start(bf16[2,64,768]{2,1,0:T(8,128)(2,1)S(1)} %constant_dynamic-update-slice_fusion), channel_id=1, source_target_pairs={{0,8},{4,12},{8,0},{12,4},{16,24},{20,28},{24,16},{28,20},{1,9},{5... | collective-permute-start | bytes 589832 | tf_op jit(solution)/shard_map/ppermute | solution.py:15
  19.1 17.2 %collective-permute-start.6 = (bf16[2,64,768]{2,1,0:T(8,128)(2,1)S(1)}, bf16[2,64,768]{2,1,0:T(8,128)(2,1)}, u32[]{:S(2)}, u32[]{:S(2)}) collective-permute-start(bf16[2,64,768]{2,1,0:T(8,128)(2,1)S(1)} %constant_dynamic-update-slice_fusion), channel_id=1, source_target_pairs={{0,16},{4,20},{8,24},{12,28},{16,0},{20,4},{24,8},{28,12},{1,17},{... | collective-permute-start | bytes 589832 | tf_op jit(solution)/shard_map/ppermute | solution.py:15
  21.7 15.2 %collective-permute-start.8 = (bf16[2,64,768]{2,1,0:T(8,128)(2,1)S(1)}, bf16[2,64,768]{2,1,0:T(8,128)(2,1)}, u32[]{:S(2)}, u32[]{:S(2)}) collective-permute-start(bf16[2,64,768]{2,1,0:T(8,128)(2,1)S(1)} %constant_dynamic-update-slice_fusion), channel_id=1, source_target_pairs={{0,24},{4,28},{8,16},{12,20},{16,8},{20,12},{24,0},{28,4},{1,25},{... | collective-permute-start | bytes 589832 | tf_op jit(solution)/shard_map/ppermute | solution.py:15
  23.8 21.5 %collective-permute-start.1 = (bf16[192,1536]{1,0:T(8,128)(2,1)S(1)}, bf16[192,1536]{1,0:T(8,128)(2,1)S(1)}, u32[]{:S(2)}, u32[]{:S(2)}) collective-permute-start(bf16[192,1536]{1,0:T(8,128)(2,1)S(1)} %constant_dynamic-slice_fusion), channel_id=1, source_target_pairs={{0,2},{1,3},{2,0},{3,1},{4,6},{5,7},{6,4},{7,5},{8,10},{9,11},{10,... | collective-permute-start | bytes 1769480 | tf_op jit(solution)/shard_map/ppermute | solution.py:15
  28.4 11.8 %collective-permute-start.5 = (bf16[2,64,768]{2,1,0:T(8,128)(2,1)}, bf16[2,64,768]{2,1,0:T(8,128)(2,1)S(1)}, u32[]{:S(2)}, u32[]{:S(2)}) collective-permute-start(bf16[2,64,768]{2,1,0:T(8,128)(2,1)} %collective-permute-done.4), channel_id=1, source_target_pairs={{0,4},{4,0},{8,12},{12,8},{16,20},{20,16},{24,28},{28,24},{1,5},{5... | collective-permute-start | bytes 589832 | tf_op jit(solution)/shard_map/ppermute | solution.py:15
  36.3 5.9 %collective-permute-start.7 = (bf16[2,64,768]{2,1,0:T(8,128)(2,1)}, bf16[2,64,768]{2,1,0:T(8,128)(2,1)S(1)}, u32[]{:S(2)}, u32[]{:S(2)}) collective-permute-start(bf16[2,64,768]{2,1,0:T(8,128)(2,1)} %collective-permute-done.6), channel_id=1, source_target_pairs={{0,4},{4,0},{8,12},{12,8},{16,20},{20,16},{24,28},{28,24},{1,5},{5... | collective-permute-start | bytes 589832 | tf_op jit(solution)/shard_map/ppermute | solution.py:15
  36.8 7.5 %collective-permute-start.9 = (bf16[2,64,768]{2,1,0:T(8,128)(2,1)}, bf16[2,64,768]{2,1,0:T(8,128)(2,1)S(1)}, u32[]{:S(2)}, u32[]{:S(2)}) collective-permute-start(bf16[2,64,768]{2,1,0:T(8,128)(2,1)} %collective-permute-done.8), channel_id=1, source_target_pairs={{0,4},{4,0},{8,12},{12,8},{16,20},{20,16},{24,28},{28,24},{1,5},{5... | collective-permute-start | bytes 589832 | tf_op jit(solution)/shard_map/ppermute | solution.py:15
  44.3 4.6 %copy-start.9 = (bf16[8,2,64,768]{3,2,1,0:T(8,128)(2,1)}, bf16[8,2,64,768]{3,2,1,0:T(8,128)(2,1)S(1)}, u32[]{:S(2)}) copy-start(bf16[8,2,64,768]{3,2,1,0:T(8,128)(2,1)S(1)} %bitcast_dynamic-update-slice_fusion.1) | copy-start | bytes 4718596
  45.2 3.7 %slice-start = ((s8[4718592]{0:T(1024)(128)(4,1)}), s8[4194304]{0:T(1024)(128)(4,1)S(1)}, s32[]{:S(2)}) async-start(s8[4718592]{0:T(1024)(128)(4,1)} %bitcast.116), calls=%async_computation | async-start | bytes 8388608
  45.2 3.7 %slice-start.1 = ((s8[4718592]{0:T(1024)(128)(4,1)}), s8[524288]{0:T(1024)(128)(4,1)S(1)}, s32[]{:S(2)}) async-start(s8[4718592]{0:T(1024)(128)(4,1)} %bitcast.116), calls=%async_computation.1 | async-start | bytes 1048576
  45.2 11.7 %collective-permute-start.11 = (bf16[2,64,768]{2,1,0:T(8,128)(2,1)}, bf16[2,64,768]{2,1,0:T(8,128)(2,1)}, u32[]{:S(2)}, u32[]{:S(2)}) collective-permute-start(bf16[2,64,768]{2,1,0:T(8,128)(2,1)} %get-tuple-element.15), channel_id=1, source_target_pairs={{0,1},{1,0},{2,3},{3,2},{4,5},{5,4},{6,7},{7,6},{8,9},{9,8},{10,11... | collective-permute-start | bytes 589832 | tf_op jit(solution)/shard_map/ppermute | solution.py:15
  51.1 37.4 %collective-permute-start.2 = (bf16[192,3072]{1,0:T(8,128)(2,1)}, bf16[192,3072]{1,0:T(8,128)(2,1)}, u32[]{:S(2)}, u32[]{:S(2)}) collective-permute-start(bf16[192,3072]{1,0:T(8,128)(2,1)} %fusion.6), channel_id=1, source_target_pairs={{0,2},{1,3},{2,0},{3,1},{4,6},{5,7},{6,4},{7,5},{8,10},{9,11},{10,... | collective-permute-start | bytes 3538952 | tf_op jit(solution)/shard_map/ppermute | solution.py:15
  54.4 33.1 %copy-start.8 = (bf16[24,24,8,128]{3,2,1,0:T(8,128)(2,1)S(1)}, bf16[24,24,8,128]{3,2,1,0:T(8,128)(2,1)}, u32[]{:S(2)}) copy-start(bf16[24,24,8,128]{3,2,1,0:T(8,128)(2,1)} %copy-done.7) | copy-start | bytes 3538948
  54.4 29.9 %collective-permute-start.13 = (bf16[2,64,768]{2,1,0:T(8,128)(2,1)}, bf16[2,64,768]{2,1,0:T(8,128)(2,1)S(1)}, u32[]{:S(2)}, u32[]{:S(2)}) collective-permute-start(bf16[2,64,768]{2,1,0:T(8,128)(2,1)} %get-tuple-element.14), channel_id=1, source_target_pairs={{0,2},{1,3},{2,0},{3,1},{4,6},{5,7},{6,4},{7,5},{8,10},{9,11},{10,... | collective-permute-start | bytes 589832 | tf_op jit(solution)/shard_map/ppermute | solution.py:15
  55.0 32.4 %collective-permute-start.15 = (bf16[2,64,768]{2,1,0:T(8,128)(2,1)}, bf16[2,64,768]{2,1,0:T(8,128)(2,1)S(1)}, u32[]{:S(2)}, u32[]{:S(2)}) collective-permute-start(bf16[2,64,768]{2,1,0:T(8,128)(2,1)} %get-tuple-element.13), channel_id=1, source_target_pairs={{0,3},{1,2},{2,1},{3,0},{4,7},{5,6},{6,5},{7,4},{8,11},{9,10},{10,... | collective-permute-start | bytes 589832 | tf_op jit(solution)/shard_map/ppermute | solution.py:15
  87.4 1.0 copy-start.1
  87.5 1.6 %copy-start.3 = (bf16[1,192,3072]{2,1,0:T(8,128)(2,1)S(1)}, bf16[1,192,3072]{2,1,0:T(8,128)(2,1)}, u32[]{:S(2)}) copy-start(bf16[1,192,3072]{2,1,0:T(8,128)(2,1)} %param.15) | copy-start | bytes 3538948
  87.5 1.9 %copy-start.4 = (bf16[1,192,3072]{2,1,0:T(8,128)(2,1)S(1)}, bf16[1,192,3072]{2,1,0:T(8,128)(2,1)}, u32[]{:S(2)}) copy-start(bf16[1,192,3072]{2,1,0:T(8,128)(2,1)} %param.14) | copy-start | bytes 3538948
  94.5 1.4 copy-start
  95.9 1.1 copy-start.2
  100.3 2.6 %collective-permute-start.16 = (bf16[128,768]{1,0:T(8,128)(2,1)S(1)}, bf16[128,768]{1,0:T(8,128)(2,1)S(1)}, u32[]{:S(2)}, u32[]{:S(2)}) collective-permute-start(bf16[128,768]{1,0:T(8,128)(2,1)S(1)} %get-tuple-element.11), channel_id=1, source_target_pairs={{0,1},{1,0},{2,3},{3,2},{4,5},{5,4},{6,7},{7,6},{8,9},{9,8},{10,11... | collective-permute-start | bytes 589832 | tf_op jit(solution)/shard_map/ppermute | solution.py:15
  100.7 7.7 %collective-permute-start.17 = (bf16[128,768]{1,0:T(8,128)(2,1)S(1)}, bf16[128,768]{1,0:T(8,128)(2,1)S(1)}, u32[]{:S(2)}, u32[]{:S(2)}) collective-permute-start(bf16[128,768]{1,0:T(8,128)(2,1)S(1)} %get-tuple-element.12), channel_id=1, source_target_pairs={{0,2},{1,3},{2,0},{3,1},{4,6},{5,7},{6,4},{7,5},{8,10},{9,11},{10,... | collective-permute-start | bytes 589832 | tf_op jit(solution)/shard_map/ppermute | solution.py:15
  102.2 9.0 %collective-permute-start.18 = (bf16[128,768]{1,0:T(8,128)(2,1)S(1)}, bf16[128,768]{1,0:T(8,128)(2,1)S(1)}, u32[]{:S(2)}, u32[]{:S(2)}) collective-permute-start(bf16[128,768]{1,0:T(8,128)(2,1)S(1)} %get-tuple-element.10), channel_id=1, source_target_pairs={{0,3},{1,2},{2,1},{3,0},{4,7},{5,6},{6,5},{7,4},{8,11},{9,10},{10,... | collective-permute-start | bytes 589832 | tf_op jit(solution)/shard_map/ppermute | solution.py:15
  112.1 18.4 %collective-permute-start.19 = (bf16[4,80,768]{2,1,0:T(8,128)(2,1)S(1)}, bf16[4,80,768]{2,1,0:T(8,128)(2,1)S(1)}, u32[]{:S(2)}, u32[]{:S(2)}) collective-permute-start(bf16[4,80,768]{2,1,0:T(8,128)(2,1)S(1)} %pad_maximum_fusion), channel_id=1, source_target_pairs={{0,4},{4,0},{8,12},{12,8},{16,20},{20,16},{24,28},{28,24},{1,5},{5... | collective-permute-start | bytes 1474568 | tf_op jit(solution)/shard_map/ppermute | solution.py:15
  112.6 9.1 %collective-permute-start.23 = (bf16[2,48,768]{2,1,0:T(8,128)(2,1)S(1)}, bf16[2,48,768]{2,1,0:T(8,128)(2,1)S(1)}, u32[]{:S(2)}, u32[]{:S(2)}) collective-permute-start(bf16[2,48,768]{2,1,0:T(8,128)(2,1)S(1)} %pad_maximum_fusion.4), channel_id=1, source_target_pairs={{0,8},{4,12},{8,0},{12,4},{16,24},{20,28},{24,16},{28,20},{1,9},{5... | collective-permute-start | bytes 442376 | tf_op jit(solution)/shard_map/ppermute | solution.py:15
  114.9 14.0 %collective-permute-start.24 = (bf16[2,48,768]{2,1,0:T(8,128)(2,1)S(1)}, bf16[2,48,768]{2,1,0:T(8,128)(2,1)S(1)}, u32[]{:S(2)}, u32[]{:S(2)}) collective-permute-start(bf16[2,48,768]{2,1,0:T(8,128)(2,1)S(1)} %pad_maximum_fusion.3), channel_id=1, source_target_pairs={{0,16},{4,20},{8,24},{12,28},{16,0},{20,4},{24,8},{28,12},{1,17},{... | collective-permute-start | bytes 442376 | tf_op jit(solution)/shard_map/ppermute | solution.py:15
  117.5 11.4 %collective-permute-start.25 = (bf16[2,48,768]{2,1,0:T(8,128)(2,1)S(1)}, bf16[2,48,768]{2,1,0:T(8,128)(2,1)S(1)}, u32[]{:S(2)}, u32[]{:S(2)}) collective-permute-start(bf16[2,48,768]{2,1,0:T(8,128)(2,1)S(1)} %pad_maximum_fusion.2), channel_id=1, source_target_pairs={{0,24},{4,28},{8,16},{12,20},{16,8},{20,12},{24,0},{28,4},{1,25},{... | collective-permute-start | bytes 442376 | tf_op jit(solution)/shard_map/ppermute | solution.py:15
  128.9 7.0 %collective-permute-start.26 = (bf16[48,768]{1,0:T(8,128)(2,1)S(1)}, bf16[48,768]{1,0:T(8,128)(2,1)S(1)}, u32[]{:S(2)}, u32[]{:S(2)}) collective-permute-start(bf16[48,768]{1,0:T(8,128)(2,1)S(1)} %fusion.86), channel_id=1, source_target_pairs={{0,4},{4,0},{8,12},{12,8},{16,20},{20,16},{24,28},{28,24},{1,5},{5... | collective-permute-start | bytes 221192 | tf_op jit(solution)/shard_map/ppermute | solution.py:15
  130.6 7.0 %collective-permute-start.20 = (bf16[80,768]{1,0:T(8,128)(2,1)S(1)}, bf16[80,768]{1,0:T(8,128)(2,1)S(1)}, u32[]{:S(2)}, u32[]{:S(2)}) collective-permute-start(bf16[80,768]{1,0:T(8,128)(2,1)S(1)} %get-tuple-element.22), channel_id=1, source_target_pairs={{0,8},{4,12},{8,0},{12,4},{16,24},{20,28},{24,16},{28,20},{1,9},{5... | collective-permute-start | bytes 368648 | tf_op jit(solution)/shard_map/ppermute | solution.py:15
  133.5 11.4 %collective-permute-start.21 = (bf16[80,768]{1,0:T(8,128)(2,1)S(1)}, bf16[80,768]{1,0:T(8,128)(2,1)S(1)}, u32[]{:S(2)}, u32[]{:S(2)}) collective-permute-start(bf16[80,768]{1,0:T(8,128)(2,1)S(1)} %get-tuple-element.24), channel_id=1, source_target_pairs={{0,16},{4,20},{8,24},{12,28},{16,0},{20,4},{24,8},{28,12},{1,17},{... | collective-permute-start | bytes 368648 | tf_op jit(solution)/shard_map/ppermute | solution.py:15
  134.6 10.3 %collective-permute-start.22 = (bf16[80,768]{1,0:T(8,128)(2,1)S(1)}, bf16[80,768]{1,0:T(8,128)(2,1)S(1)}, u32[]{:S(2)}, u32[]{:S(2)}) collective-permute-start(bf16[80,768]{1,0:T(8,128)(2,1)S(1)} %get-tuple-element.23), channel_id=1, source_target_pairs={{0,24},{4,28},{8,16},{12,20},{16,8},{20,12},{24,0},{28,4},{1,25},{... | collective-permute-start | bytes 368648 | tf_op jit(solution)/shard_map/ppermute | solution.py:15

commit v2 on v1

--- a/solution.py
+++ b/solution.py
@@ -3,6 +3,8 @@
 import jax
 import jax.numpy as jnp
 from jax import lax
+from jax.experimental import pallas as pl
+from jax.experimental.pallas import tpu as pltpu
 from jax.sharding import PartitionSpec as P
 
 HEADS = 24
@@ -72,7 +74,7 @@
     return lax.dot_general(a, b, (((ca,), (cb,)), ((), ())), preferred_element_type=F32)
 
 
-def make_per_device(frame_size, fsdp_size):
+def make_general(frame_size, fsdp_size):
     chips = fsdp_size // 2
 
     def per_device(
@@ -165,13 +167,422 @@
     return per_device
 
 
+LANES = 128
+CHUNKS = 2
+VMEM = 48 * 1024 * 1024
+SHARD, CORE, CHIP, COUNT, OFFSETS = 0, 1, 2, 3, 4
+
+
+def kernel_call(body, name, scalars, operands, out_shape, grid=None, in_specs=None, out_specs=None, scratch=()):
+    whole = lambda shape: pl.BlockSpec(shape, lambda *_: (0,) * len(shape))
+    if in_specs is None:
+        in_specs = [whole(x.shape) for x in operands]
+    if out_specs is None:
+        out_specs = jax.tree.map(lambda x: whole(x.shape), out_shape)
+    return pl.pallas_call(
+        body,
+        out_shape=out_shape,
+        grid_spec=pltpu.PrefetchScalarGridSpec(
+            num_scalar_prefetch=1,
+            grid=grid or (1,),
+            in_specs=in_specs,
+            out_specs=out_specs,
+            scratch_shapes=list(scratch),
+        ),
+        compiler_params=pltpu.CompilerParams(vmem_limit_bytes=VMEM),
+        name=name,
+    )(scalars, *operands)
+
+
+def shaped(shape, dtype=BF16):
+    return jax.ShapeDtypeStruct(shape, dtype)
+
+
+def attend_chip(scalars, queries, keys, values, chip_offset, depth):
+    slots, width = queries.shape[1:]
+    size = width // HEADS
+    heads = max(h for h in (3, 2, 1) if depth % (h * size) == 0)
+    parts = depth // (heads * size)
+
+    def body(sc, q_ref, k_ref, v_ref, out_ref):
+        seen = lax.broadcasted_iota(jnp.int32, (1, slots), 1) < sc[COUNT]
+        for h in range(heads):
+            at = slice(h * size, (h + 1) * size)
+            scores = dot(q_ref[0, :, at], k_ref[0, :, at], 1, 1) * (1.0 / math.sqrt(size))
+            scores = jnp.where(seen, scores, -1e30)
+            exponent = jnp.exp(scores - jnp.max(scores, axis=1, keepdims=True))
+            weights = exponent / jnp.sum(exponent, axis=1, keepdims=True)
+            out_ref[0, :, at] = dot(weights.astype(BF16), v_ref[0, :, at], 1, 0).astype(BF16)
+
+    def block(c, p, sc):
+        return (0, 0, ((sc[CHIP] ^ chip_offset) * 2 + (sc[CORE] ^ c)) * parts + p)
+
+    spec = pl.BlockSpec((1, slots, heads * size), block)
+    return kernel_call(
+        body,
+        "attend",
+        scalars,
+        (queries, keys, values),
+        shaped((2, slots, depth)),
+        grid=(2, parts),
+        in_specs=[spec] * 3,
+        out_specs=pl.BlockSpec((1, slots, heads * size), lambda c, p, sc: (c, 0, p)),
+    )
+
+
+def project_chunk(scalars, columns, weight, weight_near, chip_offset, chunk, size):
+    _, slots, depth = columns.shape
+    w = depth // CHUNKS
+
+    def body(sc, x_ref, own_ref, near_ref, out_ref):
+        out_ref[0] = (dot(x_ref[0], own_ref[...], 1, 0) + dot(x_ref[1], near_ref[...], 1, 0)).astype(BF16)
+
+    cols = pl.BlockSpec((depth, w), lambda k, sc: (0, (sc[SHARD] ^ (2 * chip_offset) ^ k) * CHUNKS + chunk))
+    return kernel_call(
+        body,
+        "project",
+        scalars,
+        (columns, weight, weight_near),
+        shaped((size, slots, w)),
+        grid=(size,),
+        in_specs=[pl.BlockSpec(columns.shape, lambda k, sc: (0, 0, 0)), cols, cols],
+        out_specs=pl.BlockSpec((1, slots, w), lambda k, sc: (k, 0, 0)),
+    )
+
+
+def low_rank(scalars, attended, adapters):
+    slots = attended[0].shape[1]
+    rank = adapters[0].shape[0] // 2
+    chips = len(attended)
+
+    def body(sc, *refs):
+        total = 0.0
+        for k in range(2 * chips):
+            total = total + dot(refs[k // 2][k % 2], refs[chips + k][:rank, :], 1, 1)
+        refs[-1][...] = total.astype(BF16)
+
+    return kernel_call(body, "low_rank", scalars, (*attended, *adapters), shaped((slots, rank)))
+
+
+def base_chunk(scalars, columns, weight, weight_near, low, adapters, residual, target, chunk):
+    _, slots, depth = columns.shape
+    size = len(adapters)
+    rank = adapters[0].shape[0] // 2
+    w = depth // CHUNKS
+
+    def body(sc, x_ref, own_ref, near_ref, low_ref, r_ref, t_ref, *refs):
+        k = pl.program_id(0)
+        up = refs[0][...]
+        for step in range(1, size):
+            up = jnp.where(k == step, refs[step][...], up)
+        total = dot(x_ref[0], own_ref[...], 1, 0) + dot(x_ref[1], near_ref[...], 1, 0)
+        total = total + ADAPTER_SCALE * dot(low_ref[...], up, 1, 0)
+        refs[-1][0] = total + r_ref[0].astype(F32) - t_ref[0].astype(F32)
+
+    place = lambda k, sc: (sc[SHARD] ^ k) * CHUNKS + chunk
+    cols = pl.BlockSpec((depth, w), lambda k, sc: (0, place(k, sc)))
+    tokens = pl.BlockSpec((1, slots, w), lambda k, sc: (0, 0, place(k, sc)))
+    return kernel_call(
+        body,
+        "base",
+        scalars,
+        (columns, weight, weight_near, low, residual, target, *adapters),
+        shaped((size, slots, w), F32),
+        grid=(size,),
+        in_specs=[
+            pl.BlockSpec(columns.shape, lambda k, sc: (0, 0, 0)),
+            cols,
+            cols,
+            pl.BlockSpec(low.shape, lambda k, sc: (0, 0)),
+            tokens,
+            tokens,
+        ]
+        + [pl.BlockSpec((rank, w), lambda k, sc: (1, chunk))] * size,
+        out_specs=pl.BlockSpec((1, slots, w), lambda k, sc: (k, 0, 0)),
+    )
+
+
+def error_chunk(scalars, base, received, low, adapters, before, chunk):
+    size, slots, w = base.shape
+    rank = low.shape[1]
+    width = size * w * CHUNKS
+    last = chunk == CHUNKS - 1
+    back_lanes = -(-slots // LANES) * LANES
+    ups = pl.BlockSpec((rank, w), lambda k, sc: (1, chunk))
+    whole = lambda x: pl.BlockSpec(x.shape, lambda k, sc: (0,) * len(x.shape))
+    scalar = pl.BlockSpec(memory_space=pltpu.SMEM)
+    peers = len(received)
+
+    def body(sc, base_ref, low_ref, *refs):
+        got, refs = refs[:peers], refs[peers:]
+        up_refs, refs = refs[:size], refs[size:]
+        if before:
+            (back_in, loss_in), refs = refs[:2], refs[2:]
+        pieces, (back_out, loss_out) = refs[:size], refs[size:]
+        count = sc[COUNT]
+        tokens = count.astype(F32)
+        valid = lax.broadcasted_iota(jnp.int32, (slots, 1), 0) < count
+        low_state = low_ref[...]
+        back = back_in[...] if before else jnp.zeros((rank, slots), F32)
+        squares = jnp.zeros((slots, w), F32)
+        for k in range(size):
+            error = base_ref[k]
+            for ref in got:
+                error = error + ref[k].astype(F32)
+            error = jnp.where(valid, error, 0.0)
+            squares = squares + error * error
+            cotangent = (2.0 * error / tokens).astype(BF16)
+            back = back + dot(up_refs[k][...], cotangent, 1, 1)
+            pieces[k][:, :w] = (ADAPTER_SCALE * dot(low_state, cotangent, 0, 0)).astype(BF16)
+        loss = jnp.sum(squares)
+        if before:
+            loss = loss + loss_in[0, 0]
+        if last:
+            loss = loss / (tokens * width)
+            lanes = (ADAPTER_SCALE * back).astype(BF16)
+            lanes = jnp.concatenate([lanes, jnp.zeros((rank, back_lanes - slots), BF16)], axis=1)
+            for k in range(size):
+                pieces[k][:, w:] = lanes
+        back_out[...] = back
+        loss_out[0, 0] = loss
+
+    operands = [base, low, *received, *adapters]
+    specs = [whole(base), whole(low), *[whole(x) for x in received], *[ups] * size]
+    if before:
+        operands += list(before)
+        specs += [whole(before[0]), scalar]
+    piece = shaped((rank, w + (back_lanes if last else 0)))
+    out_shape = [piece] * size + [shaped((rank, slots), F32), shaped((1, 1), F32)]
+    out_specs = [whole(x) for x in out_shape[:-1]] + [scalar]
+    out = kernel_call(body, "error", scalars, operands, out_shape, in_specs=specs, out_specs=out_specs)
+    return out[:size], out[size:]
+
+
+def join_adapters(scalars, down, up):
+    _, rank, depth = down.shape
+
+    def body(sc, down_ref, up_ref, out_ref):
+        out_ref[:rank, :] = down_ref[0]
+        out_ref[rank:, :] = up_ref[0]
+
+    return kernel_call(body, "join_adapters", scalars, (down, up), shaped((2 * rank, depth)))
+
+
+def choose_adapters(scalars, blocks, size):
+    def body(sc, *refs):
+        for k in range(size):
+            for scene in range(len(blocks)):
+
+                @pl.when(sc[OFFSETS + k] == scene)
+                def _():
+                    refs[len(blocks) + k][...] = refs[scene][...]
+
+    return kernel_call(body, "choose_adapters", scalars, blocks, [shaped(blocks[0].shape)] * size)
+
+
+def scene_sum(sc, pieces, scene):
+    total = jnp.zeros(pieces[0].shape, F32)
+    for k, piece in enumerate(pieces):
+        total = total + jnp.where(sc[OFFSETS + k] == scene, piece, 0.0)
+    return total
+
+
+def first_refs(sc, pieces, keep, sends, near, far, near_mul, far_mul):
+    for f in range(far):
+        keep[f] = scene_sum(sc, pieces, f * far_mul)
+        for s in range(1, near):
+            sends[s - 1][f] = scene_sum(sc, pieces, f * far_mul + s * near_mul).astype(BF16)
+
+
+def second_refs(keep, received, final, sends, far):
+    for f in range(far):
+        total = keep[f]
+        for ref in received:
+            total = total + ref[f].astype(F32)
+        if f == 0:
+            final[...] = total
+        else:
+            sends[f - 1][...] = total.astype(BF16)
+
+
+def make_chunked(frame_size, fsdp_size):
+    chips = fsdp_size // 2
+    outer, inner = split_axis(frame_size)
+    along_inner = (inner, outer, 1, inner)
+    along_outer = (outer, inner, inner, 1)
+
+    def send_frames(arrays, step):
+        return [xor_send(x, "frame", frame_size, (i + 1) * step) for i, x in enumerate(arrays)]
+
+    def send_shards(arrays):
+        return [arrays[0]] + [xor_send(x, "fsdp", fsdp_size, k) for k, x in enumerate(arrays) if k]
+
+    def first_shapes(rank, w, order):
+        near, far = order[:2]
+        return [shaped((far, rank, w), F32)] + [shaped((far, rank, w))] * (near - 1)
+
+    def second_shapes(rank, w, order):
+        far = order[1]
+        return [shaped((rank, w), F32)] + [shaped((rank, w))] * (far - 1)
+
+    def per_device(
+        queries,
+        keys,
+        values,
+        residual,
+        target,
+        output_weight,
+        down_adapter,
+        up_adapter,
+        scene_of_frame,
+        scene_adapter_row,
+        valid_token_count,
+    ):
+        depth = output_weight.shape[0]
+        rank = down_adapter.shape[1]
+        slots = queries.shape[1]
+        w = depth // CHUNKS
+        shard = lax.axis_index("fsdp").astype(jnp.int32)
+        group = lax.axis_index("frame").astype(jnp.int32)
+        places = [shard, shard % 2, shard // 2, valid_token_count[0]]
+        scalars = jnp.stack(places)
+
+        attended = [attend_chip(scalars, queries, keys, values, c, depth) for c in range(1, chips)]
+        theirs = [xor_send(x, "fsdp", fsdp_size, 2 * (c + 1)) for c, x in enumerate(attended)]
+        own = attend_chip(scalars, queries, keys, values, 0, depth)
+        attended = [own] + attended
+
+        block = join_adapters(scalars, down_adapter, up_adapter)
+        blocks = [block] + [xor_send(block, "frame", frame_size, o * inner) for o in range(1, outer)]
+        blocks = {o * inner: x for o, x in enumerate(blocks)}
+        for lead in range(0, frame_size, inner):
+            for step in range(1, inner):
+                blocks[lead + step] = xor_send(blocks[lead], "frame", frame_size, step)
+        blocks = [blocks[o] for o in range(frame_size)]
+
+        weight_near = xor_send(output_weight, "fsdp", fsdp_size, 1)
+        own_slot = scene_adapter_row[scene_of_frame[0]]
+        slot_list = [own_slot] + [
+            xor_send(own_slot[None], "fsdp", fsdp_size, k)[0] for k in range(1, fsdp_size)
+        ]
+        scalars = jnp.stack(places + [s ^ group for s in slot_list])
+
+        partials = []
+        for chunk in range(CHUNKS):
+            partials.append(
+                [
+                    xor_send(
+                        project_chunk(scalars, x, output_weight, weight_near, c + 1, chunk, fsdp_size),
+                        "fsdp",
+                        fsdp_size,
+                        2 * (c + 1),
+                    )
+                    for c, x in enumerate(theirs)
+                ]
+            )
+
+        columns = [None] * fsdp_size
+        for c, x in enumerate([own] + theirs):
+            columns[2 * c] = x[0]
+            columns[2 * c + 1] = xor_send(x[1], "fsdp", fsdp_size, 1)
+
+        adapters = send_shards(choose_adapters(scalars, blocks, fsdp_size))
+        low = low_rank(scalars, attended, adapters)
+
+        before = None
+        finals = []
+        for chunk in range(CHUNKS):
+            base = base_chunk(
+                scalars, own, output_weight, weight_near, low, adapters, residual, target, chunk
+            )
+            pieces, before = error_chunk(scalars, base, partials[chunk], low, adapters, before, chunk)
+            pieces = send_shards(pieces)
+            if chunk < CHUNKS - 1:
+
+                def first(sc, *refs):
+                    got = [ref[...].astype(F32) for ref in refs[:fsdp_size]]
+                    first_refs(sc, got, refs[fsdp_size], refs[fsdp_size + 1 :], *along_inner)
+
+                keep, *sends = kernel_call(first, "first", scalars, pieces, first_shapes(rank, w, along_inner))
+                got = send_frames(sends, 1)
+
+                def second(sc, keep_ref, *refs):
+                    second_refs(keep_ref, refs[: inner - 1], refs[inner - 1], refs[inner:], outer)
+
+                keep, *sends = kernel_call(
+                    second, "second", scalars, (keep, *got), second_shapes(rank, w, along_inner)
+                )
+                finals.append((keep, *send_frames(sends, inner)))
+
+        down_shapes = first_shapes(rank, depth, along_inner)
+        up_shapes = first_shapes(rank, w, along_outer)
+
+        def first_last(sc, *refs):
+            got, cols, outs = refs[:fsdp_size], refs[fsdp_size : 2 * fsdp_size], refs[2 * fsdp_size :]
+            downs = [dot(p[:, w : w + slots], c[...], 1, 0) for p, c in zip(got, cols)]
+            first_refs(sc, downs, outs[0], outs[1:inner], *along_inner)
+            ups = [p[:, :w].astype(F32) for p in got]
+            first_refs(sc, ups, outs[inner], outs[inner + 1 :], *along_outer)
+
+        out = kernel_call(first_last, "first_last", scalars, (*pieces, *columns), down_shapes + up_shapes)
+        down_keep, up_keep = out[0], out[inner]
+        down_got = send_frames(out[1:inner], 1)
+        up_got = send_frames(out[inner + 1 :], inner)
+
+        def second_last(sc, down_ref, up_ref, *refs):
+            downs, refs = refs[: inner - 1], refs[inner - 1 :]
+            ups, refs = refs[: outer - 1], refs[outer - 1 :]
+            second_refs(down_ref, downs, refs[0], refs[1:outer], outer)
+            second_refs(up_ref, ups, refs[outer], refs[outer + 1 :], inner)
+
+        out = kernel_call(
+            second_last,
+            "second_last",
+            scalars,
+            (down_keep, up_keep, *down_got, *up_got),
+            second_shapes(rank, depth, along_inner) + second_shapes(rank, w, along_outer),
+        )
+        downs = (out[0], *send_frames(out[1:outer], inner))
+        finals.append((out[outer], *send_frames(out[outer + 1 :], 1)))
+        lengths = [len(downs)] + [len(x) for x in finals]
+
+        def finish(sc, *refs):
+            down_ref, up_ref = refs[-2:]
+            start = 0
+            for part, length in enumerate(lengths):
+                total = refs[start][...]
+                for ref in refs[start + 1 : start + length]:
+                    total = total + ref[...].astype(F32)
+                start += length
+                if part == 0:
+                    down_ref[0] = total
+                else:
+                    up_ref[0, :, (part - 1) * w : part * w] = total
+
+        grad = shaped((1, rank, depth), F32)
+        grad_down, grad_up = kernel_call(
+            finish, "finish", scalars, (*downs, *[x for part in finals for x in part]), [grad, grad]
+        )
+        return grad_down, grad_up, before[1][0]
+
+    return per_device
+
+
 def solution(mesh):
+    frame_size, fsdp_size = mesh.shape["frame"], mesh.shape["fsdp"]
     rows = P(("frame", "fsdp"), None, None)
     adapter = P("frame", None, "fsdp")
     vector = P(("frame", "fsdp"))
     placed = (rows, rows, rows, rows, rows, P("fsdp", None), adapter, adapter, vector, P(), vector)
+    chunked = make_chunked(frame_size, fsdp_size)
+    general = make_general(frame_size, fsdp_size)
+
+    def per_device(*operands):
+        depth = operands[5].shape[0]
+        return (chunked if depth % (LANES * CHUNKS) == 0 else general)(*operands)
+
     return jax.shard_map(
-        make_per_device(mesh.shape["frame"], mesh.shape["fsdp"]),
+        per_device,
         mesh=mesh,
         in_specs=placed,
         out_specs=(adapter, adapter, vector),

time: 147 us -> 151 us (1.027)
  Pallas kernels: 0 us -> 42.5 us
  matrix products: 18.5 us -> 0 us
  waiting for transfers between devices: 70.6 us -> 52.2 us
  starting transfers between devices: 30.6 us -> 41.9 us
  local copies, waits for them, and re-layouts: 16.3 us -> 9.09 us
  other arithmetic: 4.09 us -> 0.08 us
  between operations: 6.79 us -> 4.71 us
    pallas_call x0 -> x16, Pallas kernels: none -> 42.5 us  [kernel_call(): pl.pallas_call(body, out_shape=out_shape, grid_spec=pltpu.PrefetchScalarG...]
    dot_general x10 -> x0, matrix products: 18.5 us -> none  [the longest x8 16.6 us: dot(): lax.dot_general(a, b, (((ca,), (cb,)), ((), ())), preferred_element_type=...]
    ppermute x27 -> x37, waiting for transfers between devices: 70.6 us -> 52.2 us  [xor_send(): return lax.ppermute(value, axis, [(i, i ^ offset) for i in range(size)])]
    ppermute x27 -> x37, starting transfers between devices: 30.6 us -> 41.9 us  [xor_send(): return lax.ppermute(value, axis, [(i, i ^ offset) for i in range(size)])]
    unnamed x35 -> x28, local copies, waits for them, and re-layouts: 10.8 us -> 8.31 us
    sub x1 -> x0, other arithmetic: 1.98 us -> none  [attend(): exponent = jnp.exp(scores - peak)]
    dynamic_update_slice x4 -> x0, local copies, waits for them, and re-layouts: 1.93 us -> none  [per_device(): lax.dynamic_update_slice_in_dim(adapters, chosen[step], (shard ^ step) *...]
  transfers between devices with their start and end apart: 27 -> 37, of which waited for: 12 -> 13; matrix products, arithmetic and copies ran while one was open for 16% -> 1% of each run, Pallas kernels for 0% -> 26%
where the time goes in v2:
time: 151 us; the launch traced here: 150 us
  waiting for transfers between devices  52.2 us (35%)
  Pallas kernels  42.5 us (28%)
  starting transfers between devices  41.9 us (28%)
  local copies, waits for them, and re-layouts  9.09 us (6%)
  between operations  4.71 us (3%)
    ppermute x37, waiting for transfers between devices, xor_send(): return lax.ppermute(value, axis, [(i, i ^ offset) for i in range(size)])  52.2 us
    pallas_call x16, Pallas kernels, kernel_call(): pl.pallas_call(body, out_shape=out_shape, grid_spec=pltpu.PrefetchScalarG...  42.5 us
    ppermute x37, starting transfers between devices, xor_send(): return lax.ppermute(value, axis, [(i, i ^ offset) for i in range(size)])  41.9 us
    unnamed x28, local copies, waits for them, and re-layouts  8.31 us
  transfers between devices with their start and end apart: 37, of which 13 were waited for; matrix products, arithmetic and copies ran while one was open for 1% of the time, Pallas kernels for 26%

profile of v2, /device:TPU:0, one launch (start us, length us, event | category | flops | bytes accessed | tf_op | source)
XLA Modules:
  0.0 150.5 jit_solution(1841936291964649596)
XLA Ops:
  1.9 1.3 copy-done.3
  3.2 1.3 copy-done.5
  4.4 1.3 copy-done.7
  5.7 5.3 %attend.3.refs_1_ = bf16[2,192,768]{2,1,0:T(8,128)(2,1)} custom-call(s32[4]{0:T(128)S(1)} %pad_add_fusion.sc, bf16[1,192,3072]{2,1,0:T(8,128)(2,1)S(1)} %copy-done.3, bf16[1,192,3072]{2,1,0:T(8,128)(2,1)S(1)} %copy-done.5, bf16[1,192,3072]{2,1,0:T(8,128)(2,1)S(1)} %copy-done.7), custom_call_target="tpu_custom_call" | custom-call | tf_op jit(solution)/shard_map/attend/pallas_call | solution.py:182
  11.0 2.5 %collective-permute-start.14 = (bf16[2,192,768]{2,1,0:T(8,128)(2,1)}, bf16[2,192,768]{2,1,0:T(8,128)(2,1)S(1)}, u32[]{:S(2)}, u32[]{:S(2)}) collective-permute-start(bf16[2,192,768]{2,1,0:T(8,128)(2,1)} %attend.3.refs_1_), channel_id=1, source_target_pairs={{0,2},{1,3},{2,0},{3,1},{4,6},{5,7},{6,4},{7,5},{8,10},{9,11},{10,... | collective-permute-start | bytes 1769480 | tf_op jit(solution)/shard_map/ppermute | solution.py:17
  13.6 1.2 join_adapters.1.refs_0_
  14.8 3.6 %collective-permute-start.9 = (bf16[128,768]{1,0:T(8,128)(2,1)}, bf16[128,768]{1,0:T(8,128)(2,1)S(1)}, u32[]{:S(2)}, u32[]{:S(2)}) collective-permute-start(bf16[128,768]{1,0:T(8,128)(2,1)} %join_adapters.1.refs_0_), channel_id=1, source_target_pairs={{0,24},{4,28},{8,16},{12,20},{16,8},{20,12},{24,0},{28,4},{1,25},{... | collective-permute-start | bytes 589832 | tf_op jit(solution)/shard_map/ppermute | solution.py:17
  19.7 7.8 %collective-permute-done.2 = s32[1]{0:T(128)} collective-permute-done((s32[1]{0:T(128)}, s32[1]{0:T(128)}, u32[]{:S(2)}, u32[]{:S(2)}) %collective-permute-start.2) | collective-permute-done | bytes 36 | tf_op jit(solution)/shard_map/ppermute | solution.py:17
  27.9 1.0 collective-permute-done
  29.0 1.6 %collective-permute-start.1 = (s32[1]{0:T(128)}, s32[1]{0:T(128)}, u32[]{:S(2)}, u32[]{:S(2)}) collective-permute-start(s32[1]{0:T(128)} %dynamic_slice.3), channel_id=1, source_target_pairs={{0,2},{1,3},{2,0},{3,1},{4,6},{5,7},{6,4},{7,5},{8,10},{9,11},{10,... | collective-permute-start | bytes 20 | tf_op jit(solution)/shard_map/ppermute | solution.py:17
  30.6 2.2 %collective-permute-done.1 = s32[1]{0:T(128)} collective-permute-done((s32[1]{0:T(128)}, s32[1]{0:T(128)}, u32[]{:S(2)}, u32[]{:S(2)}) %collective-permute-start.1) | collective-permute-done | bytes 36 | tf_op jit(solution)/shard_map/ppermute | solution.py:17
  32.8 2.7 %collective-permute-start.7 = (bf16[128,768]{1,0:T(8,128)(2,1)}, bf16[128,768]{1,0:T(8,128)(2,1)}, u32[]{:S(2)}, u32[]{:S(2)}) collective-permute-start(bf16[128,768]{1,0:T(8,128)(2,1)} %join_adapters.1.refs_0_), channel_id=1, source_target_pairs={{0,16},{4,20},{8,24},{12,28},{16,0},{20,4},{24,8},{28,12},{1,17},{... | collective-permute-start | bytes 589832 | tf_op jit(solution)/shard_map/ppermute | solution.py:17
  36.2 1.5 collective-permute-start.4
  37.7 1.3 copy-done.8
  39.0 4.7 %attend.2.refs_0_.x_ref = bf16[2,192,768]{2,1,0:T(8,128)(2,1)S(1)} custom-call(s32[4]{0:T(128)S(1)} %pad_add_fusion.sc, bf16[1,192,3072]{2,1,0:T(8,128)(2,1)S(1)} %copy-done.4, bf16[1,192,3072]{2,1,0:T(8,128)(2,1)S(1)} %copy-done.6, bf16[1,192,3072]{2,1,0:T(8,128)(2,1)S(1)} %copy-done.8), custom_call_target="tpu_custom_call" | custom-call | tf_op jit(solution)/shard_map/attend/pallas_call | solution.py:182
  46.8 1.5 collective-permute-start.6
  48.9 2.3 %copy-done = bf16[768,3072]{1,0:T(8,128)(2,1)S(1)} copy-done((bf16[768,3072]{1,0:T(8,128)(2,1)S(1)}, bf16[768,3072]{1,0:T(8,128)(2,1)}, u32[]{:S(2)}) %copy-start) | copy-done | bytes 4718616
  51.2 4.4 %project.3 = bf16[4,192,384]{2,1,0:T(8,128)(2,1)S(1)} custom-call(s32[8]{0:T(128)S(1)} %stack.37.sc, bf16[2,192,768]{2,1,0:T(8,128)(2,1)S(1)} %collective-permute-done.14.x_ref, bf16[768,3072]{1,0:T(8,128)(2,1)S(1)} %copy-done, bf16[768,3072]{1,0:T(8,128)(2,1)} %collective-permute-done.3.near_ref), custom_call_target="tpu_custom_call" | custom-call | tf_op jit(solution)/shard_map/project/pallas_call | solution.py:182
  55.6 1.6 %collective-permute-start.16 = (bf16[4,192,384]{2,1,0:T(8,128)(2,1)S(1)}, bf16[4,192,384]{2,1,0:T(8,128)(2,1)S(1)}, u32[]{:S(2)}, u32[]{:S(2)}) collective-permute-start(bf16[4,192,384]{2,1,0:T(8,128)(2,1)S(1)} %project.3), channel_id=1, source_target_pairs={{0,2},{1,3},{2,0},{3,1},{4,6},{5,7},{6,4},{7,5},{8,10},{9,11},{10,... | collective-permute-start | bytes 1769480 | tf_op jit(solution)/shard_map/ppermute | solution.py:17
  57.2 4.4 %project.2 = bf16[4,192,384]{2,1,0:T(8,128)(2,1)S(1)} custom-call(s32[8]{0:T(128)S(1)} %stack.37.sc, bf16[2,192,768]{2,1,0:T(8,128)(2,1)S(1)} %collective-permute-done.14.x_ref, bf16[768,3072]{1,0:T(8,128)(2,1)S(1)} %copy-done, bf16[768,3072]{1,0:T(8,128)(2,1)} %collective-permute-done.3.near_ref), custom_call_target="tpu_custom_call" | custom-call | tf_op jit(solution)/shard_map/project/pallas_call | solution.py:182
  62.6 2.0 %choose_adapters.1 = (bf16[128,768]{1,0:T(8,128)(2,1)S(1)}, bf16[128,768]{1,0:T(8,128)(2,1)S(1)}, bf16[128,768]{1,0:T(8,128)(2,1)S(1)}, bf16[128,768]{1,0:T(8,128)(2,1)S(1)}) custom-call(s32[8]{0:T(128)S(1)} %stack.37.sc, bf16[128,768]{1,0:T(8,128)(2,1)} %join_adapters.1.refs_0_, bf16[128,768]{1,0:T(8,128)(2,1)} %collective-permute-done.4.refs_1_, ...), custom_call_target="tpu_custom_call" | custom-call | tf_op jit(solution)/shard_map/choose_adapters/pallas_call | solution.py:182
  65.0 1.5 collective-permute-start.12
  66.6 18.6 %collective-permute-done.12.refs_4_.refs_2_.refs_3_ = bf16[128,768]{1,0:T(8,128)(2,1)S(1)} collective-permute-done((bf16[128,768]{1,0:T(8,128)(2,1)S(1)}, bf16[128,768]{1,0:T(8,128)(2,1)S(1)}, u32[]{:S(2)}, u32[]{:S(2)}) %collective-permute-start.12) | collective-permute-done | bytes 196640 | tf_op jit(solution)/shard_map/ppermute | solution.py:17
  85.2 7.1 %collective-permute-done.13.refs_5_.refs_3_.refs_4_ = bf16[128,768]{1,0:T(8,128)(2,1)S(1)} collective-permute-done((bf16[128,768]{1,0:T(8,128)(2,1)S(1)}, bf16[128,768]{1,0:T(8,128)(2,1)S(1)}, u32[]{:S(2)}, u32[]{:S(2)}) %collective-permute-start.13) | collective-permute-done | bytes 196640 | tf_op jit(solution)/shard_map/ppermute | solution.py:17
  92.3 2.0 %low_rank.1.low_ref = bf16[192,64]{1,0:T(8,128)(2,1)S(1)} custom-call(s32[8]{0:T(128)S(1)} %stack.37.sc, bf16[2,192,768]{2,1,0:T(8,128)(2,1)S(1)} %attend.2.refs_0_.x_ref, bf16[2,192,768]{2,1,0:T(8,128)(2,1)} %attend.3.refs_1_, bf16[128,768]{1,0:T(8,128)(2,1)S(1)} %get-tuple-element.38.refs_2_.refs_0_.refs_1_, ...), custom_call_target="tpu_custom_call" | custom-call | tf_op jit(solution)/shard_map/low_rank/pallas_call | solution.py:182
  94.4 4.9 %base.3.base_ref = f32[4,192,384]{2,1,0:T(8,128)S(1)} custom-call(s32[8]{0:T(128)S(1)} %stack.37.sc, bf16[2,192,768]{2,1,0:T(8,128)(2,1)S(1)} %attend.2.refs_0_.x_ref, bf16[768,3072]{1,0:T(8,128)(2,1)} %own_ref.7, bf16[768,3072]{1,0:T(8,128)(2,1)} %collective-permute-done.3.near_ref, bf16[192,64]{1,0:T(8,128)(2,1)S(1)} %low_rank.1.low_ref, ...), custom_call_target="tpu_custom_call" | custom-call | tf_op jit(solution)/shard_map/base/pallas_call | solution.py:182
  99.3 4.9 %base.2.base_ref = f32[4,192,384]{2,1,0:T(8,128)S(1)} custom-call(s32[8]{0:T(128)S(1)} %stack.37.sc, bf16[2,192,768]{2,1,0:T(8,128)(2,1)S(1)} %attend.2.refs_0_.x_ref, bf16[768,3072]{1,0:T(8,128)(2,1)} %own_ref.7, bf16[768,3072]{1,0:T(8,128)(2,1)} %collective-permute-done.3.near_ref, bf16[192,64]{1,0:T(8,128)(2,1)S(1)} %low_rank.1.low_ref, ...), custom_call_target="tpu_custom_call" | custom-call | tf_op jit(solution)/shard_map/base/pallas_call | solution.py:182
  104.2 1.6 %error.2 = (bf16[64,384]{1,0:T(8,128)(2,1)S(1)}, bf16[64,384]{1,0:T(8,128)(2,1)S(1)}, bf16[64,384]{1,0:T(8,128)(2,1)S(1)}, bf16[64,384]{1,0:T(8,128)(2,1)S(1)}, f32[64,192]{1,0:T(8,128)S(1)}, /*index=5*/f32[1,1]{1,0:T(1,128)}) custom-call(s32[8]{0:T(128)S(1)} %stack.37.sc, f32[4,192,384]{2,1,0:T(8,128)S(1)} %base.3.base_ref, ...), custom_call_target="tpu_custom_call" | custom-call | tf_op jit(solution)/shard_map/error/pallas_call | solution.py:182
  105.8 2.4 %error.3 = (bf16[64,640]{1,0:T(8,128)(2,1)S(1)}, bf16[64,640]{1,0:T(8,128)(2,1)S(1)}, bf16[64,640]{1,0:T(8,128)(2,1)S(1)}, bf16[64,640]{1,0:T(8,128)(2,1)S(1)}, f32[64,192]{1,0:T(8,128)}, /*index=5*/f32[1,1]{1,0:T(1,128)}) custom-call(s32[8]{0:T(128)S(1)} %stack.37.sc, f32[4,192,384]{2,1,0:T(8,128)S(1)} %base.2.base_ref, ...), custom_call_target="tpu_custom_call" | custom-call | tf_op jit(solution)/shard_map/error/pallas_call | solution.py:182
  109.0 1.1 collective-permute-start.19
  110.2 3.5 %collective-permute-done.18.refs_2_ = bf16[64,640]{1,0:T(8,128)(2,1)S(1)} collective-permute-done((bf16[64,640]{1,0:T(8,128)(2,1)S(1)}, bf16[64,640]{1,0:T(8,128)(2,1)S(1)}, u32[]{:S(2)}, u32[]{:S(2)}) %collective-permute-start.18) | collective-permute-done | bytes 81952 | tf_op jit(solution)/shard_map/ppermute | solution.py:17
  114.3 1.4 first_last.1
  115.8 1.6 %collective-permute-start.22 = (bf16[4,64,768]{2,1,0:T(8,128)(2,1)S(1)}, bf16[4,64,768]{2,1,0:T(8,128)(2,1)S(1)}, u32[]{:S(2)}, u32[]{:S(2)}) collective-permute-start(bf16[4,64,768]{2,1,0:T(8,128)(2,1)S(1)} %get-tuple-element.50), channel_id=1, source_target_pairs={{0,4},{4,0},{8,12},{12,8},{16,20},{20,16},{24,28},{28,24},{1,5},{5... | collective-permute-start | bytes 1179656 | tf_op jit(solution)/shard_map/ppermute | solution.py:17
  118.1 1.1 collective-permute-start.31
  119.2 2.6 %collective-permute-done.30.refs_2_ = bf16[64,384]{1,0:T(8,128)(2,1)S(1)} collective-permute-done((bf16[64,384]{1,0:T(8,128)(2,1)S(1)}, bf16[64,384]{1,0:T(8,128)(2,1)S(1)}, u32[]{:S(2)}, u32[]{:S(2)}) %collective-permute-start.30) | collective-permute-done | bytes 49184 | tf_op jit(solution)/shard_map/ppermute | solution.py:17
  123.6 1.6 %collective-permute-start.23 = (bf16[2,64,384]{2,1,0:T(8,128)(2,1)S(1)}, bf16[2,64,384]{2,1,0:T(8,128)(2,1)S(1)}, u32[]{:S(2)}, u32[]{:S(2)}) collective-permute-start(bf16[2,64,384]{2,1,0:T(8,128)(2,1)S(1)} %get-tuple-element.51), channel_id=1, source_target_pairs={{0,8},{4,12},{8,0},{12,4},{16,24},{20,28},{24,16},{28,20},{1,9},{5... | collective-permute-start | bytes 294920 | tf_op jit(solution)/shard_map/ppermute | solution.py:17
  125.1 1.7 %collective-permute-start.24 = (bf16[2,64,384]{2,1,0:T(8,128)(2,1)S(1)}, bf16[2,64,384]{2,1,0:T(8,128)(2,1)S(1)}, u32[]{:S(2)}, u32[]{:S(2)}) collective-permute-start(bf16[2,64,384]{2,1,0:T(8,128)(2,1)S(1)} %get-tuple-element.52), channel_id=1, source_target_pairs={{0,16},{4,20},{8,24},{12,28},{16,0},{20,4},{24,8},{28,12},{1,17},{... | collective-permute-start | bytes 294920 | tf_op jit(solution)/shard_map/ppermute | solution.py:17
  126.8 1.1 collective-permute-start.25
  127.9 3.5 %collective-permute-done.32.refs_0_ = bf16[4,64,384]{2,1,0:T(8,128)(2,1)S(1)} collective-permute-done((bf16[4,64,384]{2,1,0:T(8,128)(2,1)S(1)}, bf16[4,64,384]{2,1,0:T(8,128)(2,1)S(1)}, u32[]{:S(2)}, u32[]{:S(2)}) %collective-permute-start.32) | collective-permute-done | bytes 196640 | tf_op jit(solution)/shard_map/ppermute | solution.py:17
  132.0 1.6 %collective-permute-start.33 = (bf16[64,384]{1,0:T(8,128)(2,1)S(1)}, bf16[64,384]{1,0:T(8,128)(2,1)S(1)}, u32[]{:S(2)}, u32[]{:S(2)}) collective-permute-start(bf16[64,384]{1,0:T(8,128)(2,1)S(1)} %get-tuple-element.65), channel_id=1, source_target_pairs={{0,8},{4,12},{8,0},{12,4},{16,24},{20,28},{24,16},{28,20},{1,9},{5... | collective-permute-start | bytes 147464 | tf_op jit(solution)/shard_map/ppermute | solution.py:17
  133.7 1.7 %collective-permute-start.34 = (bf16[64,384]{1,0:T(8,128)(2,1)S(1)}, bf16[64,384]{1,0:T(8,128)(2,1)S(1)}, u32[]{:S(2)}, u32[]{:S(2)}) collective-permute-start(bf16[64,384]{1,0:T(8,128)(2,1)S(1)} %get-tuple-element.66), channel_id=1, source_target_pairs={{0,16},{4,20},{8,24},{12,28},{16,0},{20,4},{24,8},{28,12},{1,17},{... | collective-permute-start | bytes 147464 | tf_op jit(solution)/shard_map/ppermute | solution.py:17
  136.3 3.0 %collective-permute-start.26 = (bf16[64,768]{1,0:T(8,128)(2,1)S(1)}, bf16[64,768]{1,0:T(8,128)(2,1)S(1)}, u32[]{:S(2)}, u32[]{:S(2)}) collective-permute-start(bf16[64,768]{1,0:T(8,128)(2,1)S(1)} %get-tuple-element.55), channel_id=1, source_target_pairs={{0,8},{4,12},{8,0},{12,4},{16,24},{20,28},{24,16},{28,20},{1,9},{5... | collective-permute-start | bytes 294920 | tf_op jit(solution)/shard_map/ppermute | solution.py:17
  139.3 2.4 %collective-permute-start.28 = (bf16[64,768]{1,0:T(8,128)(2,1)S(1)}, bf16[64,768]{1,0:T(8,128)(2,1)S(1)}, u32[]{:S(2)}, u32[]{:S(2)}) collective-permute-start(bf16[64,768]{1,0:T(8,128)(2,1)S(1)} %get-tuple-element.57), channel_id=1, source_target_pairs={{0,24},{4,28},{8,16},{12,20},{16,8},{20,12},{24,0},{28,4},{1,25},{... | collective-permute-start | bytes 294920 | tf_op jit(solution)/shard_map/ppermute | solution.py:17
  141.7 1.4 collective-permute-start.35
  143.1 1.5 %collective-permute-start.36 = (bf16[64,384]{1,0:T(8,128)(2,1)S(1)}, bf16[64,384]{1,0:T(8,128)(2,1)S(1)}, u32[]{:S(2)}, u32[]{:S(2)}) collective-permute-start(bf16[64,384]{1,0:T(8,128)(2,1)S(1)} %get-tuple-element.69), channel_id=1, source_target_pairs={{0,4},{4,0},{8,12},{12,8},{16,20},{20,16},{24,28},{28,24},{1,5},{5... | collective-permute-start | bytes 147464 | tf_op jit(solution)/shard_map/ppermute | solution.py:17
  144.6 3.1 %collective-permute-done.35.refs_7_ = bf16[64,384]{1,0:T(8,128)(2,1)S(1)} collective-permute-done((bf16[64,384]{1,0:T(8,128)(2,1)S(1)}, bf16[64,384]{1,0:T(8,128)(2,1)S(1)}, u32[]{:S(2)}, u32[]{:S(2)}) %collective-permute-start.35) | collective-permute-done | bytes 49184 | tf_op jit(solution)/shard_map/ppermute | solution.py:17
  147.7 1.4 collective-permute-done.27.refs_2_
  149.2 1.3 finish.1
  (75 shorter events, 10.6 us)
Async XLA Ops:
  0.6 48.2 %collective-permute-start.3 = (bf16[768,3072]{1,0:T(8,128)(2,1)}, bf16[768,3072]{1,0:T(8,128)(2,1)}, u32[]{:S(2)}, u32[]{:S(2)}) collective-permute-start(bf16[768,3072]{1,0:T(8,128)(2,1)} %own_ref.7), channel_id=1, source_target_pairs={{0,1},{1,0},{2,3},{3,2},{4,5},{5,4},{6,7},{7,6},{8,9},{9,8},{10,11... | collective-permute-start | bytes 14155784 | tf_op jit(solution)/shard_map/ppermute | solution.py:17
  1.9 1.3 copy-start.3
  3.2 1.3 copy-start.5
  5.7 7.9 %copy-start.11 = (bf16[1,64,768]{2,1,0:T(8,128)(2,1)S(1)}, bf16[1,64,768]{2,1,0:T(8,128)(2,1)}, u32[]{:S(2)}) copy-start(bf16[1,64,768]{2,1,0:T(8,128)(2,1)} %down_ref.1) | copy-start | bytes 294916
  5.7 7.9 %copy-start.12 = (bf16[1,64,768]{2,1,0:T(8,128)(2,1)S(1)}, bf16[1,64,768]{2,1,0:T(8,128)(2,1)}, u32[]{:S(2)}) copy-start(bf16[1,64,768]{2,1,0:T(8,128)(2,1)} %up_ref.1) | copy-start | bytes 294916
  5.7 13.3 %copy-start.13 = (s32[8]{0:T(128)S(1)}, s32[8]{0:T(128)}, u32[]{:S(2)}) copy-start(s32[8]{0:T(128)} %param.20) | copy-start | bytes 100
  5.7 32.0 %copy-start.4 = (bf16[1,192,3072]{2,1,0:T(8,128)(2,1)S(1)}, bf16[1,192,3072]{2,1,0:T(8,128)(2,1)}, u32[]{:S(2)}) copy-start(bf16[1,192,3072]{2,1,0:T(8,128)(2,1)} %q_ref.3) | copy-start | bytes 3538948
  5.7 32.0 %copy-start.6 = (bf16[1,192,3072]{2,1,0:T(8,128)(2,1)S(1)}, bf16[1,192,3072]{2,1,0:T(8,128)(2,1)}, u32[]{:S(2)}) copy-start(bf16[1,192,3072]{2,1,0:T(8,128)(2,1)} %k_ref.3) | copy-start | bytes 3538948
  11.0 37.3 %collective-permute-start.14 = (bf16[2,192,768]{2,1,0:T(8,128)(2,1)}, bf16[2,192,768]{2,1,0:T(8,128)(2,1)S(1)}, u32[]{:S(2)}, u32[]{:S(2)}) collective-permute-start(bf16[2,192,768]{2,1,0:T(8,128)(2,1)} %attend.3.refs_1_), channel_id=1, source_target_pairs={{0,2},{1,3},{2,0},{3,1},{4,6},{5,7},{6,4},{7,5},{8,10},{9,11},{10,... | collective-permute-start | bytes 1769480 | tf_op jit(solution)/shard_map/ppermute | solution.py:17
  14.8 20.8 %collective-permute-start.9 = (bf16[128,768]{1,0:T(8,128)(2,1)}, bf16[128,768]{1,0:T(8,128)(2,1)S(1)}, u32[]{:S(2)}, u32[]{:S(2)}) collective-permute-start(bf16[128,768]{1,0:T(8,128)(2,1)} %join_adapters.1.refs_0_), channel_id=1, source_target_pairs={{0,24},{4,28},{8,16},{12,20},{16,8},{20,12},{24,0},{28,4},{1,25},{... | collective-permute-start | bytes 589832 | tf_op jit(solution)/shard_map/ppermute | solution.py:17
  18.4 27.8 %collective-permute-start.5 = (bf16[128,768]{1,0:T(8,128)(2,1)}, bf16[128,768]{1,0:T(8,128)(2,1)}, u32[]{:S(2)}, u32[]{:S(2)}) collective-permute-start(bf16[128,768]{1,0:T(8,128)(2,1)} %join_adapters.1.refs_0_), channel_id=1, source_target_pairs={{0,8},{4,12},{8,0},{12,4},{16,24},{20,28},{24,16},{28,20},{1,9},{5... | collective-permute-start | bytes 589832 | tf_op jit(solution)/shard_map/ppermute | solution.py:17
  19.7 7.8 %collective-permute-start.2 = (s32[1]{0:T(128)}, s32[1]{0:T(128)}, u32[]{:S(2)}, u32[]{:S(2)}) collective-permute-start(s32[1]{0:T(128)} %dynamic_slice.3), channel_id=1, source_target_pairs={{0,3},{1,2},{2,1},{3,0},{4,7},{5,6},{6,5},{7,4},{8,11},{9,10},{10,... | collective-permute-start | bytes 20 | tf_op jit(solution)/shard_map/ppermute | solution.py:17
  27.5 1.5 collective-permute-start
  29.0 3.9 %collective-permute-start.1 = (s32[1]{0:T(128)}, s32[1]{0:T(128)}, u32[]{:S(2)}, u32[]{:S(2)}) collective-permute-start(s32[1]{0:T(128)} %dynamic_slice.3), channel_id=1, source_target_pairs={{0,2},{1,3},{2,0},{3,1},{4,6},{5,7},{6,4},{7,5},{8,10},{9,11},{10,... | collective-permute-start | bytes 20 | tf_op jit(solution)/shard_map/ppermute | solution.py:17
  32.8 14.0 %collective-permute-start.7 = (bf16[128,768]{1,0:T(8,128)(2,1)}, bf16[128,768]{1,0:T(8,128)(2,1)}, u32[]{:S(2)}, u32[]{:S(2)}) collective-permute-start(bf16[128,768]{1,0:T(8,128)(2,1)} %join_adapters.1.refs_0_), channel_id=1, source_target_pairs={{0,16},{4,20},{8,24},{12,28},{16,0},{20,4},{24,8},{28,12},{1,17},{... | collective-permute-start | bytes 589832 | tf_op jit(solution)/shard_map/ppermute | solution.py:17
  36.2 25.4 %collective-permute-start.4 = (bf16[128,768]{1,0:T(8,128)(2,1)}, bf16[128,768]{1,0:T(8,128)(2,1)}, u32[]{:S(2)}, u32[]{:S(2)}) collective-permute-start(bf16[128,768]{1,0:T(8,128)(2,1)} %join_adapters.1.refs_0_), channel_id=1, source_target_pairs={{0,4},{4,0},{8,12},{12,8},{16,20},{20,16},{24,28},{28,24},{1,5},{5... | collective-permute-start | bytes 589832 | tf_op jit(solution)/shard_map/ppermute | solution.py:17
  37.7 1.3 copy-start.8
  46.2 16.0 %collective-permute-start.10 = (bf16[128,768]{1,0:T(8,128)(2,1)}, bf16[128,768]{1,0:T(8,128)(2,1)S(1)}, u32[]{:S(2)}, u32[]{:S(2)}) collective-permute-start(bf16[128,768]{1,0:T(8,128)(2,1)} %copy-done.9), channel_id=1, source_target_pairs={{0,4},{4,0},{8,12},{12,8},{16,20},{20,16},{24,28},{28,24},{1,5},{5... | collective-permute-start | bytes 589832 | tf_op jit(solution)/shard_map/ppermute | solution.py:17
  46.8 15.5 %collective-permute-start.6 = (bf16[128,768]{1,0:T(8,128)(2,1)}, bf16[128,768]{1,0:T(8,128)(2,1)S(1)}, u32[]{:S(2)}, u32[]{:S(2)}) collective-permute-start(bf16[128,768]{1,0:T(8,128)(2,1)} %collective-permute-done.5.refs_2_), channel_id=1, source_target_pairs={{0,4},{4,0},{8,12},{12,8},{16,20},{20,16},{24,28},{28,24},{1,5},{5... | collective-permute-start | bytes 589832 | tf_op jit(solution)/shard_map/ppermute | solution.py:17
  48.3 14.0 %collective-permute-start.8 = (bf16[128,768]{1,0:T(8,128)(2,1)}, bf16[128,768]{1,0:T(8,128)(2,1)S(1)}, u32[]{:S(2)}, u32[]{:S(2)}) collective-permute-start(bf16[128,768]{1,0:T(8,128)(2,1)} %collective-permute-done.7.refs_4_), channel_id=1, source_target_pairs={{0,4},{4,0},{8,12},{12,8},{16,20},{20,16},{24,28},{28,24},{1,5},{5... | collective-permute-start | bytes 589832 | tf_op jit(solution)/shard_map/ppermute | solution.py:17
  48.9 2.3 %copy-start = (bf16[768,3072]{1,0:T(8,128)(2,1)S(1)}, bf16[768,3072]{1,0:T(8,128)(2,1)}, u32[]{:S(2)}) copy-start(bf16[768,3072]{1,0:T(8,128)(2,1)} %own_ref.7) | copy-start | bytes 14155780
  55.6 48.6 %collective-permute-start.16 = (bf16[4,192,384]{2,1,0:T(8,128)(2,1)S(1)}, bf16[4,192,384]{2,1,0:T(8,128)(2,1)S(1)}, u32[]{:S(2)}, u32[]{:S(2)}) collective-permute-start(bf16[4,192,384]{2,1,0:T(8,128)(2,1)S(1)} %project.3), channel_id=1, source_target_pairs={{0,2},{1,3},{2,0},{3,1},{4,6},{5,7},{6,4},{7,5},{8,10},{9,11},{10,... | collective-permute-start | bytes 1769480 | tf_op jit(solution)/shard_map/ppermute | solution.py:17
  61.7 44.2 %collective-permute-start.15 = (bf16[4,192,384]{2,1,0:T(8,128)(2,1)S(1)}, bf16[4,192,384]{2,1,0:T(8,128)(2,1)S(1)}, u32[]{:S(2)}, u32[]{:S(2)}) collective-permute-start(bf16[4,192,384]{2,1,0:T(8,128)(2,1)S(1)} %project.2), channel_id=1, source_target_pairs={{0,2},{1,3},{2,0},{3,1},{4,6},{5,7},{6,4},{7,5},{8,10},{9,11},{10,... | collective-permute-start | bytes 1769480 | tf_op jit(solution)/shard_map/ppermute | solution.py:17
  62.3 47.9 %collective-permute-start.20 = (bf16[192,768]{1,0:T(8,128)(2,1)S(1)}, bf16[192,768]{1,0:T(8,128)(2,1)S(1)}, u32[]{:S(2)}, u32[]{:S(2)}) collective-permute-start(bf16[192,768]{1,0:T(8,128)(2,1)S(1)} %get-tuple-element.75), channel_id=1, source_target_pairs={{0,1},{1,0},{2,3},{3,2},{4,5},{5,4},{6,7},{7,6},{8,9},{9,8},{10,11... | collective-permute-start | bytes 884744 | tf_op jit(solution)/shard_map/ppermute | solution.py:17
  64.6 2.0 %collective-permute-start.11 = (bf16[128,768]{1,0:T(8,128)(2,1)S(1)}, bf16[128,768]{1,0:T(8,128)(2,1)S(1)}, u32[]{:S(2)}, u32[]{:S(2)}) collective-permute-start(bf16[128,768]{1,0:T(8,128)(2,1)S(1)} %get-tuple-element.39), channel_id=1, source_target_pairs={{0,1},{1,0},{2,3},{3,2},{4,5},{5,4},{6,7},{7,6},{8,9},{9,8},{10,11... | collective-permute-start | bytes 589832 | tf_op jit(solution)/shard_map/ppermute | solution.py:17
  65.0 20.2 %collective-permute-start.12 = (bf16[128,768]{1,0:T(8,128)(2,1)S(1)}, bf16[128,768]{1,0:T(8,128)(2,1)S(1)}, u32[]{:S(2)}, u32[]{:S(2)}) collective-permute-start(bf16[128,768]{1,0:T(8,128)(2,1)S(1)} %get-tuple-element.40), channel_id=1, source_target_pairs={{0,2},{1,3},{2,0},{3,1},{4,6},{5,7},{6,4},{7,5},{8,10},{9,11},{10,... | collective-permute-start | bytes 589832 | tf_op jit(solution)/shard_map/ppermute | solution.py:17
  66.5 27.9 %copy-start.2 = (bf16[1,192,3072]{2,1,0:T(8,128)(2,1)S(1)}, bf16[1,192,3072]{2,1,0:T(8,128)(2,1)}, u32[]{:S(2)}) copy-start(bf16[1,192,3072]{2,1,0:T(8,128)(2,1)} %t_ref.3) | copy-start | bytes 3538948
  66.5 27.9 %copy-start.1 = (bf16[1,192,3072]{2,1,0:T(8,128)(2,1)S(1)}, bf16[1,192,3072]{2,1,0:T(8,128)(2,1)}, u32[]{:S(2)}) copy-start(bf16[1,192,3072]{2,1,0:T(8,128)(2,1)} %r_ref.3) | copy-start | bytes 3538948
  66.5 43.6 %collective-permute-start.21 = (bf16[192,768]{1,0:T(8,128)(2,1)S(1)}, bf16[192,768]{1,0:T(8,128)(2,1)S(1)}, u32[]{:S(2)}, u32[]{:S(2)}) collective-permute-start(bf16[192,768]{1,0:T(8,128)(2,1)S(1)} %get-tuple-element.73), channel_id=1, source_target_pairs={{0,1},{1,0},{2,3},{3,2},{4,5},{5,4},{6,7},{7,6},{8,9},{9,8},{10,11... | collective-permute-start | bytes 884744 | tf_op jit(solution)/shard_map/ppermute | solution.py:17
  85.2 7.1 %collective-permute-start.13 = (bf16[128,768]{1,0:T(8,128)(2,1)S(1)}, bf16[128,768]{1,0:T(8,128)(2,1)S(1)}, u32[]{:S(2)}, u32[]{:S(2)}) collective-permute-start(bf16[128,768]{1,0:T(8,128)(2,1)S(1)} %get-tuple-element.41), channel_id=1, source_target_pairs={{0,3},{1,2},{2,1},{3,0},{4,7},{5,6},{6,5},{7,4},{8,11},{9,10},{10,... | collective-permute-start | bytes 589832 | tf_op jit(solution)/shard_map/ppermute | solution.py:17
  108.2 1.9 %collective-permute-start.17 = (bf16[64,640]{1,0:T(8,128)(2,1)S(1)}, bf16[64,640]{1,0:T(8,128)(2,1)S(1)}, u32[]{:S(2)}, u32[]{:S(2)}) collective-permute-start(bf16[64,640]{1,0:T(8,128)(2,1)S(1)} %get-tuple-element.45), channel_id=1, source_target_pairs={{0,1},{1,0},{2,3},{3,2},{4,5},{5,4},{6,7},{7,6},{8,9},{9,8},{10,11... | collective-permute-start | bytes 245768 | tf_op jit(solution)/shard_map/ppermute | solution.py:17
  108.4 5.3 %collective-permute-start.18 = (bf16[64,640]{1,0:T(8,128)(2,1)S(1)}, bf16[64,640]{1,0:T(8,128)(2,1)S(1)}, u32[]{:S(2)}, u32[]{:S(2)}) collective-permute-start(bf16[64,640]{1,0:T(8,128)(2,1)S(1)} %get-tuple-element.46), channel_id=1, source_target_pairs={{0,2},{1,3},{2,0},{3,1},{4,6},{5,7},{6,4},{7,5},{8,10},{9,11},{10,... | collective-permute-start | bytes 245768 | tf_op jit(solution)/shard_map/ppermute | solution.py:17
  109.0 5.3 %collective-permute-start.19 = (bf16[64,640]{1,0:T(8,128)(2,1)S(1)}, bf16[64,640]{1,0:T(8,128)(2,1)S(1)}, u32[]{:S(2)}, u32[]{:S(2)}) collective-permute-start(bf16[64,640]{1,0:T(8,128)(2,1)S(1)} %get-tuple-element.47), channel_id=1, source_target_pairs={{0,3},{1,2},{2,1},{3,0},{4,7},{5,6},{6,5},{7,4},{8,11},{9,10},{10,... | collective-permute-start | bytes 245768 | tf_op jit(solution)/shard_map/ppermute | solution.py:17
  115.8 19.9 %collective-permute-start.22 = (bf16[4,64,768]{2,1,0:T(8,128)(2,1)S(1)}, bf16[4,64,768]{2,1,0:T(8,128)(2,1)S(1)}, u32[]{:S(2)}, u32[]{:S(2)}) collective-permute-start(bf16[4,64,768]{2,1,0:T(8,128)(2,1)S(1)} %get-tuple-element.50), channel_id=1, source_target_pairs={{0,4},{4,0},{8,12},{12,8},{16,20},{20,16},{24,28},{28,24},{1,5},{5... | collective-permute-start | bytes 1179656 | tf_op jit(solution)/shard_map/ppermute | solution.py:17
  117.3 1.9 %collective-permute-start.29 = (bf16[64,384]{1,0:T(8,128)(2,1)S(1)}, bf16[64,384]{1,0:T(8,128)(2,1)S(1)}, u32[]{:S(2)}, u32[]{:S(2)}) collective-permute-start(bf16[64,384]{1,0:T(8,128)(2,1)S(1)} %get-tuple-element.59), channel_id=1, source_target_pairs={{0,1},{1,0},{2,3},{3,2},{4,5},{5,4},{6,7},{7,6},{8,9},{9,8},{10,11... | collective-permute-start | bytes 147464 | tf_op jit(solution)/shard_map/ppermute | solution.py:17
  117.4 4.4 %collective-permute-start.30 = (bf16[64,384]{1,0:T(8,128)(2,1)S(1)}, bf16[64,384]{1,0:T(8,128)(2,1)S(1)}, u32[]{:S(2)}, u32[]{:S(2)}) collective-permute-start(bf16[64,384]{1,0:T(8,128)(2,1)S(1)} %get-tuple-element.60), channel_id=1, source_target_pairs={{0,2},{1,3},{2,0},{3,1},{4,6},{5,7},{6,4},{7,5},{8,10},{9,11},{10,... | collective-permute-start | bytes 147464 | tf_op jit(solution)/shard_map/ppermute | solution.py:17
  118.1 4.0 %collective-permute-start.31 = (bf16[64,384]{1,0:T(8,128)(2,1)S(1)}, bf16[64,384]{1,0:T(8,128)(2,1)S(1)}, u32[]{:S(2)}, u32[]{:S(2)}) collective-permute-start(bf16[64,384]{1,0:T(8,128)(2,1)S(1)} %get-tuple-element.61), channel_id=1, source_target_pairs={{0,3},{1,2},{2,1},{3,0},{4,7},{5,6},{6,5},{7,4},{8,11},{9,10},{10,... | collective-permute-start | bytes 147464 | tf_op jit(solution)/shard_map/ppermute | solution.py:17
  122.9 8.5 %collective-permute-start.32 = (bf16[4,64,384]{2,1,0:T(8,128)(2,1)S(1)}, bf16[4,64,384]{2,1,0:T(8,128)(2,1)S(1)}, u32[]{:S(2)}, u32[]{:S(2)}) collective-permute-start(bf16[4,64,384]{2,1,0:T(8,128)(2,1)S(1)} %get-tuple-element.63), channel_id=1, source_target_pairs={{0,4},{4,0},{8,12},{12,8},{16,20},{20,16},{24,28},{28,24},{1,5},{5... | collective-permute-start | bytes 589832 | tf_op jit(solution)/shard_map/ppermute | solution.py:17
  123.6 10.1 %collective-permute-start.23 = (bf16[2,64,384]{2,1,0:T(8,128)(2,1)S(1)}, bf16[2,64,384]{2,1,0:T(8,128)(2,1)S(1)}, u32[]{:S(2)}, u32[]{:S(2)}) collective-permute-start(bf16[2,64,384]{2,1,0:T(8,128)(2,1)S(1)} %get-tuple-element.51), channel_id=1, source_target_pairs={{0,8},{4,12},{8,0},{12,4},{16,24},{20,28},{24,16},{28,20},{1,9},{5... | collective-permute-start | bytes 294920 | tf_op jit(solution)/shard_map/ppermute | solution.py:17
  125.1 10.5 %collective-permute-start.24 = (bf16[2,64,384]{2,1,0:T(8,128)(2,1)S(1)}, bf16[2,64,384]{2,1,0:T(8,128)(2,1)S(1)}, u32[]{:S(2)}, u32[]{:S(2)}) collective-permute-start(bf16[2,64,384]{2,1,0:T(8,128)(2,1)S(1)} %get-tuple-element.52), channel_id=1, source_target_pairs={{0,16},{4,20},{8,24},{12,28},{16,0},{20,4},{24,8},{28,12},{1,17},{... | collective-permute-start | bytes 294920 | tf_op jit(solution)/shard_map/ppermute | solution.py:17
  126.8 8.8 %collective-permute-start.25 = (bf16[2,64,384]{2,1,0:T(8,128)(2,1)S(1)}, bf16[2,64,384]{2,1,0:T(8,128)(2,1)S(1)}, u32[]{:S(2)}, u32[]{:S(2)}) collective-permute-start(bf16[2,64,384]{2,1,0:T(8,128)(2,1)S(1)} %get-tuple-element.53), channel_id=1, source_target_pairs={{0,24},{4,28},{8,16},{12,20},{16,8},{20,12},{24,0},{28,4},{1,25},{... | collective-permute-start | bytes 294920 | tf_op jit(solution)/shard_map/ppermute | solution.py:17
  132.0 9.7 %collective-permute-start.33 = (bf16[64,384]{1,0:T(8,128)(2,1)S(1)}, bf16[64,384]{1,0:T(8,128)(2,1)S(1)}, u32[]{:S(2)}, u32[]{:S(2)}) collective-permute-start(bf16[64,384]{1,0:T(8,128)(2,1)S(1)} %get-tuple-element.65), channel_id=1, source_target_pairs={{0,8},{4,12},{8,0},{12,4},{16,24},{20,28},{24,16},{28,20},{1,9},{5... | collective-permute-start | bytes 147464 | tf_op jit(solution)/shard_map/ppermute | solution.py:17
  133.7 9.5 %collective-permute-start.34 = (bf16[64,384]{1,0:T(8,128)(2,1)S(1)}, bf16[64,384]{1,0:T(8,128)(2,1)S(1)}, u32[]{:S(2)}, u32[]{:S(2)}) collective-permute-start(bf16[64,384]{1,0:T(8,128)(2,1)S(1)} %get-tuple-element.66), channel_id=1, source_target_pairs={{0,16},{4,20},{8,24},{12,28},{16,0},{20,4},{24,8},{28,12},{1,17},{... | collective-permute-start | bytes 147464 | tf_op jit(solution)/shard_map/ppermute | solution.py:17
  136.3 11.5 %collective-permute-start.26 = (bf16[64,768]{1,0:T(8,128)(2,1)S(1)}, bf16[64,768]{1,0:T(8,128)(2,1)S(1)}, u32[]{:S(2)}, u32[]{:S(2)}) collective-permute-start(bf16[64,768]{1,0:T(8,128)(2,1)S(1)} %get-tuple-element.55), channel_id=1, source_target_pairs={{0,8},{4,12},{8,0},{12,4},{16,24},{20,28},{24,16},{28,20},{1,9},{5... | collective-permute-start | bytes 294920 | tf_op jit(solution)/shard_map/ppermute | solution.py:17
  139.3 9.9 %collective-permute-start.27 = (bf16[64,768]{1,0:T(8,128)(2,1)S(1)}, bf16[64,768]{1,0:T(8,128)(2,1)S(1)}, u32[]{:S(2)}, u32[]{:S(2)}) collective-permute-start(bf16[64,768]{1,0:T(8,128)(2,1)S(1)} %get-tuple-element.56), channel_id=1, source_target_pairs={{0,16},{4,20},{8,24},{12,28},{16,0},{20,4},{24,8},{28,12},{1,17},{... | collective-permute-start | bytes 294920 | tf_op jit(solution)/shard_map/ppermute | solution.py:17
  139.3 9.9 %collective-permute-start.28 = (bf16[64,768]{1,0:T(8,128)(2,1)S(1)}, bf16[64,768]{1,0:T(8,128)(2,1)S(1)}, u32[]{:S(2)}, u32[]{:S(2)}) collective-permute-start(bf16[64,768]{1,0:T(8,128)(2,1)S(1)} %get-tuple-element.57), channel_id=1, source_target_pairs={{0,24},{4,28},{8,16},{12,20},{16,8},{20,12},{24,0},{28,4},{1,25},{... | collective-permute-start | bytes 294920 | tf_op jit(solution)/shard_map/ppermute | solution.py:17
  141.7 6.0 %collective-permute-start.35 = (bf16[64,384]{1,0:T(8,128)(2,1)S(1)}, bf16[64,384]{1,0:T(8,128)(2,1)S(1)}, u32[]{:S(2)}, u32[]{:S(2)}) collective-permute-start(bf16[64,384]{1,0:T(8,128)(2,1)S(1)} %get-tuple-element.67), channel_id=1, source_target_pairs={{0,24},{4,28},{8,16},{12,20},{16,8},{20,12},{24,0},{28,4},{1,25},{... | collective-permute-start | bytes 147464 | tf_op jit(solution)/shard_map/ppermute | solution.py:17
  143.1 4.6 %collective-permute-start.36 = (bf16[64,384]{1,0:T(8,128)(2,1)S(1)}, bf16[64,384]{1,0:T(8,128)(2,1)S(1)}, u32[]{:S(2)}, u32[]{:S(2)}) collective-permute-start(bf16[64,384]{1,0:T(8,128)(2,1)S(1)} %get-tuple-element.69), channel_id=1, source_target_pairs={{0,4},{4,0},{8,12},{12,8},{16,20},{20,16},{24,28},{28,24},{1,5},{5... | collective-permute-start | bytes 147464 | tf_op jit(solution)/shard_map/ppermute | solution.py:17
  (3 other events, 2.9 us)

commit v3 on v1

--- a/solution.py
+++ b/solution.py
@@ -3,6 +3,8 @@
 import jax
 import jax.numpy as jnp
 from jax import lax
+from jax.experimental import pallas as pl
+from jax.experimental.pallas import tpu as pltpu
 from jax.sharding import PartitionSpec as P
 
 HEADS = 24
@@ -72,7 +74,7 @@
     return lax.dot_general(a, b, (((ca,), (cb,)), ((), ())), preferred_element_type=F32)
 
 
-def make_per_device(frame_size, fsdp_size):
+def make_general(frame_size, fsdp_size):
     chips = fsdp_size // 2
 
     def per_device(
@@ -165,13 +167,461 @@
     return per_device
 
 
+LANES = 128
+CHUNKS = 2
+VMEM = 20 * 1024 * 1024
+COST = 1.5e9
+ALONE = 52 * 1024 * 1024
+SHARD, CORE, CHIP, COUNT, GROUP, OFFSETS = 0, 1, 2, 3, 4, 5
+
+
+def kernel_call(
+    body, name, scalars, operands, out_shape, micros, grid=None, in_specs=None, out_specs=None, after=(), scratch=(), vmem=VMEM
+):
+    whole = lambda shape: pl.BlockSpec(shape, lambda *_: (0,) * len(shape))
+    inner_body = body
+    ready = len(operands)
+
+    def body(sc, *refs):
+        inner_body(sc, *refs[:ready], *refs[ready + len(after) :])
+
+    if in_specs is None:
+        in_specs = [whole(x.shape) for x in operands]
+    if out_specs is None:
+        out_specs = jax.tree.map(lambda x: whole(x.shape), out_shape)
+    return pl.pallas_call(
+        body,
+        out_shape=out_shape,
+        grid_spec=pltpu.PrefetchScalarGridSpec(
+            num_scalar_prefetch=1,
+            grid=grid or (1,),
+            in_specs=[*in_specs, *[pl.BlockSpec(memory_space=pl.ANY)] * len(after)],
+            out_specs=out_specs,
+            scratch_shapes=list(scratch),
+        ),
+        compiler_params=pltpu.CompilerParams(vmem_limit_bytes=vmem),
+        cost_estimate=pl.CostEstimate(
+            flops=int(micros * COST), bytes_accessed=0, transcendentals=0
+        ),
+        name=name,
+    )(scalars, *operands, *after)
+
+
+def shaped(shape, dtype=BF16):
+    return jax.ShapeDtypeStruct(shape, dtype)
+
+
+def attend_chip(scalars, queries, keys, values, chip_offset, depth, after=()):
+    slots, width = queries.shape[1:]
+    size = width // HEADS
+    heads = depth // size
+    scale = math.log2(math.e) / math.sqrt(size)
+
+    def body(sc, q_ref, k_ref, v_ref, out_ref, held, sems):
+        def copy(c, i):
+            shard = (sc[CHIP] ^ chip_offset) * 2 + (sc[CORE] ^ c)
+            lanes = pl.ds(pl.multiple_of(shard * depth, LANES), depth)
+            return pltpu.make_async_copy((q_ref, k_ref, v_ref)[i].at[0, :, lanes], held.at[c, i], sems.at[c, i])
+
+        for c in range(2):
+            for i in range(3):
+                copy(c, i).start()
+        seen = lax.broadcasted_iota(jnp.int32, (1, slots), 1) < sc[COUNT]
+        at = [slice(h * size, (h + 1) * size) for h in range(heads)]
+        for c in range(2):
+            for i in range(3):
+                copy(c, i).wait()
+            q, k, v = (held.at[c, i] for i in range(3))
+            scores = [jnp.where(seen, dot(q[:, h], k[:, h], 1, 1), -1e30) for h in at]
+            scores = [jnp.exp2((x - jnp.max(x, axis=1, keepdims=True)) * scale) for x in scores]
+            weights = [(x * (1.0 / jnp.sum(x, axis=1, keepdims=True))).astype(BF16) for x in scores]
+            for h, x in zip(at, weights):
+                out_ref[c, :, h] = dot(x, v[:, h], 1, 0).astype(BF16)
+
+    hbm, vmem = pl.BlockSpec(memory_space=pltpu.HBM), pl.BlockSpec(memory_space=pltpu.VMEM)
+    return kernel_call(
+        body,
+        "attend",
+        scalars,
+        (queries, keys, values),
+        shaped((2, slots, depth)),
+        4.0,
+        in_specs=[hbm] * 3,
+        out_specs=vmem,
+        after=after,
+        scratch=[pltpu.VMEM((2, 3, slots, depth), BF16), pltpu.SemaphoreType.DMA((2, 3))],
+        vmem=ALONE,
+    )
+
+
+def project_chunk(scalars, columns, weight, weight_near, chip_offset, chunk, size, after):
+    _, slots, depth = columns.shape
+    w = depth // CHUNKS
+
+    def body(sc, x_ref, own_ref, near_ref, out_ref):
+        for k in range(size):
+            place = (sc[SHARD] ^ (2 * chip_offset) ^ k) * CHUNKS + chunk
+            cols = pl.ds(pl.multiple_of(place * w, LANES), w)
+            out_ref[k] = (dot(x_ref[0], own_ref[:, cols], 1, 0) + dot(x_ref[1], near_ref[:, cols], 1, 0)).astype(BF16)
+
+    vmem = pl.BlockSpec(memory_space=pltpu.VMEM)
+    return kernel_call(
+        body,
+        "project",
+        scalars,
+        (columns, weight, weight_near),
+        shaped((size, slots, w)),
+        4.0,
+        in_specs=[vmem] * 3,
+        out_specs=vmem,
+        after=after,
+    )
+
+
+def base_error(scalars, columns, weight, weight_near, residual, target, size, after):
+    _, slots, depth = columns.shape
+    w = depth // CHUNKS
+
+    def body(sc, x_ref, own_ref, near_ref, r_ref, t_ref, out_ref):
+        place = (sc[SHARD] ^ pl.program_id(1)) * CHUNKS + pl.program_id(0)
+        cols = pl.ds(pl.multiple_of(place * w, LANES), w)
+        total = dot(x_ref[0], own_ref[:, cols], 1, 0) + dot(x_ref[1], near_ref[:, cols], 1, 0)
+        out_ref[0, 0] = total + (r_ref[0].astype(F32) - t_ref[0].astype(F32))
+
+    tokens = pl.BlockSpec((1, slots, w), lambda i, k, sc: (0, 0, (sc[SHARD] ^ k) * CHUNKS + i))
+    vmem = pl.BlockSpec(memory_space=pltpu.VMEM)
+    return kernel_call(
+        body,
+        "base",
+        scalars,
+        (columns, weight, weight_near, residual, target),
+        shaped((CHUNKS, size, slots, w), F32),
+        7.0,
+        grid=(CHUNKS, size),
+        in_specs=[vmem, vmem, vmem, tokens, tokens],
+        out_specs=pl.BlockSpec((1, 1, slots, w), lambda i, k, sc: (i, k, 0, 0)),
+        after=after,
+    )
+
+
+def low_rank(scalars, attended, adapters):
+    slots = attended[0].shape[1]
+    rank = adapters[0].shape[0] // 2
+    chips = len(attended)
+
+    def body(sc, *refs):
+        total = 0.0
+        for k in range(2 * chips):
+            total = total + dot(refs[k // 2][k % 2], refs[chips + k][:rank, :], 1, 1)
+        refs[-1][...] = total.astype(BF16)
+
+    return kernel_call(body, "low_rank", scalars, (*attended, *adapters), shaped((slots, rank)), 2.0)
+
+
+def error_terms(scalars, base, received, low, adapters):
+    chunks, size, slots, w = base.shape
+    rank = low.shape[1]
+    depth = chunks * w
+    back_lanes = -(-slots // LANES) * LANES
+    peers = len(received[0])
+    flat = [x for group in received for x in group]
+
+    def body(sc, base_ref, low_ref, *refs):
+        got, up_refs, refs = refs[: len(flat)], refs[len(flat) : len(flat) + size], refs[len(flat) + size :]
+        pieces, loss_out = refs[:size], refs[size]
+        count = sc[COUNT]
+        tokens = count.astype(F32)
+        valid = lax.broadcasted_iota(jnp.int32, (slots, 1), 0) < count
+        low_state = low_ref[...]
+        back = jnp.zeros((rank, slots), F32)
+        squares = jnp.zeros((slots, w), F32)
+        for i in range(chunks):
+            at = slice(i * w, (i + 1) * w)
+            for k in range(size):
+                up = up_refs[k][:, at]
+                error = base_ref[i, k] + ADAPTER_SCALE * dot(low_state, up, 1, 0)
+                for ref in got[i * peers : (i + 1) * peers]:
+                    error = error + ref[k].astype(F32)
+                error = jnp.where(valid, error, 0.0)
+                squares = squares + error * error
+                cotangent = (2.0 * error / tokens).astype(BF16)
+                back = back + dot(up, cotangent, 1, 1)
+                pieces[k][:, at] = (ADAPTER_SCALE * dot(low_state, cotangent, 0, 0)).astype(BF16)
+        loss_out[0, 0] = jnp.sum(squares) / (tokens * (size * depth))
+        lanes = (ADAPTER_SCALE * back).astype(BF16)
+        lanes = jnp.concatenate([lanes, jnp.zeros((rank, back_lanes - slots), BF16)], axis=1)
+        for k in range(size):
+            pieces[k][:, depth:] = lanes
+
+    whole = lambda x: pl.BlockSpec(x.shape, lambda k, sc: (0,) * len(x.shape))
+    ups = pl.BlockSpec((rank, depth), lambda k, sc: (1, 0))
+    out_shape = [shaped((rank, depth + back_lanes))] * size + [shaped((1, 1), F32)]
+    out = kernel_call(
+        body,
+        "error",
+        scalars,
+        (base, low, *flat, *adapters),
+        out_shape,
+        4.0,
+        in_specs=[whole(base), whole(low), *[whole(x) for x in flat], *[ups] * size],
+        out_specs=[whole(x) for x in out_shape[:-1]] + [pl.BlockSpec(memory_space=pltpu.SMEM)],
+    )
+    return out[:size], out[size]
+
+
+def join_adapters(scalars, down, up, scene, rows, after):
+    _, rank, depth = down.shape
+
+    def body(sc, down_ref, up_ref, scene_ref, row_ref, out_ref, slot_ref):
+        out_ref[:rank, :] = down_ref[0]
+        out_ref[rank:, :] = up_ref[0]
+        slot_ref[0] = row_ref[scene_ref[0]]
+
+    vmem, smem = pl.BlockSpec(memory_space=pltpu.VMEM), pl.BlockSpec(memory_space=pltpu.SMEM)
+    return kernel_call(
+        body,
+        "join",
+        scalars,
+        (down, up, scene, rows),
+        [shaped((2 * rank, depth)), shaped((1,), jnp.int32)],
+        1.0,
+        in_specs=[vmem, vmem, smem, smem],
+        out_specs=[vmem, smem],
+        after=after,
+    )
+
+
+def pack_scalars(scalars, slots, after):
+    def body(sc, *refs):
+        for i in range(OFFSETS):
+            refs[-1][i] = sc[i]
+        for k in range(len(slots)):
+            refs[-1][OFFSETS + k] = refs[k][0] ^ sc[GROUP]
+
+    smem = pl.BlockSpec(memory_space=pltpu.SMEM)
+    return kernel_call(
+        body,
+        "pack",
+        scalars,
+        slots,
+        shaped((OFFSETS + len(slots),), jnp.int32),
+        0.5,
+        in_specs=[smem] * len(slots),
+        out_specs=smem,
+        after=after,
+    )
+
+
+def stack_blocks(scalars, blocks, after):
+    def body(sc, *refs):
+        for i in range(len(blocks)):
+            refs[-1][i] = refs[i][...]
+
+    return kernel_call(
+        body, "stack", scalars, blocks, shaped((len(blocks), *blocks[0].shape)), 1.0, after=after
+    )
+
+
+def choose_adapters(scalars, blocks, size, after):
+    arrays = []
+    for x, _ in blocks:
+        if all(x is not y for y in arrays):
+            arrays.append(x)
+    where = [next(i for i, y in enumerate(arrays) if x is y) for x, _ in blocks]
+    shape = arrays[0].shape
+
+    def body(sc, *refs):
+        for k in range(size):
+            for scene, (_, place) in enumerate(blocks):
+
+                @pl.when(sc[OFFSETS + k] == scene)
+                def _():
+                    ref = refs[where[scene]]
+                    refs[len(arrays) + k][...] = ref[...] if place is None else ref[place]
+
+    return kernel_call(body, "choose", scalars, arrays, [shaped(shape)] * size, 2.0, after=after)
+
+
+def scene_sum(sc, pieces, scene):
+    total = jnp.zeros(pieces[0].shape, F32)
+    for k, piece in enumerate(pieces):
+        total = total + jnp.where(sc[OFFSETS + k] == scene, piece, 0.0)
+    return total
+
+
+def first_refs(sc, pieces, keep, sends, near, far, near_mul, far_mul):
+    for f in range(far):
+        keep[f] = scene_sum(sc, pieces, f * far_mul)
+        for s in range(1, near):
+            sends[s - 1][f] = scene_sum(sc, pieces, f * far_mul + s * near_mul).astype(BF16)
+
+
+def second_refs(keep, received, final, sends, far):
+    for f in range(far):
+        total = keep[f]
+        for ref in received:
+            total = total + ref[f].astype(F32)
+        if f == 0:
+            final[...] = total
+        else:
+            sends[f - 1][...] = total.astype(BF16)
+
+
+def make_chunked(frame_size, fsdp_size):
+    chips = fsdp_size // 2
+    outer, inner = split_axis(frame_size)
+    along_inner = (inner, outer, 1, inner)
+    along_outer = (outer, inner, inner, 1)
+
+    def send_frames(arrays, step):
+        return [xor_send(x, "frame", frame_size, (i + 1) * step) for i, x in enumerate(arrays)]
+
+    def send_shards(arrays):
+        return [arrays[0]] + [xor_send(x, "fsdp", fsdp_size, k) for k, x in enumerate(arrays) if k]
+
+    def first_shapes(rank, w, order):
+        near, far = order[:2]
+        return [shaped((far, rank, w), F32)] + [shaped((far, rank, w))] * (near - 1)
+
+    def second_shapes(rank, w, order):
+        far = order[1]
+        return [shaped((rank, w), F32)] + [shaped((rank, w))] * (far - 1)
+
+    def per_device(
+        queries,
+        keys,
+        values,
+        residual,
+        target,
+        output_weight,
+        down_adapter,
+        up_adapter,
+        scene_of_frame,
+        scene_adapter_row,
+        valid_token_count,
+    ):
+        depth = output_weight.shape[0]
+        rank = down_adapter.shape[1]
+        slots = queries.shape[1]
+        shard = lax.axis_index("fsdp").astype(jnp.int32)
+        group = lax.axis_index("frame").astype(jnp.int32)
+        places = [shard, shard % 2, shard // 2, valid_token_count[0], group]
+        scalars = jnp.stack(places)
+
+        weight_near = xor_send(output_weight, "fsdp", fsdp_size, 1)
+
+        attended = [attend_chip(scalars, queries, keys, values, c, depth) for c in range(1, chips)]
+        theirs = [xor_send(x, "fsdp", fsdp_size, 2 * (c + 1)) for c, x in enumerate(attended)]
+        block, own_slot = join_adapters(
+            scalars, down_adapter, up_adapter, scene_of_frame, scene_adapter_row, attended[:1]
+        )
+        slot_list = send_shards([own_slot] * fsdp_size)
+        outer_blocks = [xor_send(block, "frame", frame_size, o * inner) for o in range(1, outer)]
+        inner_blocks = [xor_send(block, "frame", frame_size, s) for s in range(1, inner)]
+        own = attend_chip(scalars, queries, keys, values, 0, depth, [block])
+        attended = [own] + attended
+
+        partials = []
+        after = [own]
+        for chunk in range(CHUNKS):
+            sent = []
+            for c, x in enumerate(theirs):
+                part = project_chunk(
+                    scalars, x, output_weight, weight_near, c + 1, chunk, fsdp_size, after
+                )
+                sent.append(xor_send(part, "fsdp", fsdp_size, 2 * (c + 1)))
+            partials.append(sent)
+            after = [part, *inner_blocks]
+
+        stacked = stack_blocks(scalars, outer_blocks, [part])
+        far_blocks = [xor_send(stacked, "frame", frame_size, s) for s in range(1, inner)]
+        base = base_error(
+            scalars, own, output_weight, weight_near, residual, target, fsdp_size, [stacked]
+        )
+        blocks = [None] * frame_size
+        for o in range(outer):
+            blocks[o * inner] = (stacked, o - 1) if o else (block, None)
+            for s in range(1, inner):
+                blocks[o * inner + s] = (far_blocks[s - 1], o - 1) if o else (inner_blocks[s - 1], None)
+
+        scalars = pack_scalars(scalars, slot_list, [base])
+        adapters = send_shards(choose_adapters(scalars, blocks, fsdp_size, [base]))
+
+        columns = [None] * fsdp_size
+        for c, x in enumerate([own] + theirs):
+            columns[2 * c] = x[0]
+            columns[2 * c + 1] = xor_send(x[1], "fsdp", fsdp_size, 1)
+
+        low = low_rank(scalars, attended, adapters)
+        pieces, loss = error_terms(scalars, base, partials, low, adapters)
+        pieces = send_shards(pieces)
+
+        cut = depth // 3 // LANES * LANES
+        first_shape = first_shapes(rank, depth + cut, along_inner) + first_shapes(rank, depth - cut, along_outer)
+        second_shape = second_shapes(rank, depth + cut, along_inner) + second_shapes(
+            rank, depth - cut, along_outer
+        )
+
+        def first(sc, *refs):
+            got, cols, outs = refs[:fsdp_size], refs[fsdp_size : 2 * fsdp_size], refs[2 * fsdp_size :]
+            downs = [dot(p[:, depth : depth + slots], c[...], 1, 0) for p, c in zip(got, cols)]
+            down_outs = [ref.at[:, :, :depth] for ref in outs[:inner]]
+            first_refs(sc, downs, down_outs[0], down_outs[1:], *along_inner)
+            ups = [p[:, :cut].astype(F32) for p in got]
+            up_outs = [ref.at[:, :, depth:] for ref in outs[:inner]]
+            first_refs(sc, ups, up_outs[0], up_outs[1:], *along_inner)
+            ups = [p[:, cut:depth].astype(F32) for p in got]
+            first_refs(sc, ups, outs[inner], outs[inner + 1 :], *along_outer)
+
+        out = kernel_call(first, "first", scalars, (*pieces, *columns), first_shape, 2.0)
+        keeps = out[0], out[inner]
+        inner_got = send_frames(out[1:inner], 1)
+        outer_got = send_frames(out[inner + 1 :], inner)
+
+        def second(sc, inner_keep, outer_keep, *refs):
+            inners, refs = refs[: inner - 1], refs[inner - 1 :]
+            outers, refs = refs[: outer - 1], refs[outer - 1 :]
+            second_refs(inner_keep, inners, refs[0], refs[1:outer], outer)
+            second_refs(outer_keep, outers, refs[outer], refs[outer + 1 :], inner)
+
+        out = kernel_call(second, "second", scalars, (*keeps, *inner_got, *outer_got), second_shape, 0.8)
+        one = (out[0], *send_frames(out[1:outer], inner))
+        two = (out[outer], *send_frames(out[outer + 1 :], 1))
+
+        def finish(sc, *refs):
+            down_ref, up_ref = refs[-2:]
+            for part, which in ((0, refs[: len(one)]), (1, refs[len(one) : -2])):
+                total = which[0][...]
+                for ref in which[1:]:
+                    total = total + ref[...].astype(F32)
+                if part == 0:
+                    down_ref[0] = total[:, :depth]
+                    up_ref[0, :, :cut] = total[:, depth:]
+                else:
+                    up_ref[0, :, cut:] = total
+
+        grad = shaped((1, rank, depth), F32)
+        grad_down, grad_up = kernel_call(finish, "finish", scalars, (*one, *two), [grad, grad], 1.3)
+        return grad_down, grad_up, loss[0]
+
+    return per_device
+
+
 def solution(mesh):
+    frame_size, fsdp_size = mesh.shape["frame"], mesh.shape["fsdp"]
     rows = P(("frame", "fsdp"), None, None)
     adapter = P("frame", None, "fsdp")
     vector = P(("frame", "fsdp"))
     placed = (rows, rows, rows, rows, rows, P("fsdp", None), adapter, adapter, vector, P(), vector)
+    chunked = make_chunked(frame_size, fsdp_size)
+    general = make_general(frame_size, fsdp_size)
+
+    def per_device(*operands):
+        depth = operands[5].shape[0]
+        return (chunked if depth % (LANES * CHUNKS) == 0 else general)(*operands)
+
     return jax.shard_map(
-        make_per_device(mesh.shape["frame"], mesh.shape["fsdp"]),
+        per_device,
         mesh=mesh,
         in_specs=placed,
         out_specs=(adapter, adapter, vector),

time: 147 us -> 119 us (0.81)
  Pallas kernels: 0 us -> 36.6 us
  waiting for transfers between devices: 70.6 us -> 44 us
  matrix products: 18.5 us -> 0 us
  local copies, waits for them, and re-layouts: 16.3 us -> 1.47 us
  between operations: 6.79 us -> 2.21 us
  other arithmetic: 4.09 us -> 0.01 us
  starting transfers between devices: 30.6 us -> 34.5 us
    pallas_call x0 -> x14, Pallas kernels: none -> 36.6 us  [kernel_call(): pl.pallas_call(body, out_shape=out_shape, grid_spec=pltpu.PrefetchScalarG...]
    ppermute x27 -> x28, waiting for transfers between devices: 70.6 us -> 44 us  [xor_send(): return lax.ppermute(value, axis, [(i, i ^ offset) for i in range(size)])]
    dot_general x10 -> x0, matrix products: 18.5 us -> none  [the longest x8 16.6 us: dot(): lax.dot_general(a, b, (((ca,), (cb,)), ((), ())), preferred_element_type=...]
    unnamed x35 -> x16, local copies, waits for them, and re-layouts: 10.8 us -> 1.31 us
    ppermute x27 -> x28, starting transfers between devices: 30.6 us -> 34.5 us  [xor_send(): return lax.ppermute(value, axis, [(i, i ^ offset) for i in range(size)])]
    sub x1 -> x0, other arithmetic: 1.98 us -> none  [attend(): exponent = jnp.exp(scores - peak)]
    dynamic_update_slice x4 -> x0, local copies, waits for them, and re-layouts: 1.93 us -> none  [per_device(): lax.dynamic_update_slice_in_dim(adapters, chosen[step], (shard ^ step) *...]
  transfers between devices with their start and end apart: 27 -> 28, of which waited for: 12 -> 11; matrix products, arithmetic and copies ran while one was open for 16% -> 0% of each run, Pallas kernels for 0% -> 28%
where the time goes in v3:
time: 119 us
  waiting for transfers between devices  44 us (37%)
  Pallas kernels  36.6 us (31%)
  starting transfers between devices  34.5 us (29%)
  between operations  2.21 us (2%)
  local copies, waits for them, and re-layouts  1.47 us (1%)
    ppermute x28, waiting for transfers between devices, xor_send(): return lax.ppermute(value, axis, [(i, i ^ offset) for i in range(size)])  44 us
    pallas_call x14, Pallas kernels, kernel_call(): pl.pallas_call(body, out_shape=out_shape, grid_spec=pltpu.PrefetchScalarG...  36.6 us
    ppermute x28, starting transfers between devices, xor_send(): return lax.ppermute(value, axis, [(i, i ^ offset) for i in range(size)])  34.5 us
  transfers between devices with their start and end apart: 28, of which 11 were waited for; matrix products, arithmetic and copies ran while one was open for 0% of the time, Pallas kernels for 28%

profile of v3, /device:TPU:0, one launch (start us, length us, event | category | flops | bytes accessed | tf_op | source)
XLA Modules:
  0.0 118.8 jit_solution(1844522607173989469)
XLA Ops:
  0.6 0.5 collective-permute-start.3
  1.9 1.3 %copy-done = bf16[1,192,3072]{2,1,0:T(8,128)(2,1)S(1)} copy-done((bf16[1,192,3072]{2,1,0:T(8,128)(2,1)S(1)}, bf16[1,192,3072]{2,1,0:T(8,128)(2,1)}, u32[]{:S(2)}) %copy-start) | copy-done | bytes 1179672
  3.2 3.2 %attend.2.refs_4_.refs_1_ = bf16[2,192,768]{2,1,0:T(8,128)(2,1)S(1)} custom-call(s32[5]{0:T(128)S(1)} %stack.20.sc, bf16[1,192,3072]{2,1,0:T(8,128)(2,1)S(1)} %copy-done, bf16[1,192,3072]{2,1,0:T(8,128)(2,1)} %refs_1_.8, bf16[1,192,3072]{2,1,0:T(8,128)(2,1)} %refs_2_.4), custom_call_target="tpu_custom_call" | custom-call | flops 6000000000 | tf_op jit(solution)/shard_map/attend/pallas_call | solution.py:192
  6.3 2.6 %collective-permute-start.7 = (bf16[2,192,768]{2,1,0:T(8,128)(2,1)S(1)}, bf16[2,192,768]{2,1,0:T(8,128)(2,1)S(1)}, u32[]{:S(2)}, u32[]{:S(2)}) collective-permute-start(bf16[2,192,768]{2,1,0:T(8,128)(2,1)S(1)} %attend.2.refs_4_.refs_1_), channel_id=1, source_target_pairs={{0,2},{1,3},{2,0},{3,1},{4,6},{5,7},{6,4},{7,5},{8,10},{9,11},{10,... | collective-permute-start | bytes 1769480 | tf_op jit(solution)/shard_map/ppermute | solution.py:17
  9.6 1.6 %join.1 = (bf16[128,768]{1,0:T(8,128)(2,1)S(1)}, s32[1]{0:T(128)}) custom-call(s32[5]{0:T(128)S(1)} %stack.20.sc, bf16[1,64,768]{2,1,0:T(8,128)(2,1)S(1)} %copy-done.3, bf16[1,64,768]{2,1,0:T(8,128)(2,1)S(1)} %copy-done.4, s32[1]{0:T(128)S(6)} %copy.14.refs_2_, s32[8]{0:T(128)S(1)} %copy-done.5, bf16[2,192,768]{2,1,0:T(8,128)(2,1)S(1)} %attend.2.refs_4_.refs_1_), custom_call_target="tpu_custom_call" | custom-call | flops 1500000000 | tf_op jit(solution)/shard_map/join/pallas_call | solution.py:192
  11.2 1.6 %collective-permute-start.8 = (bf16[128,768]{1,0:T(8,128)(2,1)S(1)}, bf16[128,768]{1,0:T(8,128)(2,1)S(1)}, u32[]{:S(2)}, u32[]{:S(2)}) collective-permute-start(bf16[128,768]{1,0:T(8,128)(2,1)S(1)} %get-tuple-element.29.refs_3_.refs_0_), channel_id=1, source_target_pairs={{0,4},{4,0},{8,12},{12,8},{16,20},{20,16},{24,28},{28,24},{1,5},{5... | collective-permute-start | bytes 589832 | tf_op jit(solution)/shard_map/ppermute | solution.py:17
  12.8 1.6 %collective-permute-start.4 = (bf16[128,768]{1,0:T(8,128)(2,1)S(1)}, bf16[128,768]{1,0:T(8,128)(2,1)S(1)}, u32[]{:S(2)}, u32[]{:S(2)}) collective-permute-start(bf16[128,768]{1,0:T(8,128)(2,1)S(1)} %get-tuple-element.29.refs_3_.refs_0_), channel_id=1, source_target_pairs={{0,8},{4,12},{8,0},{12,4},{16,24},{20,28},{24,16},{28,20},{1,9},{5... | collective-permute-start | bytes 589832 | tf_op jit(solution)/shard_map/ppermute | solution.py:17
  14.4 2.6 %collective-permute-start.5 = (bf16[128,768]{1,0:T(8,128)(2,1)S(1)}, bf16[128,768]{1,0:T(8,128)(2,1)S(1)}, u32[]{:S(2)}, u32[]{:S(2)}) collective-permute-start(bf16[128,768]{1,0:T(8,128)(2,1)S(1)} %get-tuple-element.29.refs_3_.refs_0_), channel_id=1, source_target_pairs={{0,16},{4,20},{8,24},{12,28},{16,0},{20,4},{24,8},{28,12},{1,17},{... | collective-permute-start | bytes 589832 | tf_op jit(solution)/shard_map/ppermute | solution.py:17
  17.0 3.1 %attend.3.refs_3_.refs_0_ = bf16[2,192,768]{2,1,0:T(8,128)(2,1)S(1)} custom-call(s32[5]{0:T(128)S(1)} %stack.20.sc, bf16[1,192,3072]{2,1,0:T(8,128)(2,1)S(1)} %copy-done, bf16[1,192,3072]{2,1,0:T(8,128)(2,1)} %refs_1_.8, bf16[1,192,3072]{2,1,0:T(8,128)(2,1)} %refs_2_.4, bf16[128,768]{1,0:T(8,128)(2,1)S(1)} %get-tuple-element.29.refs_3_.refs_0_), custom_call_target="tpu_custom_call" | custom-call | flops 6000000000 | tf_op jit(solution)/shard_map/attend/pallas_call | solution.py:192
  20.2 2.7 %collective-permute-done.7.refs_0_ = bf16[2,192,768]{2,1,0:T(8,128)(2,1)S(1)} collective-permute-done((bf16[2,192,768]{2,1,0:T(8,128)(2,1)S(1)}, bf16[2,192,768]{2,1,0:T(8,128)(2,1)S(1)}, u32[]{:S(2)}, u32[]{:S(2)}) %collective-permute-start.7) | collective-permute-done | bytes 589856 | tf_op jit(solution)/shard_map/ppermute | solution.py:17
  22.9 3.8 %collective-permute-start.6 = (bf16[128,768]{1,0:T(8,128)(2,1)S(1)}, bf16[128,768]{1,0:T(8,128)(2,1)S(1)}, u32[]{:S(2)}, u32[]{:S(2)}) collective-permute-start(bf16[128,768]{1,0:T(8,128)(2,1)S(1)} %get-tuple-element.29.refs_3_.refs_0_), channel_id=1, source_target_pairs={{0,24},{4,28},{8,16},{12,20},{16,8},{20,12},{24,0},{28,4},{1,25},{... | collective-permute-start | bytes 589832 | tf_op jit(solution)/shard_map/ppermute | solution.py:17
  26.8 4.3 %project.2.refs_3_ = bf16[4,192,384]{2,1,0:T(8,128)(2,1)S(1)} custom-call(s32[5]{0:T(128)S(1)} %stack.20.sc, bf16[2,192,768]{2,1,0:T(8,128)(2,1)S(1)} %collective-permute-done.7.refs_0_, bf16[768,3072]{1,0:T(8,128)(2,1)S(1)} %bitcast.14, bf16[768,3072]{1,0:T(8,128)(2,1)} %collective-permute-done.3.refs_2_, bf16[2,192,768]{2,1,0:T(8,128)(2,1)S(1)} %attend.3.refs_3_.refs_0_), custom_call_target="tpu_custom_call" | custom-call | flops 6000000000 | tf_op jit(solution)/shard_map/project/pallas_call | solution.py:192
  31.1 1.6 %collective-permute-start.1 = (s32[1]{0:T(128)}, s32[1]{0:T(128)}, u32[]{:S(2)}, u32[]{:S(2)}) collective-permute-start(s32[1]{0:T(128)} %get-tuple-element.28.refs_0_), channel_id=1, source_target_pairs={{0,2},{1,3},{2,0},{3,1},{4,6},{5,7},{6,4},{7,5},{8,10},{9,11},{10,... | collective-permute-start | bytes 20 | tf_op jit(solution)/shard_map/ppermute | solution.py:17
  32.6 4.3 %project.3.refs_3_ = bf16[4,192,384]{2,1,0:T(8,128)(2,1)S(1)} custom-call(s32[5]{0:T(128)S(1)} %stack.20.sc, bf16[2,192,768]{2,1,0:T(8,128)(2,1)S(1)} %collective-permute-done.7.refs_0_, bf16[768,3072]{1,0:T(8,128)(2,1)S(1)} %bitcast.14, bf16[768,3072]{1,0:T(8,128)(2,1)} %collective-permute-done.3.refs_2_, bf16[4,192,384]{2,1,0:T(8,128)(2,1)S(1)} %project.2.refs_3_, ...), custom_call_target="tpu_custom_call" | custom-call | flops 6000000000 | tf_op jit(solution)/shard_map/project/pallas_call | solution.py:192
  37.0 0.4 collective-permute-start.2
  37.3 1.5 %collective-permute-start.14 = (bf16[4,192,384]{2,1,0:T(8,128)(2,1)S(1)}, bf16[4,192,384]{2,1,0:T(8,128)(2,1)S(1)}, u32[]{:S(2)}, u32[]{:S(2)}) collective-permute-start(bf16[4,192,384]{2,1,0:T(8,128)(2,1)S(1)} %project.3.refs_3_), channel_id=1, source_target_pairs={{0,2},{1,3},{2,0},{3,1},{4,6},{5,7},{6,4},{7,5},{8,10},{9,11},{10,... | collective-permute-start | bytes 1769480 | tf_op jit(solution)/shard_map/ppermute | solution.py:17
  38.9 0.6 stack.21.refs_5_.refs_2_
  39.5 1.6 %collective-permute-start.9 = (bf16[3,128,768]{2,1,0:T(8,128)(2,1)S(1)}, bf16[3,128,768]{2,1,0:T(8,128)(2,1)S(1)}, u32[]{:S(2)}, u32[]{:S(2)}) collective-permute-start(bf16[3,128,768]{2,1,0:T(8,128)(2,1)S(1)} %stack.21.refs_5_.refs_2_), channel_id=1, source_target_pairs={{0,4},{4,0},{8,12},{12,8},{16,20},{20,16},{24,28},{28,24},{1,5},{5... | collective-permute-start | bytes 1769480 | tf_op jit(solution)/shard_map/ppermute | solution.py:17
  41.0 7.1 %base.1.refs_4_.refs_0_ = f32[2,4,192,384]{3,2,1,0:T(8,128)S(1)} custom-call(s32[5]{0:T(128)S(1)} %stack.20.sc, bf16[2,192,768]{2,1,0:T(8,128)(2,1)S(1)} %attend.3.refs_3_.refs_0_, bf16[768,3072]{1,0:T(8,128)(2,1)S(1)} %bitcast.14, bf16[768,3072]{1,0:T(8,128)(2,1)} %collective-permute-done.3.refs_2_, bf16[1,192,3072]{2,1,0:T(8,128)(2,1)S(1)} %copy-done.1, ...), custom_call_target="tpu_custom_call" | custom-call | flops 10499999744 | tf_op jit(solution)/shard_map/base/pallas_call | solution.py:192
  48.2 0.6 collective-permute-start.13
  48.7 3.6 %pack.1.sc = s32[9]{0:T(128)S(1)} custom-call(s32[5]{0:T(128)S(1)} %stack.20.sc, s32[1]{0:T(128)} %get-tuple-element.28.refs_0_, s32[1]{0:T(128)} %collective-permute-done.refs_1_, s32[1]{0:T(128)} %collective-permute-done.1.refs_2_, s32[1]{0:T(128)} %collective-permute-done.2.refs_3_, f32[2,4,192,384]{3,2,1,0:T(8,128)S(1)} %base.1.refs_4_.refs_0_), custom_call_target="tpu_custom_call" | custom-call | flops 750000000 | tf_op jit(solution)/shard_map/pack/pallas_call | solution.py:192
  52.3 2.4 %collective-permute-done.9.refs_3_ = bf16[3,128,768]{2,1,0:T(8,128)(2,1)S(1)} collective-permute-done((bf16[3,128,768]{2,1,0:T(8,128)(2,1)S(1)}, bf16[3,128,768]{2,1,0:T(8,128)(2,1)S(1)}, u32[]{:S(2)}, u32[]{:S(2)}) %collective-permute-start.9) | collective-permute-done | bytes 589856 | tf_op jit(solution)/shard_map/ppermute | solution.py:17
  54.8 1.0 choose.1
  55.9 0.6 collective-permute-start.11
  56.4 1.3 %collective-permute-start.12 = (bf16[128,768]{1,0:T(8,128)(2,1)S(1)}, bf16[128,768]{1,0:T(8,128)(2,1)S(1)}, u32[]{:S(2)}, u32[]{:S(2)}) collective-permute-start(bf16[128,768]{1,0:T(8,128)(2,1)S(1)} %get-tuple-element.33), channel_id=1, source_target_pairs={{0,3},{1,2},{2,1},{3,0},{4,7},{5,6},{6,5},{7,4},{8,11},{9,10},{10,... | collective-permute-start | bytes 589832 | tf_op jit(solution)/shard_map/ppermute | solution.py:17
  57.8 0.4 collective-permute-start.18
  58.2 12.2 %collective-permute-done.11.refs_4_.refs_6_ = bf16[128,768]{1,0:T(8,128)(2,1)S(1)} collective-permute-done((bf16[128,768]{1,0:T(8,128)(2,1)S(1)}, bf16[128,768]{1,0:T(8,128)(2,1)S(1)}, u32[]{:S(2)}, u32[]{:S(2)}) %collective-permute-start.11) | collective-permute-done | bytes 196640 | tf_op jit(solution)/shard_map/ppermute | solution.py:17
  70.4 3.0 %collective-permute-done.12.refs_5_.refs_7_ = bf16[128,768]{1,0:T(8,128)(2,1)S(1)} collective-permute-done((bf16[128,768]{1,0:T(8,128)(2,1)S(1)}, bf16[128,768]{1,0:T(8,128)(2,1)S(1)}, u32[]{:S(2)}, u32[]{:S(2)}) %collective-permute-start.12) | collective-permute-done | bytes 196640 | tf_op jit(solution)/shard_map/ppermute | solution.py:17
  73.3 1.0 low_rank.1.refs_1_
  74.3 3.2 %error.1 = (bf16[64,1024]{1,0:T(8,128)(2,1)S(1)}, bf16[64,1024]{1,0:T(8,128)(2,1)S(1)}, bf16[64,1024]{1,0:T(8,128)(2,1)S(1)}, bf16[64,1024]{1,0:T(8,128)(2,1)S(1)}, f32[1,1]{1,0:T(1,128)}) custom-call(s32[9]{0:T(128)S(1)} %pack.1.sc, f32[2,4,192,384]{3,2,1,0:T(8,128)S(1)} %base.1.refs_4_.refs_0_, bf16[192,64]{1,0:T(8,128)(2,1)S(1)} %low_rank.1.refs_1_, ...), custom_call_target="tpu_custom_call" | custom-call | flops 6000000000 | tf_op jit(solution)/shard_map/error/pallas_call | solution.py:192
  77.5 0.5 collective-permute-start.15
  78.0 1.5 %collective-permute-start.16 = (bf16[64,1024]{1,0:T(8,128)(2,1)S(1)}, bf16[64,1024]{1,0:T(8,128)(2,1)S(1)}, u32[]{:S(2)}, u32[]{:S(2)}) collective-permute-start(bf16[64,1024]{1,0:T(8,128)(2,1)S(1)} %get-tuple-element.36), channel_id=1, source_target_pairs={{0,2},{1,3},{2,0},{3,1},{4,6},{5,7},{6,4},{7,5},{8,10},{9,11},{10,... | collective-permute-start | bytes 393224 | tf_op jit(solution)/shard_map/ppermute | solution.py:17
  79.6 4.8 %collective-permute-done.16.refs_2_ = bf16[64,1024]{1,0:T(8,128)(2,1)S(1)} collective-permute-done((bf16[64,1024]{1,0:T(8,128)(2,1)S(1)}, bf16[64,1024]{1,0:T(8,128)(2,1)S(1)}, u32[]{:S(2)}, u32[]{:S(2)}) %collective-permute-start.16) | collective-permute-done | bytes 131104 | tf_op jit(solution)/shard_map/ppermute | solution.py:17
  84.4 1.1 collective-permute-done.17.refs_3_
  85.4 1.7 %first.1 = (f32[4,64,1024]{2,1,0:T(8,128)S(1)}, bf16[4,64,1024]{2,1,0:T(8,128)(2,1)S(1)}, f32[2,64,512]{2,1,0:T(8,128)S(1)}, bf16[2,64,512]{2,1,0:T(8,128)(2,1)S...) custom-call(s32[9]{0:T(128)S(1)} %pack.1.sc, bf16[64,1024]{1,0:T(8,128)(2,1)S(1)} %get-tuple-element.34.refs_0_, ...), custom_call_target="tpu_custom_call" | custom-call | flops 3000000000 | tf_op jit(solution)/shard_map/first/pallas_call | solution.py:192
  87.1 1.6 %collective-permute-start.20 = (bf16[4,64,1024]{2,1,0:T(8,128)(2,1)S(1)}, bf16[4,64,1024]{2,1,0:T(8,128)(2,1)S(1)}, u32[]{:S(2)}, u32[]{:S(2)}) collective-permute-start(bf16[4,64,1024]{2,1,0:T(8,128)(2,1)S(1)} %get-tuple-element.40), channel_id=1, source_target_pairs={{0,4},{4,0},{8,12},{12,8},{16,20},{20,16},{24,28},{28,24},{1,5},{5... | collective-permute-start | bytes 1572872 | tf_op jit(solution)/shard_map/ppermute | solution.py:17
  88.7 0.8 collective-permute-start.22
  89.4 3.6 %collective-permute-start.23 = (bf16[2,64,512]{2,1,0:T(8,128)(2,1)S(1)}, bf16[2,64,512]{2,1,0:T(8,128)(2,1)S(1)}, u32[]{:S(2)}, u32[]{:S(2)}) collective-permute-start(bf16[2,64,512]{2,1,0:T(8,128)(2,1)S(1)} %get-tuple-element.43), channel_id=1, source_target_pairs={{0,24},{4,28},{8,16},{12,20},{16,8},{20,12},{24,0},{28,4},{1,25},{... | collective-permute-start | bytes 393224 | tf_op jit(solution)/shard_map/ppermute | solution.py:17
  93.0 2.7 %collective-permute-done.21.refs_3_ = bf16[2,64,512]{2,1,0:T(8,128)(2,1)S(1)} collective-permute-done((bf16[2,64,512]{2,1,0:T(8,128)(2,1)S(1)}, bf16[2,64,512]{2,1,0:T(8,128)(2,1)S(1)}, u32[]{:S(2)}, u32[]{:S(2)}) %collective-permute-start.21) | collective-permute-done | bytes 131104 | tf_op jit(solution)/shard_map/ppermute | solution.py:17
  95.7 5.8 %collective-permute-done.22.refs_4_ = bf16[2,64,512]{2,1,0:T(8,128)(2,1)S(1)} collective-permute-done((bf16[2,64,512]{2,1,0:T(8,128)(2,1)S(1)}, bf16[2,64,512]{2,1,0:T(8,128)(2,1)S(1)}, u32[]{:S(2)}, u32[]{:S(2)}) %collective-permute-start.22) | collective-permute-done | bytes 131104 | tf_op jit(solution)/shard_map/ppermute | solution.py:17
  101.5 0.2 collective-permute-done.20.refs_2_
  101.7 0.7 second.1
  102.4 2.8 %collective-permute-start.24 = (bf16[64,1024]{1,0:T(8,128)(2,1)S(1)}, bf16[64,1024]{1,0:T(8,128)(2,1)S(1)}, u32[]{:S(2)}, u32[]{:S(2)}) collective-permute-start(bf16[64,1024]{1,0:T(8,128)(2,1)S(1)} %get-tuple-element.45), channel_id=1, source_target_pairs={{0,8},{4,12},{8,0},{12,4},{16,24},{20,28},{24,16},{28,20},{1,9},{5... | collective-permute-start | bytes 393224 | tf_op jit(solution)/shard_map/ppermute | solution.py:17
  105.3 2.4 %collective-permute-start.26 = (bf16[64,1024]{1,0:T(8,128)(2,1)S(1)}, bf16[64,1024]{1,0:T(8,128)(2,1)S(1)}, u32[]{:S(2)}, u32[]{:S(2)}) collective-permute-start(bf16[64,1024]{1,0:T(8,128)(2,1)S(1)} %get-tuple-element.47), channel_id=1, source_target_pairs={{0,24},{4,28},{8,16},{12,20},{16,8},{20,12},{24,0},{28,4},{1,25},{... | collective-permute-start | bytes 393224 | tf_op jit(solution)/shard_map/ppermute | solution.py:17
  107.6 0.7 collective-permute-start.27
  108.3 3.6 %collective-permute-done.27.refs_5_ = bf16[64,512]{1,0:T(8,128)(2,1)S(1)} collective-permute-done((bf16[64,512]{1,0:T(8,128)(2,1)S(1)}, bf16[64,512]{1,0:T(8,128)(2,1)S(1)}, u32[]{:S(2)}, u32[]{:S(2)}) %collective-permute-start.27) | collective-permute-done | bytes 65568 | tf_op jit(solution)/shard_map/ppermute | solution.py:17
  111.9 5.6 %collective-permute-done.25.refs_2_ = bf16[64,1024]{1,0:T(8,128)(2,1)S(1)} collective-permute-done((bf16[64,1024]{1,0:T(8,128)(2,1)S(1)}, bf16[64,1024]{1,0:T(8,128)(2,1)S(1)}, u32[]{:S(2)}, u32[]{:S(2)}) %collective-permute-start.25) | collective-permute-done | bytes 131104 | tf_op jit(solution)/shard_map/ppermute | solution.py:17
  117.5 1.3 %finish.1 = (f32[1,64,768]{2,1,0:T(8,128)}, f32[1,64,768]{2,1,0:T(8,128)}) custom-call(s32[9]{0:T(128)S(1)} %pack.1.sc, f32[64,1024]{1,0:T(8,128)S(1)} %get-tuple-element.44.refs_0_, bf16[64,1024]{1,0:T(8,128)(2,1)S(1)} %collective-permute-done.24.refs_1_, bf16[64,1024]{1,0:T(8,128)(2,1)S(1)} %collective-permute-done.25.refs_2_, ...), custom_call_target="tpu_custom_call" | custom-call | flops 1950000000 | tf_op jit(solution)/shard_map/finish/pallas_call | solution.py:192
  (42 shorter events, 0.4 us)
Async XLA Ops:
  0.6 26.1 %collective-permute-start.3 = (bf16[768,3072]{1,0:T(8,128)(2,1)}, bf16[768,3072]{1,0:T(8,128)(2,1)}, u32[]{:S(2)}, u32[]{:S(2)}) collective-permute-start(bf16[768,3072]{1,0:T(8,128)(2,1)} %refs_1_.11), channel_id=1, source_target_pairs={{0,1},{1,0},{2,3},{3,2},{4,5},{5,4},{6,7},{7,6},{8,9},{9,8},{10,11... | collective-permute-start | bytes 14155784 | tf_op jit(solution)/shard_map/ppermute | solution.py:17
  1.9 1.3 %copy-start = (bf16[1,192,3072]{2,1,0:T(8,128)(2,1)S(1)}, bf16[1,192,3072]{2,1,0:T(8,128)(2,1)}, u32[]{:S(2)}) copy-start(bf16[1,192,3072]{2,1,0:T(8,128)(2,1)} %refs_0_.5) | copy-start | bytes 3538948
  3.2 6.4 %copy-start.3 = (bf16[1,64,768]{2,1,0:T(8,128)(2,1)S(1)}, bf16[1,64,768]{2,1,0:T(8,128)(2,1)}, u32[]{:S(2)}) copy-start(bf16[1,64,768]{2,1,0:T(8,128)(2,1)} %refs_0_.4) | copy-start | bytes 294916
  3.2 6.4 %copy-start.4 = (bf16[1,64,768]{2,1,0:T(8,128)(2,1)S(1)}, bf16[1,64,768]{2,1,0:T(8,128)(2,1)}, u32[]{:S(2)}) copy-start(bf16[1,64,768]{2,1,0:T(8,128)(2,1)} %refs_1_.7) | copy-start | bytes 294916
  3.2 6.4 %copy-start.5 = (s32[8]{0:T(128)S(1)}, s32[8]{0:T(128)}, u32[]{:S(2)}) copy-start(s32[8]{0:T(128)} %refs_3_.2) | copy-start | bytes 100
  6.3 16.6 %collective-permute-start.7 = (bf16[2,192,768]{2,1,0:T(8,128)(2,1)S(1)}, bf16[2,192,768]{2,1,0:T(8,128)(2,1)S(1)}, u32[]{:S(2)}, u32[]{:S(2)}) collective-permute-start(bf16[2,192,768]{2,1,0:T(8,128)(2,1)S(1)} %attend.2.refs_4_.refs_1_), channel_id=1, source_target_pairs={{0,2},{1,3},{2,0},{3,1},{4,6},{5,7},{6,4},{7,5},{8,10},{9,11},{10,... | collective-permute-start | bytes 1769480 | tf_op jit(solution)/shard_map/ppermute | solution.py:17
  9.6 17.1 %slice-start = ((s8[4718592]{0:T(1024)(128)(4,1)}), s8[4194304]{0:T(1024)(128)(4,1)S(1)}, s32[]{:S(2)}) async-start(s8[4718592]{0:T(1024)(128)(4,1)} %bitcast.13), calls=%async_computation | async-start | bytes 8388608
  11.2 15.5 %slice-start.1 = ((s8[4718592]{0:T(1024)(128)(4,1)}), s8[524288]{0:T(1024)(128)(4,1)S(1)}, s32[]{:S(2)}) async-start(s8[4718592]{0:T(1024)(128)(4,1)} %bitcast.13), calls=%async_computation.1 | async-start | bytes 1048576
  11.2 19.8 %collective-permute-start.8 = (bf16[128,768]{1,0:T(8,128)(2,1)S(1)}, bf16[128,768]{1,0:T(8,128)(2,1)S(1)}, u32[]{:S(2)}, u32[]{:S(2)}) collective-permute-start(bf16[128,768]{1,0:T(8,128)(2,1)S(1)} %get-tuple-element.29.refs_3_.refs_0_), channel_id=1, source_target_pairs={{0,4},{4,0},{8,12},{12,8},{16,20},{20,16},{24,28},{28,24},{1,5},{5... | collective-permute-start | bytes 589832 | tf_op jit(solution)/shard_map/ppermute | solution.py:17
  12.8 24.1 %collective-permute-start.4 = (bf16[128,768]{1,0:T(8,128)(2,1)S(1)}, bf16[128,768]{1,0:T(8,128)(2,1)S(1)}, u32[]{:S(2)}, u32[]{:S(2)}) collective-permute-start(bf16[128,768]{1,0:T(8,128)(2,1)S(1)} %get-tuple-element.29.refs_3_.refs_0_), channel_id=1, source_target_pairs={{0,8},{4,12},{8,0},{12,4},{16,24},{20,28},{24,16},{28,20},{1,9},{5... | collective-permute-start | bytes 589832 | tf_op jit(solution)/shard_map/ppermute | solution.py:17
  14.4 23.0 %collective-permute-start.5 = (bf16[128,768]{1,0:T(8,128)(2,1)S(1)}, bf16[128,768]{1,0:T(8,128)(2,1)S(1)}, u32[]{:S(2)}, u32[]{:S(2)}) collective-permute-start(bf16[128,768]{1,0:T(8,128)(2,1)S(1)} %get-tuple-element.29.refs_3_.refs_0_), channel_id=1, source_target_pairs={{0,16},{4,20},{8,24},{12,28},{16,0},{20,4},{24,8},{28,12},{1,17},{... | collective-permute-start | bytes 589832 | tf_op jit(solution)/shard_map/ppermute | solution.py:17
  22.9 16.0 %collective-permute-start.6 = (bf16[128,768]{1,0:T(8,128)(2,1)S(1)}, bf16[128,768]{1,0:T(8,128)(2,1)S(1)}, u32[]{:S(2)}, u32[]{:S(2)}) collective-permute-start(bf16[128,768]{1,0:T(8,128)(2,1)S(1)} %get-tuple-element.29.refs_3_.refs_0_), channel_id=1, source_target_pairs={{0,24},{4,28},{8,16},{12,20},{16,8},{20,12},{24,0},{28,4},{1,25},{... | collective-permute-start | bytes 589832 | tf_op jit(solution)/shard_map/ppermute | solution.py:17
  26.7 21.4 %collective-permute-start = (s32[1]{0:T(128)}, s32[1]{0:T(128)}, u32[]{:S(2)}, u32[]{:S(2)}) collective-permute-start(s32[1]{0:T(128)} %get-tuple-element.28.refs_0_), channel_id=1, source_target_pairs={{0,1},{1,0},{2,3},{3,2},{4,5},{5,4},{6,7},{7,6},{8,9},{9,8},{10,11... | collective-permute-start | bytes 20 | tf_op jit(solution)/shard_map/ppermute | solution.py:17
  31.1 17.7 %collective-permute-start.1 = (s32[1]{0:T(128)}, s32[1]{0:T(128)}, u32[]{:S(2)}, u32[]{:S(2)}) collective-permute-start(s32[1]{0:T(128)} %get-tuple-element.28.refs_0_), channel_id=1, source_target_pairs={{0,2},{1,3},{2,0},{3,1},{4,6},{5,7},{6,4},{7,5},{8,10},{9,11},{10,... | collective-permute-start | bytes 20 | tf_op jit(solution)/shard_map/ppermute | solution.py:17
  36.9 4.1 %copy-start.1 = (bf16[1,192,3072]{2,1,0:T(8,128)(2,1)S(1)}, bf16[1,192,3072]{2,1,0:T(8,128)(2,1)}, u32[]{:S(2)}) copy-start(bf16[1,192,3072]{2,1,0:T(8,128)(2,1)} %refs_3_.3) | copy-start | bytes 3538948
  36.9 4.1 %copy-start.2 = (bf16[1,192,3072]{2,1,0:T(8,128)(2,1)S(1)}, bf16[1,192,3072]{2,1,0:T(8,128)(2,1)}, u32[]{:S(2)}) copy-start(bf16[1,192,3072]{2,1,0:T(8,128)(2,1)} %refs_4_.1) | copy-start | bytes 3538948
  37.0 11.8 %collective-permute-start.2 = (s32[1]{0:T(128)}, s32[1]{0:T(128)}, u32[]{:S(2)}, u32[]{:S(2)}) collective-permute-start(s32[1]{0:T(128)} %get-tuple-element.28.refs_0_), channel_id=1, source_target_pairs={{0,3},{1,2},{2,1},{3,0},{4,7},{5,6},{6,5},{7,4},{8,11},{9,10},{10,... | collective-permute-start | bytes 20 | tf_op jit(solution)/shard_map/ppermute | solution.py:17
  37.3 37.0 %collective-permute-start.14 = (bf16[4,192,384]{2,1,0:T(8,128)(2,1)S(1)}, bf16[4,192,384]{2,1,0:T(8,128)(2,1)S(1)}, u32[]{:S(2)}, u32[]{:S(2)}) collective-permute-start(bf16[4,192,384]{2,1,0:T(8,128)(2,1)S(1)} %project.3.refs_3_), channel_id=1, source_target_pairs={{0,2},{1,3},{2,0},{3,1},{4,6},{5,7},{6,4},{7,5},{8,10},{9,11},{10,... | collective-permute-start | bytes 1769480 | tf_op jit(solution)/shard_map/ppermute | solution.py:17
  39.5 15.3 %collective-permute-start.9 = (bf16[3,128,768]{2,1,0:T(8,128)(2,1)S(1)}, bf16[3,128,768]{2,1,0:T(8,128)(2,1)S(1)}, u32[]{:S(2)}, u32[]{:S(2)}) collective-permute-start(bf16[3,128,768]{2,1,0:T(8,128)(2,1)S(1)} %stack.21.refs_5_.refs_2_), channel_id=1, source_target_pairs={{0,4},{4,0},{8,12},{12,8},{16,20},{20,16},{24,28},{28,24},{1,5},{5... | collective-permute-start | bytes 1769480 | tf_op jit(solution)/shard_map/ppermute | solution.py:17
  48.2 26.2 %collective-permute-start.13 = (bf16[4,192,384]{2,1,0:T(8,128)(2,1)S(1)}, bf16[4,192,384]{2,1,0:T(8,128)(2,1)S(1)}, u32[]{:S(2)}, u32[]{:S(2)}) collective-permute-start(bf16[4,192,384]{2,1,0:T(8,128)(2,1)S(1)} %project.2.refs_3_), channel_id=1, source_target_pairs={{0,2},{1,3},{2,0},{3,1},{4,6},{5,7},{6,4},{7,5},{8,10},{9,11},{10,... | collective-permute-start | bytes 1769480 | tf_op jit(solution)/shard_map/ppermute | solution.py:17
  55.8 2.0 %collective-permute-start.10 = (bf16[128,768]{1,0:T(8,128)(2,1)S(1)}, bf16[128,768]{1,0:T(8,128)(2,1)S(1)}, u32[]{:S(2)}, u32[]{:S(2)}) collective-permute-start(bf16[128,768]{1,0:T(8,128)(2,1)S(1)} %get-tuple-element.31), channel_id=1, source_target_pairs={{0,1},{1,0},{2,3},{3,2},{4,5},{5,4},{6,7},{7,6},{8,9},{9,8},{10,11... | collective-permute-start | bytes 589832 | tf_op jit(solution)/shard_map/ppermute | solution.py:17
  55.9 14.5 %collective-permute-start.11 = (bf16[128,768]{1,0:T(8,128)(2,1)S(1)}, bf16[128,768]{1,0:T(8,128)(2,1)S(1)}, u32[]{:S(2)}, u32[]{:S(2)}) collective-permute-start(bf16[128,768]{1,0:T(8,128)(2,1)S(1)} %get-tuple-element.32), channel_id=1, source_target_pairs={{0,2},{1,3},{2,0},{3,1},{4,6},{5,7},{6,4},{7,5},{8,10},{9,11},{10,... | collective-permute-start | bytes 589832 | tf_op jit(solution)/shard_map/ppermute | solution.py:17
  56.4 16.9 %collective-permute-start.12 = (bf16[128,768]{1,0:T(8,128)(2,1)S(1)}, bf16[128,768]{1,0:T(8,128)(2,1)S(1)}, u32[]{:S(2)}, u32[]{:S(2)}) collective-permute-start(bf16[128,768]{1,0:T(8,128)(2,1)S(1)} %get-tuple-element.33), channel_id=1, source_target_pairs={{0,3},{1,2},{2,1},{3,0},{4,7},{5,6},{6,5},{7,4},{8,11},{9,10},{10,... | collective-permute-start | bytes 589832 | tf_op jit(solution)/shard_map/ppermute | solution.py:17
  57.8 21.8 %collective-permute-start.18 = (bf16[192,768]{1,0:T(8,128)(2,1)S(1)}, bf16[192,768]{1,0:T(8,128)(2,1)S(1)}, u32[]{:S(2)}, u32[]{:S(2)}) collective-permute-start(bf16[192,768]{1,0:T(8,128)(2,1)S(1)} %get-tuple-element.55), channel_id=1, source_target_pairs={{0,1},{1,0},{2,3},{3,2},{4,5},{5,4},{6,7},{7,6},{8,9},{9,8},{10,11... | collective-permute-start | bytes 884744 | tf_op jit(solution)/shard_map/ppermute | solution.py:17
  70.3 9.2 %collective-permute-start.19 = (bf16[192,768]{1,0:T(8,128)(2,1)S(1)}, bf16[192,768]{1,0:T(8,128)(2,1)S(1)}, u32[]{:S(2)}, u32[]{:S(2)}) collective-permute-start(bf16[192,768]{1,0:T(8,128)(2,1)S(1)} %get-tuple-element.53), channel_id=1, source_target_pairs={{0,1},{1,0},{2,3},{3,2},{4,5},{5,4},{6,7},{7,6},{8,9},{9,8},{10,11... | collective-permute-start | bytes 884744 | tf_op jit(solution)/shard_map/ppermute | solution.py:17
  77.5 2.0 %collective-permute-start.15 = (bf16[64,1024]{1,0:T(8,128)(2,1)S(1)}, bf16[64,1024]{1,0:T(8,128)(2,1)S(1)}, u32[]{:S(2)}, u32[]{:S(2)}) collective-permute-start(bf16[64,1024]{1,0:T(8,128)(2,1)S(1)} %get-tuple-element.35), channel_id=1, source_target_pairs={{0,1},{1,0},{2,3},{3,2},{4,5},{5,4},{6,7},{7,6},{8,9},{9,8},{10,11... | collective-permute-start | bytes 393224 | tf_op jit(solution)/shard_map/ppermute | solution.py:17
  78.0 6.4 %collective-permute-start.16 = (bf16[64,1024]{1,0:T(8,128)(2,1)S(1)}, bf16[64,1024]{1,0:T(8,128)(2,1)S(1)}, u32[]{:S(2)}, u32[]{:S(2)}) collective-permute-start(bf16[64,1024]{1,0:T(8,128)(2,1)S(1)} %get-tuple-element.36), channel_id=1, source_target_pairs={{0,2},{1,3},{2,0},{3,1},{4,6},{5,7},{6,4},{7,5},{8,10},{9,11},{10,... | collective-permute-start | bytes 393224 | tf_op jit(solution)/shard_map/ppermute | solution.py:17
  79.5 5.9 %collective-permute-start.17 = (bf16[64,1024]{1,0:T(8,128)(2,1)S(1)}, bf16[64,1024]{1,0:T(8,128)(2,1)S(1)}, u32[]{:S(2)}, u32[]{:S(2)}) collective-permute-start(bf16[64,1024]{1,0:T(8,128)(2,1)S(1)} %get-tuple-element.37), channel_id=1, source_target_pairs={{0,3},{1,2},{2,1},{3,0},{4,7},{5,6},{6,5},{7,4},{8,11},{9,10},{10,... | collective-permute-start | bytes 393224 | tf_op jit(solution)/shard_map/ppermute | solution.py:17
  87.1 14.6 %collective-permute-start.20 = (bf16[4,64,1024]{2,1,0:T(8,128)(2,1)S(1)}, bf16[4,64,1024]{2,1,0:T(8,128)(2,1)S(1)}, u32[]{:S(2)}, u32[]{:S(2)}) collective-permute-start(bf16[4,64,1024]{2,1,0:T(8,128)(2,1)S(1)} %get-tuple-element.40), channel_id=1, source_target_pairs={{0,4},{4,0},{8,12},{12,8},{16,20},{20,16},{24,28},{28,24},{1,5},{5... | collective-permute-start | bytes 1572872 | tf_op jit(solution)/shard_map/ppermute | solution.py:17
  88.7 7.1 %collective-permute-start.21 = (bf16[2,64,512]{2,1,0:T(8,128)(2,1)S(1)}, bf16[2,64,512]{2,1,0:T(8,128)(2,1)S(1)}, u32[]{:S(2)}, u32[]{:S(2)}) collective-permute-start(bf16[2,64,512]{2,1,0:T(8,128)(2,1)S(1)} %get-tuple-element.41), channel_id=1, source_target_pairs={{0,8},{4,12},{8,0},{12,4},{16,24},{20,28},{24,16},{28,20},{1,9},{5... | collective-permute-start | bytes 393224 | tf_op jit(solution)/shard_map/ppermute | solution.py:17
  88.7 12.9 %collective-permute-start.22 = (bf16[2,64,512]{2,1,0:T(8,128)(2,1)S(1)}, bf16[2,64,512]{2,1,0:T(8,128)(2,1)S(1)}, u32[]{:S(2)}, u32[]{:S(2)}) collective-permute-start(bf16[2,64,512]{2,1,0:T(8,128)(2,1)S(1)} %get-tuple-element.42), channel_id=1, source_target_pairs={{0,16},{4,20},{8,24},{12,28},{16,0},{20,4},{24,8},{28,12},{1,17},{... | collective-permute-start | bytes 393224 | tf_op jit(solution)/shard_map/ppermute | solution.py:17
  89.4 12.1 %collective-permute-start.23 = (bf16[2,64,512]{2,1,0:T(8,128)(2,1)S(1)}, bf16[2,64,512]{2,1,0:T(8,128)(2,1)S(1)}, u32[]{:S(2)}, u32[]{:S(2)}) collective-permute-start(bf16[2,64,512]{2,1,0:T(8,128)(2,1)S(1)} %get-tuple-element.43), channel_id=1, source_target_pairs={{0,24},{4,28},{8,16},{12,20},{16,8},{20,12},{24,0},{28,4},{1,25},{... | collective-permute-start | bytes 393224 | tf_op jit(solution)/shard_map/ppermute | solution.py:17
  102.4 9.5 %collective-permute-start.24 = (bf16[64,1024]{1,0:T(8,128)(2,1)S(1)}, bf16[64,1024]{1,0:T(8,128)(2,1)S(1)}, u32[]{:S(2)}, u32[]{:S(2)}) collective-permute-start(bf16[64,1024]{1,0:T(8,128)(2,1)S(1)} %get-tuple-element.45), channel_id=1, source_target_pairs={{0,8},{4,12},{8,0},{12,4},{16,24},{20,28},{24,16},{28,20},{1,9},{5... | collective-permute-start | bytes 393224 | tf_op jit(solution)/shard_map/ppermute | solution.py:17
  105.2 12.3 %collective-permute-start.25 = (bf16[64,1024]{1,0:T(8,128)(2,1)S(1)}, bf16[64,1024]{1,0:T(8,128)(2,1)S(1)}, u32[]{:S(2)}, u32[]{:S(2)}) collective-permute-start(bf16[64,1024]{1,0:T(8,128)(2,1)S(1)} %get-tuple-element.46), channel_id=1, source_target_pairs={{0,16},{4,20},{8,24},{12,28},{16,0},{20,4},{24,8},{28,12},{1,17},{... | collective-permute-start | bytes 393224 | tf_op jit(solution)/shard_map/ppermute | solution.py:17
  105.3 12.2 %collective-permute-start.26 = (bf16[64,1024]{1,0:T(8,128)(2,1)S(1)}, bf16[64,1024]{1,0:T(8,128)(2,1)S(1)}, u32[]{:S(2)}, u32[]{:S(2)}) collective-permute-start(bf16[64,1024]{1,0:T(8,128)(2,1)S(1)} %get-tuple-element.47), channel_id=1, source_target_pairs={{0,24},{4,28},{8,16},{12,20},{16,8},{20,12},{24,0},{28,4},{1,25},{... | collective-permute-start | bytes 393224 | tf_op jit(solution)/shard_map/ppermute | solution.py:17
  107.6 4.3 %collective-permute-start.27 = (bf16[64,512]{1,0:T(8,128)(2,1)S(1)}, bf16[64,512]{1,0:T(8,128)(2,1)S(1)}, u32[]{:S(2)}, u32[]{:S(2)}) collective-permute-start(bf16[64,512]{1,0:T(8,128)(2,1)S(1)} %get-tuple-element.49), channel_id=1, source_target_pairs={{0,4},{4,0},{8,12},{12,8},{16,20},{20,16},{24,28},{28,24},{1,5},{5... | collective-permute-start | bytes 196616 | tf_op jit(solution)/shard_map/ppermute | solution.py:17

commit v4 on v3

--- a/solution.py
+++ b/solution.py
@@ -168,11 +168,10 @@
 
 
 LANES = 128
-CHUNKS = 2
 VMEM = 20 * 1024 * 1024
-COST = 1.5e9
+COST = 4e8
 ALONE = 52 * 1024 * 1024
-SHARD, CORE, CHIP, COUNT, GROUP, OFFSETS = 0, 1, 2, 3, 4, 5
+SHARD, CORE, CHIP, COUNT, GROUP = range(5)
 
 
 def kernel_call(
@@ -254,14 +253,19 @@
     )
 
 
-def project_chunk(scalars, columns, weight, weight_near, chip_offset, chunk, size, after):
+def chunk_lanes(depth):
+    cut = depth // 3 // LANES * LANES
+    return slice(0, cut), slice(cut, depth)
+
+
+def project_chunk(scalars, columns, weight, weight_near, chip_offset, lanes, size, after):
     _, slots, depth = columns.shape
-    w = depth // CHUNKS
+    w = lanes.stop - lanes.start
 
     def body(sc, x_ref, own_ref, near_ref, out_ref):
         for k in range(size):
-            place = (sc[SHARD] ^ (2 * chip_offset) ^ k) * CHUNKS + chunk
-            cols = pl.ds(pl.multiple_of(place * w, LANES), w)
+            start = (sc[SHARD] ^ (2 * chip_offset) ^ k) * depth + lanes.start
+            cols = pl.ds(pl.multiple_of(start, LANES), w)
             out_ref[k] = (dot(x_ref[0], own_ref[:, cols], 1, 0) + dot(x_ref[1], near_ref[:, cols], 1, 0)).astype(BF16)
 
     vmem = pl.BlockSpec(memory_space=pltpu.VMEM)
@@ -271,99 +275,89 @@
         scalars,
         (columns, weight, weight_near),
         shaped((size, slots, w)),
-        4.0,
+        8.0 * w / depth,
         in_specs=[vmem] * 3,
         out_specs=vmem,
         after=after,
     )
 
 
-def base_error(scalars, columns, weight, weight_near, residual, target, size, after):
+def base_error(scalars, columns, weight, weight_near, residual, target, received, lanes, size, after):
     _, slots, depth = columns.shape
-    w = depth // CHUNKS
-
-    def body(sc, x_ref, own_ref, near_ref, r_ref, t_ref, out_ref):
-        place = (sc[SHARD] ^ pl.program_id(1)) * CHUNKS + pl.program_id(0)
-        cols = pl.ds(pl.multiple_of(place * w, LANES), w)
+    w = lanes.stop - lanes.start
+
+    def body(sc, x_ref, own_ref, near_ref, r_ref, t_ref, *refs):
+        cols = pl.ds(pl.multiple_of((sc[SHARD] ^ pl.program_id(0)) * depth, LANES), depth)
         total = dot(x_ref[0], own_ref[:, cols], 1, 0) + dot(x_ref[1], near_ref[:, cols], 1, 0)
-        out_ref[0, 0] = total + (r_ref[0].astype(F32) - t_ref[0].astype(F32))
-
-    tokens = pl.BlockSpec((1, slots, w), lambda i, k, sc: (0, 0, (sc[SHARD] ^ k) * CHUNKS + i))
+        refs[-1][0] = total + (r_ref[0].astype(F32) - t_ref[0].astype(F32))
+        for ref in refs[:-1]:
+            refs[-1][0, :, lanes] += ref[0].astype(F32)
+
+    tokens = pl.BlockSpec((1, slots, depth), lambda k, sc: (0, 0, sc[SHARD] ^ k))
+    lead = lambda width: pl.BlockSpec((1, slots, width), lambda k, sc: (k, 0, 0))
     vmem = pl.BlockSpec(memory_space=pltpu.VMEM)
     return kernel_call(
         body,
         "base",
         scalars,
-        (columns, weight, weight_near, residual, target),
-        shaped((CHUNKS, size, slots, w), F32),
+        (columns, weight, weight_near, residual, target, *received),
+        shaped((size, slots, depth), F32),
         7.0,
-        grid=(CHUNKS, size),
-        in_specs=[vmem, vmem, vmem, tokens, tokens],
-        out_specs=pl.BlockSpec((1, 1, slots, w), lambda i, k, sc: (i, k, 0, 0)),
+        grid=(size,),
+        in_specs=[vmem, vmem, vmem, tokens, tokens, *[lead(w)] * len(received)],
+        out_specs=lead(depth),
         after=after,
     )
 
 
-def low_rank(scalars, attended, adapters):
-    slots = attended[0].shape[1]
-    rank = adapters[0].shape[0] // 2
-    chips = len(attended)
-
-    def body(sc, *refs):
-        total = 0.0
-        for k in range(2 * chips):
-            total = total + dot(refs[k // 2][k % 2], refs[chips + k][:rank, :], 1, 1)
-        refs[-1][...] = total.astype(BF16)
-
-    return kernel_call(body, "low_rank", scalars, (*attended, *adapters), shaped((slots, rank)), 2.0)
-
-
-def error_terms(scalars, base, received, low, adapters):
-    chunks, size, slots, w = base.shape
-    rank = low.shape[1]
-    depth = chunks * w
+def error_terms(scalars, base, received, lanes, low_part, adapters):
+    size, slots, depth = base.shape
+    rank = low_part.shape[0]
     back_lanes = -(-slots // LANES) * LANES
-    peers = len(received[0])
-    flat = [x for group in received for x in group]
+    peers = len(received)
+    step = math.gcd(lanes.start, depth)
 
     def body(sc, base_ref, low_ref, *refs):
-        got, up_refs, refs = refs[: len(flat)], refs[len(flat) : len(flat) + size], refs[len(flat) + size :]
-        pieces, loss_out = refs[:size], refs[size]
+        got, up_refs, pieces = refs[:peers], refs[peers : peers + size], refs[peers + size : -1]
         count = sc[COUNT]
         tokens = count.astype(F32)
         valid = lax.broadcasted_iota(jnp.int32, (slots, 1), 0) < count
-        low_state = low_ref[...]
+        low_wide = low_ref[...]
+        for ref in up_refs[1:]:
+            low_wide = low_wide + ref[:, depth : depth + slots].astype(F32)
+        low_turned = low_wide.astype(BF16)
+        low_state = low_wide.T.astype(BF16)
         back = jnp.zeros((rank, slots), F32)
-        squares = jnp.zeros((slots, w), F32)
-        for i in range(chunks):
-            at = slice(i * w, (i + 1) * w)
-            for k in range(size):
+        squares = jnp.zeros((slots, step), F32)
+        for k in range(size):
+            for start in range(0, depth, step):
+                at = slice(start, start + step)
                 up = up_refs[k][:, at]
-                error = base_ref[i, k] + ADAPTER_SCALE * dot(low_state, up, 1, 0)
-                for ref in got[i * peers : (i + 1) * peers]:
-                    error = error + ref[k].astype(F32)
+                error = base_ref[k, :, at] + ADAPTER_SCALE * dot(low_state, up, 1, 0)
+                if start >= lanes.start:
+                    for ref in got:
+                        error = error + ref[k, :, start - lanes.start : start - lanes.start + step].astype(F32)
                 error = jnp.where(valid, error, 0.0)
                 squares = squares + error * error
                 cotangent = (2.0 * error / tokens).astype(BF16)
                 back = back + dot(up, cotangent, 1, 1)
-                pieces[k][:, at] = (ADAPTER_SCALE * dot(low_state, cotangent, 0, 0)).astype(BF16)
-        loss_out[0, 0] = jnp.sum(squares) / (tokens * (size * depth))
-        lanes = (ADAPTER_SCALE * back).astype(BF16)
-        lanes = jnp.concatenate([lanes, jnp.zeros((rank, back_lanes - slots), BF16)], axis=1)
+                pieces[k][:, at] = (ADAPTER_SCALE * dot(low_turned, cotangent, 1, 0)).astype(BF16)
+        refs[-1][0, 0] = jnp.sum(squares) / (tokens * (size * depth))
+        padded = (ADAPTER_SCALE * back).astype(BF16)
+        padded = jnp.concatenate([padded, jnp.zeros((rank, back_lanes - slots), BF16)], axis=1)
         for k in range(size):
-            pieces[k][:, depth:] = lanes
+            pieces[k][:, depth:] = padded
 
     whole = lambda x: pl.BlockSpec(x.shape, lambda k, sc: (0,) * len(x.shape))
-    ups = pl.BlockSpec((rank, depth), lambda k, sc: (1, 0))
     out_shape = [shaped((rank, depth + back_lanes))] * size + [shaped((1, 1), F32)]
     out = kernel_call(
         body,
         "error",
         scalars,
-        (base, low, *flat, *adapters),
+        (base, low_part, *received, *adapters),
         out_shape,
-        4.0,
-        in_specs=[whole(base), whole(low), *[whole(x) for x in flat], *[ups] * size],
+        3.0,
+        in_specs=[whole(x) for x in (base, low_part, *received, *adapters)],
         out_specs=[whole(x) for x in out_shape[:-1]] + [pl.BlockSpec(memory_space=pltpu.SMEM)],
     )
     return out[:size], out[size]
@@ -375,7 +369,7 @@
     def body(sc, down_ref, up_ref, scene_ref, row_ref, out_ref, slot_ref):
         out_ref[:rank, :] = down_ref[0]
         out_ref[rank:, :] = up_ref[0]
-        slot_ref[0] = row_ref[scene_ref[0]]
+        slot_ref[...] = jnp.full(slot_ref.shape, row_ref[scene_ref[0]].astype(F32))
 
     vmem, smem = pl.BlockSpec(memory_space=pltpu.VMEM), pl.BlockSpec(memory_space=pltpu.SMEM)
     return kernel_call(
@@ -383,31 +377,10 @@
         "join",
         scalars,
         (down, up, scene, rows),
-        [shaped((2 * rank, depth)), shaped((1,), jnp.int32)],
+        [shaped((2 * rank, depth)), shaped((8, LANES), F32)],
         1.0,
         in_specs=[vmem, vmem, smem, smem],
-        out_specs=[vmem, smem],
-        after=after,
-    )
-
-
-def pack_scalars(scalars, slots, after):
-    def body(sc, *refs):
-        for i in range(OFFSETS):
-            refs[-1][i] = sc[i]
-        for k in range(len(slots)):
-            refs[-1][OFFSETS + k] = refs[k][0] ^ sc[GROUP]
-
-    smem = pl.BlockSpec(memory_space=pltpu.SMEM)
-    return kernel_call(
-        body,
-        "pack",
-        scalars,
-        slots,
-        shaped((OFFSETS + len(slots),), jnp.int32),
-        0.5,
-        in_specs=[smem] * len(slots),
-        out_specs=smem,
+        out_specs=[vmem, vmem],
         after=after,
     )
 
@@ -418,42 +391,72 @@
             refs[-1][i] = refs[i][...]
 
     return kernel_call(
-        body, "stack", scalars, blocks, shaped((len(blocks), *blocks[0].shape)), 1.0, after=after
-    )
-
-
-def choose_adapters(scalars, blocks, size, after):
+        body, "stack", scalars, blocks, shaped((len(blocks), *blocks[0].shape)), 0.6, after=after
+    )
+
+
+def slot_offset(sc, slot_ref):
+    return jnp.max(slot_ref[...]).astype(jnp.int32) ^ sc[GROUP]
+
+
+def choose_adapters(scalars, slot_list, blocks, columns, after):
     arrays = []
     for x, _ in blocks:
         if all(x is not y for y in arrays):
             arrays.append(x)
     where = [next(i for i, y in enumerate(arrays) if x is y) for x, _ in blocks]
-    shape = arrays[0].shape
+    rows, depth = arrays[0].shape
+    rank = rows // 2
+    size = len(slot_list)
+    slots = columns[0].shape[0]
+    padded = -(-slots // LANES) * LANES
 
     def body(sc, *refs):
+        slot_refs, column_refs, refs = refs[:size], refs[size : 2 * size], refs[2 * size :]
+        outs, low_ref, held = refs[len(arrays) : -2], refs[-2], refs[-1]
         for k in range(size):
+            offset = slot_offset(sc, slot_refs[k])
             for scene, (_, place) in enumerate(blocks):
 
-                @pl.when(sc[OFFSETS + k] == scene)
+                @pl.when(offset == scene)
                 def _():
                     ref = refs[where[scene]]
-                    refs[len(arrays) + k][...] = ref[...] if place is None else ref[place]
-
-    return kernel_call(body, "choose", scalars, arrays, [shaped(shape)] * size, 2.0, after=after)
-
-
-def scene_sum(sc, pieces, scene):
+                    held[k] = ref[...] if place is None else ref[place]
+
+        for k in range(size):
+            part = dot(held[k, :rank, :], column_refs[k][...], 1, 1)
+            if k == 0:
+                low_ref[...] = part
+            outs[k][:, :depth] = held[k, rank:, :]
+            outs[k][:, depth:] = jnp.concatenate(
+                [part.astype(BF16), jnp.zeros((rank, padded - slots), BF16)], axis=1
+            )
+
+    out = kernel_call(
+        body,
+        "choose",
+        scalars,
+        (*slot_list, *columns, *arrays),
+        [shaped((rank, depth + padded))] * size + [shaped((rank, slots), F32)],
+        2.0,
+        after=after,
+        scratch=[pltpu.VMEM((size, rows, depth), BF16)],
+    )
+    return out[:size], out[size]
+
+
+def scene_sum(offsets, pieces, scene):
     total = jnp.zeros(pieces[0].shape, F32)
-    for k, piece in enumerate(pieces):
-        total = total + jnp.where(sc[OFFSETS + k] == scene, piece, 0.0)
+    for offset, piece in zip(offsets, pieces):
+        total = total + jnp.where(offset == scene, piece, 0.0)
     return total
 
 
-def first_refs(sc, pieces, keep, sends, near, far, near_mul, far_mul):
+def first_refs(offsets, pieces, keep, sends, near, far, near_mul, far_mul):
     for f in range(far):
-        keep[f] = scene_sum(sc, pieces, f * far_mul)
+        keep[f] = scene_sum(offsets, pieces, f * far_mul)
         for s in range(1, near):
-            sends[s - 1][f] = scene_sum(sc, pieces, f * far_mul + s * near_mul).astype(BF16)
+            sends[s - 1][f] = scene_sum(offsets, pieces, f * far_mul + s * near_mul).astype(BF16)
 
 
 def second_refs(keep, received, final, sends, far):
@@ -512,31 +515,42 @@
 
         attended = [attend_chip(scalars, queries, keys, values, c, depth) for c in range(1, chips)]
         theirs = [xor_send(x, "fsdp", fsdp_size, 2 * (c + 1)) for c, x in enumerate(attended)]
+        own = attend_chip(scalars, queries, keys, values, 0, depth, attended[:1])
         block, own_slot = join_adapters(
-            scalars, down_adapter, up_adapter, scene_of_frame, scene_adapter_row, attended[:1]
+            scalars, down_adapter, up_adapter, scene_of_frame, scene_adapter_row, [own, weight_near]
         )
-        slot_list = send_shards([own_slot] * fsdp_size)
+        near_slots = [own_slot] + [xor_send(own_slot, "fsdp", fsdp_size, 2 * c) for c in range(1, chips)]
         outer_blocks = [xor_send(block, "frame", frame_size, o * inner) for o in range(1, outer)]
-        inner_blocks = [xor_send(block, "frame", frame_size, s) for s in range(1, inner)]
-        own = attend_chip(scalars, queries, keys, values, 0, depth, [block])
         attended = [own] + attended
 
         partials = []
-        after = [own]
-        for chunk in range(CHUNKS):
+        after = [block, *near_slots[1:]]
+        parts = chunk_lanes(depth)
+        for lanes in parts:
             sent = []
             for c, x in enumerate(theirs):
                 part = project_chunk(
-                    scalars, x, output_weight, weight_near, c + 1, chunk, fsdp_size, after
+                    scalars, x, output_weight, weight_near, c + 1, lanes, fsdp_size, after
                 )
                 sent.append(xor_send(part, "fsdp", fsdp_size, 2 * (c + 1)))
             partials.append(sent)
-            after = [part, *inner_blocks]
+            after = [part]
+        slot_list = [x for slot in near_slots for x in (slot, xor_send(slot, "fsdp", fsdp_size, 1))]
 
         stacked = stack_blocks(scalars, outer_blocks, [part])
+        inner_blocks = [xor_send(block, "frame", frame_size, s) for s in range(1, inner)]
         far_blocks = [xor_send(stacked, "frame", frame_size, s) for s in range(1, inner)]
         base = base_error(
-            scalars, own, output_weight, weight_near, residual, target, fsdp_size, [stacked]
+            scalars,
+            own,
+            output_weight,
+            weight_near,
+            residual,
+            target,
+            partials[0],
+            parts[0],
+            fsdp_size,
+            [stacked],
         )
         blocks = [None] * frame_size
         for o in range(outer):
@@ -544,16 +558,14 @@
             for s in range(1, inner):
                 blocks[o * inner + s] = (far_blocks[s - 1], o - 1) if o else (inner_blocks[s - 1], None)
 
-        scalars = pack_scalars(scalars, slot_list, [base])
-        adapters = send_shards(choose_adapters(scalars, blocks, fsdp_size, [base]))
-
         columns = [None] * fsdp_size
         for c, x in enumerate([own] + theirs):
             columns[2 * c] = x[0]
             columns[2 * c + 1] = xor_send(x[1], "fsdp", fsdp_size, 1)
 
-        low = low_rank(scalars, attended, adapters)
-        pieces, loss = error_terms(scalars, base, partials, low, adapters)
+        chosen, low_part = choose_adapters(scalars, slot_list, blocks, columns, [base])
+        adapters = send_shards(chosen)
+        pieces, loss = error_terms(scalars, base, partials[1], parts[1], low_part, adapters)
         pieces = send_shards(pieces)
 
         cut = depth // 3 // LANES * LANES
@@ -563,17 +575,19 @@
         )
 
         def first(sc, *refs):
-            got, cols, outs = refs[:fsdp_size], refs[fsdp_size : 2 * fsdp_size], refs[2 * fsdp_size :]
+            slot_refs, got, cols = (refs[i * fsdp_size : (i + 1) * fsdp_size] for i in range(3))
+            outs = refs[3 * fsdp_size :]
+            offsets = [slot_offset(sc, ref) for ref in slot_refs]
             downs = [dot(p[:, depth : depth + slots], c[...], 1, 0) for p, c in zip(got, cols)]
             down_outs = [ref.at[:, :, :depth] for ref in outs[:inner]]
-            first_refs(sc, downs, down_outs[0], down_outs[1:], *along_inner)
+            first_refs(offsets, downs, down_outs[0], down_outs[1:], *along_inner)
             ups = [p[:, :cut].astype(F32) for p in got]
             up_outs = [ref.at[:, :, depth:] for ref in outs[:inner]]
-            first_refs(sc, ups, up_outs[0], up_outs[1:], *along_inner)
+            first_refs(offsets, ups, up_outs[0], up_outs[1:], *along_inner)
             ups = [p[:, cut:depth].astype(F32) for p in got]
-            first_refs(sc, ups, outs[inner], outs[inner + 1 :], *along_outer)
-
-        out = kernel_call(first, "first", scalars, (*pieces, *columns), first_shape, 2.0)
+            first_refs(offsets, ups, outs[inner], outs[inner + 1 :], *along_outer)
+
+        out = kernel_call(first, "first", scalars, (*slot_list, *pieces, *columns), first_shape, 2.0)
         keeps = out[0], out[inner]
         inner_got = send_frames(out[1:inner], 1)
         outer_got = send_frames(out[inner + 1 :], inner)
@@ -618,7 +632,7 @@
 
     def per_device(*operands):
         depth = operands[5].shape[0]
-        return (chunked if depth % (LANES * CHUNKS) == 0 else general)(*operands)
+        return (chunked if depth % (3 * LANES) == 0 else general)(*operands)
 
     return jax.shard_map(
         per_device,

time: 119 us -> 113 us (0.950)
  Pallas kernels: 36.6 us -> 31.2 us
  starting transfers between devices: 34.5 us -> 31.6 us
  waiting for transfers between devices: 44 us -> 45.7 us
    pallas_call x14 -> x12, Pallas kernels: 36.6 us -> 31.2 us  [kernel_call(): pl.pallas_call(body, out_shape=out_shape, grid_spec=pltpu.PrefetchScalarG...]
    ppermute x28, starting transfers between devices: 34.5 us -> 31.6 us  [xor_send(): return lax.ppermute(value, axis, [(i, i ^ offset) for i in range(size)])]
    ppermute x28, waiting for transfers between devices: 44 us -> 45.7 us  [xor_send(): return lax.ppermute(value, axis, [(i, i ^ offset) for i in range(size)])]
  transfers between devices with their start and end apart: 28 -> 28, of which waited for: 11 -> 12; matrix products, arithmetic and copies ran while one was open for 0% -> 0% of each run, Pallas kernels for 28% -> 21%
where the time goes in v4:
time: 113 us; the launch traced here: 112 us
  waiting for transfers between devices  45.7 us (40%)
  starting transfers between devices  31.6 us (28%)
  Pallas kernels  31.2 us (28%)
  between operations  2.19 us (2%)
  local copies, waits for them, and re-layouts  1.48 us (1%)
    ppermute x28, waiting for transfers between devices, xor_send(): return lax.ppermute(value, axis, [(i, i ^ offset) for i in range(size)])  45.7 us
    ppermute x28, starting transfers between devices, xor_send(): return lax.ppermute(value, axis, [(i, i ^ offset) for i in range(size)])  31.6 us
    pallas_call x12, Pallas kernels, kernel_call(): pl.pallas_call(body, out_shape=out_shape, grid_spec=pltpu.PrefetchScalarG...  31.2 us
  transfers between devices with their start and end apart: 28, of which 12 were waited for; matrix products, arithmetic and copies ran while one was open for 0% of the time, Pallas kernels for 21%

profile of v4, /device:TPU:0, one launch (start us, length us, event | category | flops | bytes accessed | tf_op | source)
XLA Modules:
  0.0 112.2 jit_solution(14822197432101042642)
XLA Ops:
  0.6 0.5 collective-permute-start
  1.9 1.3 %copy-done.5 = bf16[1,192,3072]{2,1,0:T(8,128)(2,1)S(1)} copy-done((bf16[1,192,3072]{2,1,0:T(8,128)(2,1)S(1)}, bf16[1,192,3072]{2,1,0:T(8,128)(2,1)}, u32[]{:S(2)}) %copy-start.5) | copy-done | bytes 1179672
  3.2 3.2 %attend.2.refs_3_ = bf16[2,192,768]{2,1,0:T(8,128)(2,1)S(1)} custom-call(s32[5]{0:T(128)S(1)} %stack.20.sc, bf16[1,192,3072]{2,1,0:T(8,128)(2,1)S(1)} %copy-done.5, bf16[1,192,3072]{2,1,0:T(8,128)(2,1)} %refs_1_.7, bf16[1,192,3072]{2,1,0:T(8,128)(2,1)} %refs_2_.4), custom_call_target="tpu_custom_call" | custom-call | flops 1600000000 | tf_op jit(solution)/shard_map/attend/pallas_call | solution.py:191
  6.3 2.6 %collective-permute-start.4 = (bf16[2,192,768]{2,1,0:T(8,128)(2,1)S(1)}, bf16[2,192,768]{2,1,0:T(8,128)(2,1)S(1)}, u32[]{:S(2)}, u32[]{:S(2)}) collective-permute-start(bf16[2,192,768]{2,1,0:T(8,128)(2,1)S(1)} %attend.2.refs_3_), channel_id=1, source_target_pairs={{0,2},{1,3},{2,0},{3,1},{4,6},{5,7},{6,4},{7,5},{8,10},{9,11},{10,... | collective-permute-start | bytes 1769480 | tf_op jit(solution)/shard_map/ppermute | solution.py:17
  9.6 3.5 %attend.3.refs_4_.refs_0_ = bf16[2,192,768]{2,1,0:T(8,128)(2,1)S(1)} custom-call(s32[5]{0:T(128)S(1)} %stack.20.sc, bf16[1,192,3072]{2,1,0:T(8,128)(2,1)} %refs_0_.4, bf16[1,192,3072]{2,1,0:T(8,128)(2,1)} %refs_1_.7, bf16[1,192,3072]{2,1,0:T(8,128)(2,1)} %refs_2_.4, bf16[2,192,768]{2,1,0:T(8,128)(2,1)S(1)} %attend.2.refs_3_), custom_call_target="tpu_custom_call" | custom-call | flops 1600000000 | tf_op jit(solution)/shard_map/attend/pallas_call | solution.py:191
  13.1 1.1 join.1
  14.4 0.3 collective-permute-start.9
  14.6 2.0 %collective-permute-start.6 = (bf16[128,768]{1,0:T(8,128)(2,1)S(1)}, bf16[128,768]{1,0:T(8,128)(2,1)S(1)}, u32[]{:S(2)}, u32[]{:S(2)}) collective-permute-start(bf16[128,768]{1,0:T(8,128)(2,1)S(1)} %get-tuple-element.30.refs_3_.refs_8_), channel_id=1, source_target_pairs={{0,8},{4,12},{8,0},{12,4},{16,24},{20,28},{24,16},{28,20},{1,9},{5... | collective-permute-start | bytes 589832 | tf_op jit(solution)/shard_map/ppermute | solution.py:17
  16.6 2.6 %collective-permute-start.7 = (bf16[128,768]{1,0:T(8,128)(2,1)S(1)}, bf16[128,768]{1,0:T(8,128)(2,1)S(1)}, u32[]{:S(2)}, u32[]{:S(2)}) collective-permute-start(bf16[128,768]{1,0:T(8,128)(2,1)S(1)} %get-tuple-element.30.refs_3_.refs_8_), channel_id=1, source_target_pairs={{0,16},{4,20},{8,24},{12,28},{16,0},{20,4},{24,8},{28,12},{1,17},{... | collective-permute-start | bytes 589832 | tf_op jit(solution)/shard_map/ppermute | solution.py:17
  19.2 3.8 %collective-permute-done.4.refs_0_ = bf16[2,192,768]{2,1,0:T(8,128)(2,1)S(1)} collective-permute-done((bf16[2,192,768]{2,1,0:T(8,128)(2,1)S(1)}, bf16[2,192,768]{2,1,0:T(8,128)(2,1)S(1)}, u32[]{:S(2)}, u32[]{:S(2)}) %collective-permute-start.4) | collective-permute-done | bytes 589856 | tf_op jit(solution)/shard_map/ppermute | solution.py:17
  22.9 3.8 %collective-permute-start.8 = (bf16[128,768]{1,0:T(8,128)(2,1)S(1)}, bf16[128,768]{1,0:T(8,128)(2,1)S(1)}, u32[]{:S(2)}, u32[]{:S(2)}) collective-permute-start(bf16[128,768]{1,0:T(8,128)(2,1)S(1)} %get-tuple-element.30.refs_3_.refs_8_), channel_id=1, source_target_pairs={{0,24},{4,28},{8,16},{12,20},{16,8},{20,12},{24,0},{28,4},{1,25},{... | collective-permute-start | bytes 589832 | tf_op jit(solution)/shard_map/ppermute | solution.py:17
  26.8 3.7 %project.2.refs_3_ = bf16[4,192,256]{2,1,0:T(8,128)(2,1)S(1)} custom-call(s32[5]{0:T(128)S(1)} %stack.20.sc, bf16[2,192,768]{2,1,0:T(8,128)(2,1)S(1)} %collective-permute-done.4.refs_0_, bf16[768,3072]{1,0:T(8,128)(2,1)S(1)} %bitcast.14, bf16[768,3072]{1,0:T(8,128)(2,1)} %collective-permute-done.refs_5_.refs_2_, ...), custom_call_target="tpu_custom_call" | custom-call | flops 1066666688 | tf_op jit(solution)/shard_map/project/pallas_call | solution.py:191
  30.5 1.6 %collective-permute-start.5 = (bf16[4,192,256]{2,1,0:T(8,128)(2,1)S(1)}, bf16[4,192,256]{2,1,0:T(8,128)(2,1)S(1)}, u32[]{:S(2)}, u32[]{:S(2)}) collective-permute-start(bf16[4,192,256]{2,1,0:T(8,128)(2,1)S(1)} %project.2.refs_3_), channel_id=1, source_target_pairs={{0,2},{1,3},{2,0},{3,1},{4,6},{5,7},{6,4},{7,5},{8,10},{9,11},{10,... | collective-permute-start | bytes 1179656 | tf_op jit(solution)/shard_map/ppermute | solution.py:17
  32.1 4.3 %project.3.refs_3_ = bf16[4,192,512]{2,1,0:T(8,128)(2,1)S(1)} custom-call(s32[5]{0:T(128)S(1)} %stack.20.sc, bf16[2,192,768]{2,1,0:T(8,128)(2,1)S(1)} %collective-permute-done.4.refs_0_, bf16[768,3072]{1,0:T(8,128)(2,1)S(1)} %bitcast.14, bf16[768,3072]{1,0:T(8,128)(2,1)} %collective-permute-done.refs_5_.refs_2_, bf16[4,192,256]{2,1,0:T(8,128)(2,1)S(1)} %project.2.refs_3_), custom_call_target="tpu_custom_call" | custom-call | flops 2133333376 | tf_op jit(solution)/shard_map/project/pallas_call | solution.py:191
  36.4 0.6 collective-permute-start.13
  37.0 0.6 stack.21.refs_6_.refs_10_
  37.6 1.6 %collective-permute-start.12 = (bf16[3,128,768]{2,1,0:T(8,128)(2,1)S(1)}, bf16[3,128,768]{2,1,0:T(8,128)(2,1)S(1)}, u32[]{:S(2)}, u32[]{:S(2)}) collective-permute-start(bf16[3,128,768]{2,1,0:T(8,128)(2,1)S(1)} %stack.21.refs_6_.refs_10_), channel_id=1, source_target_pairs={{0,4},{4,0},{8,12},{12,8},{16,20},{20,16},{24,28},{28,24},{1,5},{5... | collective-permute-start | bytes 1769480 | tf_op jit(solution)/shard_map/ppermute | solution.py:17
  39.3 0.6 collective-permute-start.11
  39.9 1.0 collective-permute-done.10.refs_7_.refs_11_
  40.8 0.1 collective-permute-start.1
  41.0 1.6 %collective-permute-done.5.refs_5_ = bf16[4,192,256]{2,1,0:T(8,128)(2,1)S(1)} collective-permute-done((bf16[4,192,256]{2,1,0:T(8,128)(2,1)S(1)}, bf16[4,192,256]{2,1,0:T(8,128)(2,1)S(1)}, u32[]{:S(2)}, u32[]{:S(2)}) %collective-permute-start.5) | collective-permute-done | bytes 393248 | tf_op jit(solution)/shard_map/ppermute | solution.py:17
  42.6 5.9 %base.1.refs_12_.refs_0_ = f32[4,192,768]{2,1,0:T(8,128)S(1)} custom-call(s32[5]{0:T(128)S(1)} %stack.20.sc, bf16[2,192,768]{2,1,0:T(8,128)(2,1)S(1)} %attend.3.refs_4_.refs_0_, bf16[768,3072]{1,0:T(8,128)(2,1)S(1)} %bitcast.14, bf16[768,3072]{1,0:T(8,128)(2,1)} %collective-permute-done.refs_5_.refs_2_, bf16[1,192,3072]{2,1,0:T(8,128)(2,1)S(1)} %copy-done, ...), custom_call_target="tpu_custom_call" | custom-call | flops 2800000000 | tf_op jit(solution)/shard_map/base/pallas_call | solution.py:191
  48.5 7.4 %collective-permute-done.11.refs_9_ = bf16[128,768]{1,0:T(8,128)(2,1)S(1)} collective-permute-done((bf16[128,768]{1,0:T(8,128)(2,1)S(1)}, bf16[128,768]{1,0:T(8,128)(2,1)S(1)}, u32[]{:S(2)}, u32[]{:S(2)}) %collective-permute-start.11) | collective-permute-done | bytes 196640 | tf_op jit(solution)/shard_map/ppermute | solution.py:17
  55.9 1.7 %choose.1 = (bf16[64,1024]{1,0:T(8,128)(2,1)S(1)}, bf16[64,1024]{1,0:T(8,128)(2,1)S(1)}, bf16[64,1024]{1,0:T(8,128)(2,1)S(1)}, bf16[64,1024]{1,0:T(8,128)(2,1)S(1)}, f32[64,192]{1,0:T(8,128)S(1)}) custom-call(s32[5]{0:T(128)S(1)} %stack.20.sc, f32[8,128]{1,0:T(8,128)S(1)} %get-tuple-element.29.refs_0_, f32[8,128]{1,0:T(8,128)S(1)} %collective-permute-done.1.refs_1_, ...), custom_call_target="tpu_custom_call" | custom-call | flops 800000000 | tf_op jit(solution)/shard_map/choose/pallas_call | solution.py:191
  57.7 1.6 %collective-permute-start.15 = (bf16[64,1024]{1,0:T(8,128)(2,1)S(1)}, bf16[64,1024]{1,0:T(8,128)(2,1)S(1)}, u32[]{:S(2)}, u32[]{:S(2)}) collective-permute-start(bf16[64,1024]{1,0:T(8,128)(2,1)S(1)} %get-tuple-element.34), channel_id=1, source_target_pairs={{0,2},{1,3},{2,0},{3,1},{4,6},{5,7},{6,4},{7,5},{8,10},{9,11},{10,... | collective-permute-start | bytes 393224 | tf_op jit(solution)/shard_map/ppermute | solution.py:17
  59.3 0.2 collective-permute-start.16
  59.5 4.5 %collective-permute-done.15.refs_5_ = bf16[64,1024]{1,0:T(8,128)(2,1)S(1)} collective-permute-done((bf16[64,1024]{1,0:T(8,128)(2,1)S(1)}, bf16[64,1024]{1,0:T(8,128)(2,1)S(1)}, u32[]{:S(2)}, u32[]{:S(2)}) %collective-permute-start.15) | collective-permute-done | bytes 131104 | tf_op jit(solution)/shard_map/ppermute | solution.py:17
  64.0 1.9 %collective-permute-done.16.refs_6_ = bf16[64,1024]{1,0:T(8,128)(2,1)S(1)} collective-permute-done((bf16[64,1024]{1,0:T(8,128)(2,1)S(1)}, bf16[64,1024]{1,0:T(8,128)(2,1)S(1)}, u32[]{:S(2)}, u32[]{:S(2)}) %collective-permute-start.16) | collective-permute-done | bytes 131104 | tf_op jit(solution)/shard_map/ppermute | solution.py:17
  65.9 3.7 %error.1 = (bf16[64,1024]{1,0:T(8,128)(2,1)S(1)}, bf16[64,1024]{1,0:T(8,128)(2,1)S(1)}, bf16[64,1024]{1,0:T(8,128)(2,1)S(1)}, bf16[64,1024]{1,0:T(8,128)(2,1)S(1)}, f32[1,1]{1,0:T(1,128)}) custom-call(s32[5]{0:T(128)S(1)} %stack.20.sc, f32[4,192,768]{2,1,0:T(8,128)S(1)} %base.1.refs_12_.refs_0_, f32[64,192]{1,0:T(8,128)S(1)} %get-tuple-element.31.refs_1_, ...), custom_call_target="tpu_custom_call" | custom-call | flops 1200000000 | tf_op jit(solution)/shard_map/error/pallas_call | solution.py:191
  69.7 0.3 collective-permute-start.17
  70.0 1.6 %collective-permute-start.18 = (bf16[64,1024]{1,0:T(8,128)(2,1)S(1)}, bf16[64,1024]{1,0:T(8,128)(2,1)S(1)}, u32[]{:S(2)}, u32[]{:S(2)}) collective-permute-start(bf16[64,1024]{1,0:T(8,128)(2,1)S(1)} %get-tuple-element.38), channel_id=1, source_target_pairs={{0,2},{1,3},{2,0},{3,1},{4,6},{5,7},{6,4},{7,5},{8,10},{9,11},{10,... | collective-permute-start | bytes 393224 | tf_op jit(solution)/shard_map/ppermute | solution.py:17
  71.6 4.7 %collective-permute-done.18.refs_6_ = bf16[64,1024]{1,0:T(8,128)(2,1)S(1)} collective-permute-done((bf16[64,1024]{1,0:T(8,128)(2,1)S(1)}, bf16[64,1024]{1,0:T(8,128)(2,1)S(1)}, u32[]{:S(2)}, u32[]{:S(2)}) %collective-permute-start.18) | collective-permute-done | bytes 131104 | tf_op jit(solution)/shard_map/ppermute | solution.py:17
  76.3 1.4 %collective-permute-done.19.refs_7_ = bf16[64,1024]{1,0:T(8,128)(2,1)S(1)} collective-permute-done((bf16[64,1024]{1,0:T(8,128)(2,1)S(1)}, bf16[64,1024]{1,0:T(8,128)(2,1)S(1)}, u32[]{:S(2)}, u32[]{:S(2)}) %collective-permute-start.19) | collective-permute-done | bytes 131104 | tf_op jit(solution)/shard_map/ppermute | solution.py:17
  77.8 1.7 %first.1 = (f32[4,64,1024]{2,1,0:T(8,128)S(1)}, bf16[4,64,1024]{2,1,0:T(8,128)(2,1)S(1)}, f32[2,64,512]{2,1,0:T(8,128)S(1)}, bf16[2,64,512]{2,1,0:T(8,128)(2,1)S...) custom-call(s32[5]{0:T(128)S(1)} %stack.20.sc, f32[8,128]{1,0:T(8,128)S(1)} %get-tuple-element.29.refs_0_, ...), custom_call_target="tpu_custom_call" | custom-call | flops 800000000 | tf_op jit(solution)/shard_map/first/pallas_call | solution.py:191
  79.4 1.5 %collective-permute-start.20 = (bf16[4,64,1024]{2,1,0:T(8,128)(2,1)S(1)}, bf16[4,64,1024]{2,1,0:T(8,128)(2,1)S(1)}, u32[]{:S(2)}, u32[]{:S(2)}) collective-permute-start(bf16[4,64,1024]{2,1,0:T(8,128)(2,1)S(1)} %get-tuple-element.42), channel_id=1, source_target_pairs={{0,4},{4,0},{8,12},{12,8},{16,20},{20,16},{24,28},{28,24},{1,5},{5... | collective-permute-start | bytes 1572872 | tf_op jit(solution)/shard_map/ppermute | solution.py:17
  81.0 2.0 %collective-permute-start.21 = (bf16[2,64,512]{2,1,0:T(8,128)(2,1)S(1)}, bf16[2,64,512]{2,1,0:T(8,128)(2,1)S(1)}, u32[]{:S(2)}, u32[]{:S(2)}) collective-permute-start(bf16[2,64,512]{2,1,0:T(8,128)(2,1)S(1)} %get-tuple-element.43), channel_id=1, source_target_pairs={{0,8},{4,12},{8,0},{12,4},{16,24},{20,28},{24,16},{28,20},{1,9},{5... | collective-permute-start | bytes 393224 | tf_op jit(solution)/shard_map/ppermute | solution.py:17
  82.9 0.3 collective-permute-start.22
  83.2 2.1 %collective-permute-start.23 = (bf16[2,64,512]{2,1,0:T(8,128)(2,1)S(1)}, bf16[2,64,512]{2,1,0:T(8,128)(2,1)S(1)}, u32[]{:S(2)}, u32[]{:S(2)}) collective-permute-start(bf16[2,64,512]{2,1,0:T(8,128)(2,1)S(1)} %get-tuple-element.45), channel_id=1, source_target_pairs={{0,24},{4,28},{8,16},{12,20},{16,8},{20,12},{24,0},{28,4},{1,25},{... | collective-permute-start | bytes 393224 | tf_op jit(solution)/shard_map/ppermute | solution.py:17
  85.3 3.1 %collective-permute-done.21.refs_3_ = bf16[2,64,512]{2,1,0:T(8,128)(2,1)S(1)} collective-permute-done((bf16[2,64,512]{2,1,0:T(8,128)(2,1)S(1)}, bf16[2,64,512]{2,1,0:T(8,128)(2,1)S(1)}, u32[]{:S(2)}, u32[]{:S(2)}) %collective-permute-start.21) | collective-permute-done | bytes 131104 | tf_op jit(solution)/shard_map/ppermute | solution.py:17
  88.4 7.4 %collective-permute-done.22.refs_4_ = bf16[2,64,512]{2,1,0:T(8,128)(2,1)S(1)} collective-permute-done((bf16[2,64,512]{2,1,0:T(8,128)(2,1)S(1)}, bf16[2,64,512]{2,1,0:T(8,128)(2,1)S(1)}, u32[]{:S(2)}, u32[]{:S(2)}) %collective-permute-start.22) | collective-permute-done | bytes 131104 | tf_op jit(solution)/shard_map/ppermute | solution.py:17
  95.8 0.7 second.1
  96.5 2.5 %collective-permute-start.24 = (bf16[64,1024]{1,0:T(8,128)(2,1)S(1)}, bf16[64,1024]{1,0:T(8,128)(2,1)S(1)}, u32[]{:S(2)}, u32[]{:S(2)}) collective-permute-start(bf16[64,1024]{1,0:T(8,128)(2,1)S(1)} %get-tuple-element.47), channel_id=1, source_target_pairs={{0,8},{4,12},{8,0},{12,4},{16,24},{20,28},{24,16},{28,20},{1,9},{5... | collective-permute-start | bytes 393224 | tf_op jit(solution)/shard_map/ppermute | solution.py:17
  99.0 0.4 collective-permute-start.25
  99.4 2.1 %collective-permute-start.26 = (bf16[64,1024]{1,0:T(8,128)(2,1)S(1)}, bf16[64,1024]{1,0:T(8,128)(2,1)S(1)}, u32[]{:S(2)}, u32[]{:S(2)}) collective-permute-start(bf16[64,1024]{1,0:T(8,128)(2,1)S(1)} %get-tuple-element.49), channel_id=1, source_target_pairs={{0,24},{4,28},{8,16},{12,20},{16,8},{20,12},{24,0},{28,4},{1,25},{... | collective-permute-start | bytes 393224 | tf_op jit(solution)/shard_map/ppermute | solution.py:17
  101.4 0.5 collective-permute-start.27
  102.0 3.7 %collective-permute-done.27.refs_5_ = bf16[64,512]{1,0:T(8,128)(2,1)S(1)} collective-permute-done((bf16[64,512]{1,0:T(8,128)(2,1)S(1)}, bf16[64,512]{1,0:T(8,128)(2,1)S(1)}, u32[]{:S(2)}, u32[]{:S(2)}) %collective-permute-start.27) | collective-permute-done | bytes 65568 | tf_op jit(solution)/shard_map/ppermute | solution.py:17
  105.7 5.2 %collective-permute-done.25.refs_2_ = bf16[64,1024]{1,0:T(8,128)(2,1)S(1)} collective-permute-done((bf16[64,1024]{1,0:T(8,128)(2,1)S(1)}, bf16[64,1024]{1,0:T(8,128)(2,1)S(1)}, u32[]{:S(2)}, u32[]{:S(2)}) %collective-permute-start.25) | collective-permute-done | bytes 131104 | tf_op jit(solution)/shard_map/ppermute | solution.py:17
  110.9 1.3 %finish.1 = (f32[1,64,768]{2,1,0:T(8,128)}, f32[1,64,768]{2,1,0:T(8,128)}) custom-call(s32[5]{0:T(128)S(1)} %stack.20.sc, f32[64,1024]{1,0:T(8,128)S(1)} %get-tuple-element.46.refs_0_, bf16[64,1024]{1,0:T(8,128)(2,1)S(1)} %collective-permute-done.24.refs_1_, bf16[64,1024]{1,0:T(8,128)(2,1)S(1)} %collective-permute-done.25.refs_2_, ...), custom_call_target="tpu_custom_call" | custom-call | flops 520000000 | tf_op jit(solution)/shard_map/finish/pallas_call | solution.py:191
  (40 shorter events, 0.5 us)
Async XLA Ops:
  0.6 12.5 %collective-permute-start = (bf16[768,3072]{1,0:T(8,128)(2,1)}, bf16[768,3072]{1,0:T(8,128)(2,1)}, u32[]{:S(2)}, u32[]{:S(2)}) collective-permute-start(bf16[768,3072]{1,0:T(8,128)(2,1)} %refs_1_.11), channel_id=1, source_target_pairs={{0,1},{1,0},{2,3},{3,2},{4,5},{5,4},{6,7},{7,6},{8,9},{9,8},{10,11... | collective-permute-start | bytes 14155784 | tf_op jit(solution)/shard_map/ppermute | solution.py:17
  1.9 1.3 %copy-start.5 = (bf16[1,192,3072]{2,1,0:T(8,128)(2,1)S(1)}, bf16[1,192,3072]{2,1,0:T(8,128)(2,1)}, u32[]{:S(2)}) copy-start(bf16[1,192,3072]{2,1,0:T(8,128)(2,1)} %refs_0_.4) | copy-start | bytes 3538948
  3.2 23.6 %slice-start = ((s8[4718592]{0:T(1024)(128)(4,1)}), s8[524288]{0:T(1024)(128)(4,1)S(1)}, s32[]{:S(2)}) async-start(s8[4718592]{0:T(1024)(128)(4,1)} %bitcast.13), calls=%async_computation | async-start | bytes 1048576
  6.3 16.6 %collective-permute-start.4 = (bf16[2,192,768]{2,1,0:T(8,128)(2,1)S(1)}, bf16[2,192,768]{2,1,0:T(8,128)(2,1)S(1)}, u32[]{:S(2)}, u32[]{:S(2)}) collective-permute-start(bf16[2,192,768]{2,1,0:T(8,128)(2,1)S(1)} %attend.2.refs_3_), channel_id=1, source_target_pairs={{0,2},{1,3},{2,0},{3,1},{4,6},{5,7},{6,4},{7,5},{8,10},{9,11},{10,... | collective-permute-start | bytes 1769480 | tf_op jit(solution)/shard_map/ppermute | solution.py:17
  9.6 3.5 %copy-start.2 = (bf16[1,64,768]{2,1,0:T(8,128)(2,1)S(1)}, bf16[1,64,768]{2,1,0:T(8,128)(2,1)}, u32[]{:S(2)}) copy-start(bf16[1,64,768]{2,1,0:T(8,128)(2,1)} %refs_0_.5) | copy-start | bytes 294916
  9.6 3.5 %copy-start.3 = (bf16[1,64,768]{2,1,0:T(8,128)(2,1)S(1)}, bf16[1,64,768]{2,1,0:T(8,128)(2,1)}, u32[]{:S(2)}) copy-start(bf16[1,64,768]{2,1,0:T(8,128)(2,1)} %refs_1_.8) | copy-start | bytes 294916
  9.6 3.5 %copy-start.4 = (s32[8]{0:T(128)S(1)}, s32[8]{0:T(128)}, u32[]{:S(2)}) copy-start(s32[8]{0:T(128)} %refs_3_.2) | copy-start | bytes 100
  9.6 17.2 %slice-start.1 = ((s8[4718592]{0:T(1024)(128)(4,1)}), s8[4194304]{0:T(1024)(128)(4,1)S(1)}, s32[]{:S(2)}) async-start(s8[4718592]{0:T(1024)(128)(4,1)} %bitcast.13), calls=%async_computation.1 | async-start | bytes 8388608
  14.2 12.5 %collective-permute-start.2 = (f32[8,128]{1,0:T(8,128)S(1)}, f32[8,128]{1,0:T(8,128)S(1)}, u32[]{:S(2)}, u32[]{:S(2)}) collective-permute-start(f32[8,128]{1,0:T(8,128)S(1)} %get-tuple-element.29.refs_0_), channel_id=1, source_target_pairs={{0,2},{1,3},{2,0},{3,1},{4,6},{5,7},{6,4},{7,5},{8,10},{9,11},{10,... | collective-permute-start | bytes 12296 | tf_op jit(solution)/shard_map/ppermute | solution.py:17
  14.4 24.9 %collective-permute-start.9 = (bf16[192,768]{1,0:T(8,128)(2,1)S(1)}, bf16[192,768]{1,0:T(8,128)(2,1)S(1)}, u32[]{:S(2)}, u32[]{:S(2)}) collective-permute-start(bf16[192,768]{1,0:T(8,128)(2,1)S(1)} %get-tuple-element.57), channel_id=1, source_target_pairs={{0,1},{1,0},{2,3},{3,2},{4,5},{5,4},{6,7},{7,6},{8,9},{9,8},{10,11... | collective-permute-start | bytes 884744 | tf_op jit(solution)/shard_map/ppermute | solution.py:17
  14.6 21.8 %collective-permute-start.6 = (bf16[128,768]{1,0:T(8,128)(2,1)S(1)}, bf16[128,768]{1,0:T(8,128)(2,1)S(1)}, u32[]{:S(2)}, u32[]{:S(2)}) collective-permute-start(bf16[128,768]{1,0:T(8,128)(2,1)S(1)} %get-tuple-element.30.refs_3_.refs_8_), channel_id=1, source_target_pairs={{0,8},{4,12},{8,0},{12,4},{16,24},{20,28},{24,16},{28,20},{1,9},{5... | collective-permute-start | bytes 589832 | tf_op jit(solution)/shard_map/ppermute | solution.py:17
  16.6 20.4 %collective-permute-start.7 = (bf16[128,768]{1,0:T(8,128)(2,1)S(1)}, bf16[128,768]{1,0:T(8,128)(2,1)S(1)}, u32[]{:S(2)}, u32[]{:S(2)}) collective-permute-start(bf16[128,768]{1,0:T(8,128)(2,1)S(1)} %get-tuple-element.30.refs_3_.refs_8_), channel_id=1, source_target_pairs={{0,16},{4,20},{8,24},{12,28},{16,0},{20,4},{24,8},{28,12},{1,17},{... | collective-permute-start | bytes 589832 | tf_op jit(solution)/shard_map/ppermute | solution.py:17
  22.9 14.0 %collective-permute-start.8 = (bf16[128,768]{1,0:T(8,128)(2,1)S(1)}, bf16[128,768]{1,0:T(8,128)(2,1)S(1)}, u32[]{:S(2)}, u32[]{:S(2)}) collective-permute-start(bf16[128,768]{1,0:T(8,128)(2,1)S(1)} %get-tuple-element.30.refs_3_.refs_8_), channel_id=1, source_target_pairs={{0,24},{4,28},{8,16},{12,20},{16,8},{20,12},{24,0},{28,4},{1,25},{... | collective-permute-start | bytes 589832 | tf_op jit(solution)/shard_map/ppermute | solution.py:17
  30.5 12.1 %collective-permute-start.5 = (bf16[4,192,256]{2,1,0:T(8,128)(2,1)S(1)}, bf16[4,192,256]{2,1,0:T(8,128)(2,1)S(1)}, u32[]{:S(2)}, u32[]{:S(2)}) collective-permute-start(bf16[4,192,256]{2,1,0:T(8,128)(2,1)S(1)} %project.2.refs_3_), channel_id=1, source_target_pairs={{0,2},{1,3},{2,0},{3,1},{4,6},{5,7},{6,4},{7,5},{8,10},{9,11},{10,... | collective-permute-start | bytes 1179656 | tf_op jit(solution)/shard_map/ppermute | solution.py:17
  36.4 6.2 %copy-start = (bf16[1,192,3072]{2,1,0:T(8,128)(2,1)S(1)}, bf16[1,192,3072]{2,1,0:T(8,128)(2,1)}, u32[]{:S(2)}) copy-start(bf16[1,192,3072]{2,1,0:T(8,128)(2,1)} %refs_3_.3) | copy-start | bytes 3538948
  36.4 6.2 %copy-start.1 = (bf16[1,192,3072]{2,1,0:T(8,128)(2,1)S(1)}, bf16[1,192,3072]{2,1,0:T(8,128)(2,1)}, u32[]{:S(2)}) copy-start(bf16[1,192,3072]{2,1,0:T(8,128)(2,1)} %refs_4_.1) | copy-start | bytes 3538948
  36.4 23.1 %collective-permute-start.13 = (bf16[4,192,512]{2,1,0:T(8,128)(2,1)S(1)}, bf16[4,192,512]{2,1,0:T(8,128)(2,1)S(1)}, u32[]{:S(2)}, u32[]{:S(2)}) collective-permute-start(bf16[4,192,512]{2,1,0:T(8,128)(2,1)S(1)} %project.3.refs_3_), channel_id=1, source_target_pairs={{0,2},{1,3},{2,0},{3,1},{4,6},{5,7},{6,4},{7,5},{8,10},{9,11},{10,... | collective-permute-start | bytes 2359304 | tf_op jit(solution)/shard_map/ppermute | solution.py:17
  37.6 18.3 %collective-permute-start.12 = (bf16[3,128,768]{2,1,0:T(8,128)(2,1)S(1)}, bf16[3,128,768]{2,1,0:T(8,128)(2,1)S(1)}, u32[]{:S(2)}, u32[]{:S(2)}) collective-permute-start(bf16[3,128,768]{2,1,0:T(8,128)(2,1)S(1)} %stack.21.refs_6_.refs_10_), channel_id=1, source_target_pairs={{0,4},{4,0},{8,12},{12,8},{16,20},{20,16},{24,28},{28,24},{1,5},{5... | collective-permute-start | bytes 1769480 | tf_op jit(solution)/shard_map/ppermute | solution.py:17
  39.2 1.6 %collective-permute-start.10 = (bf16[192,768]{1,0:T(8,128)(2,1)S(1)}, bf16[192,768]{1,0:T(8,128)(2,1)S(1)}, u32[]{:S(2)}, u32[]{:S(2)}) collective-permute-start(bf16[192,768]{1,0:T(8,128)(2,1)S(1)} %get-tuple-element.55), channel_id=1, source_target_pairs={{0,1},{1,0},{2,3},{3,2},{4,5},{5,4},{6,7},{7,6},{8,9},{9,8},{10,11... | collective-permute-start | bytes 884744 | tf_op jit(solution)/shard_map/ppermute | solution.py:17
  39.3 16.6 %collective-permute-start.11 = (bf16[128,768]{1,0:T(8,128)(2,1)S(1)}, bf16[128,768]{1,0:T(8,128)(2,1)S(1)}, u32[]{:S(2)}, u32[]{:S(2)}) collective-permute-start(bf16[128,768]{1,0:T(8,128)(2,1)S(1)} %get-tuple-element.30.refs_3_.refs_8_), channel_id=1, source_target_pairs={{0,4},{4,0},{8,12},{12,8},{16,20},{20,16},{24,28},{28,24},{1,5},{5... | collective-permute-start | bytes 589832 | tf_op jit(solution)/shard_map/ppermute | solution.py:17
  40.8 7.7 %collective-permute-start.1 = (f32[8,128]{1,0:T(8,128)S(1)}, f32[8,128]{1,0:T(8,128)S(1)}, u32[]{:S(2)}, u32[]{:S(2)}) collective-permute-start(f32[8,128]{1,0:T(8,128)S(1)} %get-tuple-element.29.refs_0_), channel_id=1, source_target_pairs={{0,1},{1,0},{2,3},{3,2},{4,5},{5,4},{6,7},{7,6},{8,9},{9,8},{10,11... | collective-permute-start | bytes 12296 | tf_op jit(solution)/shard_map/ppermute | solution.py:17
  42.6 5.9 %collective-permute-start.3 = (f32[8,128]{1,0:T(8,128)S(1)}, f32[8,128]{1,0:T(8,128)S(1)}, u32[]{:S(2)}, u32[]{:S(2)}) collective-permute-start(f32[8,128]{1,0:T(8,128)S(1)} %collective-permute-done.2.refs_4_.refs_2_), channel_id=1, source_target_pairs={{0,1},{1,0},{2,3},{3,2},{4,5},{5,4},{6,7},{7,6},{8,9},{9,8},{10,11... | collective-permute-start | bytes 12296 | tf_op jit(solution)/shard_map/ppermute | solution.py:17
  57.6 1.9 %collective-permute-start.14 = (bf16[64,1024]{1,0:T(8,128)(2,1)S(1)}, bf16[64,1024]{1,0:T(8,128)(2,1)S(1)}, u32[]{:S(2)}, u32[]{:S(2)}) collective-permute-start(bf16[64,1024]{1,0:T(8,128)(2,1)S(1)} %get-tuple-element.33), channel_id=1, source_target_pairs={{0,1},{1,0},{2,3},{3,2},{4,5},{5,4},{6,7},{7,6},{8,9},{9,8},{10,11... | collective-permute-start | bytes 393224 | tf_op jit(solution)/shard_map/ppermute | solution.py:17
  57.7 6.4 %collective-permute-start.15 = (bf16[64,1024]{1,0:T(8,128)(2,1)S(1)}, bf16[64,1024]{1,0:T(8,128)(2,1)S(1)}, u32[]{:S(2)}, u32[]{:S(2)}) collective-permute-start(bf16[64,1024]{1,0:T(8,128)(2,1)S(1)} %get-tuple-element.34), channel_id=1, source_target_pairs={{0,2},{1,3},{2,0},{3,1},{4,6},{5,7},{6,4},{7,5},{8,10},{9,11},{10,... | collective-permute-start | bytes 393224 | tf_op jit(solution)/shard_map/ppermute | solution.py:17
  59.3 6.6 %collective-permute-start.16 = (bf16[64,1024]{1,0:T(8,128)(2,1)S(1)}, bf16[64,1024]{1,0:T(8,128)(2,1)S(1)}, u32[]{:S(2)}, u32[]{:S(2)}) collective-permute-start(bf16[64,1024]{1,0:T(8,128)(2,1)S(1)} %get-tuple-element.35), channel_id=1, source_target_pairs={{0,3},{1,2},{2,1},{3,0},{4,7},{5,6},{6,5},{7,4},{8,11},{9,10},{10,... | collective-permute-start | bytes 393224 | tf_op jit(solution)/shard_map/ppermute | solution.py:17
  69.7 1.9 %collective-permute-start.17 = (bf16[64,1024]{1,0:T(8,128)(2,1)S(1)}, bf16[64,1024]{1,0:T(8,128)(2,1)S(1)}, u32[]{:S(2)}, u32[]{:S(2)}) collective-permute-start(bf16[64,1024]{1,0:T(8,128)(2,1)S(1)} %get-tuple-element.37), channel_id=1, source_target_pairs={{0,1},{1,0},{2,3},{3,2},{4,5},{5,4},{6,7},{7,6},{8,9},{9,8},{10,11... | collective-permute-start | bytes 393224 | tf_op jit(solution)/shard_map/ppermute | solution.py:17
  70.0 6.3 %collective-permute-start.18 = (bf16[64,1024]{1,0:T(8,128)(2,1)S(1)}, bf16[64,1024]{1,0:T(8,128)(2,1)S(1)}, u32[]{:S(2)}, u32[]{:S(2)}) collective-permute-start(bf16[64,1024]{1,0:T(8,128)(2,1)S(1)} %get-tuple-element.38), channel_id=1, source_target_pairs={{0,2},{1,3},{2,0},{3,1},{4,6},{5,7},{6,4},{7,5},{8,10},{9,11},{10,... | collective-permute-start | bytes 393224 | tf_op jit(solution)/shard_map/ppermute | solution.py:17
  71.6 6.2 %collective-permute-start.19 = (bf16[64,1024]{1,0:T(8,128)(2,1)S(1)}, bf16[64,1024]{1,0:T(8,128)(2,1)S(1)}, u32[]{:S(2)}, u32[]{:S(2)}) collective-permute-start(bf16[64,1024]{1,0:T(8,128)(2,1)S(1)} %get-tuple-element.39), channel_id=1, source_target_pairs={{0,3},{1,2},{2,1},{3,0},{4,7},{5,6},{6,5},{7,4},{8,11},{9,10},{10,... | collective-permute-start | bytes 393224 | tf_op jit(solution)/shard_map/ppermute | solution.py:17
  79.4 16.4 %collective-permute-start.20 = (bf16[4,64,1024]{2,1,0:T(8,128)(2,1)S(1)}, bf16[4,64,1024]{2,1,0:T(8,128)(2,1)S(1)}, u32[]{:S(2)}, u32[]{:S(2)}) collective-permute-start(bf16[4,64,1024]{2,1,0:T(8,128)(2,1)S(1)} %get-tuple-element.42), channel_id=1, source_target_pairs={{0,4},{4,0},{8,12},{12,8},{16,20},{20,16},{24,28},{28,24},{1,5},{5... | collective-permute-start | bytes 1572872 | tf_op jit(solution)/shard_map/ppermute | solution.py:17
  81.0 7.5 %collective-permute-start.21 = (bf16[2,64,512]{2,1,0:T(8,128)(2,1)S(1)}, bf16[2,64,512]{2,1,0:T(8,128)(2,1)S(1)}, u32[]{:S(2)}, u32[]{:S(2)}) collective-permute-start(bf16[2,64,512]{2,1,0:T(8,128)(2,1)S(1)} %get-tuple-element.43), channel_id=1, source_target_pairs={{0,8},{4,12},{8,0},{12,4},{16,24},{20,28},{24,16},{28,20},{1,9},{5... | collective-permute-start | bytes 393224 | tf_op jit(solution)/shard_map/ppermute | solution.py:17
  82.9 12.9 %collective-permute-start.22 = (bf16[2,64,512]{2,1,0:T(8,128)(2,1)S(1)}, bf16[2,64,512]{2,1,0:T(8,128)(2,1)S(1)}, u32[]{:S(2)}, u32[]{:S(2)}) collective-permute-start(bf16[2,64,512]{2,1,0:T(8,128)(2,1)S(1)} %get-tuple-element.44), channel_id=1, source_target_pairs={{0,16},{4,20},{8,24},{12,28},{16,0},{20,4},{24,8},{28,12},{1,17},{... | collective-permute-start | bytes 393224 | tf_op jit(solution)/shard_map/ppermute | solution.py:17
  83.2 12.6 %collective-permute-start.23 = (bf16[2,64,512]{2,1,0:T(8,128)(2,1)S(1)}, bf16[2,64,512]{2,1,0:T(8,128)(2,1)S(1)}, u32[]{:S(2)}, u32[]{:S(2)}) collective-permute-start(bf16[2,64,512]{2,1,0:T(8,128)(2,1)S(1)} %get-tuple-element.45), channel_id=1, source_target_pairs={{0,24},{4,28},{8,16},{12,20},{16,8},{20,12},{24,0},{28,4},{1,25},{... | collective-permute-start | bytes 393224 | tf_op jit(solution)/shard_map/ppermute | solution.py:17
  96.5 9.2 %collective-permute-start.24 = (bf16[64,1024]{1,0:T(8,128)(2,1)S(1)}, bf16[64,1024]{1,0:T(8,128)(2,1)S(1)}, u32[]{:S(2)}, u32[]{:S(2)}) collective-permute-start(bf16[64,1024]{1,0:T(8,128)(2,1)S(1)} %get-tuple-element.47), channel_id=1, source_target_pairs={{0,8},{4,12},{8,0},{12,4},{16,24},{20,28},{24,16},{28,20},{1,9},{5... | collective-permute-start | bytes 393224 | tf_op jit(solution)/shard_map/ppermute | solution.py:17
  99.0 11.9 %collective-permute-start.25 = (bf16[64,1024]{1,0:T(8,128)(2,1)S(1)}, bf16[64,1024]{1,0:T(8,128)(2,1)S(1)}, u32[]{:S(2)}, u32[]{:S(2)}) collective-permute-start(bf16[64,1024]{1,0:T(8,128)(2,1)S(1)} %get-tuple-element.48), channel_id=1, source_target_pairs={{0,16},{4,20},{8,24},{12,28},{16,0},{20,4},{24,8},{28,12},{1,17},{... | collective-permute-start | bytes 393224 | tf_op jit(solution)/shard_map/ppermute | solution.py:17
  99.4 11.6 %collective-permute-start.26 = (bf16[64,1024]{1,0:T(8,128)(2,1)S(1)}, bf16[64,1024]{1,0:T(8,128)(2,1)S(1)}, u32[]{:S(2)}, u32[]{:S(2)}) collective-permute-start(bf16[64,1024]{1,0:T(8,128)(2,1)S(1)} %get-tuple-element.49), channel_id=1, source_target_pairs={{0,24},{4,28},{8,16},{12,20},{16,8},{20,12},{24,0},{28,4},{1,25},{... | collective-permute-start | bytes 393224 | tf_op jit(solution)/shard_map/ppermute | solution.py:17
  101.4 4.3 %collective-permute-start.27 = (bf16[64,512]{1,0:T(8,128)(2,1)S(1)}, bf16[64,512]{1,0:T(8,128)(2,1)S(1)}, u32[]{:S(2)}, u32[]{:S(2)}) collective-permute-start(bf16[64,512]{1,0:T(8,128)(2,1)S(1)} %get-tuple-element.51), channel_id=1, source_target_pairs={{0,4},{4,0},{8,12},{12,8},{16,20},{20,16},{24,28},{28,24},{1,5},{5... | collective-permute-start | bytes 196616 | tf_op jit(solution)/shard_map/ppermute | solution.py:17

commit v5 on v4

--- a/solution.py
+++ b/solution.py
@@ -169,7 +169,7 @@
 
 LANES = 128
 VMEM = 20 * 1024 * 1024
-COST = 4e8
+COST = 6.5e8
 ALONE = 52 * 1024 * 1024
 SHARD, CORE, CHIP, COUNT, GROUP = range(5)
 
@@ -206,6 +206,15 @@
     )(scalars, *operands, *after)
 
 
+def ordered_call(body, name, scalars, operands, out_shape, micros, order):
+    def inner_body(sc, *refs):
+        outs = refs[len(operands) :]
+        body(sc, *refs[: len(operands)], *[outs[order.index(i)] for i in range(len(order))])
+
+    out = kernel_call(inner_body, name, scalars, operands, [out_shape[i] for i in order], micros)
+    return [out[order.index(i)] for i in range(len(order))]
+
+
 def shaped(shape, dtype=BF16):
     return jax.ShapeDtypeStruct(shape, dtype)
 
@@ -222,14 +231,16 @@
             lanes = pl.ds(pl.multiple_of(shard * depth, LANES), depth)
             return pltpu.make_async_copy((q_ref, k_ref, v_ref)[i].at[0, :, lanes], held.at[c, i], sems.at[c, i])
 
-        for c in range(2):
-            for i in range(3):
-                copy(c, i).start()
+        for i in range(3):
+            copy(0, i).start()
         seen = lax.broadcasted_iota(jnp.int32, (1, slots), 1) < sc[COUNT]
         at = [slice(h * size, (h + 1) * size) for h in range(heads)]
         for c in range(2):
             for i in range(3):
                 copy(c, i).wait()
+            if c == 0:
+                for i in range(3):
+                    copy(1, i).start()
             q, k, v = (held.at[c, i] for i in range(3))
             scores = [jnp.where(seen, dot(q[:, h], k[:, h], 1, 1), -1e30) for h in at]
             scores = [jnp.exp2((x - jnp.max(x, axis=1, keepdims=True)) * scale) for x in scores]
@@ -321,27 +332,28 @@
         got, up_refs, pieces = refs[:peers], refs[peers : peers + size], refs[peers + size : -1]
         count = sc[COUNT]
         tokens = count.astype(F32)
+        per_token = 2.0 / tokens
         valid = lax.broadcasted_iota(jnp.int32, (slots, 1), 0) < count
         low_wide = low_ref[...]
         for ref in up_refs[1:]:
             low_wide = low_wide + ref[:, depth : depth + slots].astype(F32)
-        low_turned = low_wide.astype(BF16)
-        low_state = low_wide.T.astype(BF16)
+        low_turned = ADAPTER_SCALE * low_wide.astype(BF16)
+        low_state = ADAPTER_SCALE * low_wide.T.astype(BF16)
         back = jnp.zeros((rank, slots), F32)
         squares = jnp.zeros((slots, step), F32)
         for k in range(size):
             for start in range(0, depth, step):
                 at = slice(start, start + step)
                 up = up_refs[k][:, at]
-                error = base_ref[k, :, at] + ADAPTER_SCALE * dot(low_state, up, 1, 0)
+                error = base_ref[k, :, at] + dot(low_state, up, 1, 0)
                 if start >= lanes.start:
                     for ref in got:
                         error = error + ref[k, :, start - lanes.start : start - lanes.start + step].astype(F32)
                 error = jnp.where(valid, error, 0.0)
                 squares = squares + error * error
-                cotangent = (2.0 * error / tokens).astype(BF16)
+                cotangent = (error * per_token).astype(BF16)
                 back = back + dot(up, cotangent, 1, 1)
-                pieces[k][:, at] = (ADAPTER_SCALE * dot(low_turned, cotangent, 1, 0)).astype(BF16)
+                pieces[k][:, at] = dot(low_turned, cotangent, 1, 0).astype(BF16)
         refs[-1][0, 0] = jnp.sum(squares) / (tokens * (size * depth))
         padded = (ADAPTER_SCALE * back).astype(BF16)
         padded = jnp.concatenate([padded, jnp.zeros((rank, back_lanes - slots), BF16)], axis=1)
@@ -385,14 +397,26 @@
     )
 
 
-def stack_blocks(scalars, blocks, after):
+def stack_blocks(scalars, blocks, columns, after):
+    count = len(blocks)
+
     def body(sc, *refs):
-        for i in range(len(blocks)):
-            refs[-1][i] = refs[i][...]
-
-    return kernel_call(
-        body, "stack", scalars, blocks, shaped((len(blocks), *blocks[0].shape)), 0.6, after=after
-    )
+        ins, out_ref, others = refs[: count + len(columns)], refs[count + len(columns)], refs[count + len(columns) + 1 :]
+        for i in range(count):
+            out_ref[i] = ins[i][...]
+        for ref, other in zip(ins[count:], others):
+            other[...] = ref[1]
+
+    out = kernel_call(
+        body,
+        "stack",
+        scalars,
+        (*blocks, *columns),
+        [shaped((count, *blocks[0].shape))] + [shaped(x.shape[1:]) for x in columns],
+        0.8,
+        after=after,
+    )
+    return out[0], out[1:]
 
 
 def slot_offset(sc, slot_ref):
@@ -537,8 +561,8 @@
             after = [part]
         slot_list = [x for slot in near_slots for x in (slot, xor_send(slot, "fsdp", fsdp_size, 1))]
 
-        stacked = stack_blocks(scalars, outer_blocks, [part])
         inner_blocks = [xor_send(block, "frame", frame_size, s) for s in range(1, inner)]
+        stacked, others = stack_blocks(scalars, outer_blocks, [own, *theirs], [part, *inner_blocks])
         far_blocks = [xor_send(stacked, "frame", frame_size, s) for s in range(1, inner)]
         base = base_error(
             scalars,
@@ -559,9 +583,9 @@
                 blocks[o * inner + s] = (far_blocks[s - 1], o - 1) if o else (inner_blocks[s - 1], None)
 
         columns = [None] * fsdp_size
-        for c, x in enumerate([own] + theirs):
+        for c, (x, other) in enumerate(zip([own] + theirs, others)):
             columns[2 * c] = x[0]
-            columns[2 * c + 1] = xor_send(x[1], "fsdp", fsdp_size, 1)
+            columns[2 * c + 1] = xor_send(other, "fsdp", fsdp_size, 1)
 
         chosen, low_part = choose_adapters(scalars, slot_list, blocks, columns, [base])
         adapters = send_shards(chosen)
@@ -587,10 +611,13 @@
             ups = [p[:, cut:depth].astype(F32) for p in got]
             first_refs(offsets, ups, outs[inner], outs[inner + 1 :], *along_outer)
 
-        out = kernel_call(first, "first", scalars, (*slot_list, *pieces, *columns), first_shape, 2.0)
+        far = [o for o in range(1, outer) if 2 * o >= outer]
+        near = [o for o in range(1, outer) if 2 * o < outer]
+        order = [0, inner, *[inner + o for o in far], *range(1, inner), *[inner + o for o in near]]
+        out = ordered_call(first, "first", scalars, (*slot_list, *pieces, *columns), first_shape, 2.0, order)
         keeps = out[0], out[inner]
+        outer_got = send_frames(out[inner + 1 :], inner)
         inner_got = send_frames(out[1:inner], 1)
-        outer_got = send_frames(out[inner + 1 :], inner)
 
         def second(sc, inner_keep, outer_keep, *refs):
             inners, refs = refs[: inner - 1], refs[inner - 1 :]
@@ -598,7 +625,9 @@
             second_refs(inner_keep, inners, refs[0], refs[1:outer], outer)
             second_refs(outer_keep, outers, refs[outer], refs[outer + 1 :], inner)
 
-        out = kernel_call(second, "second", scalars, (*keeps, *inner_got, *outer_got), second_shape, 0.8)
+        order = [0, outer, *far, *near, *[outer + i for i in range(1, inner)]]
+        operands = (*keeps, *inner_got, *outer_got)
+        out = ordered_call(second, "second", scalars, operands, second_shape, 0.8, order)
         one = (out[0], *send_frames(out[1:outer], inner))
         two = (out[outer], *send_frames(out[outer + 1 :], 1))
 

time: 113 us -> 108 us (0.956)
  waiting for transfers between devices: 45.7 us -> 42 us
  starting transfers between devices: 31.6 us -> 29.6 us
    ppermute x28, waiting for transfers between devices: 45.7 us -> 42 us  [xor_send(): return lax.ppermute(value, axis, [(i, i ^ offset) for i in range(size)])]
    ppermute x28, starting transfers between devices: 31.6 us -> 29.6 us  [xor_send(): return lax.ppermute(value, axis, [(i, i ^ offset) for i in range(size)])]
  transfers between devices with their start and end apart: 28 -> 28, of which waited for: 12 -> 12; matrix products, arithmetic and copies ran while one was open for 0% -> 0% of each run, Pallas kernels for 21% -> 23%
where the time goes in v5:
time: 108 us; the launch traced here: 107 us
  waiting for transfers between devices  42 us (39%)
  Pallas kernels  31.8 us (29%)
  starting transfers between devices  29.6 us (27%)
  between operations  2.36 us (2%)
  local copies, waits for them, and re-layouts  1.44 us (1%)
    ppermute x28, waiting for transfers between devices, xor_send(): return lax.ppermute(value, axis, [(i, i ^ offset) for i in range(size)])  42 us
    pallas_call x12, Pallas kernels, kernel_call(): pl.pallas_call(body, out_shape=out_shape, grid_spec=pltpu.PrefetchScalarG...  31.8 us
    ppermute x28, starting transfers between devices, xor_send(): return lax.ppermute(value, axis, [(i, i ^ offset) for i in range(size)])  29.6 us
  transfers between devices with their start and end apart: 28, of which 12 were waited for; matrix products, arithmetic and copies ran while one was open for 0% of the time, Pallas kernels for 23%

profile of v5, /device:TPU:0, one launch (start us, length us, event | category | flops | bytes accessed | tf_op | source)
XLA Modules:
  0.0 107.2 jit_solution(16574947987580143209)
XLA Ops:
  0.6 0.5 collective-permute-start
  1.8 0.1 stack.20.sc
  1.9 1.3 %copy-done.3 = bf16[1,192,3072]{2,1,0:T(8,128)(2,1)S(1)} copy-done((bf16[1,192,3072]{2,1,0:T(8,128)(2,1)S(1)}, bf16[1,192,3072]{2,1,0:T(8,128)(2,1)}, u32[]{:S(2)}) %copy-start.3) | copy-done | bytes 1179672
  3.2 3.5 %attend.2.refs_3_ = bf16[2,192,768]{2,1,0:T(8,128)(2,1)S(1)} custom-call(s32[5]{0:T(128)S(1)} %stack.20.sc, bf16[1,192,3072]{2,1,0:T(8,128)(2,1)S(1)} %copy-done.3, bf16[1,192,3072]{2,1,0:T(8,128)(2,1)} %refs_1_.7, bf16[1,192,3072]{2,1,0:T(8,128)(2,1)} %refs_2_.4), custom_call_target="tpu_custom_call" | custom-call | flops 2600000000 | tf_op jit(solution)/shard_map/attend/pallas_call | solution.py:191
  6.7 2.6 %collective-permute-start.4 = (bf16[2,192,768]{2,1,0:T(8,128)(2,1)S(1)}, bf16[2,192,768]{2,1,0:T(8,128)(2,1)S(1)}, u32[]{:S(2)}, u32[]{:S(2)}) collective-permute-start(bf16[2,192,768]{2,1,0:T(8,128)(2,1)S(1)} %attend.2.refs_3_), channel_id=1, source_target_pairs={{0,2},{1,3},{2,0},{3,1},{4,6},{5,7},{6,4},{7,5},{8,10},{9,11},{10,... | collective-permute-start | bytes 1769480 | tf_op jit(solution)/shard_map/ppermute | solution.py:17
  10.1 3.8 %attend.3.refs_4_.refs_3_.refs_0_ = bf16[2,192,768]{2,1,0:T(8,128)(2,1)S(1)} custom-call(s32[5]{0:T(128)S(1)} %stack.20.sc, bf16[1,192,3072]{2,1,0:T(8,128)(2,1)} %refs_0_.4, bf16[1,192,3072]{2,1,0:T(8,128)(2,1)} %refs_1_.7, bf16[1,192,3072]{2,1,0:T(8,128)(2,1)} %refs_2_.4, bf16[2,192,768]{2,1,0:T(8,128)(2,1)S(1)} %attend.2.refs_3_), custom_call_target="tpu_custom_call" | custom-call | flops 2600000000 | tf_op jit(solution)/shard_map/attend/pallas_call | solution.py:191
  13.9 1.1 %join.1 = (bf16[128,768]{1,0:T(8,128)(2,1)S(1)}, f32[8,128]{1,0:T(8,128)S(1)}) custom-call(s32[5]{0:T(128)S(1)} %stack.20.sc, bf16[1,64,768]{2,1,0:T(8,128)(2,1)S(1)} %copy-done, bf16[1,64,768]{2,1,0:T(8,128)(2,1)S(1)} %copy-done.1, s32[1]{0:T(128)S(6)} %copy.14.refs_2_, s32[8]{0:T(128)S(1)} %copy-done.2, ...), custom_call_target="tpu_custom_call" | custom-call | flops 650000000 | tf_op jit(solution)/shard_map/join/pallas_call | solution.py:191
  15.0 0.1 collective-permute-start.2
  15.1 2.1 %collective-permute-start.6 = (bf16[128,768]{1,0:T(8,128)(2,1)S(1)}, bf16[128,768]{1,0:T(8,128)(2,1)S(1)}, u32[]{:S(2)}, u32[]{:S(2)}) collective-permute-start(bf16[128,768]{1,0:T(8,128)(2,1)S(1)} %get-tuple-element.33.refs_3_.refs_8_), channel_id=1, source_target_pairs={{0,8},{4,12},{8,0},{12,4},{16,24},{20,28},{24,16},{28,20},{1,9},{5... | collective-permute-start | bytes 589832 | tf_op jit(solution)/shard_map/ppermute | solution.py:17
  17.3 2.6 %collective-permute-start.7 = (bf16[128,768]{1,0:T(8,128)(2,1)S(1)}, bf16[128,768]{1,0:T(8,128)(2,1)S(1)}, u32[]{:S(2)}, u32[]{:S(2)}) collective-permute-start(bf16[128,768]{1,0:T(8,128)(2,1)S(1)} %get-tuple-element.33.refs_3_.refs_8_), channel_id=1, source_target_pairs={{0,16},{4,20},{8,24},{12,28},{16,0},{20,4},{24,8},{28,12},{1,17},{... | collective-permute-start | bytes 589832 | tf_op jit(solution)/shard_map/ppermute | solution.py:17
  19.9 3.4 %collective-permute-done.4.refs_0_.refs_4_ = bf16[2,192,768]{2,1,0:T(8,128)(2,1)S(1)} collective-permute-done((bf16[2,192,768]{2,1,0:T(8,128)(2,1)S(1)}, bf16[2,192,768]{2,1,0:T(8,128)(2,1)S(1)}, u32[]{:S(2)}, u32[]{:S(2)}) %collective-permute-start.4) | collective-permute-done | bytes 589856 | tf_op jit(solution)/shard_map/ppermute | solution.py:17
  23.3 1.7 %collective-permute-start.9 = (bf16[128,768]{1,0:T(8,128)(2,1)S(1)}, bf16[128,768]{1,0:T(8,128)(2,1)S(1)}, u32[]{:S(2)}, u32[]{:S(2)}) collective-permute-start(bf16[128,768]{1,0:T(8,128)(2,1)S(1)} %get-tuple-element.33.refs_3_.refs_8_), channel_id=1, source_target_pairs={{0,4},{4,0},{8,12},{12,8},{16,20},{20,16},{24,28},{28,24},{1,5},{5... | collective-permute-start | bytes 589832 | tf_op jit(solution)/shard_map/ppermute | solution.py:17
  25.0 3.7 %project.2.refs_3_ = bf16[4,192,256]{2,1,0:T(8,128)(2,1)S(1)} custom-call(s32[5]{0:T(128)S(1)} %stack.20.sc, bf16[2,192,768]{2,1,0:T(8,128)(2,1)S(1)} %collective-permute-done.4.refs_0_.refs_4_, bf16[768,3072]{1,0:T(8,128)(2,1)S(1)} %bitcast.10, bf16[768,3072]{1,0:T(8,128)(2,1)} %collective-permute-done.refs_5_.refs_2_, ...), custom_call_target="tpu_custom_call" | custom-call | flops 1733333376 | tf_op jit(solution)/shard_map/project/pallas_call | solution.py:191
  28.7 1.6 %collective-permute-start.5 = (bf16[4,192,256]{2,1,0:T(8,128)(2,1)S(1)}, bf16[4,192,256]{2,1,0:T(8,128)(2,1)S(1)}, u32[]{:S(2)}, u32[]{:S(2)}) collective-permute-start(bf16[4,192,256]{2,1,0:T(8,128)(2,1)S(1)} %project.2.refs_3_), channel_id=1, source_target_pairs={{0,2},{1,3},{2,0},{3,1},{4,6},{5,7},{6,4},{7,5},{8,10},{9,11},{10,... | collective-permute-start | bytes 1179656 | tf_op jit(solution)/shard_map/ppermute | solution.py:17
  30.3 4.3 %project.3.refs_5_ = bf16[4,192,512]{2,1,0:T(8,128)(2,1)S(1)} custom-call(s32[5]{0:T(128)S(1)} %stack.20.sc, bf16[2,192,768]{2,1,0:T(8,128)(2,1)S(1)} %collective-permute-done.4.refs_0_.refs_4_, bf16[768,3072]{1,0:T(8,128)(2,1)S(1)} %bitcast.10, bf16[768,3072]{1,0:T(8,128)(2,1)} %collective-permute-done.refs_5_.refs_2_, bf16[4,192,256]{2,1,0:T(8,128)(2,1)S(1)} %project.2.refs_3_), custom_call_target="tpu_custom_call" | custom-call | flops 3466666752 | tf_op jit(solution)/shard_map/project/pallas_call | solution.py:191
  34.7 1.2 %collective-permute-start.13 = (bf16[4,192,512]{2,1,0:T(8,128)(2,1)S(1)}, bf16[4,192,512]{2,1,0:T(8,128)(2,1)S(1)}, u32[]{:S(2)}, u32[]{:S(2)}) collective-permute-start(bf16[4,192,512]{2,1,0:T(8,128)(2,1)S(1)} %project.3.refs_5_), channel_id=1, source_target_pairs={{0,2},{1,3},{2,0},{3,1},{4,6},{5,7},{6,4},{7,5},{8,10},{9,11},{10,... | collective-permute-start | bytes 2359304 | tf_op jit(solution)/shard_map/ppermute | solution.py:17
  35.9 0.6 stack.21
  36.6 1.6 %collective-permute-start.12 = (bf16[3,128,768]{2,1,0:T(8,128)(2,1)S(1)}, bf16[3,128,768]{2,1,0:T(8,128)(2,1)S(1)}, u32[]{:S(2)}, u32[]{:S(2)}) collective-permute-start(bf16[3,128,768]{2,1,0:T(8,128)(2,1)S(1)} %get-tuple-element.34.refs_6_.refs_10_), channel_id=1, source_target_pairs={{0,4},{4,0},{8,12},{12,8},{16,20},{20,16},{24,28},{28,24},{1,5},{5... | collective-permute-start | bytes 1769480 | tf_op jit(solution)/shard_map/ppermute | solution.py:17
  38.2 0.5 collective-permute-start.10
  38.7 1.7 %collective-permute-done.5.refs_5_ = bf16[4,192,256]{2,1,0:T(8,128)(2,1)S(1)} collective-permute-done((bf16[4,192,256]{2,1,0:T(8,128)(2,1)S(1)}, bf16[4,192,256]{2,1,0:T(8,128)(2,1)S(1)}, u32[]{:S(2)}, u32[]{:S(2)}) %collective-permute-start.5) | collective-permute-done | bytes 393248 | tf_op jit(solution)/shard_map/ppermute | solution.py:17
  40.4 5.9 %base.1.refs_12_.refs_0_ = f32[4,192,768]{2,1,0:T(8,128)S(1)} custom-call(s32[5]{0:T(128)S(1)} %stack.20.sc, bf16[2,192,768]{2,1,0:T(8,128)(2,1)S(1)} %attend.3.refs_4_.refs_3_.refs_0_, bf16[768,3072]{1,0:T(8,128)(2,1)S(1)} %bitcast.10, bf16[768,3072]{1,0:T(8,128)(2,1)} %collective-permute-done.refs_5_.refs_2_, bf16[1,192,3072]{2,1,0:T(8,128)(2,1)S(1)} %copy-done.4, ...), custom_call_target="tpu_custom_call" | custom-call | flops 4550000128 | tf_op jit(solution)/shard_map/base/pallas_call | solution.py:191
  46.4 5.0 %collective-permute-done.12.refs_11_ = bf16[3,128,768]{2,1,0:T(8,128)(2,1)S(1)} collective-permute-done((bf16[3,128,768]{2,1,0:T(8,128)(2,1)S(1)}, bf16[3,128,768]{2,1,0:T(8,128)(2,1)S(1)}, u32[]{:S(2)}, u32[]{:S(2)}) %collective-permute-start.12) | collective-permute-done | bytes 589856 | tf_op jit(solution)/shard_map/ppermute | solution.py:17
  51.4 1.7 %choose.1 = (bf16[64,1024]{1,0:T(8,128)(2,1)S(1)}, bf16[64,1024]{1,0:T(8,128)(2,1)S(1)}, bf16[64,1024]{1,0:T(8,128)(2,1)S(1)}, bf16[64,1024]{1,0:T(8,128)(2,1)S(1)}, f32[64,192]{1,0:T(8,128)S(1)}) custom-call(s32[5]{0:T(128)S(1)} %stack.20.sc, f32[8,128]{1,0:T(8,128)S(1)} %get-tuple-element.32.refs_0_, f32[8,128]{1,0:T(8,128)S(1)} %collective-permute-done.1.refs_1_, ...), custom_call_target="tpu_custom_call" | custom-call | flops 1300000000 | tf_op jit(solution)/shard_map/choose/pallas_call | solution.py:191
  53.1 1.6 %collective-permute-start.15 = (bf16[64,1024]{1,0:T(8,128)(2,1)S(1)}, bf16[64,1024]{1,0:T(8,128)(2,1)S(1)}, u32[]{:S(2)}, u32[]{:S(2)}) collective-permute-start(bf16[64,1024]{1,0:T(8,128)(2,1)S(1)} %get-tuple-element.40), channel_id=1, source_target_pairs={{0,2},{1,3},{2,0},{3,1},{4,6},{5,7},{6,4},{7,5},{8,10},{9,11},{10,... | collective-permute-start | bytes 393224 | tf_op jit(solution)/shard_map/ppermute | solution.py:17
  54.7 0.3 collective-permute-start.16
  55.0 1.0 collective-permute-done.13.refs_2_
  56.0 3.5 %collective-permute-done.15.refs_5_ = bf16[64,1024]{1,0:T(8,128)(2,1)S(1)} collective-permute-done((bf16[64,1024]{1,0:T(8,128)(2,1)S(1)}, bf16[64,1024]{1,0:T(8,128)(2,1)S(1)}, u32[]{:S(2)}, u32[]{:S(2)}) %collective-permute-start.15) | collective-permute-done | bytes 131104 | tf_op jit(solution)/shard_map/ppermute | solution.py:17
  59.5 1.9 %collective-permute-done.16.refs_6_ = bf16[64,1024]{1,0:T(8,128)(2,1)S(1)} collective-permute-done((bf16[64,1024]{1,0:T(8,128)(2,1)S(1)}, bf16[64,1024]{1,0:T(8,128)(2,1)S(1)}, u32[]{:S(2)}, u32[]{:S(2)}) %collective-permute-start.16) | collective-permute-done | bytes 131104 | tf_op jit(solution)/shard_map/ppermute | solution.py:17
  61.4 3.6 %error.1 = (bf16[64,1024]{1,0:T(8,128)(2,1)S(1)}, bf16[64,1024]{1,0:T(8,128)(2,1)S(1)}, bf16[64,1024]{1,0:T(8,128)(2,1)S(1)}, bf16[64,1024]{1,0:T(8,128)(2,1)S(1)}, f32[1,1]{1,0:T(1,128)}) custom-call(s32[5]{0:T(128)S(1)} %stack.20.sc, f32[4,192,768]{2,1,0:T(8,128)S(1)} %base.1.refs_12_.refs_0_, f32[64,192]{1,0:T(8,128)S(1)} %get-tuple-element.37.refs_1_, ...), custom_call_target="tpu_custom_call" | custom-call | flops 1950000000 | tf_op jit(solution)/shard_map/error/pallas_call | solution.py:191
  65.0 0.3 collective-permute-start.17
  65.4 1.5 %collective-permute-start.18 = (bf16[64,1024]{1,0:T(8,128)(2,1)S(1)}, bf16[64,1024]{1,0:T(8,128)(2,1)S(1)}, u32[]{:S(2)}, u32[]{:S(2)}) collective-permute-start(bf16[64,1024]{1,0:T(8,128)(2,1)S(1)} %get-tuple-element.44), channel_id=1, source_target_pairs={{0,2},{1,3},{2,0},{3,1},{4,6},{5,7},{6,4},{7,5},{8,10},{9,11},{10,... | collective-permute-start | bytes 393224 | tf_op jit(solution)/shard_map/ppermute | solution.py:17
  67.0 4.7 %collective-permute-done.18.refs_6_ = bf16[64,1024]{1,0:T(8,128)(2,1)S(1)} collective-permute-done((bf16[64,1024]{1,0:T(8,128)(2,1)S(1)}, bf16[64,1024]{1,0:T(8,128)(2,1)S(1)}, u32[]{:S(2)}, u32[]{:S(2)}) %collective-permute-start.18) | collective-permute-done | bytes 131104 | tf_op jit(solution)/shard_map/ppermute | solution.py:17
  71.7 1.4 %collective-permute-done.19.refs_7_ = bf16[64,1024]{1,0:T(8,128)(2,1)S(1)} collective-permute-done((bf16[64,1024]{1,0:T(8,128)(2,1)S(1)}, bf16[64,1024]{1,0:T(8,128)(2,1)S(1)}, u32[]{:S(2)}, u32[]{:S(2)}) %collective-permute-start.19) | collective-permute-done | bytes 131104 | tf_op jit(solution)/shard_map/ppermute | solution.py:17
  73.1 1.7 %first.1 = (f32[4,64,1024]{2,1,0:T(8,128)S(1)}, f32[2,64,512]{2,1,0:T(8,128)S(1)}, bf16[2,64,512]{2,1,0:T(8,128)(2,1)S(1)}, bf16[2,64,512]{2,1,0:T(8,128)(2,1)S(...) custom-call(s32[5]{0:T(128)S(1)} %stack.20.sc, f32[8,128]{1,0:T(8,128)S(1)} %get-tuple-element.32.refs_0_, ...), custom_call_target="tpu_custom_call" | custom-call | flops 1300000000 | tf_op jit(solution)/shard_map/first/pallas_call | solution.py:191
  74.8 0.4 collective-permute-start.20
  75.2 2.4 %collective-permute-start.21 = (bf16[2,64,512]{2,1,0:T(8,128)(2,1)S(1)}, bf16[2,64,512]{2,1,0:T(8,128)(2,1)S(1)}, u32[]{:S(2)}, u32[]{:S(2)}) collective-permute-start(bf16[2,64,512]{2,1,0:T(8,128)(2,1)S(1)} %get-tuple-element.49), channel_id=1, source_target_pairs={{0,8},{4,12},{8,0},{12,4},{16,24},{20,28},{24,16},{28,20},{1,9},{5... | collective-permute-start | bytes 393224 | tf_op jit(solution)/shard_map/ppermute | solution.py:17
  77.6 2.0 %collective-permute-start.22 = (bf16[2,64,512]{2,1,0:T(8,128)(2,1)S(1)}, bf16[2,64,512]{2,1,0:T(8,128)(2,1)S(1)}, u32[]{:S(2)}, u32[]{:S(2)}) collective-permute-start(bf16[2,64,512]{2,1,0:T(8,128)(2,1)S(1)} %get-tuple-element.50), channel_id=1, source_target_pairs={{0,16},{4,20},{8,24},{12,28},{16,0},{20,4},{24,8},{28,12},{1,17},{... | collective-permute-start | bytes 393224 | tf_op jit(solution)/shard_map/ppermute | solution.py:17
  79.6 0.5 collective-permute-start.23
  80.0 3.4 %collective-permute-done.21.refs_3_ = bf16[2,64,512]{2,1,0:T(8,128)(2,1)S(1)} collective-permute-done((bf16[2,64,512]{2,1,0:T(8,128)(2,1)S(1)}, bf16[2,64,512]{2,1,0:T(8,128)(2,1)S(1)}, u32[]{:S(2)}, u32[]{:S(2)}) %collective-permute-start.21) | collective-permute-done | bytes 131104 | tf_op jit(solution)/shard_map/ppermute | solution.py:17
  83.4 7.0 %collective-permute-done.22.refs_4_ = bf16[2,64,512]{2,1,0:T(8,128)(2,1)S(1)} collective-permute-done((bf16[2,64,512]{2,1,0:T(8,128)(2,1)S(1)}, bf16[2,64,512]{2,1,0:T(8,128)(2,1)S(1)}, u32[]{:S(2)}, u32[]{:S(2)}) %collective-permute-start.22) | collective-permute-done | bytes 131104 | tf_op jit(solution)/shard_map/ppermute | solution.py:17
  90.4 0.7 second.1
  91.1 2.5 %collective-permute-start.24 = (bf16[64,1024]{1,0:T(8,128)(2,1)S(1)}, bf16[64,1024]{1,0:T(8,128)(2,1)S(1)}, u32[]{:S(2)}, u32[]{:S(2)}) collective-permute-start(bf16[64,1024]{1,0:T(8,128)(2,1)S(1)} %get-tuple-element.53), channel_id=1, source_target_pairs={{0,8},{4,12},{8,0},{12,4},{16,24},{20,28},{24,16},{28,20},{1,9},{5... | collective-permute-start | bytes 393224 | tf_op jit(solution)/shard_map/ppermute | solution.py:17
  93.6 1.0 collective-permute-start.25
  94.6 1.4 %collective-permute-start.26 = (bf16[64,1024]{1,0:T(8,128)(2,1)S(1)}, bf16[64,1024]{1,0:T(8,128)(2,1)S(1)}, u32[]{:S(2)}, u32[]{:S(2)}) collective-permute-start(bf16[64,1024]{1,0:T(8,128)(2,1)S(1)} %get-tuple-element.55), channel_id=1, source_target_pairs={{0,24},{4,28},{8,16},{12,20},{16,8},{20,12},{24,0},{28,4},{1,25},{... | collective-permute-start | bytes 393224 | tf_op jit(solution)/shard_map/ppermute | solution.py:17
  96.1 1.0 collective-permute-start.27
  97.0 3.3 %collective-permute-done.27.refs_5_ = bf16[64,512]{1,0:T(8,128)(2,1)S(1)} collective-permute-done((bf16[64,512]{1,0:T(8,128)(2,1)S(1)}, bf16[64,512]{1,0:T(8,128)(2,1)S(1)}, u32[]{:S(2)}, u32[]{:S(2)}) %collective-permute-start.27) | collective-permute-done | bytes 65568 | tf_op jit(solution)/shard_map/ppermute | solution.py:17
  100.3 5.5 %collective-permute-done.25.refs_2_ = bf16[64,1024]{1,0:T(8,128)(2,1)S(1)} collective-permute-done((bf16[64,1024]{1,0:T(8,128)(2,1)S(1)}, bf16[64,1024]{1,0:T(8,128)(2,1)S(1)}, u32[]{:S(2)}, u32[]{:S(2)}) %collective-permute-start.25) | collective-permute-done | bytes 131104 | tf_op jit(solution)/shard_map/ppermute | solution.py:17
  105.9 1.3 %finish.1 = (f32[1,64,768]{2,1,0:T(8,128)}, f32[1,64,768]{2,1,0:T(8,128)}) custom-call(s32[5]{0:T(128)S(1)} %stack.20.sc, f32[64,1024]{1,0:T(8,128)S(1)} %get-tuple-element.52.refs_0_, bf16[64,1024]{1,0:T(8,128)(2,1)S(1)} %collective-permute-done.24.refs_1_, bf16[64,1024]{1,0:T(8,128)(2,1)S(1)} %collective-permute-done.25.refs_2_, ...), custom_call_target="tpu_custom_call" | custom-call | flops 845000000 | tf_op jit(solution)/shard_map/finish/pallas_call | solution.py:191
  (40 shorter events, 0.4 us)
Async XLA Ops:
  0.6 13.3 %collective-permute-start = (bf16[768,3072]{1,0:T(8,128)(2,1)}, bf16[768,3072]{1,0:T(8,128)(2,1)}, u32[]{:S(2)}, u32[]{:S(2)}) collective-permute-start(bf16[768,3072]{1,0:T(8,128)(2,1)} %refs_1_.11), channel_id=1, source_target_pairs={{0,1},{1,0},{2,3},{3,2},{4,5},{5,4},{6,7},{7,6},{8,9},{9,8},{10,11... | collective-permute-start | bytes 14155784 | tf_op jit(solution)/shard_map/ppermute | solution.py:17
  1.9 1.3 %copy-start.3 = (bf16[1,192,3072]{2,1,0:T(8,128)(2,1)S(1)}, bf16[1,192,3072]{2,1,0:T(8,128)(2,1)}, u32[]{:S(2)}) copy-start(bf16[1,192,3072]{2,1,0:T(8,128)(2,1)} %refs_0_.4) | copy-start | bytes 3538948
  6.7 16.6 %collective-permute-start.4 = (bf16[2,192,768]{2,1,0:T(8,128)(2,1)S(1)}, bf16[2,192,768]{2,1,0:T(8,128)(2,1)S(1)}, u32[]{:S(2)}, u32[]{:S(2)}) collective-permute-start(bf16[2,192,768]{2,1,0:T(8,128)(2,1)S(1)} %attend.2.refs_3_), channel_id=1, source_target_pairs={{0,2},{1,3},{2,0},{3,1},{4,6},{5,7},{6,4},{7,5},{8,10},{9,11},{10,... | collective-permute-start | bytes 1769480 | tf_op jit(solution)/shard_map/ppermute | solution.py:17
  9.3 15.7 %slice-start = ((s8[4718592]{0:T(1024)(128)(4,1)}), s8[4194304]{0:T(1024)(128)(4,1)S(1)}, s32[]{:S(2)}) async-start(s8[4718592]{0:T(1024)(128)(4,1)} %bitcast.9), calls=%async_computation | async-start | bytes 8388608
  10.1 3.8 %copy-start = (bf16[1,64,768]{2,1,0:T(8,128)(2,1)S(1)}, bf16[1,64,768]{2,1,0:T(8,128)(2,1)}, u32[]{:S(2)}) copy-start(bf16[1,64,768]{2,1,0:T(8,128)(2,1)} %refs_0_.5) | copy-start | bytes 294916
  10.1 3.8 %copy-start.1 = (bf16[1,64,768]{2,1,0:T(8,128)(2,1)S(1)}, bf16[1,64,768]{2,1,0:T(8,128)(2,1)}, u32[]{:S(2)}) copy-start(bf16[1,64,768]{2,1,0:T(8,128)(2,1)} %refs_1_.8) | copy-start | bytes 294916
  10.1 3.8 %copy-start.2 = (s32[8]{0:T(128)S(1)}, s32[8]{0:T(128)}, u32[]{:S(2)}) copy-start(s32[8]{0:T(128)} %refs_3_.2) | copy-start | bytes 100
  10.1 14.9 %slice-start.1 = ((s8[4718592]{0:T(1024)(128)(4,1)}), s8[524288]{0:T(1024)(128)(4,1)S(1)}, s32[]{:S(2)}) async-start(s8[4718592]{0:T(1024)(128)(4,1)} %bitcast.9), calls=%async_computation.1 | async-start | bytes 1048576
  15.0 10.0 %collective-permute-start.2 = (f32[8,128]{1,0:T(8,128)S(1)}, f32[8,128]{1,0:T(8,128)S(1)}, u32[]{:S(2)}, u32[]{:S(2)}) collective-permute-start(f32[8,128]{1,0:T(8,128)S(1)} %get-tuple-element.32.refs_0_), channel_id=1, source_target_pairs={{0,2},{1,3},{2,0},{3,1},{4,6},{5,7},{6,4},{7,5},{8,10},{9,11},{10,... | collective-permute-start | bytes 12296 | tf_op jit(solution)/shard_map/ppermute | solution.py:17
  15.1 19.5 %collective-permute-start.6 = (bf16[128,768]{1,0:T(8,128)(2,1)S(1)}, bf16[128,768]{1,0:T(8,128)(2,1)S(1)}, u32[]{:S(2)}, u32[]{:S(2)}) collective-permute-start(bf16[128,768]{1,0:T(8,128)(2,1)S(1)} %get-tuple-element.33.refs_3_.refs_8_), channel_id=1, source_target_pairs={{0,8},{4,12},{8,0},{12,4},{16,24},{20,28},{24,16},{28,20},{1,9},{5... | collective-permute-start | bytes 589832 | tf_op jit(solution)/shard_map/ppermute | solution.py:17
  17.3 17.4 %collective-permute-start.7 = (bf16[128,768]{1,0:T(8,128)(2,1)S(1)}, bf16[128,768]{1,0:T(8,128)(2,1)S(1)}, u32[]{:S(2)}, u32[]{:S(2)}) collective-permute-start(bf16[128,768]{1,0:T(8,128)(2,1)S(1)} %get-tuple-element.33.refs_3_.refs_8_), channel_id=1, source_target_pairs={{0,16},{4,20},{8,24},{12,28},{16,0},{20,4},{24,8},{28,12},{1,17},{... | collective-permute-start | bytes 589832 | tf_op jit(solution)/shard_map/ppermute | solution.py:17
  19.8 16.1 %collective-permute-start.8 = (bf16[128,768]{1,0:T(8,128)(2,1)S(1)}, bf16[128,768]{1,0:T(8,128)(2,1)S(1)}, u32[]{:S(2)}, u32[]{:S(2)}) collective-permute-start(bf16[128,768]{1,0:T(8,128)(2,1)S(1)} %get-tuple-element.33.refs_3_.refs_8_), channel_id=1, source_target_pairs={{0,24},{4,28},{8,16},{12,20},{16,8},{20,12},{24,0},{28,4},{1,25},{... | collective-permute-start | bytes 589832 | tf_op jit(solution)/shard_map/ppermute | solution.py:17
  23.3 12.7 %collective-permute-start.9 = (bf16[128,768]{1,0:T(8,128)(2,1)S(1)}, bf16[128,768]{1,0:T(8,128)(2,1)S(1)}, u32[]{:S(2)}, u32[]{:S(2)}) collective-permute-start(bf16[128,768]{1,0:T(8,128)(2,1)S(1)} %get-tuple-element.33.refs_3_.refs_8_), channel_id=1, source_target_pairs={{0,4},{4,0},{8,12},{12,8},{16,20},{20,16},{24,28},{28,24},{1,5},{5... | collective-permute-start | bytes 589832 | tf_op jit(solution)/shard_map/ppermute | solution.py:17
  28.7 11.7 %collective-permute-start.5 = (bf16[4,192,256]{2,1,0:T(8,128)(2,1)S(1)}, bf16[4,192,256]{2,1,0:T(8,128)(2,1)S(1)}, u32[]{:S(2)}, u32[]{:S(2)}) collective-permute-start(bf16[4,192,256]{2,1,0:T(8,128)(2,1)S(1)} %project.2.refs_3_), channel_id=1, source_target_pairs={{0,2},{1,3},{2,0},{3,1},{4,6},{5,7},{6,4},{7,5},{8,10},{9,11},{10,... | collective-permute-start | bytes 1179656 | tf_op jit(solution)/shard_map/ppermute | solution.py:17
  34.6 5.8 %copy-start.4 = (bf16[1,192,3072]{2,1,0:T(8,128)(2,1)S(1)}, bf16[1,192,3072]{2,1,0:T(8,128)(2,1)}, u32[]{:S(2)}) copy-start(bf16[1,192,3072]{2,1,0:T(8,128)(2,1)} %refs_3_.3) | copy-start | bytes 3538948
  34.6 5.8 %copy-start.5 = (bf16[1,192,3072]{2,1,0:T(8,128)(2,1)S(1)}, bf16[1,192,3072]{2,1,0:T(8,128)(2,1)}, u32[]{:S(2)}) copy-start(bf16[1,192,3072]{2,1,0:T(8,128)(2,1)} %refs_4_.1) | copy-start | bytes 3538948
  34.6 3.6 %collective-permute-start.1 = (f32[8,128]{1,0:T(8,128)S(1)}, f32[8,128]{1,0:T(8,128)S(1)}, u32[]{:S(2)}, u32[]{:S(2)}) collective-permute-start(f32[8,128]{1,0:T(8,128)S(1)} %get-tuple-element.32.refs_0_), channel_id=1, source_target_pairs={{0,1},{1,0},{2,3},{3,2},{4,5},{5,4},{6,7},{7,6},{8,9},{9,8},{10,11... | collective-permute-start | bytes 12296 | tf_op jit(solution)/shard_map/ppermute | solution.py:17
  34.7 21.3 %collective-permute-start.13 = (bf16[4,192,512]{2,1,0:T(8,128)(2,1)S(1)}, bf16[4,192,512]{2,1,0:T(8,128)(2,1)S(1)}, u32[]{:S(2)}, u32[]{:S(2)}) collective-permute-start(bf16[4,192,512]{2,1,0:T(8,128)(2,1)S(1)} %project.3.refs_5_), channel_id=1, source_target_pairs={{0,2},{1,3},{2,0},{3,1},{4,6},{5,7},{6,4},{7,5},{8,10},{9,11},{10,... | collective-permute-start | bytes 2359304 | tf_op jit(solution)/shard_map/ppermute | solution.py:17
  36.6 14.8 %collective-permute-start.12 = (bf16[3,128,768]{2,1,0:T(8,128)(2,1)S(1)}, bf16[3,128,768]{2,1,0:T(8,128)(2,1)S(1)}, u32[]{:S(2)}, u32[]{:S(2)}) collective-permute-start(bf16[3,128,768]{2,1,0:T(8,128)(2,1)S(1)} %get-tuple-element.34.refs_6_.refs_10_), channel_id=1, source_target_pairs={{0,4},{4,0},{8,12},{12,8},{16,20},{20,16},{24,28},{28,24},{1,5},{5... | collective-permute-start | bytes 1769480 | tf_op jit(solution)/shard_map/ppermute | solution.py:17
  38.1 8.2 %collective-permute-start.3 = (f32[8,128]{1,0:T(8,128)S(1)}, f32[8,128]{1,0:T(8,128)S(1)}, u32[]{:S(2)}, u32[]{:S(2)}) collective-permute-start(f32[8,128]{1,0:T(8,128)S(1)} %collective-permute-done.2.refs_4_.refs_2_), channel_id=1, source_target_pairs={{0,1},{1,0},{2,3},{3,2},{4,5},{5,4},{6,7},{7,6},{8,9},{9,8},{10,11... | collective-permute-start | bytes 12296 | tf_op jit(solution)/shard_map/ppermute | solution.py:17
  38.2 8.1 %collective-permute-start.10 = (bf16[192,768]{1,0:T(8,128)(2,1)S(1)}, bf16[192,768]{1,0:T(8,128)(2,1)S(1)}, u32[]{:S(2)}, u32[]{:S(2)}) collective-permute-start(bf16[192,768]{1,0:T(8,128)(2,1)S(1)} %get-tuple-element.35), channel_id=1, source_target_pairs={{0,1},{1,0},{2,3},{3,2},{4,5},{5,4},{6,7},{7,6},{8,9},{9,8},{10,11... | collective-permute-start | bytes 884744 | tf_op jit(solution)/shard_map/ppermute | solution.py:17
  40.4 5.9 %collective-permute-start.11 = (bf16[192,768]{1,0:T(8,128)(2,1)S(1)}, bf16[192,768]{1,0:T(8,128)(2,1)S(1)}, u32[]{:S(2)}, u32[]{:S(2)}) collective-permute-start(bf16[192,768]{1,0:T(8,128)(2,1)S(1)} %get-tuple-element.36), channel_id=1, source_target_pairs={{0,1},{1,0},{2,3},{3,2},{4,5},{5,4},{6,7},{7,6},{8,9},{9,8},{10,11... | collective-permute-start | bytes 884744 | tf_op jit(solution)/shard_map/ppermute | solution.py:17
  53.1 2.9 %collective-permute-start.14 = (bf16[64,1024]{1,0:T(8,128)(2,1)S(1)}, bf16[64,1024]{1,0:T(8,128)(2,1)S(1)}, u32[]{:S(2)}, u32[]{:S(2)}) collective-permute-start(bf16[64,1024]{1,0:T(8,128)(2,1)S(1)} %get-tuple-element.39), channel_id=1, source_target_pairs={{0,1},{1,0},{2,3},{3,2},{4,5},{5,4},{6,7},{7,6},{8,9},{9,8},{10,11... | collective-permute-start | bytes 393224 | tf_op jit(solution)/shard_map/ppermute | solution.py:17
  53.1 6.4 %collective-permute-start.15 = (bf16[64,1024]{1,0:T(8,128)(2,1)S(1)}, bf16[64,1024]{1,0:T(8,128)(2,1)S(1)}, u32[]{:S(2)}, u32[]{:S(2)}) collective-permute-start(bf16[64,1024]{1,0:T(8,128)(2,1)S(1)} %get-tuple-element.40), channel_id=1, source_target_pairs={{0,2},{1,3},{2,0},{3,1},{4,6},{5,7},{6,4},{7,5},{8,10},{9,11},{10,... | collective-permute-start | bytes 393224 | tf_op jit(solution)/shard_map/ppermute | solution.py:17
  54.7 6.7 %collective-permute-start.16 = (bf16[64,1024]{1,0:T(8,128)(2,1)S(1)}, bf16[64,1024]{1,0:T(8,128)(2,1)S(1)}, u32[]{:S(2)}, u32[]{:S(2)}) collective-permute-start(bf16[64,1024]{1,0:T(8,128)(2,1)S(1)} %get-tuple-element.41), channel_id=1, source_target_pairs={{0,3},{1,2},{2,1},{3,0},{4,7},{5,6},{6,5},{7,4},{8,11},{9,10},{10,... | collective-permute-start | bytes 393224 | tf_op jit(solution)/shard_map/ppermute | solution.py:17
  65.0 1.9 %collective-permute-start.17 = (bf16[64,1024]{1,0:T(8,128)(2,1)S(1)}, bf16[64,1024]{1,0:T(8,128)(2,1)S(1)}, u32[]{:S(2)}, u32[]{:S(2)}) collective-permute-start(bf16[64,1024]{1,0:T(8,128)(2,1)S(1)} %get-tuple-element.43), channel_id=1, source_target_pairs={{0,1},{1,0},{2,3},{3,2},{4,5},{5,4},{6,7},{7,6},{8,9},{9,8},{10,11... | collective-permute-start | bytes 393224 | tf_op jit(solution)/shard_map/ppermute | solution.py:17
  65.4 6.3 %collective-permute-start.18 = (bf16[64,1024]{1,0:T(8,128)(2,1)S(1)}, bf16[64,1024]{1,0:T(8,128)(2,1)S(1)}, u32[]{:S(2)}, u32[]{:S(2)}) collective-permute-start(bf16[64,1024]{1,0:T(8,128)(2,1)S(1)} %get-tuple-element.44), channel_id=1, source_target_pairs={{0,2},{1,3},{2,0},{3,1},{4,6},{5,7},{6,4},{7,5},{8,10},{9,11},{10,... | collective-permute-start | bytes 393224 | tf_op jit(solution)/shard_map/ppermute | solution.py:17
  66.9 6.2 %collective-permute-start.19 = (bf16[64,1024]{1,0:T(8,128)(2,1)S(1)}, bf16[64,1024]{1,0:T(8,128)(2,1)S(1)}, u32[]{:S(2)}, u32[]{:S(2)}) collective-permute-start(bf16[64,1024]{1,0:T(8,128)(2,1)S(1)} %get-tuple-element.45), channel_id=1, source_target_pairs={{0,3},{1,2},{2,1},{3,0},{4,7},{5,6},{6,5},{7,4},{8,11},{9,10},{10,... | collective-permute-start | bytes 393224 | tf_op jit(solution)/shard_map/ppermute | solution.py:17
  74.8 15.7 %collective-permute-start.20 = (bf16[4,64,1024]{2,1,0:T(8,128)(2,1)S(1)}, bf16[4,64,1024]{2,1,0:T(8,128)(2,1)S(1)}, u32[]{:S(2)}, u32[]{:S(2)}) collective-permute-start(bf16[4,64,1024]{2,1,0:T(8,128)(2,1)S(1)} %get-tuple-element.48), channel_id=1, source_target_pairs={{0,4},{4,0},{8,12},{12,8},{16,20},{20,16},{24,28},{28,24},{1,5},{5... | collective-permute-start | bytes 1572872 | tf_op jit(solution)/shard_map/ppermute | solution.py:17
  75.2 8.3 %collective-permute-start.21 = (bf16[2,64,512]{2,1,0:T(8,128)(2,1)S(1)}, bf16[2,64,512]{2,1,0:T(8,128)(2,1)S(1)}, u32[]{:S(2)}, u32[]{:S(2)}) collective-permute-start(bf16[2,64,512]{2,1,0:T(8,128)(2,1)S(1)} %get-tuple-element.49), channel_id=1, source_target_pairs={{0,8},{4,12},{8,0},{12,4},{16,24},{20,28},{24,16},{28,20},{1,9},{5... | collective-permute-start | bytes 393224 | tf_op jit(solution)/shard_map/ppermute | solution.py:17
  77.6 12.9 %collective-permute-start.22 = (bf16[2,64,512]{2,1,0:T(8,128)(2,1)S(1)}, bf16[2,64,512]{2,1,0:T(8,128)(2,1)S(1)}, u32[]{:S(2)}, u32[]{:S(2)}) collective-permute-start(bf16[2,64,512]{2,1,0:T(8,128)(2,1)S(1)} %get-tuple-element.50), channel_id=1, source_target_pairs={{0,16},{4,20},{8,24},{12,28},{16,0},{20,4},{24,8},{28,12},{1,17},{... | collective-permute-start | bytes 393224 | tf_op jit(solution)/shard_map/ppermute | solution.py:17
  79.6 10.9 %collective-permute-start.23 = (bf16[2,64,512]{2,1,0:T(8,128)(2,1)S(1)}, bf16[2,64,512]{2,1,0:T(8,128)(2,1)S(1)}, u32[]{:S(2)}, u32[]{:S(2)}) collective-permute-start(bf16[2,64,512]{2,1,0:T(8,128)(2,1)S(1)} %get-tuple-element.51), channel_id=1, source_target_pairs={{0,24},{4,28},{8,16},{12,20},{16,8},{20,12},{24,0},{28,4},{1,25},{... | collective-permute-start | bytes 393224 | tf_op jit(solution)/shard_map/ppermute | solution.py:17
  91.1 9.2 %collective-permute-start.24 = (bf16[64,1024]{1,0:T(8,128)(2,1)S(1)}, bf16[64,1024]{1,0:T(8,128)(2,1)S(1)}, u32[]{:S(2)}, u32[]{:S(2)}) collective-permute-start(bf16[64,1024]{1,0:T(8,128)(2,1)S(1)} %get-tuple-element.53), channel_id=1, source_target_pairs={{0,8},{4,12},{8,0},{12,4},{16,24},{20,28},{24,16},{28,20},{1,9},{5... | collective-permute-start | bytes 393224 | tf_op jit(solution)/shard_map/ppermute | solution.py:17
  93.6 12.2 %collective-permute-start.25 = (bf16[64,1024]{1,0:T(8,128)(2,1)S(1)}, bf16[64,1024]{1,0:T(8,128)(2,1)S(1)}, u32[]{:S(2)}, u32[]{:S(2)}) collective-permute-start(bf16[64,1024]{1,0:T(8,128)(2,1)S(1)} %get-tuple-element.54), channel_id=1, source_target_pairs={{0,16},{4,20},{8,24},{12,28},{16,0},{20,4},{24,8},{28,12},{1,17},{... | collective-permute-start | bytes 393224 | tf_op jit(solution)/shard_map/ppermute | solution.py:17
  94.6 11.2 %collective-permute-start.26 = (bf16[64,1024]{1,0:T(8,128)(2,1)S(1)}, bf16[64,1024]{1,0:T(8,128)(2,1)S(1)}, u32[]{:S(2)}, u32[]{:S(2)}) collective-permute-start(bf16[64,1024]{1,0:T(8,128)(2,1)S(1)} %get-tuple-element.55), channel_id=1, source_target_pairs={{0,24},{4,28},{8,16},{12,20},{16,8},{20,12},{24,0},{28,4},{1,25},{... | collective-permute-start | bytes 393224 | tf_op jit(solution)/shard_map/ppermute | solution.py:17
  96.1 4.3 %collective-permute-start.27 = (bf16[64,512]{1,0:T(8,128)(2,1)S(1)}, bf16[64,512]{1,0:T(8,128)(2,1)S(1)}, u32[]{:S(2)}, u32[]{:S(2)}) collective-permute-start(bf16[64,512]{1,0:T(8,128)(2,1)S(1)} %get-tuple-element.57), channel_id=1, source_target_pairs={{0,4},{4,0},{8,12},{12,8},{16,20},{20,16},{24,28},{28,24},{1,5},{5... | collective-permute-start | bytes 196616 | tf_op jit(solution)/shard_map/ppermute | solution.py:17

commit v6 on v5

--- a/solution.py
+++ b/solution.py
@@ -169,7 +169,7 @@
 
 LANES = 128
 VMEM = 20 * 1024 * 1024
-COST = 6.5e8
+COST = 7e8
 ALONE = 52 * 1024 * 1024
 SHARD, CORE, CHIP, COUNT, GROUP = range(5)
 
@@ -264,19 +264,43 @@
     )
 
 
-def chunk_lanes(depth):
-    cut = depth // 3 // LANES * LANES
-    return slice(0, cut), slice(cut, depth)
-
-
-def project_chunk(scalars, columns, weight, weight_near, chip_offset, lanes, size, after):
+def bring_weight(scalars, weight, scene, rows_of, after):
+    pieces = 4
+    rows = weight.shape[0] // pieces
+
+    def body(sc, in_ref, scene_ref, row_ref, out_ref, slot_ref, sems):
+        copies = []
+        for i in range(pieces):
+            at = pl.ds(i * rows, rows)
+            copies.append(pltpu.make_async_copy(in_ref.at[at], out_ref.at[at], sems.at[i]))
+        for copy in copies:
+            copy.start()
+        slot_ref[...] = jnp.full(slot_ref.shape, row_ref[scene_ref[0]].astype(F32))
+        for copy in copies:
+            copy.wait()
+
+    vmem, smem = pl.BlockSpec(memory_space=pltpu.VMEM), pl.BlockSpec(memory_space=pltpu.SMEM)
+    return kernel_call(
+        body,
+        "bring_weight",
+        scalars,
+        (weight, scene, rows_of),
+        [shaped(weight.shape), shaped((8, LANES), F32)],
+        3.0,
+        in_specs=[pl.BlockSpec(memory_space=pl.ANY), smem, smem],
+        out_specs=[vmem, vmem],
+        after=after,
+        scratch=[pltpu.SemaphoreType.DMA((pieces,))],
+    )
+
+
+def project(scalars, columns, weight, weight_near, chip_offset, size, after):
     _, slots, depth = columns.shape
-    w = lanes.stop - lanes.start
 
     def body(sc, x_ref, own_ref, near_ref, out_ref):
         for k in range(size):
-            start = (sc[SHARD] ^ (2 * chip_offset) ^ k) * depth + lanes.start
-            cols = pl.ds(pl.multiple_of(start, LANES), w)
+            start = (sc[SHARD] ^ (2 * chip_offset) ^ k) * depth
+            cols = pl.ds(pl.multiple_of(start, LANES), depth)
             out_ref[k] = (dot(x_ref[0], own_ref[:, cols], 1, 0) + dot(x_ref[1], near_ref[:, cols], 1, 0)).astype(BF16)
 
     vmem = pl.BlockSpec(memory_space=pltpu.VMEM)
@@ -285,51 +309,47 @@
         "project",
         scalars,
         (columns, weight, weight_near),
-        shaped((size, slots, w)),
-        8.0 * w / depth,
+        shaped((size, slots, depth)),
+        3.0,
         in_specs=[vmem] * 3,
         out_specs=vmem,
         after=after,
     )
 
 
-def base_error(scalars, columns, weight, weight_near, residual, target, received, lanes, size, after):
+def base_error(scalars, columns, weight, weight_near, residual, target, size, after):
     _, slots, depth = columns.shape
-    w = lanes.stop - lanes.start
-
-    def body(sc, x_ref, own_ref, near_ref, r_ref, t_ref, *refs):
+
+    def body(sc, x_ref, own_ref, near_ref, r_ref, t_ref, out_ref):
         cols = pl.ds(pl.multiple_of((sc[SHARD] ^ pl.program_id(0)) * depth, LANES), depth)
         total = dot(x_ref[0], own_ref[:, cols], 1, 0) + dot(x_ref[1], near_ref[:, cols], 1, 0)
-        refs[-1][0] = total + (r_ref[0].astype(F32) - t_ref[0].astype(F32))
-        for ref in refs[:-1]:
-            refs[-1][0, :, lanes] += ref[0].astype(F32)
+        out_ref[0] = total + (r_ref[0].astype(F32) - t_ref[0].astype(F32))
 
     tokens = pl.BlockSpec((1, slots, depth), lambda k, sc: (0, 0, sc[SHARD] ^ k))
-    lead = lambda width: pl.BlockSpec((1, slots, width), lambda k, sc: (k, 0, 0))
     vmem = pl.BlockSpec(memory_space=pltpu.VMEM)
     return kernel_call(
         body,
         "base",
         scalars,
-        (columns, weight, weight_near, residual, target, *received),
+        (columns, weight, weight_near, residual, target),
         shaped((size, slots, depth), F32),
         7.0,
         grid=(size,),
-        in_specs=[vmem, vmem, vmem, tokens, tokens, *[lead(w)] * len(received)],
-        out_specs=lead(depth),
+        in_specs=[vmem, vmem, vmem, tokens, tokens],
+        out_specs=pl.BlockSpec((1, slots, depth), lambda k, sc: (k, 0, 0)),
         after=after,
     )
 
 
-def error_terms(scalars, base, received, lanes, low_part, adapters):
+def error_terms(scalars, base, received, low_part, adapters):
     size, slots, depth = base.shape
     rank = low_part.shape[0]
     back_lanes = -(-slots // LANES) * LANES
     peers = len(received)
-    step = math.gcd(lanes.start, depth)
+    step = depth // 3
 
     def body(sc, base_ref, low_ref, *refs):
-        got, up_refs, pieces = refs[:peers], refs[peers : peers + size], refs[peers + size : -1]
+        got, up_refs, pieces = refs[:peers], refs[peers : peers + size][::-1], refs[peers + size : -1]
         count = sc[COUNT]
         tokens = count.astype(F32)
         per_token = 2.0 / tokens
@@ -339,23 +359,22 @@
             low_wide = low_wide + ref[:, depth : depth + slots].astype(F32)
         low_turned = ADAPTER_SCALE * low_wide.astype(BF16)
         low_state = ADAPTER_SCALE * low_wide.T.astype(BF16)
-        back = jnp.zeros((rank, slots), F32)
+        back = jnp.zeros((slots, rank), F32)
         squares = jnp.zeros((slots, step), F32)
         for k in range(size):
             for start in range(0, depth, step):
                 at = slice(start, start + step)
                 up = up_refs[k][:, at]
                 error = base_ref[k, :, at] + dot(low_state, up, 1, 0)
-                if start >= lanes.start:
-                    for ref in got:
-                        error = error + ref[k, :, start - lanes.start : start - lanes.start + step].astype(F32)
+                for ref in got:
+                    error = error + ref[k, :, at].astype(F32)
                 error = jnp.where(valid, error, 0.0)
                 squares = squares + error * error
                 cotangent = (error * per_token).astype(BF16)
-                back = back + dot(up, cotangent, 1, 1)
+                back = back + dot(cotangent, up, 1, 1)
                 pieces[k][:, at] = dot(low_turned, cotangent, 1, 0).astype(BF16)
         refs[-1][0, 0] = jnp.sum(squares) / (tokens * (size * depth))
-        padded = (ADAPTER_SCALE * back).astype(BF16)
+        padded = (ADAPTER_SCALE * back).T.astype(BF16)
         padded = jnp.concatenate([padded, jnp.zeros((rank, back_lanes - slots), BF16)], axis=1)
         for k in range(size):
             pieces[k][:, depth:] = padded
@@ -366,57 +385,48 @@
         body,
         "error",
         scalars,
-        (base, low_part, *received, *adapters),
+        (base, low_part, *received, *adapters[::-1]),
         out_shape,
         3.0,
-        in_specs=[whole(x) for x in (base, low_part, *received, *adapters)],
+        in_specs=[whole(x) for x in (base, low_part, *received, *adapters[::-1])],
         out_specs=[whole(x) for x in out_shape[:-1]] + [pl.BlockSpec(memory_space=pltpu.SMEM)],
     )
     return out[:size], out[size]
 
 
-def join_adapters(scalars, down, up, scene, rows, after):
+def join_adapters(scalars, down, up, after):
     _, rank, depth = down.shape
 
-    def body(sc, down_ref, up_ref, scene_ref, row_ref, out_ref, slot_ref):
+    def body(sc, down_ref, up_ref, out_ref):
         out_ref[:rank, :] = down_ref[0]
         out_ref[rank:, :] = up_ref[0]
-        slot_ref[...] = jnp.full(slot_ref.shape, row_ref[scene_ref[0]].astype(F32))
-
-    vmem, smem = pl.BlockSpec(memory_space=pltpu.VMEM), pl.BlockSpec(memory_space=pltpu.SMEM)
-    return kernel_call(
-        body,
-        "join",
-        scalars,
-        (down, up, scene, rows),
-        [shaped((2 * rank, depth)), shaped((8, LANES), F32)],
-        1.0,
-        in_specs=[vmem, vmem, smem, smem],
-        out_specs=[vmem, vmem],
-        after=after,
-    )
-
-
-def stack_blocks(scalars, blocks, columns, after):
-    count = len(blocks)
+
+    return kernel_call(body, "join", scalars, (down, up), shaped((2 * rank, depth)), 1.0, after=after)
+
+
+def stack_blocks(scalars, blocks, places, columns, slot_tiles, after):
+    count, chips = len(blocks), len(columns)
 
     def body(sc, *refs):
-        ins, out_ref, others = refs[: count + len(columns)], refs[count + len(columns)], refs[count + len(columns) + 1 :]
+        ins, out_ref, others = refs[: count + 2 * chips], refs[count + 2 * chips], refs[count + 2 * chips + 1 :]
         for i in range(count):
-            out_ref[i] = ins[i][...]
-        for ref, other in zip(ins[count:], others):
-            other[...] = ref[1]
+            out_ref[places[i]] = ins[i][...]
+        for i in range(chips):
+            others[i][...] = ins[count + i][1]
+            others[chips + i][...] = ins[count + chips + i][...]
 
     out = kernel_call(
         body,
         "stack",
         scalars,
-        (*blocks, *columns),
-        [shaped((count, *blocks[0].shape))] + [shaped(x.shape[1:]) for x in columns],
+        (*blocks, *columns, *slot_tiles),
+        [shaped((count, *blocks[0].shape))]
+        + [shaped(x.shape[1:]) for x in columns]
+        + [shaped(x.shape, F32) for x in slot_tiles],
         0.8,
         after=after,
     )
-    return out[0], out[1:]
+    return out[0], out[1 : 1 + chips], out[1 + chips :]
 
 
 def slot_offset(sc, slot_ref):
@@ -429,7 +439,7 @@
         if all(x is not y for y in arrays):
             arrays.append(x)
     where = [next(i for i, y in enumerate(arrays) if x is y) for x, _ in blocks]
-    rows, depth = arrays[0].shape
+    _, rows, depth = arrays[0].shape
     rank = rows // 2
     size = len(slot_list)
     slots = columns[0].shape[0]
@@ -444,8 +454,7 @@
 
                 @pl.when(offset == scene)
                 def _():
-                    ref = refs[where[scene]]
-                    held[k] = ref[...] if place is None else ref[place]
+                    held[k] = refs[where[scene]][place]
 
         for k in range(size):
             part = dot(held[k, :rank, :], column_refs[k][...], 1, 1)
@@ -539,30 +548,32 @@
 
         attended = [attend_chip(scalars, queries, keys, values, c, depth) for c in range(1, chips)]
         theirs = [xor_send(x, "fsdp", fsdp_size, 2 * (c + 1)) for c, x in enumerate(attended)]
-        own = attend_chip(scalars, queries, keys, values, 0, depth, attended[:1])
-        block, own_slot = join_adapters(
-            scalars, down_adapter, up_adapter, scene_of_frame, scene_adapter_row, [own, weight_near]
+        block = join_adapters(scalars, down_adapter, up_adapter, attended[:1])
+        outer_blocks = {
+            o: xor_send(block, "frame", frame_size, o * inner)
+            for o in sorted(range(1, outer), key=lambda o: -o.bit_length())
+        }
+        own = attend_chip(scalars, queries, keys, values, 0, depth, [block, weight_near])
+        attended = [own] + attended
+
+        weight_near, own_slot = bring_weight(
+            scalars, weight_near, scene_of_frame, scene_adapter_row, [own]
         )
         near_slots = [own_slot] + [xor_send(own_slot, "fsdp", fsdp_size, 2 * c) for c in range(1, chips)]
-        outer_blocks = [xor_send(block, "frame", frame_size, o * inner) for o in range(1, outer)]
-        attended = [own] + attended
-
         partials = []
-        after = [block, *near_slots[1:]]
-        parts = chunk_lanes(depth)
-        for lanes in parts:
-            sent = []
-            for c, x in enumerate(theirs):
-                part = project_chunk(
-                    scalars, x, output_weight, weight_near, c + 1, lanes, fsdp_size, after
-                )
-                sent.append(xor_send(part, "fsdp", fsdp_size, 2 * (c + 1)))
-            partials.append(sent)
-            after = [part]
+        after = [own]
+        for c, x in enumerate(theirs):
+            part = project(scalars, x, output_weight, weight_near, c + 1, fsdp_size, after)
+            partials.append(xor_send(part, "fsdp", fsdp_size, 2 * (c + 1)))
+        stacked, others, near_slots = stack_blocks(
+            scalars,
+            [*outer_blocks.values(), block],
+            [*outer_blocks, 0],
+            [own, *theirs],
+            near_slots,
+            [part],
+        )
         slot_list = [x for slot in near_slots for x in (slot, xor_send(slot, "fsdp", fsdp_size, 1))]
-
-        inner_blocks = [xor_send(block, "frame", frame_size, s) for s in range(1, inner)]
-        stacked, others = stack_blocks(scalars, outer_blocks, [own, *theirs], [part, *inner_blocks])
         far_blocks = [xor_send(stacked, "frame", frame_size, s) for s in range(1, inner)]
         base = base_error(
             scalars,
@@ -571,16 +582,10 @@
             weight_near,
             residual,
             target,
-            partials[0],
-            parts[0],
             fsdp_size,
             [stacked],
         )
-        blocks = [None] * frame_size
-        for o in range(outer):
-            blocks[o * inner] = (stacked, o - 1) if o else (block, None)
-            for s in range(1, inner):
-                blocks[o * inner + s] = (far_blocks[s - 1], o - 1) if o else (inner_blocks[s - 1], None)
+        blocks = [((stacked, *far_blocks)[s], o) for o in range(outer) for s in range(inner)]
 
         columns = [None] * fsdp_size
         for c, (x, other) in enumerate(zip([own] + theirs, others)):
@@ -589,7 +594,7 @@
 
         chosen, low_part = choose_adapters(scalars, slot_list, blocks, columns, [base])
         adapters = send_shards(chosen)
-        pieces, loss = error_terms(scalars, base, partials[1], parts[1], low_part, adapters)
+        pieces, loss = error_terms(scalars, base, partials, low_part, adapters)
         pieces = send_shards(pieces)
 
         cut = depth // 3 // LANES * LANES
@@ -600,6 +605,7 @@
 
         def first(sc, *refs):
             slot_refs, got, cols = (refs[i * fsdp_size : (i + 1) * fsdp_size] for i in range(3))
+            got = got[::-1]
             outs = refs[3 * fsdp_size :]
             offsets = [slot_offset(sc, ref) for ref in slot_refs]
             downs = [dot(p[:, depth : depth + slots], c[...], 1, 0) for p, c in zip(got, cols)]
@@ -614,21 +620,27 @@
         far = [o for o in range(1, outer) if 2 * o >= outer]
         near = [o for o in range(1, outer) if 2 * o < outer]
         order = [0, inner, *[inner + o for o in far], *range(1, inner), *[inner + o for o in near]]
-        out = ordered_call(first, "first", scalars, (*slot_list, *pieces, *columns), first_shape, 2.0, order)
+        out = ordered_call(first, "first", scalars, (*slot_list, *pieces[::-1], *columns), first_shape, 2.0, order)
         keeps = out[0], out[inner]
         outer_got = send_frames(out[inner + 1 :], inner)
         inner_got = send_frames(out[1:inner], 1)
 
+        ways = [("outer", o) for o in far] + [("inner", i) for i in range(1, inner)] + [("outer", o) for o in near]
+
         def second(sc, inner_keep, outer_keep, *refs):
-            inners, refs = refs[: inner - 1], refs[inner - 1 :]
-            outers, refs = refs[: outer - 1], refs[outer - 1 :]
-            second_refs(inner_keep, inners, refs[0], refs[1:outer], outer)
-            second_refs(outer_keep, outers, refs[outer], refs[outer + 1 :], inner)
+            got = dict(zip(ways, refs))
+            outs = refs[len(ways) :]
+            inners = [got["inner", i] for i in range(1, inner)]
+            outers = [got["outer", o] for o in range(1, outer)]
+            second_refs(inner_keep, inners, outs[0], outs[1:outer], outer)
+            second_refs(outer_keep, outers, outs[outer], outs[outer + 1 :], inner)
 
         order = [0, outer, *far, *near, *[outer + i for i in range(1, inner)]]
-        operands = (*keeps, *inner_got, *outer_got)
+        sent = {"inner": inner_got, "outer": outer_got}
+        operands = (*keeps, *[sent[way][i - 1] for way, i in ways])
         out = ordered_call(second, "second", scalars, operands, second_shape, 0.8, order)
-        one = (out[0], *send_frames(out[1:outer], inner))
+        sent = send_frames(out[1:outer], inner)
+        one = (out[0], *[sent[o - 1] for o in far + near])
         two = (out[outer], *send_frames(out[outer + 1 :], 1))
 
         def finish(sc, *refs):

time: 108 us -> 105 us (0.972)
  waiting for transfers between devices: 42 us -> 47.3 us
  Pallas kernels: 31.8 us -> 26.7 us
  starting transfers between devices: 29.6 us -> 27.1 us
    ppermute x28 -> x26, waiting for transfers between devices: 42 us -> 47.3 us  [xor_send(): return lax.ppermute(value, axis, [(i, i ^ offset) for i in range(size)])]
    pallas_call x12, Pallas kernels: 31.8 us -> 26.7 us  [kernel_call(): pl.pallas_call(body, out_shape=out_shape, grid_spec=pltpu.PrefetchScalarG...]
    ppermute x28 -> x26, starting transfers between devices: 29.6 us -> 27.1 us  [xor_send(): return lax.ppermute(value, axis, [(i, i ^ offset) for i in range(size)])]
  transfers between devices with their start and end apart: 28 -> 26, of which waited for: 12 -> 12; matrix products, arithmetic and copies ran while one was open for 0% -> 0% of each run, Pallas kernels for 23% -> 19%
where the time goes in v6:
time: 105 us
  waiting for transfers between devices  47.3 us (45%)
  starting transfers between devices  27.1 us (26%)
  Pallas kernels  26.7 us (25%)
  between operations  2.31 us (2%)
  local copies, waits for them, and re-layouts  1.43 us (1%)
    ppermute x26, waiting for transfers between devices, xor_send(): return lax.ppermute(value, axis, [(i, i ^ offset) for i in range(size)])  47.3 us
    ppermute x26, starting transfers between devices, xor_send(): return lax.ppermute(value, axis, [(i, i ^ offset) for i in range(size)])  27.1 us
    pallas_call x12, Pallas kernels, kernel_call(): pl.pallas_call(body, out_shape=out_shape, grid_spec=pltpu.PrefetchScalarG...  26.7 us
  transfers between devices with their start and end apart: 26, of which 12 were waited for; matrix products, arithmetic and copies ran while one was open for 0% of the time, Pallas kernels for 19%

profile of v6, /device:TPU:0, one launch (start us, length us, event | category | flops | bytes accessed | tf_op | source)
XLA Modules:
  0.0 104.8 jit_solution(8119897981207631434)
XLA Ops:
  0.6 0.5 collective-permute-start.3
  1.8 0.1 stack.20.sc
  1.9 1.3 %copy-done = bf16[1,192,3072]{2,1,0:T(8,128)(2,1)S(1)} copy-done((bf16[1,192,3072]{2,1,0:T(8,128)(2,1)S(1)}, bf16[1,192,3072]{2,1,0:T(8,128)(2,1)}, u32[]{:S(2)}) %copy-start) | copy-done | bytes 1179672
  3.2 3.5 %attend.2.refs_2_ = bf16[2,192,768]{2,1,0:T(8,128)(2,1)S(1)} custom-call(s32[5]{0:T(128)S(1)} %stack.20.sc, bf16[1,192,3072]{2,1,0:T(8,128)(2,1)S(1)} %copy-done, bf16[1,192,3072]{2,1,0:T(8,128)(2,1)} %refs_1_.8, bf16[1,192,3072]{2,1,0:T(8,128)(2,1)} %refs_2_.4), custom_call_target="tpu_custom_call" | custom-call | flops 2800000000 | tf_op jit(solution)/shard_map/attend/pallas_call | solution.py:191
  6.7 2.6 %collective-permute-start.4 = (bf16[2,192,768]{2,1,0:T(8,128)(2,1)S(1)}, bf16[2,192,768]{2,1,0:T(8,128)(2,1)S(1)}, u32[]{:S(2)}, u32[]{:S(2)}) collective-permute-start(bf16[2,192,768]{2,1,0:T(8,128)(2,1)S(1)} %attend.2.refs_2_), channel_id=1, source_target_pairs={{0,2},{1,3},{2,0},{3,1},{4,6},{5,7},{6,4},{7,5},{8,10},{9,11},{10,... | collective-permute-start | bytes 1769480 | tf_op jit(solution)/shard_map/ppermute | solution.py:17
  9.3 0.6 join.1.refs_3_
  9.8 2.7 %collective-permute-start = (bf16[128,768]{1,0:T(8,128)(2,1)S(1)}, bf16[128,768]{1,0:T(8,128)(2,1)S(1)}, u32[]{:S(2)}, u32[]{:S(2)}) collective-permute-start(bf16[128,768]{1,0:T(8,128)(2,1)S(1)} %join.1.refs_3_), channel_id=1, source_target_pairs={{0,16},{4,20},{8,24},{12,28},{16,0},{20,4},{24,8},{28,12},{1,17},{... | collective-permute-start | bytes 589832 | tf_op jit(solution)/shard_map/ppermute | solution.py:17
  12.5 1.4 %collective-permute-start.1 = (bf16[128,768]{1,0:T(8,128)(2,1)S(1)}, bf16[128,768]{1,0:T(8,128)(2,1)S(1)}, u32[]{:S(2)}, u32[]{:S(2)}) collective-permute-start(bf16[128,768]{1,0:T(8,128)(2,1)S(1)} %join.1.refs_3_), channel_id=1, source_target_pairs={{0,24},{4,28},{8,16},{12,20},{16,8},{20,12},{24,0},{28,4},{1,25},{... | collective-permute-start | bytes 589832 | tf_op jit(solution)/shard_map/ppermute | solution.py:17
  13.8 0.2 collective-permute-start.2
  14.9 3.5 %attend.3.refs_3_.refs_4_.refs_0_ = bf16[2,192,768]{2,1,0:T(8,128)(2,1)S(1)} custom-call(s32[5]{0:T(128)S(1)} %stack.20.sc, bf16[1,192,3072]{2,1,0:T(8,128)(2,1)S(1)} %copy-done, bf16[1,192,3072]{2,1,0:T(8,128)(2,1)} %refs_1_.8, bf16[1,192,3072]{2,1,0:T(8,128)(2,1)} %refs_2_.4, bf16[128,768]{1,0:T(8,128)(2,1)S(1)} %join.1.refs_3_, ...), custom_call_target="tpu_custom_call" | custom-call | flops 2800000000 | tf_op jit(solution)/shard_map/attend/pallas_call | solution.py:191
  18.4 3.5 %bring_weight.1 = (bf16[768,3072]{1,0:T(8,128)(2,1)S(1)}, f32[8,128]{1,0:T(8,128)S(1)}) custom-call(s32[5]{0:T(128)S(1)} %stack.20.sc, bf16[768,3072]{1,0:T(8,128)(2,1)} %collective-permute-done.3.refs_4_.refs_0_, s32[1]{0:T(128)S(6)} %copy.14.refs_1_, s32[8]{0:T(128)S(1)} %copy-done.5, bf16[2,192,768]{2,1,0:T(8,128)(2,1)S(1)} %attend.3.refs_3_.refs_4_.refs_0_), custom_call_target="tpu_custom_call" | custom-call | flops 2100000000 | tf_op jit(solution)/shard_map/bring_weight/pallas_call | solution.py:191
  21.9 0.6 collective-permute-start.5
  22.5 0.8 collective-permute-done.4.refs_0_.refs_5_
  23.3 2.6 %project.1.refs_8_ = bf16[4,192,768]{2,1,0:T(8,128)(2,1)S(1)} custom-call(s32[5]{0:T(128)S(1)} %stack.20.sc, bf16[2,192,768]{2,1,0:T(8,128)(2,1)S(1)} %collective-permute-done.4.refs_0_.refs_5_, bf16[768,3072]{1,0:T(8,128)(2,1)S(1)} %bitcast.10, bf16[768,3072]{1,0:T(8,128)(2,1)S(1)} %get-tuple-element.35.refs_2_, ...), custom_call_target="tpu_custom_call" | custom-call | flops 2100000000 | tf_op jit(solution)/shard_map/project/pallas_call | solution.py:191
  25.9 1.9 %collective-permute-start.11 = (bf16[4,192,768]{2,1,0:T(8,128)(2,1)S(1)}, bf16[4,192,768]{2,1,0:T(8,128)(2,1)S(1)}, u32[]{:S(2)}, u32[]{:S(2)}) collective-permute-start(bf16[4,192,768]{2,1,0:T(8,128)(2,1)S(1)} %project.1.refs_8_), channel_id=1, source_target_pairs={{0,2},{1,3},{2,0},{3,1},{4,6},{5,7},{6,4},{7,5},{8,10},{9,11},{10,... | collective-permute-start | bytes 3538952 | tf_op jit(solution)/shard_map/ppermute | solution.py:17
  27.8 0.6 stack.21
  28.4 1.5 %collective-permute-start.10 = (bf16[4,128,768]{2,1,0:T(8,128)(2,1)S(1)}, bf16[4,128,768]{2,1,0:T(8,128)(2,1)S(1)}, u32[]{:S(2)}, u32[]{:S(2)}) collective-permute-start(bf16[4,128,768]{2,1,0:T(8,128)(2,1)S(1)} %get-tuple-element.38.refs_5_.refs_8_), channel_id=1, source_target_pairs={{0,4},{4,0},{8,12},{12,8},{16,20},{20,16},{24,28},{28,24},{1,5},{5... | collective-permute-start | bytes 2359304 | tf_op jit(solution)/shard_map/ppermute | solution.py:17
  30.1 0.6 collective-permute-start.8
  30.8 0.5 collective-permute-done.6.refs_1_
  31.2 0.2 collective-permute-start.7
  31.4 3.5 %base.1.refs_10_.refs_0_ = f32[4,192,768]{2,1,0:T(8,128)S(1)} custom-call(s32[5]{0:T(128)S(1)} %stack.20.sc, bf16[2,192,768]{2,1,0:T(8,128)(2,1)S(1)} %attend.3.refs_3_.refs_4_.refs_0_, bf16[768,3072]{1,0:T(8,128)(2,1)S(1)} %bitcast.10, bf16[768,3072]{1,0:T(8,128)(2,1)S(1)} %get-tuple-element.35.refs_2_, bf16[1,192,3072]{2,1,0:T(8,128)(2,1)S(1)} %copy-done.1, ...), custom_call_target="tpu_custom_call" | custom-call | flops 4899999744 | tf_op jit(solution)/shard_map/base/pallas_call | solution.py:191
  35.0 12.4 %collective-permute-done.10.refs_9_ = bf16[4,128,768]{2,1,0:T(8,128)(2,1)S(1)} collective-permute-done((bf16[4,128,768]{2,1,0:T(8,128)(2,1)S(1)}, bf16[4,128,768]{2,1,0:T(8,128)(2,1)S(1)}, u32[]{:S(2)}, u32[]{:S(2)}) %collective-permute-start.10) | collective-permute-done | bytes 786464 | tf_op jit(solution)/shard_map/ppermute | solution.py:17
  47.4 1.7 %choose.1 = (bf16[64,1024]{1,0:T(8,128)(2,1)S(1)}, bf16[64,1024]{1,0:T(8,128)(2,1)S(1)}, bf16[64,1024]{1,0:T(8,128)(2,1)S(1)}, bf16[64,1024]{1,0:T(8,128)(2,1)S(1)}, f32[64,192]{1,0:T(8,128)S(1)}) custom-call(s32[5]{0:T(128)S(1)} %stack.20.sc, f32[8,128]{1,0:T(8,128)S(1)} %get-tuple-element.36.refs_0_, f32[8,128]{1,0:T(8,128)S(1)} %collective-permute-done.6.refs_1_, ...), custom_call_target="tpu_custom_call" | custom-call | flops 1400000000 | tf_op jit(solution)/shard_map/choose/pallas_call | solution.py:191
  49.2 0.5 collective-permute-start.13
  49.7 1.3 %collective-permute-start.14 = (bf16[64,1024]{1,0:T(8,128)(2,1)S(1)}, bf16[64,1024]{1,0:T(8,128)(2,1)S(1)}, u32[]{:S(2)}, u32[]{:S(2)}) collective-permute-start(bf16[64,1024]{1,0:T(8,128)(2,1)S(1)} %get-tuple-element.44), channel_id=1, source_target_pairs={{0,1},{1,0},{2,3},{3,2},{4,5},{5,4},{6,7},{7,6},{8,9},{9,8},{10,11... | collective-permute-start | bytes 393224 | tf_op jit(solution)/shard_map/ppermute | solution.py:17
  51.0 5.9 %collective-permute-done.12.refs_3_ = bf16[64,1024]{1,0:T(8,128)(2,1)S(1)} collective-permute-done((bf16[64,1024]{1,0:T(8,128)(2,1)S(1)}, bf16[64,1024]{1,0:T(8,128)(2,1)S(1)}, u32[]{:S(2)}, u32[]{:S(2)}) %collective-permute-start.12) | collective-permute-done | bytes 131104 | tf_op jit(solution)/shard_map/ppermute | solution.py:17
  57.0 2.5 %collective-permute-done.13.refs_4_ = bf16[64,1024]{1,0:T(8,128)(2,1)S(1)} collective-permute-done((bf16[64,1024]{1,0:T(8,128)(2,1)S(1)}, bf16[64,1024]{1,0:T(8,128)(2,1)S(1)}, u32[]{:S(2)}, u32[]{:S(2)}) %collective-permute-start.13) | collective-permute-done | bytes 131104 | tf_op jit(solution)/shard_map/ppermute | solution.py:17
  59.4 3.5 %error.1 = (bf16[64,1024]{1,0:T(8,128)(2,1)S(1)}, bf16[64,1024]{1,0:T(8,128)(2,1)S(1)}, bf16[64,1024]{1,0:T(8,128)(2,1)S(1)}, bf16[64,1024]{1,0:T(8,128)(2,1)S(1)}, f32[1,1]{1,0:T(1,128)}) custom-call(s32[5]{0:T(128)S(1)} %stack.20.sc, f32[4,192,768]{2,1,0:T(8,128)S(1)} %base.1.refs_10_.refs_0_, f32[64,192]{1,0:T(8,128)S(1)} %get-tuple-element.41.refs_1_, ...), custom_call_target="tpu_custom_call" | custom-call | flops 2100000000 | tf_op jit(solution)/shard_map/error/pallas_call | solution.py:191
  63.0 1.6 %collective-permute-start.16 = (bf16[64,1024]{1,0:T(8,128)(2,1)S(1)}, bf16[64,1024]{1,0:T(8,128)(2,1)S(1)}, u32[]{:S(2)}, u32[]{:S(2)}) collective-permute-start(bf16[64,1024]{1,0:T(8,128)(2,1)S(1)} %get-tuple-element.47), channel_id=1, source_target_pairs={{0,2},{1,3},{2,0},{3,1},{4,6},{5,7},{6,4},{7,5},{8,10},{9,11},{10,... | collective-permute-start | bytes 393224 | tf_op jit(solution)/shard_map/ppermute | solution.py:17
  64.7 0.2 collective-permute-start.17
  64.9 3.8 %collective-permute-done.15.refs_4_ = bf16[64,1024]{1,0:T(8,128)(2,1)S(1)} collective-permute-done((bf16[64,1024]{1,0:T(8,128)(2,1)S(1)}, bf16[64,1024]{1,0:T(8,128)(2,1)S(1)}, u32[]{:S(2)}, u32[]{:S(2)}) %collective-permute-start.15) | collective-permute-done | bytes 131104 | tf_op jit(solution)/shard_map/ppermute | solution.py:17
  68.7 2.9 %collective-permute-done.16.refs_5_ = bf16[64,1024]{1,0:T(8,128)(2,1)S(1)} collective-permute-done((bf16[64,1024]{1,0:T(8,128)(2,1)S(1)}, bf16[64,1024]{1,0:T(8,128)(2,1)S(1)}, u32[]{:S(2)}, u32[]{:S(2)}) %collective-permute-start.16) | collective-permute-done | bytes 131104 | tf_op jit(solution)/shard_map/ppermute | solution.py:17
  71.6 1.7 %first.1 = (f32[4,64,1024]{2,1,0:T(8,128)S(1)}, f32[2,64,512]{2,1,0:T(8,128)S(1)}, bf16[2,64,512]{2,1,0:T(8,128)(2,1)S(1)}, bf16[2,64,512]{2,1,0:T(8,128)(2,1)S(...) custom-call(s32[5]{0:T(128)S(1)} %stack.20.sc, f32[8,128]{1,0:T(8,128)S(1)} %get-tuple-element.36.refs_0_, ...), custom_call_target="tpu_custom_call" | custom-call | flops 1400000000 | tf_op jit(solution)/shard_map/first/pallas_call | solution.py:191
  73.3 1.5 %collective-permute-start.20 = (bf16[4,64,1024]{2,1,0:T(8,128)(2,1)S(1)}, bf16[4,64,1024]{2,1,0:T(8,128)(2,1)S(1)}, u32[]{:S(2)}, u32[]{:S(2)}) collective-permute-start(bf16[4,64,1024]{2,1,0:T(8,128)(2,1)S(1)} %get-tuple-element.54), channel_id=1, source_target_pairs={{0,4},{4,0},{8,12},{12,8},{16,20},{20,16},{24,28},{28,24},{1,5},{5... | collective-permute-start | bytes 1572872 | tf_op jit(solution)/shard_map/ppermute | solution.py:17
  74.8 3.1 %collective-permute-start.18 = (bf16[2,64,512]{2,1,0:T(8,128)(2,1)S(1)}, bf16[2,64,512]{2,1,0:T(8,128)(2,1)S(1)}, u32[]{:S(2)}, u32[]{:S(2)}) collective-permute-start(bf16[2,64,512]{2,1,0:T(8,128)(2,1)S(1)} %get-tuple-element.52), channel_id=1, source_target_pairs={{0,16},{4,20},{8,24},{12,28},{16,0},{20,4},{24,8},{28,12},{1,17},{... | collective-permute-start | bytes 393224 | tf_op jit(solution)/shard_map/ppermute | solution.py:17
  78.0 0.5 collective-permute-start.19
  78.5 0.6 collective-permute-start.21
  79.0 8.6 %collective-permute-done.18.refs_2_ = bf16[2,64,512]{2,1,0:T(8,128)(2,1)S(1)} collective-permute-done((bf16[2,64,512]{2,1,0:T(8,128)(2,1)S(1)}, bf16[2,64,512]{2,1,0:T(8,128)(2,1)S(1)}, u32[]{:S(2)}, u32[]{:S(2)}) %collective-permute-start.18) | collective-permute-done | bytes 131104 | tf_op jit(solution)/shard_map/ppermute | solution.py:17
  87.7 0.3 collective-permute-done.21.refs_5_
  88.0 0.7 second.1
  88.7 4.1 %collective-permute-start.22 = (bf16[64,1024]{1,0:T(8,128)(2,1)S(1)}, bf16[64,1024]{1,0:T(8,128)(2,1)S(1)}, u32[]{:S(2)}, u32[]{:S(2)}) collective-permute-start(bf16[64,1024]{1,0:T(8,128)(2,1)S(1)} %get-tuple-element.57), channel_id=1, source_target_pairs={{0,16},{4,20},{8,24},{12,28},{16,0},{20,4},{24,8},{28,12},{1,17},{... | collective-permute-start | bytes 393224 | tf_op jit(solution)/shard_map/ppermute | solution.py:17
  92.8 0.4 collective-permute-start.23
  93.2 0.2 collective-permute-start.24
  93.4 0.5 collective-permute-start.25
  94.0 3.7 %collective-permute-done.25.refs_5_ = bf16[64,512]{1,0:T(8,128)(2,1)S(1)} collective-permute-done((bf16[64,512]{1,0:T(8,128)(2,1)S(1)}, bf16[64,512]{1,0:T(8,128)(2,1)S(1)}, u32[]{:S(2)}, u32[]{:S(2)}) %collective-permute-start.25) | collective-permute-done | bytes 65568 | tf_op jit(solution)/shard_map/ppermute | solution.py:17
  97.7 4.7 %collective-permute-done.22.refs_1_ = bf16[64,1024]{1,0:T(8,128)(2,1)S(1)} collective-permute-done((bf16[64,1024]{1,0:T(8,128)(2,1)S(1)}, bf16[64,1024]{1,0:T(8,128)(2,1)S(1)}, u32[]{:S(2)}, u32[]{:S(2)}) %collective-permute-start.22) | collective-permute-done | bytes 131104 | tf_op jit(solution)/shard_map/ppermute | solution.py:17
  102.4 1.1 %collective-permute-done.24.refs_3_ = bf16[64,1024]{1,0:T(8,128)(2,1)S(1)} collective-permute-done((bf16[64,1024]{1,0:T(8,128)(2,1)S(1)}, bf16[64,1024]{1,0:T(8,128)(2,1)S(1)}, u32[]{:S(2)}, u32[]{:S(2)}) %collective-permute-start.24) | collective-permute-done | bytes 131104 | tf_op jit(solution)/shard_map/ppermute | solution.py:17
  103.5 1.3 %finish.1 = (f32[1,64,768]{2,1,0:T(8,128)}, f32[1,64,768]{2,1,0:T(8,128)}) custom-call(s32[5]{0:T(128)S(1)} %stack.20.sc, f32[64,1024]{1,0:T(8,128)S(1)} %get-tuple-element.56.refs_0_, bf16[64,1024]{1,0:T(8,128)(2,1)S(1)} %collective-permute-done.22.refs_1_, bf16[64,1024]{1,0:T(8,128)(2,1)S(1)} %collective-permute-done.23.refs_2_, ...), custom_call_target="tpu_custom_call" | custom-call | flops 910000000 | tf_op jit(solution)/shard_map/finish/pallas_call | solution.py:191
  (36 shorter events, 0.4 us)
Async XLA Ops:
  0.6 14.3 %collective-permute-start.3 = (bf16[768,3072]{1,0:T(8,128)(2,1)}, bf16[768,3072]{1,0:T(8,128)(2,1)}, u32[]{:S(2)}, u32[]{:S(2)}) collective-permute-start(bf16[768,3072]{1,0:T(8,128)(2,1)} %refs_1_.10), channel_id=1, source_target_pairs={{0,1},{1,0},{2,3},{3,2},{4,5},{5,4},{6,7},{7,6},{8,9},{9,8},{10,11... | collective-permute-start | bytes 14155784 | tf_op jit(solution)/shard_map/ppermute | solution.py:17
  1.9 1.3 %copy-start = (bf16[1,192,3072]{2,1,0:T(8,128)(2,1)S(1)}, bf16[1,192,3072]{2,1,0:T(8,128)(2,1)}, u32[]{:S(2)}) copy-start(bf16[1,192,3072]{2,1,0:T(8,128)(2,1)} %refs_0_.5) | copy-start | bytes 3538948
  3.2 6.1 %copy-start.3 = (bf16[1,64,768]{2,1,0:T(8,128)(2,1)S(1)}, bf16[1,64,768]{2,1,0:T(8,128)(2,1)}, u32[]{:S(2)}) copy-start(bf16[1,64,768]{2,1,0:T(8,128)(2,1)} %refs_0_.4) | copy-start | bytes 294916
  3.2 6.1 %copy-start.4 = (bf16[1,64,768]{2,1,0:T(8,128)(2,1)S(1)}, bf16[1,64,768]{2,1,0:T(8,128)(2,1)}, u32[]{:S(2)}) copy-start(bf16[1,64,768]{2,1,0:T(8,128)(2,1)} %refs_1_.7) | copy-start | bytes 294916
  6.7 16.6 %collective-permute-start.4 = (bf16[2,192,768]{2,1,0:T(8,128)(2,1)S(1)}, bf16[2,192,768]{2,1,0:T(8,128)(2,1)S(1)}, u32[]{:S(2)}, u32[]{:S(2)}) collective-permute-start(bf16[2,192,768]{2,1,0:T(8,128)(2,1)S(1)} %attend.2.refs_2_), channel_id=1, source_target_pairs={{0,2},{1,3},{2,0},{3,1},{4,6},{5,7},{6,4},{7,5},{8,10},{9,11},{10,... | collective-permute-start | bytes 1769480 | tf_op jit(solution)/shard_map/ppermute | solution.py:17
  9.8 17.9 %collective-permute-start = (bf16[128,768]{1,0:T(8,128)(2,1)S(1)}, bf16[128,768]{1,0:T(8,128)(2,1)S(1)}, u32[]{:S(2)}, u32[]{:S(2)}) collective-permute-start(bf16[128,768]{1,0:T(8,128)(2,1)S(1)} %join.1.refs_3_), channel_id=1, source_target_pairs={{0,16},{4,20},{8,24},{12,28},{16,0},{20,4},{24,8},{28,12},{1,17},{... | collective-permute-start | bytes 589832 | tf_op jit(solution)/shard_map/ppermute | solution.py:17
  12.5 15.3 %collective-permute-start.1 = (bf16[128,768]{1,0:T(8,128)(2,1)S(1)}, bf16[128,768]{1,0:T(8,128)(2,1)S(1)}, u32[]{:S(2)}, u32[]{:S(2)}) collective-permute-start(bf16[128,768]{1,0:T(8,128)(2,1)S(1)} %join.1.refs_3_), channel_id=1, source_target_pairs={{0,24},{4,28},{8,16},{12,20},{16,8},{20,12},{24,0},{28,4},{1,25},{... | collective-permute-start | bytes 589832 | tf_op jit(solution)/shard_map/ppermute | solution.py:17
  13.8 13.9 %collective-permute-start.2 = (bf16[128,768]{1,0:T(8,128)(2,1)S(1)}, bf16[128,768]{1,0:T(8,128)(2,1)S(1)}, u32[]{:S(2)}, u32[]{:S(2)}) collective-permute-start(bf16[128,768]{1,0:T(8,128)(2,1)S(1)} %join.1.refs_3_), channel_id=1, source_target_pairs={{0,8},{4,12},{8,0},{12,4},{16,24},{20,28},{24,16},{28,20},{1,9},{5... | collective-permute-start | bytes 589832 | tf_op jit(solution)/shard_map/ppermute | solution.py:17
  14.1 9.2 %slice-start = ((s8[4718592]{0:T(1024)(128)(4,1)}), s8[4194304]{0:T(1024)(128)(4,1)S(1)}, s32[]{:S(2)}) async-start(s8[4718592]{0:T(1024)(128)(4,1)} %bitcast.9), calls=%async_computation | async-start | bytes 8388608
  14.9 3.6 %copy-start.5 = (s32[8]{0:T(128)S(1)}, s32[8]{0:T(128)}, u32[]{:S(2)}) copy-start(s32[8]{0:T(128)} %refs_2_.5) | copy-start | bytes 100
  14.9 8.4 %slice-start.1 = ((s8[4718592]{0:T(1024)(128)(4,1)}), s8[524288]{0:T(1024)(128)(4,1)S(1)}, s32[]{:S(2)}) async-start(s8[4718592]{0:T(1024)(128)(4,1)} %bitcast.9), calls=%async_computation.1 | async-start | bytes 1048576
  21.9 5.9 %collective-permute-start.5 = (f32[8,128]{1,0:T(8,128)S(1)}, f32[8,128]{1,0:T(8,128)S(1)}, u32[]{:S(2)}, u32[]{:S(2)}) collective-permute-start(f32[8,128]{1,0:T(8,128)S(1)} %get-tuple-element.34.refs_6_), channel_id=1, source_target_pairs={{0,2},{1,3},{2,0},{3,1},{4,6},{5,7},{6,4},{7,5},{8,10},{9,11},{10,... | collective-permute-start | bytes 12296 | tf_op jit(solution)/shard_map/ppermute | solution.py:17
  25.9 33.5 %collective-permute-start.11 = (bf16[4,192,768]{2,1,0:T(8,128)(2,1)S(1)}, bf16[4,192,768]{2,1,0:T(8,128)(2,1)S(1)}, u32[]{:S(2)}, u32[]{:S(2)}) collective-permute-start(bf16[4,192,768]{2,1,0:T(8,128)(2,1)S(1)} %project.1.refs_8_), channel_id=1, source_target_pairs={{0,2},{1,3},{2,0},{3,1},{4,6},{5,7},{6,4},{7,5},{8,10},{9,11},{10,... | collective-permute-start | bytes 3538952 | tf_op jit(solution)/shard_map/ppermute | solution.py:17
  27.8 3.6 %copy-start.2 = (bf16[1,192,3072]{2,1,0:T(8,128)(2,1)S(1)}, bf16[1,192,3072]{2,1,0:T(8,128)(2,1)}, u32[]{:S(2)}) copy-start(bf16[1,192,3072]{2,1,0:T(8,128)(2,1)} %refs_4_.1) | copy-start | bytes 3538948
  28.4 3.0 %copy-start.1 = (bf16[1,192,3072]{2,1,0:T(8,128)(2,1)S(1)}, bf16[1,192,3072]{2,1,0:T(8,128)(2,1)}, u32[]{:S(2)}) copy-start(bf16[1,192,3072]{2,1,0:T(8,128)(2,1)} %refs_3_.1) | copy-start | bytes 3538948
  28.4 18.9 %collective-permute-start.10 = (bf16[4,128,768]{2,1,0:T(8,128)(2,1)S(1)}, bf16[4,128,768]{2,1,0:T(8,128)(2,1)S(1)}, u32[]{:S(2)}, u32[]{:S(2)}) collective-permute-start(bf16[4,128,768]{2,1,0:T(8,128)(2,1)S(1)} %get-tuple-element.38.refs_5_.refs_8_), channel_id=1, source_target_pairs={{0,4},{4,0},{8,12},{12,8},{16,20},{20,16},{24,28},{28,24},{1,5},{5... | collective-permute-start | bytes 2359304 | tf_op jit(solution)/shard_map/ppermute | solution.py:17
  30.0 1.2 %collective-permute-start.6 = (f32[8,128]{1,0:T(8,128)S(1)}, f32[8,128]{1,0:T(8,128)S(1)}, u32[]{:S(2)}, u32[]{:S(2)}) collective-permute-start(f32[8,128]{1,0:T(8,128)S(1)} %get-tuple-element.36.refs_0_), channel_id=1, source_target_pairs={{0,1},{1,0},{2,3},{3,2},{4,5},{5,4},{6,7},{7,6},{8,9},{9,8},{10,11... | collective-permute-start | bytes 12296 | tf_op jit(solution)/shard_map/ppermute | solution.py:17
  30.1 4.8 %collective-permute-start.8 = (bf16[192,768]{1,0:T(8,128)(2,1)S(1)}, bf16[192,768]{1,0:T(8,128)(2,1)S(1)}, u32[]{:S(2)}, u32[]{:S(2)}) collective-permute-start(bf16[192,768]{1,0:T(8,128)(2,1)S(1)} %get-tuple-element.39), channel_id=1, source_target_pairs={{0,1},{1,0},{2,3},{3,2},{4,5},{5,4},{6,7},{7,6},{8,9},{9,8},{10,11... | collective-permute-start | bytes 884744 | tf_op jit(solution)/shard_map/ppermute | solution.py:17
  30.7 4.3 %collective-permute-start.9 = (bf16[192,768]{1,0:T(8,128)(2,1)S(1)}, bf16[192,768]{1,0:T(8,128)(2,1)S(1)}, u32[]{:S(2)}, u32[]{:S(2)}) collective-permute-start(bf16[192,768]{1,0:T(8,128)(2,1)S(1)} %get-tuple-element.40), channel_id=1, source_target_pairs={{0,1},{1,0},{2,3},{3,2},{4,5},{5,4},{6,7},{7,6},{8,9},{9,8},{10,11... | collective-permute-start | bytes 884744 | tf_op jit(solution)/shard_map/ppermute | solution.py:17
  31.2 3.7 %collective-permute-start.7 = (f32[8,128]{1,0:T(8,128)S(1)}, f32[8,128]{1,0:T(8,128)S(1)}, u32[]{:S(2)}, u32[]{:S(2)}) collective-permute-start(f32[8,128]{1,0:T(8,128)S(1)} %get-tuple-element.37.refs_2_), channel_id=1, source_target_pairs={{0,1},{1,0},{2,3},{3,2},{4,5},{5,4},{6,7},{7,6},{8,9},{9,8},{10,11... | collective-permute-start | bytes 12296 | tf_op jit(solution)/shard_map/ppermute | solution.py:17
  49.1 7.9 %collective-permute-start.12 = (bf16[64,1024]{1,0:T(8,128)(2,1)S(1)}, bf16[64,1024]{1,0:T(8,128)(2,1)S(1)}, u32[]{:S(2)}, u32[]{:S(2)}) collective-permute-start(bf16[64,1024]{1,0:T(8,128)(2,1)S(1)} %get-tuple-element.42), channel_id=1, source_target_pairs={{0,3},{1,2},{2,1},{3,0},{4,7},{5,6},{6,5},{7,4},{8,11},{9,10},{10,... | collective-permute-start | bytes 393224 | tf_op jit(solution)/shard_map/ppermute | solution.py:17
  49.2 10.2 %collective-permute-start.13 = (bf16[64,1024]{1,0:T(8,128)(2,1)S(1)}, bf16[64,1024]{1,0:T(8,128)(2,1)S(1)}, u32[]{:S(2)}, u32[]{:S(2)}) collective-permute-start(bf16[64,1024]{1,0:T(8,128)(2,1)S(1)} %get-tuple-element.43), channel_id=1, source_target_pairs={{0,2},{1,3},{2,0},{3,1},{4,6},{5,7},{6,4},{7,5},{8,10},{9,11},{10,... | collective-permute-start | bytes 393224 | tf_op jit(solution)/shard_map/ppermute | solution.py:17
  49.7 9.7 %collective-permute-start.14 = (bf16[64,1024]{1,0:T(8,128)(2,1)S(1)}, bf16[64,1024]{1,0:T(8,128)(2,1)S(1)}, u32[]{:S(2)}, u32[]{:S(2)}) collective-permute-start(bf16[64,1024]{1,0:T(8,128)(2,1)S(1)} %get-tuple-element.44), channel_id=1, source_target_pairs={{0,1},{1,0},{2,3},{3,2},{4,5},{5,4},{6,7},{7,6},{8,9},{9,8},{10,11... | collective-permute-start | bytes 393224 | tf_op jit(solution)/shard_map/ppermute | solution.py:17
  63.0 5.8 %collective-permute-start.15 = (bf16[64,1024]{1,0:T(8,128)(2,1)S(1)}, bf16[64,1024]{1,0:T(8,128)(2,1)S(1)}, u32[]{:S(2)}, u32[]{:S(2)}) collective-permute-start(bf16[64,1024]{1,0:T(8,128)(2,1)S(1)} %get-tuple-element.46), channel_id=1, source_target_pairs={{0,3},{1,2},{2,1},{3,0},{4,7},{5,6},{6,5},{7,4},{8,11},{9,10},{10,... | collective-permute-start | bytes 393224 | tf_op jit(solution)/shard_map/ppermute | solution.py:17
  63.0 8.6 %collective-permute-start.16 = (bf16[64,1024]{1,0:T(8,128)(2,1)S(1)}, bf16[64,1024]{1,0:T(8,128)(2,1)S(1)}, u32[]{:S(2)}, u32[]{:S(2)}) collective-permute-start(bf16[64,1024]{1,0:T(8,128)(2,1)S(1)} %get-tuple-element.47), channel_id=1, source_target_pairs={{0,2},{1,3},{2,0},{3,1},{4,6},{5,7},{6,4},{7,5},{8,10},{9,11},{10,... | collective-permute-start | bytes 393224 | tf_op jit(solution)/shard_map/ppermute | solution.py:17
  64.7 7.0 %collective-permute-start.17 = (bf16[64,1024]{1,0:T(8,128)(2,1)S(1)}, bf16[64,1024]{1,0:T(8,128)(2,1)S(1)}, u32[]{:S(2)}, u32[]{:S(2)}) collective-permute-start(bf16[64,1024]{1,0:T(8,128)(2,1)S(1)} %get-tuple-element.48), channel_id=1, source_target_pairs={{0,1},{1,0},{2,3},{3,2},{4,5},{5,4},{6,7},{7,6},{8,9},{9,8},{10,11... | collective-permute-start | bytes 393224 | tf_op jit(solution)/shard_map/ppermute | solution.py:17
  73.3 14.7 %collective-permute-start.20 = (bf16[4,64,1024]{2,1,0:T(8,128)(2,1)S(1)}, bf16[4,64,1024]{2,1,0:T(8,128)(2,1)S(1)}, u32[]{:S(2)}, u32[]{:S(2)}) collective-permute-start(bf16[4,64,1024]{2,1,0:T(8,128)(2,1)S(1)} %get-tuple-element.54), channel_id=1, source_target_pairs={{0,4},{4,0},{8,12},{12,8},{16,20},{20,16},{24,28},{28,24},{1,5},{5... | collective-permute-start | bytes 1572872 | tf_op jit(solution)/shard_map/ppermute | solution.py:17
  74.8 12.8 %collective-permute-start.18 = (bf16[2,64,512]{2,1,0:T(8,128)(2,1)S(1)}, bf16[2,64,512]{2,1,0:T(8,128)(2,1)S(1)}, u32[]{:S(2)}, u32[]{:S(2)}) collective-permute-start(bf16[2,64,512]{2,1,0:T(8,128)(2,1)S(1)} %get-tuple-element.52), channel_id=1, source_target_pairs={{0,16},{4,20},{8,24},{12,28},{16,0},{20,4},{24,8},{28,12},{1,17},{... | collective-permute-start | bytes 393224 | tf_op jit(solution)/shard_map/ppermute | solution.py:17
  78.0 9.7 %collective-permute-start.19 = (bf16[2,64,512]{2,1,0:T(8,128)(2,1)S(1)}, bf16[2,64,512]{2,1,0:T(8,128)(2,1)S(1)}, u32[]{:S(2)}, u32[]{:S(2)}) collective-permute-start(bf16[2,64,512]{2,1,0:T(8,128)(2,1)S(1)} %get-tuple-element.53), channel_id=1, source_target_pairs={{0,24},{4,28},{8,16},{12,20},{16,8},{20,12},{24,0},{28,4},{1,25},{... | collective-permute-start | bytes 393224 | tf_op jit(solution)/shard_map/ppermute | solution.py:17
  78.5 9.5 %collective-permute-start.21 = (bf16[2,64,512]{2,1,0:T(8,128)(2,1)S(1)}, bf16[2,64,512]{2,1,0:T(8,128)(2,1)S(1)}, u32[]{:S(2)}, u32[]{:S(2)}) collective-permute-start(bf16[2,64,512]{2,1,0:T(8,128)(2,1)S(1)} %get-tuple-element.55), channel_id=1, source_target_pairs={{0,8},{4,12},{8,0},{12,4},{16,24},{20,28},{24,16},{28,20},{1,9},{5... | collective-permute-start | bytes 393224 | tf_op jit(solution)/shard_map/ppermute | solution.py:17
  88.7 13.7 %collective-permute-start.22 = (bf16[64,1024]{1,0:T(8,128)(2,1)S(1)}, bf16[64,1024]{1,0:T(8,128)(2,1)S(1)}, u32[]{:S(2)}, u32[]{:S(2)}) collective-permute-start(bf16[64,1024]{1,0:T(8,128)(2,1)S(1)} %get-tuple-element.57), channel_id=1, source_target_pairs={{0,16},{4,20},{8,24},{12,28},{16,0},{20,4},{24,8},{28,12},{1,17},{... | collective-permute-start | bytes 393224 | tf_op jit(solution)/shard_map/ppermute | solution.py:17
  92.8 9.6 %collective-permute-start.23 = (bf16[64,1024]{1,0:T(8,128)(2,1)S(1)}, bf16[64,1024]{1,0:T(8,128)(2,1)S(1)}, u32[]{:S(2)}, u32[]{:S(2)}) collective-permute-start(bf16[64,1024]{1,0:T(8,128)(2,1)S(1)} %get-tuple-element.58), channel_id=1, source_target_pairs={{0,24},{4,28},{8,16},{12,20},{16,8},{20,12},{24,0},{28,4},{1,25},{... | collective-permute-start | bytes 393224 | tf_op jit(solution)/shard_map/ppermute | solution.py:17
  93.2 10.2 %collective-permute-start.24 = (bf16[64,1024]{1,0:T(8,128)(2,1)S(1)}, bf16[64,1024]{1,0:T(8,128)(2,1)S(1)}, u32[]{:S(2)}, u32[]{:S(2)}) collective-permute-start(bf16[64,1024]{1,0:T(8,128)(2,1)S(1)} %get-tuple-element.59), channel_id=1, source_target_pairs={{0,8},{4,12},{8,0},{12,4},{16,24},{20,28},{24,16},{28,20},{1,9},{5... | collective-permute-start | bytes 393224 | tf_op jit(solution)/shard_map/ppermute | solution.py:17
  93.4 4.3 %collective-permute-start.25 = (bf16[64,512]{1,0:T(8,128)(2,1)S(1)}, bf16[64,512]{1,0:T(8,128)(2,1)S(1)}, u32[]{:S(2)}, u32[]{:S(2)}) collective-permute-start(bf16[64,512]{1,0:T(8,128)(2,1)S(1)} %get-tuple-element.61), channel_id=1, source_target_pairs={{0,4},{4,0},{8,12},{12,8},{16,20},{20,16},{24,28},{28,24},{1,5},{5... | collective-permute-start | bytes 196616 | tf_op jit(solution)/shard_map/ppermute | solution.py:17

commit v7 on v6

--- a/solution.py
+++ b/solution.py
@@ -219,7 +219,7 @@
     return jax.ShapeDtypeStruct(shape, dtype)
 
 
-def attend_chip(scalars, queries, keys, values, chip_offset, depth, after=()):
+def attend_chip(counts, queries, keys, values, chip_offset, depth, after=()):
     slots, width = queries.shape[1:]
     size = width // HEADS
     heads = depth // size
@@ -227,13 +227,13 @@
 
     def body(sc, q_ref, k_ref, v_ref, out_ref, held, sems):
         def copy(c, i):
-            shard = (sc[CHIP] ^ chip_offset) * 2 + (sc[CORE] ^ c)
+            shard = lax.axis_index("fsdp") ^ (2 * chip_offset + c)
             lanes = pl.ds(pl.multiple_of(shard * depth, LANES), depth)
             return pltpu.make_async_copy((q_ref, k_ref, v_ref)[i].at[0, :, lanes], held.at[c, i], sems.at[c, i])
 
         for i in range(3):
             copy(0, i).start()
-        seen = lax.broadcasted_iota(jnp.int32, (1, slots), 1) < sc[COUNT]
+        seen = lax.broadcasted_iota(jnp.int32, (1, slots), 1) < sc[0]
         at = [slice(h * size, (h + 1) * size) for h in range(heads)]
         for c in range(2):
             for i in range(3):
@@ -252,7 +252,7 @@
     return kernel_call(
         body,
         "attend",
-        scalars,
+        counts,
         (queries, keys, values),
         shaped((2, slots, depth)),
         4.0,
@@ -346,7 +346,6 @@
     rank = low_part.shape[0]
     back_lanes = -(-slots // LANES) * LANES
     peers = len(received)
-    step = depth // 3
 
     def body(sc, base_ref, low_ref, *refs):
         got, up_refs, pieces = refs[:peers], refs[peers : peers + size][::-1], refs[peers + size : -1]
@@ -360,19 +359,17 @@
         low_turned = ADAPTER_SCALE * low_wide.astype(BF16)
         low_state = ADAPTER_SCALE * low_wide.T.astype(BF16)
         back = jnp.zeros((slots, rank), F32)
-        squares = jnp.zeros((slots, step), F32)
+        squares = jnp.zeros((slots, depth), F32)
         for k in range(size):
-            for start in range(0, depth, step):
-                at = slice(start, start + step)
-                up = up_refs[k][:, at]
-                error = base_ref[k, :, at] + dot(low_state, up, 1, 0)
-                for ref in got:
-                    error = error + ref[k, :, at].astype(F32)
-                error = jnp.where(valid, error, 0.0)
-                squares = squares + error * error
-                cotangent = (error * per_token).astype(BF16)
-                back = back + dot(cotangent, up, 1, 1)
-                pieces[k][:, at] = dot(low_turned, cotangent, 1, 0).astype(BF16)
+            up = up_refs[k][:, :depth]
+            error = base_ref[k] + dot(low_state, up, 1, 0)
+            for ref in got:
+                error = error + ref[k].astype(F32)
+            error = jnp.where(valid, error, 0.0)
+            squares = squares + error * error
+            cotangent = (error * per_token).astype(BF16)
+            back = back + dot(cotangent, up, 1, 1)
+            pieces[k][:, :depth] = dot(low_turned, cotangent, 1, 0).astype(BF16)
         refs[-1][0, 0] = jnp.sum(squares) / (tokens * (size * depth))
         padded = (ADAPTER_SCALE * back).T.astype(BF16)
         padded = jnp.concatenate([padded, jnp.zeros((rank, back_lanes - slots), BF16)], axis=1)
@@ -546,14 +543,14 @@
 
         weight_near = xor_send(output_weight, "fsdp", fsdp_size, 1)
 
-        attended = [attend_chip(scalars, queries, keys, values, c, depth) for c in range(1, chips)]
+        attended = [attend_chip(valid_token_count, queries, keys, values, c, depth) for c in range(1, chips)]
         theirs = [xor_send(x, "fsdp", fsdp_size, 2 * (c + 1)) for c, x in enumerate(attended)]
         block = join_adapters(scalars, down_adapter, up_adapter, attended[:1])
         outer_blocks = {
             o: xor_send(block, "frame", frame_size, o * inner)
             for o in sorted(range(1, outer), key=lambda o: -o.bit_length())
         }
-        own = attend_chip(scalars, queries, keys, values, 0, depth, [block, weight_near])
+        own = attend_chip(valid_token_count, queries, keys, values, 0, depth, [block, weight_near])
         attended = [own] + attended
 
         weight_near, own_slot = bring_weight(
@@ -597,7 +594,7 @@
         pieces, loss = error_terms(scalars, base, partials, low_part, adapters)
         pieces = send_shards(pieces)
 
-        cut = depth // 3 // LANES * LANES
+        cut = depth // 2 // LANES * LANES
         first_shape = first_shapes(rank, depth + cut, along_inner) + first_shapes(rank, depth - cut, along_outer)
         second_shape = second_shapes(rank, depth + cut, along_inner) + second_shapes(
             rank, depth - cut, along_outer

time: 105 us -> 103 us (0.981)
  Pallas kernels: 26.7 us -> 25.1 us
  waiting for transfers between devices: 47.3 us -> 46.1 us
    pallas_call x12, Pallas kernels: 26.7 us -> 25.1 us  [kernel_call(): pl.pallas_call(body, out_shape=out_shape, grid_spec=pltpu.PrefetchScalarG...]
    ppermute x26, waiting for transfers between devices: 47.3 us -> 46.1 us  [xor_send(): return lax.ppermute(value, axis, [(i, i ^ offset) for i in range(size)])]
  transfers between devices with their start and end apart: 26 -> 26, of which waited for: 12 -> 13; matrix products, arithmetic and copies ran while one was open for 0% -> 0% of each run, Pallas kernels for 19% -> 18%
where the time goes in v7:
time: 103 us
  waiting for transfers between devices  46.1 us (45%)
  starting transfers between devices  27.6 us (27%)
  Pallas kernels  25.1 us (24%)
  between operations  2.32 us (2%)
  local copies, waits for them, and re-layouts  1.43 us (1%)
    ppermute x26, waiting for transfers between devices, xor_send(): return lax.ppermute(value, axis, [(i, i ^ offset) for i in range(size)])  46.1 us
    ppermute x26, starting transfers between devices, xor_send(): return lax.ppermute(value, axis, [(i, i ^ offset) for i in range(size)])  27.6 us
    pallas_call x12, Pallas kernels, kernel_call(): pl.pallas_call(body, out_shape=out_shape, grid_spec=pltpu.PrefetchScalarG...  25.1 us
  transfers between devices with their start and end apart: 26, of which 13 were waited for; matrix products, arithmetic and copies ran while one was open for 0% of the time, Pallas kernels for 18%

profile of v7, /device:TPU:0, one launch (start us, length us, event | category | flops | bytes accessed | tf_op | source)
XLA Modules:
  0.0 102.5 jit_solution(9422491117687311066)
XLA Ops:
  0.6 0.5 collective-permute-start.3
  1.8 1.3 %copy-done = bf16[1,192,3072]{2,1,0:T(8,128)(2,1)S(1)} copy-done((bf16[1,192,3072]{2,1,0:T(8,128)(2,1)S(1)}, bf16[1,192,3072]{2,1,0:T(8,128)(2,1)}, u32[]{:S(2)}) %copy-start) | copy-done | bytes 1179672
  3.1 3.0 %attend.2.refs_2_ = bf16[2,192,768]{2,1,0:T(8,128)(2,1)S(1)} custom-call(s32[1]{0:T(128)S(6)} %copy.15.sc, bf16[1,192,3072]{2,1,0:T(8,128)(2,1)S(1)} %copy-done, bf16[1,192,3072]{2,1,0:T(8,128)(2,1)} %refs_1_.8, bf16[1,192,3072]{2,1,0:T(8,128)(2,1)} %refs_2_.4), custom_call_target="tpu_custom_call" | custom-call | flops 2800000000 | tf_op jit(solution)/shard_map/attend/pallas_call | solution.py:191
  6.1 2.6 %collective-permute-start.4 = (bf16[2,192,768]{2,1,0:T(8,128)(2,1)S(1)}, bf16[2,192,768]{2,1,0:T(8,128)(2,1)S(1)}, u32[]{:S(2)}, u32[]{:S(2)}) collective-permute-start(bf16[2,192,768]{2,1,0:T(8,128)(2,1)S(1)} %attend.2.refs_2_), channel_id=1, source_target_pairs={{0,2},{1,3},{2,0},{3,1},{4,6},{5,7},{6,4},{7,5},{8,10},{9,11},{10,... | collective-permute-start | bytes 1769480 | tf_op jit(solution)/shard_map/ppermute | solution.py:17
  8.7 0.6 join.1.refs_3_
  9.3 2.7 %collective-permute-start = (bf16[128,768]{1,0:T(8,128)(2,1)S(1)}, bf16[128,768]{1,0:T(8,128)(2,1)S(1)}, u32[]{:S(2)}, u32[]{:S(2)}) collective-permute-start(bf16[128,768]{1,0:T(8,128)(2,1)S(1)} %join.1.refs_3_), channel_id=1, source_target_pairs={{0,16},{4,20},{8,24},{12,28},{16,0},{20,4},{24,8},{28,12},{1,17},{... | collective-permute-start | bytes 589832 | tf_op jit(solution)/shard_map/ppermute | solution.py:17
  12.0 1.3 %collective-permute-start.1 = (bf16[128,768]{1,0:T(8,128)(2,1)S(1)}, bf16[128,768]{1,0:T(8,128)(2,1)S(1)}, u32[]{:S(2)}, u32[]{:S(2)}) collective-permute-start(bf16[128,768]{1,0:T(8,128)(2,1)S(1)} %join.1.refs_3_), channel_id=1, source_target_pairs={{0,24},{4,28},{8,16},{12,20},{16,8},{20,12},{24,0},{28,4},{1,25},{... | collective-permute-start | bytes 589832 | tf_op jit(solution)/shard_map/ppermute | solution.py:17
  13.3 0.2 collective-permute-start.2
  14.4 3.4 %attend.3.refs_3_.refs_4_.refs_0_ = bf16[2,192,768]{2,1,0:T(8,128)(2,1)S(1)} custom-call(s32[1]{0:T(128)S(6)} %copy.15.sc, bf16[1,192,3072]{2,1,0:T(8,128)(2,1)S(1)} %copy-done.1, bf16[1,192,3072]{2,1,0:T(8,128)(2,1)} %refs_1_.8, bf16[1,192,3072]{2,1,0:T(8,128)(2,1)} %refs_2_.4, bf16[128,768]{1,0:T(8,128)(2,1)S(1)} %join.1.refs_3_, ...), custom_call_target="tpu_custom_call" | custom-call | flops 2800000000 | tf_op jit(solution)/shard_map/attend/pallas_call | solution.py:191
  17.8 3.5 %bring_weight.1 = (bf16[768,3072]{1,0:T(8,128)(2,1)S(1)}, f32[8,128]{1,0:T(8,128)S(1)}) custom-call(s32[5]{0:T(128)S(1)} %stack.20.sc, bf16[768,3072]{1,0:T(8,128)(2,1)} %collective-permute-done.3.refs_4_.refs_0_, s32[1]{0:T(128)S(6)} %copy.14.refs_1_, s32[8]{0:T(128)S(1)} %copy-done.6, bf16[2,192,768]{2,1,0:T(8,128)(2,1)S(1)} %attend.3.refs_3_.refs_4_.refs_0_), custom_call_target="tpu_custom_call" | custom-call | flops 2100000000 | tf_op jit(solution)/shard_map/bring_weight/pallas_call | solution.py:191
  21.3 0.6 collective-permute-start.5
  21.8 0.8 collective-permute-done.4.refs_0_.refs_5_
  22.6 2.6 %project.1.refs_8_ = bf16[4,192,768]{2,1,0:T(8,128)(2,1)S(1)} custom-call(s32[5]{0:T(128)S(1)} %stack.20.sc, bf16[2,192,768]{2,1,0:T(8,128)(2,1)S(1)} %collective-permute-done.4.refs_0_.refs_5_, bf16[768,3072]{1,0:T(8,128)(2,1)S(1)} %bitcast.10, bf16[768,3072]{1,0:T(8,128)(2,1)S(1)} %get-tuple-element.35.refs_2_, ...), custom_call_target="tpu_custom_call" | custom-call | flops 2100000000 | tf_op jit(solution)/shard_map/project/pallas_call | solution.py:191
  25.3 1.8 %collective-permute-start.11 = (bf16[4,192,768]{2,1,0:T(8,128)(2,1)S(1)}, bf16[4,192,768]{2,1,0:T(8,128)(2,1)S(1)}, u32[]{:S(2)}, u32[]{:S(2)}) collective-permute-start(bf16[4,192,768]{2,1,0:T(8,128)(2,1)S(1)} %project.1.refs_8_), channel_id=1, source_target_pairs={{0,2},{1,3},{2,0},{3,1},{4,6},{5,7},{6,4},{7,5},{8,10},{9,11},{10,... | collective-permute-start | bytes 3538952 | tf_op jit(solution)/shard_map/ppermute | solution.py:17
  27.2 0.6 stack.21
  27.8 1.6 %collective-permute-start.10 = (bf16[4,128,768]{2,1,0:T(8,128)(2,1)S(1)}, bf16[4,128,768]{2,1,0:T(8,128)(2,1)S(1)}, u32[]{:S(2)}, u32[]{:S(2)}) collective-permute-start(bf16[4,128,768]{2,1,0:T(8,128)(2,1)S(1)} %get-tuple-element.38.refs_5_.refs_8_), channel_id=1, source_target_pairs={{0,4},{4,0},{8,12},{12,8},{16,20},{20,16},{24,28},{28,24},{1,5},{5... | collective-permute-start | bytes 2359304 | tf_op jit(solution)/shard_map/ppermute | solution.py:17
  29.5 0.6 collective-permute-start.8
  30.1 0.5 collective-permute-done.6.refs_1_
  30.6 0.2 collective-permute-start.7
  30.8 3.5 %base.1.refs_10_.refs_0_ = f32[4,192,768]{2,1,0:T(8,128)S(1)} custom-call(s32[5]{0:T(128)S(1)} %stack.20.sc, bf16[2,192,768]{2,1,0:T(8,128)(2,1)S(1)} %attend.3.refs_3_.refs_4_.refs_0_, bf16[768,3072]{1,0:T(8,128)(2,1)S(1)} %bitcast.10, bf16[768,3072]{1,0:T(8,128)(2,1)S(1)} %get-tuple-element.35.refs_2_, bf16[1,192,3072]{2,1,0:T(8,128)(2,1)S(1)} %copy-done.2, ...), custom_call_target="tpu_custom_call" | custom-call | flops 4899999744 | tf_op jit(solution)/shard_map/base/pallas_call | solution.py:191
  34.3 12.4 %collective-permute-done.10.refs_9_ = bf16[4,128,768]{2,1,0:T(8,128)(2,1)S(1)} collective-permute-done((bf16[4,128,768]{2,1,0:T(8,128)(2,1)S(1)}, bf16[4,128,768]{2,1,0:T(8,128)(2,1)S(1)}, u32[]{:S(2)}, u32[]{:S(2)}) %collective-permute-start.10) | collective-permute-done | bytes 786464 | tf_op jit(solution)/shard_map/ppermute | solution.py:17
  46.8 1.7 %choose.1 = (bf16[64,1024]{1,0:T(8,128)(2,1)S(1)}, bf16[64,1024]{1,0:T(8,128)(2,1)S(1)}, bf16[64,1024]{1,0:T(8,128)(2,1)S(1)}, bf16[64,1024]{1,0:T(8,128)(2,1)S(1)}, f32[64,192]{1,0:T(8,128)S(1)}) custom-call(s32[5]{0:T(128)S(1)} %stack.20.sc, f32[8,128]{1,0:T(8,128)S(1)} %get-tuple-element.36.refs_0_, f32[8,128]{1,0:T(8,128)S(1)} %collective-permute-done.6.refs_1_, ...), custom_call_target="tpu_custom_call" | custom-call | flops 1400000000 | tf_op jit(solution)/shard_map/choose/pallas_call | solution.py:191
  48.5 0.5 collective-permute-start.13
  49.1 1.3 %collective-permute-start.14 = (bf16[64,1024]{1,0:T(8,128)(2,1)S(1)}, bf16[64,1024]{1,0:T(8,128)(2,1)S(1)}, u32[]{:S(2)}, u32[]{:S(2)}) collective-permute-start(bf16[64,1024]{1,0:T(8,128)(2,1)S(1)} %get-tuple-element.44), channel_id=1, source_target_pairs={{0,1},{1,0},{2,3},{3,2},{4,5},{5,4},{6,7},{7,6},{8,9},{9,8},{10,11... | collective-permute-start | bytes 393224 | tf_op jit(solution)/shard_map/ppermute | solution.py:17
  50.4 5.9 %collective-permute-done.12.refs_3_ = bf16[64,1024]{1,0:T(8,128)(2,1)S(1)} collective-permute-done((bf16[64,1024]{1,0:T(8,128)(2,1)S(1)}, bf16[64,1024]{1,0:T(8,128)(2,1)S(1)}, u32[]{:S(2)}, u32[]{:S(2)}) %collective-permute-start.12) | collective-permute-done | bytes 131104 | tf_op jit(solution)/shard_map/ppermute | solution.py:17
  56.3 2.4 %collective-permute-done.13.refs_4_ = bf16[64,1024]{1,0:T(8,128)(2,1)S(1)} collective-permute-done((bf16[64,1024]{1,0:T(8,128)(2,1)S(1)}, bf16[64,1024]{1,0:T(8,128)(2,1)S(1)}, u32[]{:S(2)}, u32[]{:S(2)}) %collective-permute-start.13) | collective-permute-done | bytes 131104 | tf_op jit(solution)/shard_map/ppermute | solution.py:17
  58.8 2.5 %error.1 = (bf16[64,1024]{1,0:T(8,128)(2,1)S(1)}, bf16[64,1024]{1,0:T(8,128)(2,1)S(1)}, bf16[64,1024]{1,0:T(8,128)(2,1)S(1)}, bf16[64,1024]{1,0:T(8,128)(2,1)S(1)}, f32[1,1]{1,0:T(1,128)}) custom-call(s32[5]{0:T(128)S(1)} %stack.20.sc, f32[4,192,768]{2,1,0:T(8,128)S(1)} %base.1.refs_10_.refs_0_, f32[64,192]{1,0:T(8,128)S(1)} %get-tuple-element.41.refs_1_, ...), custom_call_target="tpu_custom_call" | custom-call | flops 2100000000 | tf_op jit(solution)/shard_map/error/pallas_call | solution.py:191
  61.4 1.6 %collective-permute-start.16 = (bf16[64,1024]{1,0:T(8,128)(2,1)S(1)}, bf16[64,1024]{1,0:T(8,128)(2,1)S(1)}, u32[]{:S(2)}, u32[]{:S(2)}) collective-permute-start(bf16[64,1024]{1,0:T(8,128)(2,1)S(1)} %get-tuple-element.47), channel_id=1, source_target_pairs={{0,2},{1,3},{2,0},{3,1},{4,6},{5,7},{6,4},{7,5},{8,10},{9,11},{10,... | collective-permute-start | bytes 393224 | tf_op jit(solution)/shard_map/ppermute | solution.py:17
  63.0 0.2 collective-permute-start.17
  63.2 3.8 %collective-permute-done.15.refs_4_ = bf16[64,1024]{1,0:T(8,128)(2,1)S(1)} collective-permute-done((bf16[64,1024]{1,0:T(8,128)(2,1)S(1)}, bf16[64,1024]{1,0:T(8,128)(2,1)S(1)}, u32[]{:S(2)}, u32[]{:S(2)}) %collective-permute-start.15) | collective-permute-done | bytes 131104 | tf_op jit(solution)/shard_map/ppermute | solution.py:17
  67.0 2.9 %collective-permute-done.16.refs_5_ = bf16[64,1024]{1,0:T(8,128)(2,1)S(1)} collective-permute-done((bf16[64,1024]{1,0:T(8,128)(2,1)S(1)}, bf16[64,1024]{1,0:T(8,128)(2,1)S(1)}, u32[]{:S(2)}, u32[]{:S(2)}) %collective-permute-start.16) | collective-permute-done | bytes 131104 | tf_op jit(solution)/shard_map/ppermute | solution.py:17
  70.0 1.6 %first.1 = (f32[4,64,1152]{2,1,0:T(8,128)S(1)}, f32[2,64,384]{2,1,0:T(8,128)S(1)}, bf16[2,64,384]{2,1,0:T(8,128)(2,1)S(1)}, bf16[2,64,384]{2,1,0:T(8,128)(2,1)S(...) custom-call(s32[5]{0:T(128)S(1)} %stack.20.sc, f32[8,128]{1,0:T(8,128)S(1)} %get-tuple-element.36.refs_0_, ...), custom_call_target="tpu_custom_call" | custom-call | flops 1400000000 | tf_op jit(solution)/shard_map/first/pallas_call | solution.py:191
  71.6 1.6 %collective-permute-start.20 = (bf16[4,64,1152]{2,1,0:T(8,128)(2,1)S(1)}, bf16[4,64,1152]{2,1,0:T(8,128)(2,1)S(1)}, u32[]{:S(2)}, u32[]{:S(2)}) collective-permute-start(bf16[4,64,1152]{2,1,0:T(8,128)(2,1)S(1)} %get-tuple-element.54), channel_id=1, source_target_pairs={{0,4},{4,0},{8,12},{12,8},{16,20},{20,16},{24,28},{28,24},{1,5},{5... | collective-permute-start | bytes 1769480 | tf_op jit(solution)/shard_map/ppermute | solution.py:17
  73.2 3.2 %collective-permute-start.18 = (bf16[2,64,384]{2,1,0:T(8,128)(2,1)S(1)}, bf16[2,64,384]{2,1,0:T(8,128)(2,1)S(1)}, u32[]{:S(2)}, u32[]{:S(2)}) collective-permute-start(bf16[2,64,384]{2,1,0:T(8,128)(2,1)S(1)} %get-tuple-element.52), channel_id=1, source_target_pairs={{0,16},{4,20},{8,24},{12,28},{16,0},{20,4},{24,8},{28,12},{1,17},{... | collective-permute-start | bytes 294920 | tf_op jit(solution)/shard_map/ppermute | solution.py:17
  76.5 0.4 collective-permute-start.19
  76.9 0.5 collective-permute-start.21
  77.4 6.5 %collective-permute-done.18.refs_2_ = bf16[2,64,384]{2,1,0:T(8,128)(2,1)S(1)} collective-permute-done((bf16[2,64,384]{2,1,0:T(8,128)(2,1)S(1)}, bf16[2,64,384]{2,1,0:T(8,128)(2,1)S(1)}, u32[]{:S(2)}, u32[]{:S(2)}) %collective-permute-start.18) | collective-permute-done | bytes 98336 | tf_op jit(solution)/shard_map/ppermute | solution.py:17
  84.0 0.4 collective-permute-done.21.refs_5_
  84.3 2.6 %collective-permute-done.20.refs_4_ = bf16[4,64,1152]{2,1,0:T(8,128)(2,1)S(1)} collective-permute-done((bf16[4,64,1152]{2,1,0:T(8,128)(2,1)S(1)}, bf16[4,64,1152]{2,1,0:T(8,128)(2,1)S(1)}, u32[]{:S(2)}, u32[]{:S(2)}) %collective-permute-start.20) | collective-permute-done | bytes 589856 | tf_op jit(solution)/shard_map/ppermute | solution.py:17
  86.9 0.7 second.1
  87.6 3.0 %collective-permute-start.22 = (bf16[64,1152]{1,0:T(8,128)(2,1)S(1)}, bf16[64,1152]{1,0:T(8,128)(2,1)S(1)}, u32[]{:S(2)}, u32[]{:S(2)}) collective-permute-start(bf16[64,1152]{1,0:T(8,128)(2,1)S(1)} %get-tuple-element.57), channel_id=1, source_target_pairs={{0,16},{4,20},{8,24},{12,28},{16,0},{20,4},{24,8},{28,12},{1,17},{... | collective-permute-start | bytes 442376 | tf_op jit(solution)/shard_map/ppermute | solution.py:17
  90.6 0.8 collective-permute-start.23
  91.4 0.5 collective-permute-start.24
  91.9 1.5 %collective-permute-start.25 = (bf16[64,384]{1,0:T(8,128)(2,1)S(1)}, bf16[64,384]{1,0:T(8,128)(2,1)S(1)}, u32[]{:S(2)}, u32[]{:S(2)}) collective-permute-start(bf16[64,384]{1,0:T(8,128)(2,1)S(1)} %get-tuple-element.61), channel_id=1, source_target_pairs={{0,4},{4,0},{8,12},{12,8},{16,20},{20,16},{24,28},{28,24},{1,5},{5... | collective-permute-start | bytes 147464 | tf_op jit(solution)/shard_map/ppermute | solution.py:17
  93.4 2.6 %collective-permute-done.25.refs_5_ = bf16[64,384]{1,0:T(8,128)(2,1)S(1)} collective-permute-done((bf16[64,384]{1,0:T(8,128)(2,1)S(1)}, bf16[64,384]{1,0:T(8,128)(2,1)S(1)}, u32[]{:S(2)}, u32[]{:S(2)}) %collective-permute-start.25) | collective-permute-done | bytes 49184 | tf_op jit(solution)/shard_map/ppermute | solution.py:17
  96.0 5.0 %collective-permute-done.22.refs_1_ = bf16[64,1152]{1,0:T(8,128)(2,1)S(1)} collective-permute-done((bf16[64,1152]{1,0:T(8,128)(2,1)S(1)}, bf16[64,1152]{1,0:T(8,128)(2,1)S(1)}, u32[]{:S(2)}, u32[]{:S(2)}) %collective-permute-start.22) | collective-permute-done | bytes 147488 | tf_op jit(solution)/shard_map/ppermute | solution.py:17
  101.0 0.2 collective-permute-done.24.refs_3_
  101.2 1.3 %finish.1 = (f32[1,64,768]{2,1,0:T(8,128)}, f32[1,64,768]{2,1,0:T(8,128)}) custom-call(s32[5]{0:T(128)S(1)} %stack.20.sc, f32[64,1152]{1,0:T(8,128)S(1)} %get-tuple-element.56.refs_0_, bf16[64,1152]{1,0:T(8,128)(2,1)S(1)} %collective-permute-done.22.refs_1_, bf16[64,1152]{1,0:T(8,128)(2,1)S(1)} %collective-permute-done.23.refs_2_, ...), custom_call_target="tpu_custom_call" | custom-call | flops 910000000 | tf_op jit(solution)/shard_map/finish/pallas_call | solution.py:191
  (38 shorter events, 0.5 us)
Async XLA Ops:
  0.6 13.7 %collective-permute-start.3 = (bf16[768,3072]{1,0:T(8,128)(2,1)}, bf16[768,3072]{1,0:T(8,128)(2,1)}, u32[]{:S(2)}, u32[]{:S(2)}) collective-permute-start(bf16[768,3072]{1,0:T(8,128)(2,1)} %refs_1_.10), channel_id=1, source_target_pairs={{0,1},{1,0},{2,3},{3,2},{4,5},{5,4},{6,7},{7,6},{8,9},{9,8},{10,11... | collective-permute-start | bytes 14155784 | tf_op jit(solution)/shard_map/ppermute | solution.py:17
  1.8 1.3 %copy-start = (bf16[1,192,3072]{2,1,0:T(8,128)(2,1)S(1)}, bf16[1,192,3072]{2,1,0:T(8,128)(2,1)}, u32[]{:S(2)}) copy-start(bf16[1,192,3072]{2,1,0:T(8,128)(2,1)} %refs_0_.5) | copy-start | bytes 3538948
  3.1 5.7 %copy-start.4 = (bf16[1,64,768]{2,1,0:T(8,128)(2,1)S(1)}, bf16[1,64,768]{2,1,0:T(8,128)(2,1)}, u32[]{:S(2)}) copy-start(bf16[1,64,768]{2,1,0:T(8,128)(2,1)} %refs_0_.4) | copy-start | bytes 294916
  3.1 5.7 %copy-start.5 = (bf16[1,64,768]{2,1,0:T(8,128)(2,1)S(1)}, bf16[1,64,768]{2,1,0:T(8,128)(2,1)}, u32[]{:S(2)}) copy-start(bf16[1,64,768]{2,1,0:T(8,128)(2,1)} %refs_1_.7) | copy-start | bytes 294916
  6.1 16.6 %collective-permute-start.4 = (bf16[2,192,768]{2,1,0:T(8,128)(2,1)S(1)}, bf16[2,192,768]{2,1,0:T(8,128)(2,1)S(1)}, u32[]{:S(2)}, u32[]{:S(2)}) collective-permute-start(bf16[2,192,768]{2,1,0:T(8,128)(2,1)S(1)} %attend.2.refs_2_), channel_id=1, source_target_pairs={{0,2},{1,3},{2,0},{3,1},{4,6},{5,7},{6,4},{7,5},{8,10},{9,11},{10,... | collective-permute-start | bytes 1769480 | tf_op jit(solution)/shard_map/ppermute | solution.py:17
  8.7 5.6 %copy-start.1 = (bf16[1,192,3072]{2,1,0:T(8,128)(2,1)S(1)}, bf16[1,192,3072]{2,1,0:T(8,128)(2,1)}, u32[]{:S(2)}) copy-start(bf16[1,192,3072]{2,1,0:T(8,128)(2,1)} %refs_0_.5) | copy-start | bytes 3538948
  9.3 17.8 %collective-permute-start = (bf16[128,768]{1,0:T(8,128)(2,1)S(1)}, bf16[128,768]{1,0:T(8,128)(2,1)S(1)}, u32[]{:S(2)}, u32[]{:S(2)}) collective-permute-start(bf16[128,768]{1,0:T(8,128)(2,1)S(1)} %join.1.refs_3_), channel_id=1, source_target_pairs={{0,16},{4,20},{8,24},{12,28},{16,0},{20,4},{24,8},{28,12},{1,17},{... | collective-permute-start | bytes 589832 | tf_op jit(solution)/shard_map/ppermute | solution.py:17
  12.0 15.2 %collective-permute-start.1 = (bf16[128,768]{1,0:T(8,128)(2,1)S(1)}, bf16[128,768]{1,0:T(8,128)(2,1)S(1)}, u32[]{:S(2)}, u32[]{:S(2)}) collective-permute-start(bf16[128,768]{1,0:T(8,128)(2,1)S(1)} %join.1.refs_3_), channel_id=1, source_target_pairs={{0,24},{4,28},{8,16},{12,20},{16,8},{20,12},{24,0},{28,4},{1,25},{... | collective-permute-start | bytes 589832 | tf_op jit(solution)/shard_map/ppermute | solution.py:17
  13.3 13.8 %collective-permute-start.2 = (bf16[128,768]{1,0:T(8,128)(2,1)S(1)}, bf16[128,768]{1,0:T(8,128)(2,1)S(1)}, u32[]{:S(2)}, u32[]{:S(2)}) collective-permute-start(bf16[128,768]{1,0:T(8,128)(2,1)S(1)} %join.1.refs_3_), channel_id=1, source_target_pairs={{0,8},{4,12},{8,0},{12,4},{16,24},{20,28},{24,16},{28,20},{1,9},{5... | collective-permute-start | bytes 589832 | tf_op jit(solution)/shard_map/ppermute | solution.py:17
  13.5 9.1 %slice-start = ((s8[4718592]{0:T(1024)(128)(4,1)}), s8[4194304]{0:T(1024)(128)(4,1)S(1)}, s32[]{:S(2)}) async-start(s8[4718592]{0:T(1024)(128)(4,1)} %bitcast.9), calls=%async_computation | async-start | bytes 8388608
  14.3 3.5 %copy-start.6 = (s32[8]{0:T(128)S(1)}, s32[8]{0:T(128)}, u32[]{:S(2)}) copy-start(s32[8]{0:T(128)} %refs_2_.5) | copy-start | bytes 100
  14.4 8.3 %slice-start.1 = ((s8[4718592]{0:T(1024)(128)(4,1)}), s8[524288]{0:T(1024)(128)(4,1)S(1)}, s32[]{:S(2)}) async-start(s8[4718592]{0:T(1024)(128)(4,1)} %bitcast.9), calls=%async_computation.1 | async-start | bytes 1048576
  21.3 5.9 %collective-permute-start.5 = (f32[8,128]{1,0:T(8,128)S(1)}, f32[8,128]{1,0:T(8,128)S(1)}, u32[]{:S(2)}, u32[]{:S(2)}) collective-permute-start(f32[8,128]{1,0:T(8,128)S(1)} %get-tuple-element.34.refs_6_), channel_id=1, source_target_pairs={{0,2},{1,3},{2,0},{3,1},{4,6},{5,7},{6,4},{7,5},{8,10},{9,11},{10,... | collective-permute-start | bytes 12296 | tf_op jit(solution)/shard_map/ppermute | solution.py:17
  25.3 33.5 %collective-permute-start.11 = (bf16[4,192,768]{2,1,0:T(8,128)(2,1)S(1)}, bf16[4,192,768]{2,1,0:T(8,128)(2,1)S(1)}, u32[]{:S(2)}, u32[]{:S(2)}) collective-permute-start(bf16[4,192,768]{2,1,0:T(8,128)(2,1)S(1)} %project.1.refs_8_), channel_id=1, source_target_pairs={{0,2},{1,3},{2,0},{3,1},{4,6},{5,7},{6,4},{7,5},{8,10},{9,11},{10,... | collective-permute-start | bytes 3538952 | tf_op jit(solution)/shard_map/ppermute | solution.py:17
  27.2 3.6 %copy-start.3 = (bf16[1,192,3072]{2,1,0:T(8,128)(2,1)S(1)}, bf16[1,192,3072]{2,1,0:T(8,128)(2,1)}, u32[]{:S(2)}) copy-start(bf16[1,192,3072]{2,1,0:T(8,128)(2,1)} %refs_4_.1) | copy-start | bytes 3538948
  27.8 3.0 %copy-start.2 = (bf16[1,192,3072]{2,1,0:T(8,128)(2,1)S(1)}, bf16[1,192,3072]{2,1,0:T(8,128)(2,1)}, u32[]{:S(2)}) copy-start(bf16[1,192,3072]{2,1,0:T(8,128)(2,1)} %refs_3_.1) | copy-start | bytes 3538948
  27.8 18.9 %collective-permute-start.10 = (bf16[4,128,768]{2,1,0:T(8,128)(2,1)S(1)}, bf16[4,128,768]{2,1,0:T(8,128)(2,1)S(1)}, u32[]{:S(2)}, u32[]{:S(2)}) collective-permute-start(bf16[4,128,768]{2,1,0:T(8,128)(2,1)S(1)} %get-tuple-element.38.refs_5_.refs_8_), channel_id=1, source_target_pairs={{0,4},{4,0},{8,12},{12,8},{16,20},{20,16},{24,28},{28,24},{1,5},{5... | collective-permute-start | bytes 2359304 | tf_op jit(solution)/shard_map/ppermute | solution.py:17
  29.4 1.2 %collective-permute-start.6 = (f32[8,128]{1,0:T(8,128)S(1)}, f32[8,128]{1,0:T(8,128)S(1)}, u32[]{:S(2)}, u32[]{:S(2)}) collective-permute-start(f32[8,128]{1,0:T(8,128)S(1)} %get-tuple-element.36.refs_0_), channel_id=1, source_target_pairs={{0,1},{1,0},{2,3},{3,2},{4,5},{5,4},{6,7},{7,6},{8,9},{9,8},{10,11... | collective-permute-start | bytes 12296 | tf_op jit(solution)/shard_map/ppermute | solution.py:17
  29.5 4.8 %collective-permute-start.8 = (bf16[192,768]{1,0:T(8,128)(2,1)S(1)}, bf16[192,768]{1,0:T(8,128)(2,1)S(1)}, u32[]{:S(2)}, u32[]{:S(2)}) collective-permute-start(bf16[192,768]{1,0:T(8,128)(2,1)S(1)} %get-tuple-element.39), channel_id=1, source_target_pairs={{0,1},{1,0},{2,3},{3,2},{4,5},{5,4},{6,7},{7,6},{8,9},{9,8},{10,11... | collective-permute-start | bytes 884744 | tf_op jit(solution)/shard_map/ppermute | solution.py:17
  30.1 4.2 %collective-permute-start.9 = (bf16[192,768]{1,0:T(8,128)(2,1)S(1)}, bf16[192,768]{1,0:T(8,128)(2,1)S(1)}, u32[]{:S(2)}, u32[]{:S(2)}) collective-permute-start(bf16[192,768]{1,0:T(8,128)(2,1)S(1)} %get-tuple-element.40), channel_id=1, source_target_pairs={{0,1},{1,0},{2,3},{3,2},{4,5},{5,4},{6,7},{7,6},{8,9},{9,8},{10,11... | collective-permute-start | bytes 884744 | tf_op jit(solution)/shard_map/ppermute | solution.py:17
  30.6 3.7 %collective-permute-start.7 = (f32[8,128]{1,0:T(8,128)S(1)}, f32[8,128]{1,0:T(8,128)S(1)}, u32[]{:S(2)}, u32[]{:S(2)}) collective-permute-start(f32[8,128]{1,0:T(8,128)S(1)} %get-tuple-element.37.refs_2_), channel_id=1, source_target_pairs={{0,1},{1,0},{2,3},{3,2},{4,5},{5,4},{6,7},{7,6},{8,9},{9,8},{10,11... | collective-permute-start | bytes 12296 | tf_op jit(solution)/shard_map/ppermute | solution.py:17
  48.5 7.9 %collective-permute-start.12 = (bf16[64,1024]{1,0:T(8,128)(2,1)S(1)}, bf16[64,1024]{1,0:T(8,128)(2,1)S(1)}, u32[]{:S(2)}, u32[]{:S(2)}) collective-permute-start(bf16[64,1024]{1,0:T(8,128)(2,1)S(1)} %get-tuple-element.42), channel_id=1, source_target_pairs={{0,3},{1,2},{2,1},{3,0},{4,7},{5,6},{6,5},{7,4},{8,11},{9,10},{10,... | collective-permute-start | bytes 393224 | tf_op jit(solution)/shard_map/ppermute | solution.py:17
  48.5 10.2 %collective-permute-start.13 = (bf16[64,1024]{1,0:T(8,128)(2,1)S(1)}, bf16[64,1024]{1,0:T(8,128)(2,1)S(1)}, u32[]{:S(2)}, u32[]{:S(2)}) collective-permute-start(bf16[64,1024]{1,0:T(8,128)(2,1)S(1)} %get-tuple-element.43), channel_id=1, source_target_pairs={{0,2},{1,3},{2,0},{3,1},{4,6},{5,7},{6,4},{7,5},{8,10},{9,11},{10,... | collective-permute-start | bytes 393224 | tf_op jit(solution)/shard_map/ppermute | solution.py:17
  49.1 9.7 %collective-permute-start.14 = (bf16[64,1024]{1,0:T(8,128)(2,1)S(1)}, bf16[64,1024]{1,0:T(8,128)(2,1)S(1)}, u32[]{:S(2)}, u32[]{:S(2)}) collective-permute-start(bf16[64,1024]{1,0:T(8,128)(2,1)S(1)} %get-tuple-element.44), channel_id=1, source_target_pairs={{0,1},{1,0},{2,3},{3,2},{4,5},{5,4},{6,7},{7,6},{8,9},{9,8},{10,11... | collective-permute-start | bytes 393224 | tf_op jit(solution)/shard_map/ppermute | solution.py:17
  61.3 5.7 %collective-permute-start.15 = (bf16[64,1024]{1,0:T(8,128)(2,1)S(1)}, bf16[64,1024]{1,0:T(8,128)(2,1)S(1)}, u32[]{:S(2)}, u32[]{:S(2)}) collective-permute-start(bf16[64,1024]{1,0:T(8,128)(2,1)S(1)} %get-tuple-element.46), channel_id=1, source_target_pairs={{0,3},{1,2},{2,1},{3,0},{4,7},{5,6},{6,5},{7,4},{8,11},{9,10},{10,... | collective-permute-start | bytes 393224 | tf_op jit(solution)/shard_map/ppermute | solution.py:17
  61.4 8.6 %collective-permute-start.16 = (bf16[64,1024]{1,0:T(8,128)(2,1)S(1)}, bf16[64,1024]{1,0:T(8,128)(2,1)S(1)}, u32[]{:S(2)}, u32[]{:S(2)}) collective-permute-start(bf16[64,1024]{1,0:T(8,128)(2,1)S(1)} %get-tuple-element.47), channel_id=1, source_target_pairs={{0,2},{1,3},{2,0},{3,1},{4,6},{5,7},{6,4},{7,5},{8,10},{9,11},{10,... | collective-permute-start | bytes 393224 | tf_op jit(solution)/shard_map/ppermute | solution.py:17
  63.0 7.0 %collective-permute-start.17 = (bf16[64,1024]{1,0:T(8,128)(2,1)S(1)}, bf16[64,1024]{1,0:T(8,128)(2,1)S(1)}, u32[]{:S(2)}, u32[]{:S(2)}) collective-permute-start(bf16[64,1024]{1,0:T(8,128)(2,1)S(1)} %get-tuple-element.48), channel_id=1, source_target_pairs={{0,1},{1,0},{2,3},{3,2},{4,5},{5,4},{6,7},{7,6},{8,9},{9,8},{10,11... | collective-permute-start | bytes 393224 | tf_op jit(solution)/shard_map/ppermute | solution.py:17
  71.6 15.3 %collective-permute-start.20 = (bf16[4,64,1152]{2,1,0:T(8,128)(2,1)S(1)}, bf16[4,64,1152]{2,1,0:T(8,128)(2,1)S(1)}, u32[]{:S(2)}, u32[]{:S(2)}) collective-permute-start(bf16[4,64,1152]{2,1,0:T(8,128)(2,1)S(1)} %get-tuple-element.54), channel_id=1, source_target_pairs={{0,4},{4,0},{8,12},{12,8},{16,20},{20,16},{24,28},{28,24},{1,5},{5... | collective-permute-start | bytes 1769480 | tf_op jit(solution)/shard_map/ppermute | solution.py:17
  73.2 10.7 %collective-permute-start.18 = (bf16[2,64,384]{2,1,0:T(8,128)(2,1)S(1)}, bf16[2,64,384]{2,1,0:T(8,128)(2,1)S(1)}, u32[]{:S(2)}, u32[]{:S(2)}) collective-permute-start(bf16[2,64,384]{2,1,0:T(8,128)(2,1)S(1)} %get-tuple-element.52), channel_id=1, source_target_pairs={{0,16},{4,20},{8,24},{12,28},{16,0},{20,4},{24,8},{28,12},{1,17},{... | collective-permute-start | bytes 294920 | tf_op jit(solution)/shard_map/ppermute | solution.py:17
  76.5 7.5 %collective-permute-start.19 = (bf16[2,64,384]{2,1,0:T(8,128)(2,1)S(1)}, bf16[2,64,384]{2,1,0:T(8,128)(2,1)S(1)}, u32[]{:S(2)}, u32[]{:S(2)}) collective-permute-start(bf16[2,64,384]{2,1,0:T(8,128)(2,1)S(1)} %get-tuple-element.53), channel_id=1, source_target_pairs={{0,24},{4,28},{8,16},{12,20},{16,8},{20,12},{24,0},{28,4},{1,25},{... | collective-permute-start | bytes 294920 | tf_op jit(solution)/shard_map/ppermute | solution.py:17
  76.9 7.5 %collective-permute-start.21 = (bf16[2,64,384]{2,1,0:T(8,128)(2,1)S(1)}, bf16[2,64,384]{2,1,0:T(8,128)(2,1)S(1)}, u32[]{:S(2)}, u32[]{:S(2)}) collective-permute-start(bf16[2,64,384]{2,1,0:T(8,128)(2,1)S(1)} %get-tuple-element.55), channel_id=1, source_target_pairs={{0,8},{4,12},{8,0},{12,4},{16,24},{20,28},{24,16},{28,20},{1,9},{5... | collective-permute-start | bytes 294920 | tf_op jit(solution)/shard_map/ppermute | solution.py:17
  87.6 13.4 %collective-permute-start.22 = (bf16[64,1152]{1,0:T(8,128)(2,1)S(1)}, bf16[64,1152]{1,0:T(8,128)(2,1)S(1)}, u32[]{:S(2)}, u32[]{:S(2)}) collective-permute-start(bf16[64,1152]{1,0:T(8,128)(2,1)S(1)} %get-tuple-element.57), channel_id=1, source_target_pairs={{0,16},{4,20},{8,24},{12,28},{16,0},{20,4},{24,8},{28,12},{1,17},{... | collective-permute-start | bytes 442376 | tf_op jit(solution)/shard_map/ppermute | solution.py:17
  90.6 10.4 %collective-permute-start.23 = (bf16[64,1152]{1,0:T(8,128)(2,1)S(1)}, bf16[64,1152]{1,0:T(8,128)(2,1)S(1)}, u32[]{:S(2)}, u32[]{:S(2)}) collective-permute-start(bf16[64,1152]{1,0:T(8,128)(2,1)S(1)} %get-tuple-element.58), channel_id=1, source_target_pairs={{0,24},{4,28},{8,16},{12,20},{16,8},{20,12},{24,0},{28,4},{1,25},{... | collective-permute-start | bytes 442376 | tf_op jit(solution)/shard_map/ppermute | solution.py:17
  91.4 9.8 %collective-permute-start.24 = (bf16[64,1152]{1,0:T(8,128)(2,1)S(1)}, bf16[64,1152]{1,0:T(8,128)(2,1)S(1)}, u32[]{:S(2)}, u32[]{:S(2)}) collective-permute-start(bf16[64,1152]{1,0:T(8,128)(2,1)S(1)} %get-tuple-element.59), channel_id=1, source_target_pairs={{0,8},{4,12},{8,0},{12,4},{16,24},{20,28},{24,16},{28,20},{1,9},{5... | collective-permute-start | bytes 442376 | tf_op jit(solution)/shard_map/ppermute | solution.py:17
  91.9 4.1 %collective-permute-start.25 = (bf16[64,384]{1,0:T(8,128)(2,1)S(1)}, bf16[64,384]{1,0:T(8,128)(2,1)S(1)}, u32[]{:S(2)}, u32[]{:S(2)}) collective-permute-start(bf16[64,384]{1,0:T(8,128)(2,1)S(1)} %get-tuple-element.61), channel_id=1, source_target_pairs={{0,4},{4,0},{8,12},{12,8},{16,20},{20,16},{24,28},{28,24},{1,5},{5... | collective-permute-start | bytes 147464 | tf_op jit(solution)/shard_map/ppermute | solution.py:17

commit v8 on v7

--- a/solution.py
+++ b/solution.py
@@ -215,6 +215,22 @@
     return [out[order.index(i)] for i in range(len(order))]
 
 
+def fold_rows(rank, slots, depth):
+    return rank * slots // depth
+
+
+def fold_into(ref, rank, value):
+    rows, depth = ref.shape[0] - rank, ref.shape[1]
+    slots = value.shape[1]
+    for i in range(depth // slots):
+        ref[rank:, i * slots : (i + 1) * slots] = value[i * rows : (i + 1) * rows]
+
+
+def unfold(ref, rank, slots):
+    count = ref.shape[1] // slots
+    return jnp.concatenate([ref[rank:, i * slots : (i + 1) * slots] for i in range(count)])
+
+
 def shaped(shape, dtype=BF16):
     return jax.ShapeDtypeStruct(shape, dtype)
 
@@ -344,7 +360,6 @@
 def error_terms(scalars, base, received, low_part, adapters):
     size, slots, depth = base.shape
     rank = low_part.shape[0]
-    back_lanes = -(-slots // LANES) * LANES
     peers = len(received)
 
     def body(sc, base_ref, low_ref, *refs):
@@ -355,13 +370,13 @@
         valid = lax.broadcasted_iota(jnp.int32, (slots, 1), 0) < count
         low_wide = low_ref[...]
         for ref in up_refs[1:]:
-            low_wide = low_wide + ref[:, depth : depth + slots].astype(F32)
+            low_wide = low_wide + unfold(ref, rank, slots).astype(F32)
         low_turned = ADAPTER_SCALE * low_wide.astype(BF16)
         low_state = ADAPTER_SCALE * low_wide.T.astype(BF16)
         back = jnp.zeros((slots, rank), F32)
         squares = jnp.zeros((slots, depth), F32)
         for k in range(size):
-            up = up_refs[k][:, :depth]
+            up = up_refs[k][:rank, :]
             error = base_ref[k] + dot(low_state, up, 1, 0)
             for ref in got:
                 error = error + ref[k].astype(F32)
@@ -369,15 +384,14 @@
             squares = squares + error * error
             cotangent = (error * per_token).astype(BF16)
             back = back + dot(cotangent, up, 1, 1)
-            pieces[k][:, :depth] = dot(low_turned, cotangent, 1, 0).astype(BF16)
+            pieces[k][:rank, :] = dot(low_turned, cotangent, 1, 0).astype(BF16)
         refs[-1][0, 0] = jnp.sum(squares) / (tokens * (size * depth))
-        padded = (ADAPTER_SCALE * back).T.astype(BF16)
-        padded = jnp.concatenate([padded, jnp.zeros((rank, back_lanes - slots), BF16)], axis=1)
+        turned = (ADAPTER_SCALE * back).T.astype(BF16)
         for k in range(size):
-            pieces[k][:, depth:] = padded
+            fold_into(pieces[k], rank, turned)
 
     whole = lambda x: pl.BlockSpec(x.shape, lambda k, sc: (0,) * len(x.shape))
-    out_shape = [shaped((rank, depth + back_lanes))] * size + [shaped((1, 1), F32)]
+    out_shape = [shaped((rank + fold_rows(rank, slots, depth), depth))] * size + [shaped((1, 1), F32)]
     out = kernel_call(
         body,
         "error",
@@ -440,7 +454,6 @@
     rank = rows // 2
     size = len(slot_list)
     slots = columns[0].shape[0]
-    padded = -(-slots // LANES) * LANES
 
     def body(sc, *refs):
         slot_refs, column_refs, refs = refs[:size], refs[size : 2 * size], refs[2 * size :]
@@ -457,17 +470,15 @@
             part = dot(held[k, :rank, :], column_refs[k][...], 1, 1)
             if k == 0:
                 low_ref[...] = part
-            outs[k][:, :depth] = held[k, rank:, :]
-            outs[k][:, depth:] = jnp.concatenate(
-                [part.astype(BF16), jnp.zeros((rank, padded - slots), BF16)], axis=1
-            )
+            outs[k][:rank, :] = held[k, rank:, :]
+            fold_into(outs[k], rank, part.astype(BF16))
 
     out = kernel_call(
         body,
         "choose",
         scalars,
         (*slot_list, *columns, *arrays),
-        [shaped((rank, depth + padded))] * size + [shaped((rank, slots), F32)],
+        [shaped((rank + fold_rows(rank, slots, depth), depth))] * size + [shaped((rank, slots), F32)],
         2.0,
         after=after,
         scratch=[pltpu.VMEM((size, rows, depth), BF16)],
@@ -605,13 +616,13 @@
             got = got[::-1]
             outs = refs[3 * fsdp_size :]
             offsets = [slot_offset(sc, ref) for ref in slot_refs]
-            downs = [dot(p[:, depth : depth + slots], c[...], 1, 0) for p, c in zip(got, cols)]
+            downs = [dot(unfold(p, rank, slots), c[...], 1, 0) for p, c in zip(got, cols)]
             down_outs = [ref.at[:, :, :depth] for ref in outs[:inner]]
             first_refs(offsets, downs, down_outs[0], down_outs[1:], *along_inner)
-            ups = [p[:, :cut].astype(F32) for p in got]
+            ups = [p[:rank, :cut].astype(F32) for p in got]
             up_outs = [ref.at[:, :, depth:] for ref in outs[:inner]]
             first_refs(offsets, ups, up_outs[0], up_outs[1:], *along_inner)
-            ups = [p[:, cut:depth].astype(F32) for p in got]
+            ups = [p[:rank, cut:depth].astype(F32) for p in got]
             first_refs(offsets, ups, outs[inner], outs[inner + 1 :], *along_outer)
 
         far = [o for o in range(1, outer) if 2 * o >= outer]
@@ -670,7 +681,7 @@
 
     def per_device(*operands):
         depth = operands[5].shape[0]
-        return (chunked if depth % (3 * LANES) == 0 else general)(*operands)
+        return (chunked if depth % (3 * LANES) == 0 and depth <= 4 * operands[0].shape[1] else general)(*operands)
 
     return jax.shard_map(
         per_device,

time: 103 us -> 103 us (level)
  transfers between devices with their start and end apart: 26 -> 26, of which waited for: 13 -> 13; matrix products, arithmetic and copies ran while one was open for 0% -> 0% of each run, Pallas kernels for 18% -> 19%
where the time goes in v8:
time: 103 us; the launch traced here: 102 us
  waiting for transfers between devices  45.4 us (44%)
  starting transfers between devices  27.6 us (27%)
  Pallas kernels  25.2 us (24%)
  between operations  2.32 us (2%)
  local copies, waits for them, and re-layouts  1.43 us (1%)
    ppermute x26, waiting for transfers between devices, xor_send(): return lax.ppermute(value, axis, [(i, i ^ offset) for i in range(size)])  45.4 us
    ppermute x26, starting transfers between devices, xor_send(): return lax.ppermute(value, axis, [(i, i ^ offset) for i in range(size)])  27.6 us
    pallas_call x12, Pallas kernels, kernel_call(): pl.pallas_call(body, out_shape=out_shape, grid_spec=pltpu.PrefetchScalarG...  25.2 us
  transfers between devices with their start and end apart: 26, of which 13 were waited for; matrix products, arithmetic and copies ran while one was open for 0% of the time, Pallas kernels for 19%

profile of v8, /device:TPU:0, one launch (start us, length us, event | category | flops | bytes accessed | tf_op | source)
XLA Modules:
  0.0 101.9 jit_solution(4695646703372752322)
XLA Ops:
  0.6 0.5 collective-permute-start.3
  1.8 1.3 %copy-done = bf16[1,192,3072]{2,1,0:T(8,128)(2,1)S(1)} copy-done((bf16[1,192,3072]{2,1,0:T(8,128)(2,1)S(1)}, bf16[1,192,3072]{2,1,0:T(8,128)(2,1)}, u32[]{:S(2)}) %copy-start) | copy-done | bytes 1179672
  3.1 3.0 %attend.2.refs_2_ = bf16[2,192,768]{2,1,0:T(8,128)(2,1)S(1)} custom-call(s32[1]{0:T(128)S(6)} %copy.15.sc, bf16[1,192,3072]{2,1,0:T(8,128)(2,1)S(1)} %copy-done, bf16[1,192,3072]{2,1,0:T(8,128)(2,1)} %refs_1_.8, bf16[1,192,3072]{2,1,0:T(8,128)(2,1)} %refs_2_.4), custom_call_target="tpu_custom_call" | custom-call | flops 2800000000 | tf_op jit(solution)/shard_map/attend/pallas_call | solution.py:191
  6.1 2.6 %collective-permute-start.4 = (bf16[2,192,768]{2,1,0:T(8,128)(2,1)S(1)}, bf16[2,192,768]{2,1,0:T(8,128)(2,1)S(1)}, u32[]{:S(2)}, u32[]{:S(2)}) collective-permute-start(bf16[2,192,768]{2,1,0:T(8,128)(2,1)S(1)} %attend.2.refs_2_), channel_id=1, source_target_pairs={{0,2},{1,3},{2,0},{3,1},{4,6},{5,7},{6,4},{7,5},{8,10},{9,11},{10,... | collective-permute-start | bytes 1769480 | tf_op jit(solution)/shard_map/ppermute | solution.py:17
  8.7 0.6 join.1.refs_3_
  9.3 2.7 %collective-permute-start = (bf16[128,768]{1,0:T(8,128)(2,1)S(1)}, bf16[128,768]{1,0:T(8,128)(2,1)S(1)}, u32[]{:S(2)}, u32[]{:S(2)}) collective-permute-start(bf16[128,768]{1,0:T(8,128)(2,1)S(1)} %join.1.refs_3_), channel_id=1, source_target_pairs={{0,16},{4,20},{8,24},{12,28},{16,0},{20,4},{24,8},{28,12},{1,17},{... | collective-permute-start | bytes 589832 | tf_op jit(solution)/shard_map/ppermute | solution.py:17
  12.0 1.3 %collective-permute-start.1 = (bf16[128,768]{1,0:T(8,128)(2,1)S(1)}, bf16[128,768]{1,0:T(8,128)(2,1)S(1)}, u32[]{:S(2)}, u32[]{:S(2)}) collective-permute-start(bf16[128,768]{1,0:T(8,128)(2,1)S(1)} %join.1.refs_3_), channel_id=1, source_target_pairs={{0,24},{4,28},{8,16},{12,20},{16,8},{20,12},{24,0},{28,4},{1,25},{... | collective-permute-start | bytes 589832 | tf_op jit(solution)/shard_map/ppermute | solution.py:17
  13.3 0.2 collective-permute-start.2
  14.4 3.4 %attend.3.refs_3_.refs_4_.refs_0_ = bf16[2,192,768]{2,1,0:T(8,128)(2,1)S(1)} custom-call(s32[1]{0:T(128)S(6)} %copy.15.sc, bf16[1,192,3072]{2,1,0:T(8,128)(2,1)S(1)} %copy-done.1, bf16[1,192,3072]{2,1,0:T(8,128)(2,1)} %refs_1_.8, bf16[1,192,3072]{2,1,0:T(8,128)(2,1)} %refs_2_.4, bf16[128,768]{1,0:T(8,128)(2,1)S(1)} %join.1.refs_3_, ...), custom_call_target="tpu_custom_call" | custom-call | flops 2800000000 | tf_op jit(solution)/shard_map/attend/pallas_call | solution.py:191
  17.8 3.5 %bring_weight.1 = (bf16[768,3072]{1,0:T(8,128)(2,1)S(1)}, f32[8,128]{1,0:T(8,128)S(1)}) custom-call(s32[5]{0:T(128)S(1)} %stack.20.sc, bf16[768,3072]{1,0:T(8,128)(2,1)} %collective-permute-done.3.refs_4_.refs_0_, s32[1]{0:T(128)S(6)} %copy.14.refs_1_, s32[8]{0:T(128)S(1)} %copy-done.6, bf16[2,192,768]{2,1,0:T(8,128)(2,1)S(1)} %attend.3.refs_3_.refs_4_.refs_0_), custom_call_target="tpu_custom_call" | custom-call | flops 2100000000 | tf_op jit(solution)/shard_map/bring_weight/pallas_call | solution.py:191
  21.3 0.6 collective-permute-start.5
  21.8 0.8 collective-permute-done.4.refs_0_.refs_5_
  22.6 2.6 %project.1.refs_8_ = bf16[4,192,768]{2,1,0:T(8,128)(2,1)S(1)} custom-call(s32[5]{0:T(128)S(1)} %stack.20.sc, bf16[2,192,768]{2,1,0:T(8,128)(2,1)S(1)} %collective-permute-done.4.refs_0_.refs_5_, bf16[768,3072]{1,0:T(8,128)(2,1)S(1)} %bitcast.10, bf16[768,3072]{1,0:T(8,128)(2,1)S(1)} %get-tuple-element.35.refs_2_, ...), custom_call_target="tpu_custom_call" | custom-call | flops 2100000000 | tf_op jit(solution)/shard_map/project/pallas_call | solution.py:191
  25.3 1.8 %collective-permute-start.11 = (bf16[4,192,768]{2,1,0:T(8,128)(2,1)S(1)}, bf16[4,192,768]{2,1,0:T(8,128)(2,1)S(1)}, u32[]{:S(2)}, u32[]{:S(2)}) collective-permute-start(bf16[4,192,768]{2,1,0:T(8,128)(2,1)S(1)} %project.1.refs_8_), channel_id=1, source_target_pairs={{0,2},{1,3},{2,0},{3,1},{4,6},{5,7},{6,4},{7,5},{8,10},{9,11},{10,... | collective-permute-start | bytes 3538952 | tf_op jit(solution)/shard_map/ppermute | solution.py:17
  27.2 0.6 stack.21
  27.8 1.6 %collective-permute-start.10 = (bf16[4,128,768]{2,1,0:T(8,128)(2,1)S(1)}, bf16[4,128,768]{2,1,0:T(8,128)(2,1)S(1)}, u32[]{:S(2)}, u32[]{:S(2)}) collective-permute-start(bf16[4,128,768]{2,1,0:T(8,128)(2,1)S(1)} %get-tuple-element.38.refs_5_.refs_8_), channel_id=1, source_target_pairs={{0,4},{4,0},{8,12},{12,8},{16,20},{20,16},{24,28},{28,24},{1,5},{5... | collective-permute-start | bytes 2359304 | tf_op jit(solution)/shard_map/ppermute | solution.py:17
  29.5 0.6 collective-permute-start.8
  30.1 0.5 collective-permute-done.6.refs_1_
  30.6 0.2 collective-permute-start.7
  30.8 3.5 %base.1.refs_10_.refs_0_ = f32[4,192,768]{2,1,0:T(8,128)S(1)} custom-call(s32[5]{0:T(128)S(1)} %stack.20.sc, bf16[2,192,768]{2,1,0:T(8,128)(2,1)S(1)} %attend.3.refs_3_.refs_4_.refs_0_, bf16[768,3072]{1,0:T(8,128)(2,1)S(1)} %bitcast.10, bf16[768,3072]{1,0:T(8,128)(2,1)S(1)} %get-tuple-element.35.refs_2_, bf16[1,192,3072]{2,1,0:T(8,128)(2,1)S(1)} %copy-done.2, ...), custom_call_target="tpu_custom_call" | custom-call | flops 4899999744 | tf_op jit(solution)/shard_map/base/pallas_call | solution.py:191
  34.3 12.4 %collective-permute-done.10.refs_9_ = bf16[4,128,768]{2,1,0:T(8,128)(2,1)S(1)} collective-permute-done((bf16[4,128,768]{2,1,0:T(8,128)(2,1)S(1)}, bf16[4,128,768]{2,1,0:T(8,128)(2,1)S(1)}, u32[]{:S(2)}, u32[]{:S(2)}) %collective-permute-start.10) | collective-permute-done | bytes 786464 | tf_op jit(solution)/shard_map/ppermute | solution.py:17
  46.8 1.8 %choose.1 = (bf16[80,768]{1,0:T(8,128)(2,1)S(1)}, bf16[80,768]{1,0:T(8,128)(2,1)S(1)}, bf16[80,768]{1,0:T(8,128)(2,1)S(1)}, bf16[80,768]{1,0:T(8,128)(2,1)S(1)}, f32[64,192]{1,0:T(8,128)S(1)}) custom-call(s32[5]{0:T(128)S(1)} %stack.20.sc, f32[8,128]{1,0:T(8,128)S(1)} %get-tuple-element.36.refs_0_, f32[8,128]{1,0:T(8,128)S(1)} %collective-permute-done.6.refs_1_, ...), custom_call_target="tpu_custom_call" | custom-call | flops 1400000000 | tf_op jit(solution)/shard_map/choose/pallas_call | solution.py:191
  48.6 0.5 collective-permute-start.13
  49.1 1.3 %collective-permute-start.14 = (bf16[80,768]{1,0:T(8,128)(2,1)S(1)}, bf16[80,768]{1,0:T(8,128)(2,1)S(1)}, u32[]{:S(2)}, u32[]{:S(2)}) collective-permute-start(bf16[80,768]{1,0:T(8,128)(2,1)S(1)} %get-tuple-element.44), channel_id=1, source_target_pairs={{0,1},{1,0},{2,3},{3,2},{4,5},{5,4},{6,7},{7,6},{8,9},{9,8},{10,11... | collective-permute-start | bytes 368648 | tf_op jit(solution)/shard_map/ppermute | solution.py:17
  50.5 5.7 %collective-permute-done.12.refs_3_ = bf16[80,768]{1,0:T(8,128)(2,1)S(1)} collective-permute-done((bf16[80,768]{1,0:T(8,128)(2,1)S(1)}, bf16[80,768]{1,0:T(8,128)(2,1)S(1)}, u32[]{:S(2)}, u32[]{:S(2)}) %collective-permute-start.12) | collective-permute-done | bytes 122912 | tf_op jit(solution)/shard_map/ppermute | solution.py:17
  56.2 2.2 %collective-permute-done.13.refs_4_ = bf16[80,768]{1,0:T(8,128)(2,1)S(1)} collective-permute-done((bf16[80,768]{1,0:T(8,128)(2,1)S(1)}, bf16[80,768]{1,0:T(8,128)(2,1)S(1)}, u32[]{:S(2)}, u32[]{:S(2)}) %collective-permute-start.13) | collective-permute-done | bytes 122912 | tf_op jit(solution)/shard_map/ppermute | solution.py:17
  58.4 2.6 %error.1 = (bf16[80,768]{1,0:T(8,128)(2,1)S(1)}, bf16[80,768]{1,0:T(8,128)(2,1)S(1)}, bf16[80,768]{1,0:T(8,128)(2,1)S(1)}, bf16[80,768]{1,0:T(8,128)(2,1)S(1)}, f32[1,1]{1,0:T(1,128)}) custom-call(s32[5]{0:T(128)S(1)} %stack.20.sc, f32[4,192,768]{2,1,0:T(8,128)S(1)} %base.1.refs_10_.refs_0_, f32[64,192]{1,0:T(8,128)S(1)} %get-tuple-element.41.refs_1_, ...), custom_call_target="tpu_custom_call" | custom-call | flops 2100000000 | tf_op jit(solution)/shard_map/error/pallas_call | solution.py:191
  61.1 1.6 %collective-permute-start.16 = (bf16[80,768]{1,0:T(8,128)(2,1)S(1)}, bf16[80,768]{1,0:T(8,128)(2,1)S(1)}, u32[]{:S(2)}, u32[]{:S(2)}) collective-permute-start(bf16[80,768]{1,0:T(8,128)(2,1)S(1)} %get-tuple-element.47), channel_id=1, source_target_pairs={{0,2},{1,3},{2,0},{3,1},{4,6},{5,7},{6,4},{7,5},{8,10},{9,11},{10,... | collective-permute-start | bytes 368648 | tf_op jit(solution)/shard_map/ppermute | solution.py:17
  62.8 0.2 collective-permute-start.17
  63.0 3.6 %collective-permute-done.15.refs_4_ = bf16[80,768]{1,0:T(8,128)(2,1)S(1)} collective-permute-done((bf16[80,768]{1,0:T(8,128)(2,1)S(1)}, bf16[80,768]{1,0:T(8,128)(2,1)S(1)}, u32[]{:S(2)}, u32[]{:S(2)}) %collective-permute-start.15) | collective-permute-done | bytes 122912 | tf_op jit(solution)/shard_map/ppermute | solution.py:17
  66.6 2.8 %collective-permute-done.16.refs_5_ = bf16[80,768]{1,0:T(8,128)(2,1)S(1)} collective-permute-done((bf16[80,768]{1,0:T(8,128)(2,1)S(1)}, bf16[80,768]{1,0:T(8,128)(2,1)S(1)}, u32[]{:S(2)}, u32[]{:S(2)}) %collective-permute-start.16) | collective-permute-done | bytes 122912 | tf_op jit(solution)/shard_map/ppermute | solution.py:17
  69.4 1.7 %first.1 = (f32[4,64,1152]{2,1,0:T(8,128)S(1)}, f32[2,64,384]{2,1,0:T(8,128)S(1)}, bf16[2,64,384]{2,1,0:T(8,128)(2,1)S(1)}, bf16[2,64,384]{2,1,0:T(8,128)(2,1)S(...) custom-call(s32[5]{0:T(128)S(1)} %stack.20.sc, f32[8,128]{1,0:T(8,128)S(1)} %get-tuple-element.36.refs_0_, ...), custom_call_target="tpu_custom_call" | custom-call | flops 1400000000 | tf_op jit(solution)/shard_map/first/pallas_call | solution.py:191
  71.0 1.6 %collective-permute-start.20 = (bf16[4,64,1152]{2,1,0:T(8,128)(2,1)S(1)}, bf16[4,64,1152]{2,1,0:T(8,128)(2,1)S(1)}, u32[]{:S(2)}, u32[]{:S(2)}) collective-permute-start(bf16[4,64,1152]{2,1,0:T(8,128)(2,1)S(1)} %get-tuple-element.54), channel_id=1, source_target_pairs={{0,4},{4,0},{8,12},{12,8},{16,20},{20,16},{24,28},{28,24},{1,5},{5... | collective-permute-start | bytes 1769480 | tf_op jit(solution)/shard_map/ppermute | solution.py:17
  72.6 3.3 %collective-permute-start.18 = (bf16[2,64,384]{2,1,0:T(8,128)(2,1)S(1)}, bf16[2,64,384]{2,1,0:T(8,128)(2,1)S(1)}, u32[]{:S(2)}, u32[]{:S(2)}) collective-permute-start(bf16[2,64,384]{2,1,0:T(8,128)(2,1)S(1)} %get-tuple-element.52), channel_id=1, source_target_pairs={{0,16},{4,20},{8,24},{12,28},{16,0},{20,4},{24,8},{28,12},{1,17},{... | collective-permute-start | bytes 294920 | tf_op jit(solution)/shard_map/ppermute | solution.py:17
  75.9 0.4 collective-permute-start.19
  76.3 0.5 collective-permute-start.21
  76.8 6.5 %collective-permute-done.18.refs_2_ = bf16[2,64,384]{2,1,0:T(8,128)(2,1)S(1)} collective-permute-done((bf16[2,64,384]{2,1,0:T(8,128)(2,1)S(1)}, bf16[2,64,384]{2,1,0:T(8,128)(2,1)S(1)}, u32[]{:S(2)}, u32[]{:S(2)}) %collective-permute-start.18) | collective-permute-done | bytes 98336 | tf_op jit(solution)/shard_map/ppermute | solution.py:17
  83.3 0.5 collective-permute-done.21.refs_5_
  83.8 2.5 %collective-permute-done.20.refs_4_ = bf16[4,64,1152]{2,1,0:T(8,128)(2,1)S(1)} collective-permute-done((bf16[4,64,1152]{2,1,0:T(8,128)(2,1)S(1)}, bf16[4,64,1152]{2,1,0:T(8,128)(2,1)S(1)}, u32[]{:S(2)}, u32[]{:S(2)}) %collective-permute-start.20) | collective-permute-done | bytes 589856 | tf_op jit(solution)/shard_map/ppermute | solution.py:17
  86.3 0.7 second.1
  87.0 3.0 %collective-permute-start.22 = (bf16[64,1152]{1,0:T(8,128)(2,1)S(1)}, bf16[64,1152]{1,0:T(8,128)(2,1)S(1)}, u32[]{:S(2)}, u32[]{:S(2)}) collective-permute-start(bf16[64,1152]{1,0:T(8,128)(2,1)S(1)} %get-tuple-element.57), channel_id=1, source_target_pairs={{0,16},{4,20},{8,24},{12,28},{16,0},{20,4},{24,8},{28,12},{1,17},{... | collective-permute-start | bytes 442376 | tf_op jit(solution)/shard_map/ppermute | solution.py:17
  90.0 0.7 collective-permute-start.23
  90.8 0.5 collective-permute-start.24
  91.3 1.5 %collective-permute-start.25 = (bf16[64,384]{1,0:T(8,128)(2,1)S(1)}, bf16[64,384]{1,0:T(8,128)(2,1)S(1)}, u32[]{:S(2)}, u32[]{:S(2)}) collective-permute-start(bf16[64,384]{1,0:T(8,128)(2,1)S(1)} %get-tuple-element.61), channel_id=1, source_target_pairs={{0,4},{4,0},{8,12},{12,8},{16,20},{20,16},{24,28},{28,24},{1,5},{5... | collective-permute-start | bytes 147464 | tf_op jit(solution)/shard_map/ppermute | solution.py:17
  92.8 2.6 %collective-permute-done.25.refs_5_ = bf16[64,384]{1,0:T(8,128)(2,1)S(1)} collective-permute-done((bf16[64,384]{1,0:T(8,128)(2,1)S(1)}, bf16[64,384]{1,0:T(8,128)(2,1)S(1)}, u32[]{:S(2)}, u32[]{:S(2)}) %collective-permute-start.25) | collective-permute-done | bytes 49184 | tf_op jit(solution)/shard_map/ppermute | solution.py:17
  95.4 5.0 %collective-permute-done.22.refs_1_ = bf16[64,1152]{1,0:T(8,128)(2,1)S(1)} collective-permute-done((bf16[64,1152]{1,0:T(8,128)(2,1)S(1)}, bf16[64,1152]{1,0:T(8,128)(2,1)S(1)}, u32[]{:S(2)}, u32[]{:S(2)}) %collective-permute-start.22) | collective-permute-done | bytes 147488 | tf_op jit(solution)/shard_map/ppermute | solution.py:17
  100.4 0.2 collective-permute-done.24.refs_3_
  100.6 1.3 %finish.1 = (f32[1,64,768]{2,1,0:T(8,128)}, f32[1,64,768]{2,1,0:T(8,128)}) custom-call(s32[5]{0:T(128)S(1)} %stack.20.sc, f32[64,1152]{1,0:T(8,128)S(1)} %get-tuple-element.56.refs_0_, bf16[64,1152]{1,0:T(8,128)(2,1)S(1)} %collective-permute-done.22.refs_1_, bf16[64,1152]{1,0:T(8,128)(2,1)S(1)} %collective-permute-done.23.refs_2_, ...), custom_call_target="tpu_custom_call" | custom-call | flops 910000000 | tf_op jit(solution)/shard_map/finish/pallas_call | solution.py:191
  (38 shorter events, 0.5 us)
Async XLA Ops:
  0.6 13.7 %collective-permute-start.3 = (bf16[768,3072]{1,0:T(8,128)(2,1)}, bf16[768,3072]{1,0:T(8,128)(2,1)}, u32[]{:S(2)}, u32[]{:S(2)}) collective-permute-start(bf16[768,3072]{1,0:T(8,128)(2,1)} %refs_1_.10), channel_id=1, source_target_pairs={{0,1},{1,0},{2,3},{3,2},{4,5},{5,4},{6,7},{7,6},{8,9},{9,8},{10,11... | collective-permute-start | bytes 14155784 | tf_op jit(solution)/shard_map/ppermute | solution.py:17
  1.8 1.3 %copy-start = (bf16[1,192,3072]{2,1,0:T(8,128)(2,1)S(1)}, bf16[1,192,3072]{2,1,0:T(8,128)(2,1)}, u32[]{:S(2)}) copy-start(bf16[1,192,3072]{2,1,0:T(8,128)(2,1)} %refs_0_.5) | copy-start | bytes 3538948
  3.1 5.7 %copy-start.4 = (bf16[1,64,768]{2,1,0:T(8,128)(2,1)S(1)}, bf16[1,64,768]{2,1,0:T(8,128)(2,1)}, u32[]{:S(2)}) copy-start(bf16[1,64,768]{2,1,0:T(8,128)(2,1)} %refs_0_.4) | copy-start | bytes 294916
  3.1 5.7 %copy-start.5 = (bf16[1,64,768]{2,1,0:T(8,128)(2,1)S(1)}, bf16[1,64,768]{2,1,0:T(8,128)(2,1)}, u32[]{:S(2)}) copy-start(bf16[1,64,768]{2,1,0:T(8,128)(2,1)} %refs_1_.7) | copy-start | bytes 294916
  6.1 16.6 %collective-permute-start.4 = (bf16[2,192,768]{2,1,0:T(8,128)(2,1)S(1)}, bf16[2,192,768]{2,1,0:T(8,128)(2,1)S(1)}, u32[]{:S(2)}, u32[]{:S(2)}) collective-permute-start(bf16[2,192,768]{2,1,0:T(8,128)(2,1)S(1)} %attend.2.refs_2_), channel_id=1, source_target_pairs={{0,2},{1,3},{2,0},{3,1},{4,6},{5,7},{6,4},{7,5},{8,10},{9,11},{10,... | collective-permute-start | bytes 1769480 | tf_op jit(solution)/shard_map/ppermute | solution.py:17
  8.7 5.6 %copy-start.1 = (bf16[1,192,3072]{2,1,0:T(8,128)(2,1)S(1)}, bf16[1,192,3072]{2,1,0:T(8,128)(2,1)}, u32[]{:S(2)}) copy-start(bf16[1,192,3072]{2,1,0:T(8,128)(2,1)} %refs_0_.5) | copy-start | bytes 3538948
  9.3 17.8 %collective-permute-start = (bf16[128,768]{1,0:T(8,128)(2,1)S(1)}, bf16[128,768]{1,0:T(8,128)(2,1)S(1)}, u32[]{:S(2)}, u32[]{:S(2)}) collective-permute-start(bf16[128,768]{1,0:T(8,128)(2,1)S(1)} %join.1.refs_3_), channel_id=1, source_target_pairs={{0,16},{4,20},{8,24},{12,28},{16,0},{20,4},{24,8},{28,12},{1,17},{... | collective-permute-start | bytes 589832 | tf_op jit(solution)/shard_map/ppermute | solution.py:17
  12.0 15.2 %collective-permute-start.1 = (bf16[128,768]{1,0:T(8,128)(2,1)S(1)}, bf16[128,768]{1,0:T(8,128)(2,1)S(1)}, u32[]{:S(2)}, u32[]{:S(2)}) collective-permute-start(bf16[128,768]{1,0:T(8,128)(2,1)S(1)} %join.1.refs_3_), channel_id=1, source_target_pairs={{0,24},{4,28},{8,16},{12,20},{16,8},{20,12},{24,0},{28,4},{1,25},{... | collective-permute-start | bytes 589832 | tf_op jit(solution)/shard_map/ppermute | solution.py:17
  13.3 13.8 %collective-permute-start.2 = (bf16[128,768]{1,0:T(8,128)(2,1)S(1)}, bf16[128,768]{1,0:T(8,128)(2,1)S(1)}, u32[]{:S(2)}, u32[]{:S(2)}) collective-permute-start(bf16[128,768]{1,0:T(8,128)(2,1)S(1)} %join.1.refs_3_), channel_id=1, source_target_pairs={{0,8},{4,12},{8,0},{12,4},{16,24},{20,28},{24,16},{28,20},{1,9},{5... | collective-permute-start | bytes 589832 | tf_op jit(solution)/shard_map/ppermute | solution.py:17
  13.5 9.1 %slice-start = ((s8[4718592]{0:T(1024)(128)(4,1)}), s8[4194304]{0:T(1024)(128)(4,1)S(1)}, s32[]{:S(2)}) async-start(s8[4718592]{0:T(1024)(128)(4,1)} %bitcast.9), calls=%async_computation | async-start | bytes 8388608
  14.3 3.5 %copy-start.6 = (s32[8]{0:T(128)S(1)}, s32[8]{0:T(128)}, u32[]{:S(2)}) copy-start(s32[8]{0:T(128)} %refs_2_.5) | copy-start | bytes 100
  14.4 8.3 %slice-start.1 = ((s8[4718592]{0:T(1024)(128)(4,1)}), s8[524288]{0:T(1024)(128)(4,1)S(1)}, s32[]{:S(2)}) async-start(s8[4718592]{0:T(1024)(128)(4,1)} %bitcast.9), calls=%async_computation.1 | async-start | bytes 1048576
  21.3 5.9 %collective-permute-start.5 = (f32[8,128]{1,0:T(8,128)S(1)}, f32[8,128]{1,0:T(8,128)S(1)}, u32[]{:S(2)}, u32[]{:S(2)}) collective-permute-start(f32[8,128]{1,0:T(8,128)S(1)} %get-tuple-element.34.refs_6_), channel_id=1, source_target_pairs={{0,2},{1,3},{2,0},{3,1},{4,6},{5,7},{6,4},{7,5},{8,10},{9,11},{10,... | collective-permute-start | bytes 12296 | tf_op jit(solution)/shard_map/ppermute | solution.py:17
  25.3 33.1 %collective-permute-start.11 = (bf16[4,192,768]{2,1,0:T(8,128)(2,1)S(1)}, bf16[4,192,768]{2,1,0:T(8,128)(2,1)S(1)}, u32[]{:S(2)}, u32[]{:S(2)}) collective-permute-start(bf16[4,192,768]{2,1,0:T(8,128)(2,1)S(1)} %project.1.refs_8_), channel_id=1, source_target_pairs={{0,2},{1,3},{2,0},{3,1},{4,6},{5,7},{6,4},{7,5},{8,10},{9,11},{10,... | collective-permute-start | bytes 3538952 | tf_op jit(solution)/shard_map/ppermute | solution.py:17
  27.2 3.6 %copy-start.3 = (bf16[1,192,3072]{2,1,0:T(8,128)(2,1)S(1)}, bf16[1,192,3072]{2,1,0:T(8,128)(2,1)}, u32[]{:S(2)}) copy-start(bf16[1,192,3072]{2,1,0:T(8,128)(2,1)} %refs_4_.1) | copy-start | bytes 3538948
  27.8 3.0 %copy-start.2 = (bf16[1,192,3072]{2,1,0:T(8,128)(2,1)S(1)}, bf16[1,192,3072]{2,1,0:T(8,128)(2,1)}, u32[]{:S(2)}) copy-start(bf16[1,192,3072]{2,1,0:T(8,128)(2,1)} %refs_3_.1) | copy-start | bytes 3538948
  27.8 18.9 %collective-permute-start.10 = (bf16[4,128,768]{2,1,0:T(8,128)(2,1)S(1)}, bf16[4,128,768]{2,1,0:T(8,128)(2,1)S(1)}, u32[]{:S(2)}, u32[]{:S(2)}) collective-permute-start(bf16[4,128,768]{2,1,0:T(8,128)(2,1)S(1)} %get-tuple-element.38.refs_5_.refs_8_), channel_id=1, source_target_pairs={{0,4},{4,0},{8,12},{12,8},{16,20},{20,16},{24,28},{28,24},{1,5},{5... | collective-permute-start | bytes 2359304 | tf_op jit(solution)/shard_map/ppermute | solution.py:17
  29.4 1.2 %collective-permute-start.6 = (f32[8,128]{1,0:T(8,128)S(1)}, f32[8,128]{1,0:T(8,128)S(1)}, u32[]{:S(2)}, u32[]{:S(2)}) collective-permute-start(f32[8,128]{1,0:T(8,128)S(1)} %get-tuple-element.36.refs_0_), channel_id=1, source_target_pairs={{0,1},{1,0},{2,3},{3,2},{4,5},{5,4},{6,7},{7,6},{8,9},{9,8},{10,11... | collective-permute-start | bytes 12296 | tf_op jit(solution)/shard_map/ppermute | solution.py:17
  29.5 4.8 %collective-permute-start.8 = (bf16[192,768]{1,0:T(8,128)(2,1)S(1)}, bf16[192,768]{1,0:T(8,128)(2,1)S(1)}, u32[]{:S(2)}, u32[]{:S(2)}) collective-permute-start(bf16[192,768]{1,0:T(8,128)(2,1)S(1)} %get-tuple-element.39), channel_id=1, source_target_pairs={{0,1},{1,0},{2,3},{3,2},{4,5},{5,4},{6,7},{7,6},{8,9},{9,8},{10,11... | collective-permute-start | bytes 884744 | tf_op jit(solution)/shard_map/ppermute | solution.py:17
  30.1 4.2 %collective-permute-start.9 = (bf16[192,768]{1,0:T(8,128)(2,1)S(1)}, bf16[192,768]{1,0:T(8,128)(2,1)S(1)}, u32[]{:S(2)}, u32[]{:S(2)}) collective-permute-start(bf16[192,768]{1,0:T(8,128)(2,1)S(1)} %get-tuple-element.40), channel_id=1, source_target_pairs={{0,1},{1,0},{2,3},{3,2},{4,5},{5,4},{6,7},{7,6},{8,9},{9,8},{10,11... | collective-permute-start | bytes 884744 | tf_op jit(solution)/shard_map/ppermute | solution.py:17
  30.6 3.7 %collective-permute-start.7 = (f32[8,128]{1,0:T(8,128)S(1)}, f32[8,128]{1,0:T(8,128)S(1)}, u32[]{:S(2)}, u32[]{:S(2)}) collective-permute-start(f32[8,128]{1,0:T(8,128)S(1)} %get-tuple-element.37.refs_2_), channel_id=1, source_target_pairs={{0,1},{1,0},{2,3},{3,2},{4,5},{5,4},{6,7},{7,6},{8,9},{9,8},{10,11... | collective-permute-start | bytes 12296 | tf_op jit(solution)/shard_map/ppermute | solution.py:17
  48.5 7.6 %collective-permute-start.12 = (bf16[80,768]{1,0:T(8,128)(2,1)S(1)}, bf16[80,768]{1,0:T(8,128)(2,1)S(1)}, u32[]{:S(2)}, u32[]{:S(2)}) collective-permute-start(bf16[80,768]{1,0:T(8,128)(2,1)S(1)} %get-tuple-element.42), channel_id=1, source_target_pairs={{0,3},{1,2},{2,1},{3,0},{4,7},{5,6},{6,5},{7,4},{8,11},{9,10},{10,... | collective-permute-start | bytes 368648 | tf_op jit(solution)/shard_map/ppermute | solution.py:17
  48.6 9.8 %collective-permute-start.13 = (bf16[80,768]{1,0:T(8,128)(2,1)S(1)}, bf16[80,768]{1,0:T(8,128)(2,1)S(1)}, u32[]{:S(2)}, u32[]{:S(2)}) collective-permute-start(bf16[80,768]{1,0:T(8,128)(2,1)S(1)} %get-tuple-element.43), channel_id=1, source_target_pairs={{0,2},{1,3},{2,0},{3,1},{4,6},{5,7},{6,4},{7,5},{8,10},{9,11},{10,... | collective-permute-start | bytes 368648 | tf_op jit(solution)/shard_map/ppermute | solution.py:17
  49.1 9.3 %collective-permute-start.14 = (bf16[80,768]{1,0:T(8,128)(2,1)S(1)}, bf16[80,768]{1,0:T(8,128)(2,1)S(1)}, u32[]{:S(2)}, u32[]{:S(2)}) collective-permute-start(bf16[80,768]{1,0:T(8,128)(2,1)S(1)} %get-tuple-element.44), channel_id=1, source_target_pairs={{0,1},{1,0},{2,3},{3,2},{4,5},{5,4},{6,7},{7,6},{8,9},{9,8},{10,11... | collective-permute-start | bytes 368648 | tf_op jit(solution)/shard_map/ppermute | solution.py:17
  61.0 5.6 %collective-permute-start.15 = (bf16[80,768]{1,0:T(8,128)(2,1)S(1)}, bf16[80,768]{1,0:T(8,128)(2,1)S(1)}, u32[]{:S(2)}, u32[]{:S(2)}) collective-permute-start(bf16[80,768]{1,0:T(8,128)(2,1)S(1)} %get-tuple-element.46), channel_id=1, source_target_pairs={{0,3},{1,2},{2,1},{3,0},{4,7},{5,6},{6,5},{7,4},{8,11},{9,10},{10,... | collective-permute-start | bytes 368648 | tf_op jit(solution)/shard_map/ppermute | solution.py:17
  61.1 8.2 %collective-permute-start.16 = (bf16[80,768]{1,0:T(8,128)(2,1)S(1)}, bf16[80,768]{1,0:T(8,128)(2,1)S(1)}, u32[]{:S(2)}, u32[]{:S(2)}) collective-permute-start(bf16[80,768]{1,0:T(8,128)(2,1)S(1)} %get-tuple-element.47), channel_id=1, source_target_pairs={{0,2},{1,3},{2,0},{3,1},{4,6},{5,7},{6,4},{7,5},{8,10},{9,11},{10,... | collective-permute-start | bytes 368648 | tf_op jit(solution)/shard_map/ppermute | solution.py:17
  62.8 6.6 %collective-permute-start.17 = (bf16[80,768]{1,0:T(8,128)(2,1)S(1)}, bf16[80,768]{1,0:T(8,128)(2,1)S(1)}, u32[]{:S(2)}, u32[]{:S(2)}) collective-permute-start(bf16[80,768]{1,0:T(8,128)(2,1)S(1)} %get-tuple-element.48), channel_id=1, source_target_pairs={{0,1},{1,0},{2,3},{3,2},{4,5},{5,4},{6,7},{7,6},{8,9},{9,8},{10,11... | collective-permute-start | bytes 368648 | tf_op jit(solution)/shard_map/ppermute | solution.py:17
  71.0 15.3 %collective-permute-start.20 = (bf16[4,64,1152]{2,1,0:T(8,128)(2,1)S(1)}, bf16[4,64,1152]{2,1,0:T(8,128)(2,1)S(1)}, u32[]{:S(2)}, u32[]{:S(2)}) collective-permute-start(bf16[4,64,1152]{2,1,0:T(8,128)(2,1)S(1)} %get-tuple-element.54), channel_id=1, source_target_pairs={{0,4},{4,0},{8,12},{12,8},{16,20},{20,16},{24,28},{28,24},{1,5},{5... | collective-permute-start | bytes 1769480 | tf_op jit(solution)/shard_map/ppermute | solution.py:17
  72.6 10.7 %collective-permute-start.18 = (bf16[2,64,384]{2,1,0:T(8,128)(2,1)S(1)}, bf16[2,64,384]{2,1,0:T(8,128)(2,1)S(1)}, u32[]{:S(2)}, u32[]{:S(2)}) collective-permute-start(bf16[2,64,384]{2,1,0:T(8,128)(2,1)S(1)} %get-tuple-element.52), channel_id=1, source_target_pairs={{0,16},{4,20},{8,24},{12,28},{16,0},{20,4},{24,8},{28,12},{1,17},{... | collective-permute-start | bytes 294920 | tf_op jit(solution)/shard_map/ppermute | solution.py:17
  75.9 7.4 %collective-permute-start.19 = (bf16[2,64,384]{2,1,0:T(8,128)(2,1)S(1)}, bf16[2,64,384]{2,1,0:T(8,128)(2,1)S(1)}, u32[]{:S(2)}, u32[]{:S(2)}) collective-permute-start(bf16[2,64,384]{2,1,0:T(8,128)(2,1)S(1)} %get-tuple-element.53), channel_id=1, source_target_pairs={{0,24},{4,28},{8,16},{12,20},{16,8},{20,12},{24,0},{28,4},{1,25},{... | collective-permute-start | bytes 294920 | tf_op jit(solution)/shard_map/ppermute | solution.py:17
  76.3 7.5 %collective-permute-start.21 = (bf16[2,64,384]{2,1,0:T(8,128)(2,1)S(1)}, bf16[2,64,384]{2,1,0:T(8,128)(2,1)S(1)}, u32[]{:S(2)}, u32[]{:S(2)}) collective-permute-start(bf16[2,64,384]{2,1,0:T(8,128)(2,1)S(1)} %get-tuple-element.55), channel_id=1, source_target_pairs={{0,8},{4,12},{8,0},{12,4},{16,24},{20,28},{24,16},{28,20},{1,9},{5... | collective-permute-start | bytes 294920 | tf_op jit(solution)/shard_map/ppermute | solution.py:17
  87.0 13.4 %collective-permute-start.22 = (bf16[64,1152]{1,0:T(8,128)(2,1)S(1)}, bf16[64,1152]{1,0:T(8,128)(2,1)S(1)}, u32[]{:S(2)}, u32[]{:S(2)}) collective-permute-start(bf16[64,1152]{1,0:T(8,128)(2,1)S(1)} %get-tuple-element.57), channel_id=1, source_target_pairs={{0,16},{4,20},{8,24},{12,28},{16,0},{20,4},{24,8},{28,12},{1,17},{... | collective-permute-start | bytes 442376 | tf_op jit(solution)/shard_map/ppermute | solution.py:17
  90.0 10.3 %collective-permute-start.23 = (bf16[64,1152]{1,0:T(8,128)(2,1)S(1)}, bf16[64,1152]{1,0:T(8,128)(2,1)S(1)}, u32[]{:S(2)}, u32[]{:S(2)}) collective-permute-start(bf16[64,1152]{1,0:T(8,128)(2,1)S(1)} %get-tuple-element.58), channel_id=1, source_target_pairs={{0,24},{4,28},{8,16},{12,20},{16,8},{20,12},{24,0},{28,4},{1,25},{... | collective-permute-start | bytes 442376 | tf_op jit(solution)/shard_map/ppermute | solution.py:17
  90.8 9.8 %collective-permute-start.24 = (bf16[64,1152]{1,0:T(8,128)(2,1)S(1)}, bf16[64,1152]{1,0:T(8,128)(2,1)S(1)}, u32[]{:S(2)}, u32[]{:S(2)}) collective-permute-start(bf16[64,1152]{1,0:T(8,128)(2,1)S(1)} %get-tuple-element.59), channel_id=1, source_target_pairs={{0,8},{4,12},{8,0},{12,4},{16,24},{20,28},{24,16},{28,20},{1,9},{5... | collective-permute-start | bytes 442376 | tf_op jit(solution)/shard_map/ppermute | solution.py:17
  91.3 4.1 %collective-permute-start.25 = (bf16[64,384]{1,0:T(8,128)(2,1)S(1)}, bf16[64,384]{1,0:T(8,128)(2,1)S(1)}, u32[]{:S(2)}, u32[]{:S(2)}) collective-permute-start(bf16[64,384]{1,0:T(8,128)(2,1)S(1)} %get-tuple-element.61), channel_id=1, source_target_pairs={{0,4},{4,0},{8,12},{12,8},{16,20},{20,16},{24,28},{28,24},{1,5},{5... | collective-permute-start | bytes 147464 | tf_op jit(solution)/shard_map/ppermute | solution.py:17

commit v9 on v8

--- a/solution.py
+++ b/solution.py
@@ -171,6 +171,7 @@
 VMEM = 20 * 1024 * 1024
 COST = 7e8
 ALONE = 52 * 1024 * 1024
+FIRST = 62 * 1024 * 1024
 SHARD, CORE, CHIP, COUNT, GROUP = range(5)
 
 
@@ -235,7 +236,7 @@
     return jax.ShapeDtypeStruct(shape, dtype)
 
 
-def attend_chip(counts, queries, keys, values, chip_offset, depth, after=()):
+def attend_chip(counts, queries, keys, values, chip_offset, depth, after=(), limit=ALONE):
     slots, width = queries.shape[1:]
     size = width // HEADS
     heads = depth // size
@@ -276,7 +277,7 @@
         out_specs=vmem,
         after=after,
         scratch=[pltpu.VMEM((2, 3, slots, depth), BF16), pltpu.SemaphoreType.DMA((2, 3))],
-        vmem=ALONE,
+        vmem=limit,
     )
 
 
@@ -554,7 +555,7 @@
 
         weight_near = xor_send(output_weight, "fsdp", fsdp_size, 1)
 
-        attended = [attend_chip(valid_token_count, queries, keys, values, c, depth) for c in range(1, chips)]
+        attended = [attend_chip(valid_token_count, queries, keys, values, c, depth, limit=FIRST) for c in range(1, chips)]
         theirs = [xor_send(x, "fsdp", fsdp_size, 2 * (c + 1)) for c, x in enumerate(attended)]
         block = join_adapters(scalars, down_adapter, up_adapter, attended[:1])
         outer_blocks = {

time: 103 us -> 103 us (level)
  transfers between devices with their start and end apart: 26 -> 26, of which waited for: 13 -> 14; matrix products, arithmetic and copies ran while one was open for 0% -> 0% of each run, Pallas kernels for 19% -> 19%
where the time goes in v9:
time: 103 us
  waiting for transfers between devices  45 us (44%)
  starting transfers between devices  27.9 us (27%)
  Pallas kernels  26.1 us (25%)
  between operations  2.32 us (2%)
  local copies, waits for them, and re-layouts  1.23 us (1%)
    ppermute x26, waiting for transfers between devices, xor_send(): return lax.ppermute(value, axis, [(i, i ^ offset) for i in range(size)])  45 us
    ppermute x26, starting transfers between devices, xor_send(): return lax.ppermute(value, axis, [(i, i ^ offset) for i in range(size)])  27.9 us
    pallas_call x12, Pallas kernels, kernel_call(): pl.pallas_call(body, out_shape=out_shape, grid_spec=pltpu.PrefetchScalarG...  26.1 us
  transfers between devices with their start and end apart: 26, of which 14 were waited for; matrix products, arithmetic and copies ran while one was open for 0% of the time, Pallas kernels for 19%

profile of v9, /device:TPU:0, one launch (start us, length us, event | category | flops | bytes accessed | tf_op | source)
XLA Modules:
  0.0 102.6 jit_solution(444421716085256252)
XLA Ops:
  0.6 0.5 collective-permute-start.3
  1.8 4.0 %attend.2.refs_2_ = bf16[2,192,768]{2,1,0:T(8,128)(2,1)} custom-call(s32[1]{0:T(128)S(6)} %copy.15.sc, bf16[1,192,3072]{2,1,0:T(8,128)(2,1)} %refs_0_.5, bf16[1,192,3072]{2,1,0:T(8,128)(2,1)} %refs_1_.8, bf16[1,192,3072]{2,1,0:T(8,128)(2,1)} %refs_2_.4), custom_call_target="tpu_custom_call" | custom-call | flops 2800000000 | tf_op jit(solution)/shard_map/attend/pallas_call | solution.py:192
  5.8 2.6 %collective-permute-start.4 = (bf16[2,192,768]{2,1,0:T(8,128)(2,1)}, bf16[2,192,768]{2,1,0:T(8,128)(2,1)S(1)}, u32[]{:S(2)}, u32[]{:S(2)}) collective-permute-start(bf16[2,192,768]{2,1,0:T(8,128)(2,1)} %attend.2.refs_2_), channel_id=1, source_target_pairs={{0,2},{1,3},{2,0},{3,1},{4,6},{5,7},{6,4},{7,5},{8,10},{9,11},{10,... | collective-permute-start | bytes 1769480 | tf_op jit(solution)/shard_map/ppermute | solution.py:17
  8.5 1.1 %copy-done.3 = bf16[2,192,768]{2,1,0:T(8,128)(2,1)S(1)} copy-done((bf16[2,192,768]{2,1,0:T(8,128)(2,1)S(1)}, bf16[2,192,768]{2,1,0:T(8,128)(2,1)}, u32[]{:S(2)}) %copy-start.3) | copy-done | bytes 589848
  9.5 0.6 join.1.refs_3_
  10.1 2.7 %collective-permute-start = (bf16[128,768]{1,0:T(8,128)(2,1)S(1)}, bf16[128,768]{1,0:T(8,128)(2,1)S(1)}, u32[]{:S(2)}, u32[]{:S(2)}) collective-permute-start(bf16[128,768]{1,0:T(8,128)(2,1)S(1)} %join.1.refs_3_), channel_id=1, source_target_pairs={{0,16},{4,20},{8,24},{12,28},{16,0},{20,4},{24,8},{28,12},{1,17},{... | collective-permute-start | bytes 589832 | tf_op jit(solution)/shard_map/ppermute | solution.py:17
  12.8 1.4 %collective-permute-start.1 = (bf16[128,768]{1,0:T(8,128)(2,1)S(1)}, bf16[128,768]{1,0:T(8,128)(2,1)S(1)}, u32[]{:S(2)}, u32[]{:S(2)}) collective-permute-start(bf16[128,768]{1,0:T(8,128)(2,1)S(1)} %join.1.refs_3_), channel_id=1, source_target_pairs={{0,24},{4,28},{8,16},{12,20},{16,8},{20,12},{24,0},{28,4},{1,25},{... | collective-permute-start | bytes 589832 | tf_op jit(solution)/shard_map/ppermute | solution.py:17
  14.1 0.2 collective-permute-start.2
  15.2 3.4 %attend.3.refs_3_.refs_4_.refs_0_ = bf16[2,192,768]{2,1,0:T(8,128)(2,1)S(1)} custom-call(s32[1]{0:T(128)S(6)} %copy.15.sc, bf16[1,192,3072]{2,1,0:T(8,128)(2,1)S(1)} %copy-done, bf16[1,192,3072]{2,1,0:T(8,128)(2,1)} %refs_1_.8, bf16[1,192,3072]{2,1,0:T(8,128)(2,1)} %refs_2_.4, bf16[128,768]{1,0:T(8,128)(2,1)S(1)} %join.1.refs_3_, ...), custom_call_target="tpu_custom_call" | custom-call | flops 2800000000 | tf_op jit(solution)/shard_map/attend/pallas_call | solution.py:192
  18.6 3.5 %bring_weight.1 = (bf16[768,3072]{1,0:T(8,128)(2,1)S(1)}, f32[8,128]{1,0:T(8,128)S(1)}) custom-call(s32[5]{0:T(128)S(1)} %stack.20.sc, bf16[768,3072]{1,0:T(8,128)(2,1)} %collective-permute-done.3.refs_4_.refs_0_, s32[1]{0:T(128)S(6)} %copy.14.refs_1_, s32[8]{0:T(128)S(1)} %copy-done.6, bf16[2,192,768]{2,1,0:T(8,128)(2,1)S(1)} %attend.3.refs_3_.refs_4_.refs_0_), custom_call_target="tpu_custom_call" | custom-call | flops 2100000000 | tf_op jit(solution)/shard_map/bring_weight/pallas_call | solution.py:192
  22.1 0.6 collective-permute-start.5
  22.7 2.6 %project.1.refs_8_ = bf16[4,192,768]{2,1,0:T(8,128)(2,1)S(1)} custom-call(s32[5]{0:T(128)S(1)} %stack.20.sc, bf16[2,192,768]{2,1,0:T(8,128)(2,1)S(1)} %collective-permute-done.4.refs_0_.refs_5_, bf16[768,3072]{1,0:T(8,128)(2,1)S(1)} %bitcast.10, bf16[768,3072]{1,0:T(8,128)(2,1)S(1)} %get-tuple-element.35.refs_2_, ...), custom_call_target="tpu_custom_call" | custom-call | flops 2100000000 | tf_op jit(solution)/shard_map/project/pallas_call | solution.py:192
  25.3 1.8 %collective-permute-start.11 = (bf16[4,192,768]{2,1,0:T(8,128)(2,1)S(1)}, bf16[4,192,768]{2,1,0:T(8,128)(2,1)S(1)}, u32[]{:S(2)}, u32[]{:S(2)}) collective-permute-start(bf16[4,192,768]{2,1,0:T(8,128)(2,1)S(1)} %project.1.refs_8_), channel_id=1, source_target_pairs={{0,2},{1,3},{2,0},{3,1},{4,6},{5,7},{6,4},{7,5},{8,10},{9,11},{10,... | collective-permute-start | bytes 3538952 | tf_op jit(solution)/shard_map/ppermute | solution.py:17
  27.1 0.2 collective-permute-done.refs_0_
  27.3 0.6 collective-permute-done.2.refs_2_
  27.9 0.6 stack.21
  28.6 1.5 %collective-permute-start.10 = (bf16[4,128,768]{2,1,0:T(8,128)(2,1)S(1)}, bf16[4,128,768]{2,1,0:T(8,128)(2,1)S(1)}, u32[]{:S(2)}, u32[]{:S(2)}) collective-permute-start(bf16[4,128,768]{2,1,0:T(8,128)(2,1)S(1)} %get-tuple-element.38.refs_5_.refs_8_), channel_id=1, source_target_pairs={{0,4},{4,0},{8,12},{12,8},{16,20},{20,16},{24,28},{28,24},{1,5},{5... | collective-permute-start | bytes 2359304 | tf_op jit(solution)/shard_map/ppermute | solution.py:17
  30.2 0.6 collective-permute-start.8
  30.9 0.5 collective-permute-done.6.refs_1_
  31.4 0.2 collective-permute-start.7
  31.5 3.5 %base.1.refs_10_.refs_0_ = f32[4,192,768]{2,1,0:T(8,128)S(1)} custom-call(s32[5]{0:T(128)S(1)} %stack.20.sc, bf16[2,192,768]{2,1,0:T(8,128)(2,1)S(1)} %attend.3.refs_3_.refs_4_.refs_0_, bf16[768,3072]{1,0:T(8,128)(2,1)S(1)} %bitcast.10, bf16[768,3072]{1,0:T(8,128)(2,1)S(1)} %get-tuple-element.35.refs_2_, bf16[1,192,3072]{2,1,0:T(8,128)(2,1)S(1)} %copy-done.1, ...), custom_call_target="tpu_custom_call" | custom-call | flops 4899999744 | tf_op jit(solution)/shard_map/base/pallas_call | solution.py:192
  35.1 11.7 %collective-permute-done.10.refs_9_ = bf16[4,128,768]{2,1,0:T(8,128)(2,1)S(1)} collective-permute-done((bf16[4,128,768]{2,1,0:T(8,128)(2,1)S(1)}, bf16[4,128,768]{2,1,0:T(8,128)(2,1)S(1)}, u32[]{:S(2)}, u32[]{:S(2)}) %collective-permute-start.10) | collective-permute-done | bytes 786464 | tf_op jit(solution)/shard_map/ppermute | solution.py:17
  46.7 1.8 %choose.1 = (bf16[80,768]{1,0:T(8,128)(2,1)S(1)}, bf16[80,768]{1,0:T(8,128)(2,1)S(1)}, bf16[80,768]{1,0:T(8,128)(2,1)S(1)}, bf16[80,768]{1,0:T(8,128)(2,1)S(1)}, f32[64,192]{1,0:T(8,128)S(1)}) custom-call(s32[5]{0:T(128)S(1)} %stack.20.sc, f32[8,128]{1,0:T(8,128)S(1)} %get-tuple-element.36.refs_0_, f32[8,128]{1,0:T(8,128)S(1)} %collective-permute-done.6.refs_1_, ...), custom_call_target="tpu_custom_call" | custom-call | flops 1400000000 | tf_op jit(solution)/shard_map/choose/pallas_call | solution.py:192
  48.6 0.6 collective-permute-start.13
  49.1 1.3 %collective-permute-start.14 = (bf16[80,768]{1,0:T(8,128)(2,1)S(1)}, bf16[80,768]{1,0:T(8,128)(2,1)S(1)}, u32[]{:S(2)}, u32[]{:S(2)}) collective-permute-start(bf16[80,768]{1,0:T(8,128)(2,1)S(1)} %get-tuple-element.44), channel_id=1, source_target_pairs={{0,1},{1,0},{2,3},{3,2},{4,5},{5,4},{6,7},{7,6},{8,9},{9,8},{10,11... | collective-permute-start | bytes 368648 | tf_op jit(solution)/shard_map/ppermute | solution.py:17
  50.4 5.7 %collective-permute-done.12.refs_3_ = bf16[80,768]{1,0:T(8,128)(2,1)S(1)} collective-permute-done((bf16[80,768]{1,0:T(8,128)(2,1)S(1)}, bf16[80,768]{1,0:T(8,128)(2,1)S(1)}, u32[]{:S(2)}, u32[]{:S(2)}) %collective-permute-start.12) | collective-permute-done | bytes 122912 | tf_op jit(solution)/shard_map/ppermute | solution.py:17
  56.1 2.3 %collective-permute-done.13.refs_4_ = bf16[80,768]{1,0:T(8,128)(2,1)S(1)} collective-permute-done((bf16[80,768]{1,0:T(8,128)(2,1)S(1)}, bf16[80,768]{1,0:T(8,128)(2,1)S(1)}, u32[]{:S(2)}, u32[]{:S(2)}) %collective-permute-start.13) | collective-permute-done | bytes 122912 | tf_op jit(solution)/shard_map/ppermute | solution.py:17
  58.4 2.6 %error.1 = (bf16[80,768]{1,0:T(8,128)(2,1)S(1)}, bf16[80,768]{1,0:T(8,128)(2,1)S(1)}, bf16[80,768]{1,0:T(8,128)(2,1)S(1)}, bf16[80,768]{1,0:T(8,128)(2,1)S(1)}, f32[1,1]{1,0:T(1,128)}) custom-call(s32[5]{0:T(128)S(1)} %stack.20.sc, f32[4,192,768]{2,1,0:T(8,128)S(1)} %base.1.refs_10_.refs_0_, f32[64,192]{1,0:T(8,128)S(1)} %get-tuple-element.41.refs_1_, ...), custom_call_target="tpu_custom_call" | custom-call | flops 2100000000 | tf_op jit(solution)/shard_map/error/pallas_call | solution.py:192
  61.1 1.6 %collective-permute-start.16 = (bf16[80,768]{1,0:T(8,128)(2,1)S(1)}, bf16[80,768]{1,0:T(8,128)(2,1)S(1)}, u32[]{:S(2)}, u32[]{:S(2)}) collective-permute-start(bf16[80,768]{1,0:T(8,128)(2,1)S(1)} %get-tuple-element.47), channel_id=1, source_target_pairs={{0,2},{1,3},{2,0},{3,1},{4,6},{5,7},{6,4},{7,5},{8,10},{9,11},{10,... | collective-permute-start | bytes 368648 | tf_op jit(solution)/shard_map/ppermute | solution.py:17
  62.7 0.3 collective-permute-start.17
  62.9 3.7 %collective-permute-done.15.refs_4_ = bf16[80,768]{1,0:T(8,128)(2,1)S(1)} collective-permute-done((bf16[80,768]{1,0:T(8,128)(2,1)S(1)}, bf16[80,768]{1,0:T(8,128)(2,1)S(1)}, u32[]{:S(2)}, u32[]{:S(2)}) %collective-permute-start.15) | collective-permute-done | bytes 122912 | tf_op jit(solution)/shard_map/ppermute | solution.py:17
  66.6 2.7 %collective-permute-done.16.refs_5_ = bf16[80,768]{1,0:T(8,128)(2,1)S(1)} collective-permute-done((bf16[80,768]{1,0:T(8,128)(2,1)S(1)}, bf16[80,768]{1,0:T(8,128)(2,1)S(1)}, u32[]{:S(2)}, u32[]{:S(2)}) %collective-permute-start.16) | collective-permute-done | bytes 122912 | tf_op jit(solution)/shard_map/ppermute | solution.py:17
  69.3 1.7 %first.1 = (f32[4,64,1152]{2,1,0:T(8,128)S(1)}, f32[2,64,384]{2,1,0:T(8,128)S(1)}, bf16[2,64,384]{2,1,0:T(8,128)(2,1)S(1)}, bf16[2,64,384]{2,1,0:T(8,128)(2,1)S(...) custom-call(s32[5]{0:T(128)S(1)} %stack.20.sc, f32[8,128]{1,0:T(8,128)S(1)} %get-tuple-element.36.refs_0_, ...), custom_call_target="tpu_custom_call" | custom-call | flops 1400000000 | tf_op jit(solution)/shard_map/first/pallas_call | solution.py:192
  71.0 1.6 %collective-permute-start.20 = (bf16[4,64,1152]{2,1,0:T(8,128)(2,1)S(1)}, bf16[4,64,1152]{2,1,0:T(8,128)(2,1)S(1)}, u32[]{:S(2)}, u32[]{:S(2)}) collective-permute-start(bf16[4,64,1152]{2,1,0:T(8,128)(2,1)S(1)} %get-tuple-element.54), channel_id=1, source_target_pairs={{0,4},{4,0},{8,12},{12,8},{16,20},{20,16},{24,28},{28,24},{1,5},{5... | collective-permute-start | bytes 1769480 | tf_op jit(solution)/shard_map/ppermute | solution.py:17
  72.6 4.0 %collective-permute-start.18 = (bf16[2,64,384]{2,1,0:T(8,128)(2,1)S(1)}, bf16[2,64,384]{2,1,0:T(8,128)(2,1)S(1)}, u32[]{:S(2)}, u32[]{:S(2)}) collective-permute-start(bf16[2,64,384]{2,1,0:T(8,128)(2,1)S(1)} %get-tuple-element.52), channel_id=1, source_target_pairs={{0,16},{4,20},{8,24},{12,28},{16,0},{20,4},{24,8},{28,12},{1,17},{... | collective-permute-start | bytes 294920 | tf_op jit(solution)/shard_map/ppermute | solution.py:17
  76.6 0.5 collective-permute-start.19
  77.2 6.3 %collective-permute-done.18.refs_2_ = bf16[2,64,384]{2,1,0:T(8,128)(2,1)S(1)} collective-permute-done((bf16[2,64,384]{2,1,0:T(8,128)(2,1)S(1)}, bf16[2,64,384]{2,1,0:T(8,128)(2,1)S(1)}, u32[]{:S(2)}, u32[]{:S(2)}) %collective-permute-start.18) | collective-permute-done | bytes 98336 | tf_op jit(solution)/shard_map/ppermute | solution.py:17
  83.5 0.6 collective-permute-done.21.refs_5_
  84.1 2.2 %collective-permute-done.20.refs_4_ = bf16[4,64,1152]{2,1,0:T(8,128)(2,1)S(1)} collective-permute-done((bf16[4,64,1152]{2,1,0:T(8,128)(2,1)S(1)}, bf16[4,64,1152]{2,1,0:T(8,128)(2,1)S(1)}, u32[]{:S(2)}, u32[]{:S(2)}) %collective-permute-start.20) | collective-permute-done | bytes 589856 | tf_op jit(solution)/shard_map/ppermute | solution.py:17
  86.3 0.7 second.1
  87.0 3.8 %collective-permute-start.22 = (bf16[64,1152]{1,0:T(8,128)(2,1)S(1)}, bf16[64,1152]{1,0:T(8,128)(2,1)S(1)}, u32[]{:S(2)}, u32[]{:S(2)}) collective-permute-start(bf16[64,1152]{1,0:T(8,128)(2,1)S(1)} %get-tuple-element.57), channel_id=1, source_target_pairs={{0,16},{4,20},{8,24},{12,28},{16,0},{20,4},{24,8},{28,12},{1,17},{... | collective-permute-start | bytes 442376 | tf_op jit(solution)/shard_map/ppermute | solution.py:17
  90.8 0.4 collective-permute-start.23
  91.2 0.2 collective-permute-start.24
  91.4 1.4 %collective-permute-start.25 = (bf16[64,384]{1,0:T(8,128)(2,1)S(1)}, bf16[64,384]{1,0:T(8,128)(2,1)S(1)}, u32[]{:S(2)}, u32[]{:S(2)}) collective-permute-start(bf16[64,384]{1,0:T(8,128)(2,1)S(1)} %get-tuple-element.61), channel_id=1, source_target_pairs={{0,4},{4,0},{8,12},{12,8},{16,20},{20,16},{24,28},{28,24},{1,5},{5... | collective-permute-start | bytes 147464 | tf_op jit(solution)/shard_map/ppermute | solution.py:17
  92.8 2.7 %collective-permute-done.25.refs_5_ = bf16[64,384]{1,0:T(8,128)(2,1)S(1)} collective-permute-done((bf16[64,384]{1,0:T(8,128)(2,1)S(1)}, bf16[64,384]{1,0:T(8,128)(2,1)S(1)}, u32[]{:S(2)}, u32[]{:S(2)}) %collective-permute-start.25) | collective-permute-done | bytes 49184 | tf_op jit(solution)/shard_map/ppermute | solution.py:17
  95.5 4.9 %collective-permute-done.22.refs_1_ = bf16[64,1152]{1,0:T(8,128)(2,1)S(1)} collective-permute-done((bf16[64,1152]{1,0:T(8,128)(2,1)S(1)}, bf16[64,1152]{1,0:T(8,128)(2,1)S(1)}, u32[]{:S(2)}, u32[]{:S(2)}) %collective-permute-start.22) | collective-permute-done | bytes 147488 | tf_op jit(solution)/shard_map/ppermute | solution.py:17
  100.4 0.9 collective-permute-done.24.refs_3_
  101.3 1.3 %finish.1 = (f32[1,64,768]{2,1,0:T(8,128)}, f32[1,64,768]{2,1,0:T(8,128)}) custom-call(s32[5]{0:T(128)S(1)} %stack.20.sc, f32[64,1152]{1,0:T(8,128)S(1)} %get-tuple-element.56.refs_0_, bf16[64,1152]{1,0:T(8,128)(2,1)S(1)} %collective-permute-done.22.refs_1_, bf16[64,1152]{1,0:T(8,128)(2,1)S(1)} %collective-permute-done.23.refs_2_, ...), custom_call_target="tpu_custom_call" | custom-call | flops 910000000 | tf_op jit(solution)/shard_map/finish/pallas_call | solution.py:192
  (38 shorter events, 0.6 us)
Async XLA Ops:
  0.6 14.5 %collective-permute-start.3 = (bf16[768,3072]{1,0:T(8,128)(2,1)}, bf16[768,3072]{1,0:T(8,128)(2,1)}, u32[]{:S(2)}, u32[]{:S(2)}) collective-permute-start(bf16[768,3072]{1,0:T(8,128)(2,1)} %refs_1_.10), channel_id=1, source_target_pairs={{0,1},{1,0},{2,3},{3,2},{4,5},{5,4},{6,7},{7,6},{8,9},{9,8},{10,11... | collective-permute-start | bytes 14155784 | tf_op jit(solution)/shard_map/ppermute | solution.py:17
  1.8 6.7 %copy-start.4 = (bf16[1,64,768]{2,1,0:T(8,128)(2,1)S(1)}, bf16[1,64,768]{2,1,0:T(8,128)(2,1)}, u32[]{:S(2)}) copy-start(bf16[1,64,768]{2,1,0:T(8,128)(2,1)} %refs_0_.4) | copy-start | bytes 294916
  1.8 6.7 %copy-start.5 = (bf16[1,64,768]{2,1,0:T(8,128)(2,1)S(1)}, bf16[1,64,768]{2,1,0:T(8,128)(2,1)}, u32[]{:S(2)}) copy-start(bf16[1,64,768]{2,1,0:T(8,128)(2,1)} %refs_1_.7) | copy-start | bytes 294916
  5.8 16.8 %collective-permute-start.4 = (bf16[2,192,768]{2,1,0:T(8,128)(2,1)}, bf16[2,192,768]{2,1,0:T(8,128)(2,1)S(1)}, u32[]{:S(2)}, u32[]{:S(2)}) collective-permute-start(bf16[2,192,768]{2,1,0:T(8,128)(2,1)} %attend.2.refs_2_), channel_id=1, source_target_pairs={{0,2},{1,3},{2,0},{3,1},{4,6},{5,7},{6,4},{7,5},{8,10},{9,11},{10,... | collective-permute-start | bytes 1769480 | tf_op jit(solution)/shard_map/ppermute | solution.py:17
  8.5 1.1 %copy-start.3 = (bf16[2,192,768]{2,1,0:T(8,128)(2,1)S(1)}, bf16[2,192,768]{2,1,0:T(8,128)(2,1)}, u32[]{:S(2)}) copy-start(bf16[2,192,768]{2,1,0:T(8,128)(2,1)} %attend.2.refs_2_) | copy-start | bytes 1769476
  9.5 5.6 %copy-start = (bf16[1,192,3072]{2,1,0:T(8,128)(2,1)S(1)}, bf16[1,192,3072]{2,1,0:T(8,128)(2,1)}, u32[]{:S(2)}) copy-start(bf16[1,192,3072]{2,1,0:T(8,128)(2,1)} %refs_0_.5) | copy-start | bytes 3538948
  10.1 17.2 %collective-permute-start = (bf16[128,768]{1,0:T(8,128)(2,1)S(1)}, bf16[128,768]{1,0:T(8,128)(2,1)S(1)}, u32[]{:S(2)}, u32[]{:S(2)}) collective-permute-start(bf16[128,768]{1,0:T(8,128)(2,1)S(1)} %join.1.refs_3_), channel_id=1, source_target_pairs={{0,16},{4,20},{8,24},{12,28},{16,0},{20,4},{24,8},{28,12},{1,17},{... | collective-permute-start | bytes 589832 | tf_op jit(solution)/shard_map/ppermute | solution.py:17
  12.8 14.5 %collective-permute-start.1 = (bf16[128,768]{1,0:T(8,128)(2,1)S(1)}, bf16[128,768]{1,0:T(8,128)(2,1)S(1)}, u32[]{:S(2)}, u32[]{:S(2)}) collective-permute-start(bf16[128,768]{1,0:T(8,128)(2,1)S(1)} %join.1.refs_3_), channel_id=1, source_target_pairs={{0,24},{4,28},{8,16},{12,20},{16,8},{20,12},{24,0},{28,4},{1,25},{... | collective-permute-start | bytes 589832 | tf_op jit(solution)/shard_map/ppermute | solution.py:17
  14.1 13.8 %collective-permute-start.2 = (bf16[128,768]{1,0:T(8,128)(2,1)S(1)}, bf16[128,768]{1,0:T(8,128)(2,1)S(1)}, u32[]{:S(2)}, u32[]{:S(2)}) collective-permute-start(bf16[128,768]{1,0:T(8,128)(2,1)S(1)} %join.1.refs_3_), channel_id=1, source_target_pairs={{0,8},{4,12},{8,0},{12,4},{16,24},{20,28},{24,16},{28,20},{1,9},{5... | collective-permute-start | bytes 589832 | tf_op jit(solution)/shard_map/ppermute | solution.py:17
  14.3 8.3 %slice-start = ((s8[4718592]{0:T(1024)(128)(4,1)}), s8[4194304]{0:T(1024)(128)(4,1)S(1)}, s32[]{:S(2)}) async-start(s8[4718592]{0:T(1024)(128)(4,1)} %bitcast.9), calls=%async_computation | async-start | bytes 8388608
  15.1 3.5 %copy-start.6 = (s32[8]{0:T(128)S(1)}, s32[8]{0:T(128)}, u32[]{:S(2)}) copy-start(s32[8]{0:T(128)} %refs_2_.5) | copy-start | bytes 100
  15.2 7.5 %slice-start.1 = ((s8[4718592]{0:T(1024)(128)(4,1)}), s8[524288]{0:T(1024)(128)(4,1)S(1)}, s32[]{:S(2)}) async-start(s8[4718592]{0:T(1024)(128)(4,1)} %bitcast.9), calls=%async_computation.1 | async-start | bytes 1048576
  22.1 5.8 %collective-permute-start.5 = (f32[8,128]{1,0:T(8,128)S(1)}, f32[8,128]{1,0:T(8,128)S(1)}, u32[]{:S(2)}, u32[]{:S(2)}) collective-permute-start(f32[8,128]{1,0:T(8,128)S(1)} %get-tuple-element.34.refs_6_), channel_id=1, source_target_pairs={{0,2},{1,3},{2,0},{3,1},{4,6},{5,7},{6,4},{7,5},{8,10},{9,11},{10,... | collective-permute-start | bytes 12296 | tf_op jit(solution)/shard_map/ppermute | solution.py:17
  25.3 33.1 %collective-permute-start.11 = (bf16[4,192,768]{2,1,0:T(8,128)(2,1)S(1)}, bf16[4,192,768]{2,1,0:T(8,128)(2,1)S(1)}, u32[]{:S(2)}, u32[]{:S(2)}) collective-permute-start(bf16[4,192,768]{2,1,0:T(8,128)(2,1)S(1)} %project.1.refs_8_), channel_id=1, source_target_pairs={{0,2},{1,3},{2,0},{3,1},{4,6},{5,7},{6,4},{7,5},{8,10},{9,11},{10,... | collective-permute-start | bytes 3538952 | tf_op jit(solution)/shard_map/ppermute | solution.py:17
  27.9 3.6 %copy-start.2 = (bf16[1,192,3072]{2,1,0:T(8,128)(2,1)S(1)}, bf16[1,192,3072]{2,1,0:T(8,128)(2,1)}, u32[]{:S(2)}) copy-start(bf16[1,192,3072]{2,1,0:T(8,128)(2,1)} %refs_4_.1) | copy-start | bytes 3538948
  28.6 3.0 %copy-start.1 = (bf16[1,192,3072]{2,1,0:T(8,128)(2,1)S(1)}, bf16[1,192,3072]{2,1,0:T(8,128)(2,1)}, u32[]{:S(2)}) copy-start(bf16[1,192,3072]{2,1,0:T(8,128)(2,1)} %refs_3_.1) | copy-start | bytes 3538948
  28.6 18.2 %collective-permute-start.10 = (bf16[4,128,768]{2,1,0:T(8,128)(2,1)S(1)}, bf16[4,128,768]{2,1,0:T(8,128)(2,1)S(1)}, u32[]{:S(2)}, u32[]{:S(2)}) collective-permute-start(bf16[4,128,768]{2,1,0:T(8,128)(2,1)S(1)} %get-tuple-element.38.refs_5_.refs_8_), channel_id=1, source_target_pairs={{0,4},{4,0},{8,12},{12,8},{16,20},{20,16},{24,28},{28,24},{1,5},{5... | collective-permute-start | bytes 2359304 | tf_op jit(solution)/shard_map/ppermute | solution.py:17
  30.1 1.2 %collective-permute-start.6 = (f32[8,128]{1,0:T(8,128)S(1)}, f32[8,128]{1,0:T(8,128)S(1)}, u32[]{:S(2)}, u32[]{:S(2)}) collective-permute-start(f32[8,128]{1,0:T(8,128)S(1)} %get-tuple-element.36.refs_0_), channel_id=1, source_target_pairs={{0,1},{1,0},{2,3},{3,2},{4,5},{5,4},{6,7},{7,6},{8,9},{9,8},{10,11... | collective-permute-start | bytes 12296 | tf_op jit(solution)/shard_map/ppermute | solution.py:17
  30.2 4.8 %collective-permute-start.8 = (bf16[192,768]{1,0:T(8,128)(2,1)S(1)}, bf16[192,768]{1,0:T(8,128)(2,1)S(1)}, u32[]{:S(2)}, u32[]{:S(2)}) collective-permute-start(bf16[192,768]{1,0:T(8,128)(2,1)S(1)} %get-tuple-element.39), channel_id=1, source_target_pairs={{0,1},{1,0},{2,3},{3,2},{4,5},{5,4},{6,7},{7,6},{8,9},{9,8},{10,11... | collective-permute-start | bytes 884744 | tf_op jit(solution)/shard_map/ppermute | solution.py:17
  30.8 4.3 %collective-permute-start.9 = (bf16[192,768]{1,0:T(8,128)(2,1)S(1)}, bf16[192,768]{1,0:T(8,128)(2,1)S(1)}, u32[]{:S(2)}, u32[]{:S(2)}) collective-permute-start(bf16[192,768]{1,0:T(8,128)(2,1)S(1)} %get-tuple-element.40), channel_id=1, source_target_pairs={{0,1},{1,0},{2,3},{3,2},{4,5},{5,4},{6,7},{7,6},{8,9},{9,8},{10,11... | collective-permute-start | bytes 884744 | tf_op jit(solution)/shard_map/ppermute | solution.py:17
  31.4 3.7 %collective-permute-start.7 = (f32[8,128]{1,0:T(8,128)S(1)}, f32[8,128]{1,0:T(8,128)S(1)}, u32[]{:S(2)}, u32[]{:S(2)}) collective-permute-start(f32[8,128]{1,0:T(8,128)S(1)} %get-tuple-element.37.refs_2_), channel_id=1, source_target_pairs={{0,1},{1,0},{2,3},{3,2},{4,5},{5,4},{6,7},{7,6},{8,9},{9,8},{10,11... | collective-permute-start | bytes 12296 | tf_op jit(solution)/shard_map/ppermute | solution.py:17
  48.5 7.6 %collective-permute-start.12 = (bf16[80,768]{1,0:T(8,128)(2,1)S(1)}, bf16[80,768]{1,0:T(8,128)(2,1)S(1)}, u32[]{:S(2)}, u32[]{:S(2)}) collective-permute-start(bf16[80,768]{1,0:T(8,128)(2,1)S(1)} %get-tuple-element.42), channel_id=1, source_target_pairs={{0,3},{1,2},{2,1},{3,0},{4,7},{5,6},{6,5},{7,4},{8,11},{9,10},{10,... | collective-permute-start | bytes 368648 | tf_op jit(solution)/shard_map/ppermute | solution.py:17
  48.6 9.9 %collective-permute-start.13 = (bf16[80,768]{1,0:T(8,128)(2,1)S(1)}, bf16[80,768]{1,0:T(8,128)(2,1)S(1)}, u32[]{:S(2)}, u32[]{:S(2)}) collective-permute-start(bf16[80,768]{1,0:T(8,128)(2,1)S(1)} %get-tuple-element.43), channel_id=1, source_target_pairs={{0,2},{1,3},{2,0},{3,1},{4,6},{5,7},{6,4},{7,5},{8,10},{9,11},{10,... | collective-permute-start | bytes 368648 | tf_op jit(solution)/shard_map/ppermute | solution.py:17
  49.1 9.3 %collective-permute-start.14 = (bf16[80,768]{1,0:T(8,128)(2,1)S(1)}, bf16[80,768]{1,0:T(8,128)(2,1)S(1)}, u32[]{:S(2)}, u32[]{:S(2)}) collective-permute-start(bf16[80,768]{1,0:T(8,128)(2,1)S(1)} %get-tuple-element.44), channel_id=1, source_target_pairs={{0,1},{1,0},{2,3},{3,2},{4,5},{5,4},{6,7},{7,6},{8,9},{9,8},{10,11... | collective-permute-start | bytes 368648 | tf_op jit(solution)/shard_map/ppermute | solution.py:17
  61.0 5.6 %collective-permute-start.15 = (bf16[80,768]{1,0:T(8,128)(2,1)S(1)}, bf16[80,768]{1,0:T(8,128)(2,1)S(1)}, u32[]{:S(2)}, u32[]{:S(2)}) collective-permute-start(bf16[80,768]{1,0:T(8,128)(2,1)S(1)} %get-tuple-element.46), channel_id=1, source_target_pairs={{0,3},{1,2},{2,1},{3,0},{4,7},{5,6},{6,5},{7,4},{8,11},{9,10},{10,... | collective-permute-start | bytes 368648 | tf_op jit(solution)/shard_map/ppermute | solution.py:17
  61.1 8.2 %collective-permute-start.16 = (bf16[80,768]{1,0:T(8,128)(2,1)S(1)}, bf16[80,768]{1,0:T(8,128)(2,1)S(1)}, u32[]{:S(2)}, u32[]{:S(2)}) collective-permute-start(bf16[80,768]{1,0:T(8,128)(2,1)S(1)} %get-tuple-element.47), channel_id=1, source_target_pairs={{0,2},{1,3},{2,0},{3,1},{4,6},{5,7},{6,4},{7,5},{8,10},{9,11},{10,... | collective-permute-start | bytes 368648 | tf_op jit(solution)/shard_map/ppermute | solution.py:17
  62.7 6.7 %collective-permute-start.17 = (bf16[80,768]{1,0:T(8,128)(2,1)S(1)}, bf16[80,768]{1,0:T(8,128)(2,1)S(1)}, u32[]{:S(2)}, u32[]{:S(2)}) collective-permute-start(bf16[80,768]{1,0:T(8,128)(2,1)S(1)} %get-tuple-element.48), channel_id=1, source_target_pairs={{0,1},{1,0},{2,3},{3,2},{4,5},{5,4},{6,7},{7,6},{8,9},{9,8},{10,11... | collective-permute-start | bytes 368648 | tf_op jit(solution)/shard_map/ppermute | solution.py:17
  71.0 15.3 %collective-permute-start.20 = (bf16[4,64,1152]{2,1,0:T(8,128)(2,1)S(1)}, bf16[4,64,1152]{2,1,0:T(8,128)(2,1)S(1)}, u32[]{:S(2)}, u32[]{:S(2)}) collective-permute-start(bf16[4,64,1152]{2,1,0:T(8,128)(2,1)S(1)} %get-tuple-element.54), channel_id=1, source_target_pairs={{0,4},{4,0},{8,12},{12,8},{16,20},{20,16},{24,28},{28,24},{1,5},{5... | collective-permute-start | bytes 1769480 | tf_op jit(solution)/shard_map/ppermute | solution.py:17
  72.6 10.9 %collective-permute-start.18 = (bf16[2,64,384]{2,1,0:T(8,128)(2,1)S(1)}, bf16[2,64,384]{2,1,0:T(8,128)(2,1)S(1)}, u32[]{:S(2)}, u32[]{:S(2)}) collective-permute-start(bf16[2,64,384]{2,1,0:T(8,128)(2,1)S(1)} %get-tuple-element.52), channel_id=1, source_target_pairs={{0,16},{4,20},{8,24},{12,28},{16,0},{20,4},{24,8},{28,12},{1,17},{... | collective-permute-start | bytes 294920 | tf_op jit(solution)/shard_map/ppermute | solution.py:17
  76.6 6.9 %collective-permute-start.19 = (bf16[2,64,384]{2,1,0:T(8,128)(2,1)S(1)}, bf16[2,64,384]{2,1,0:T(8,128)(2,1)S(1)}, u32[]{:S(2)}, u32[]{:S(2)}) collective-permute-start(bf16[2,64,384]{2,1,0:T(8,128)(2,1)S(1)} %get-tuple-element.53), channel_id=1, source_target_pairs={{0,24},{4,28},{8,16},{12,20},{16,8},{20,12},{24,0},{28,4},{1,25},{... | collective-permute-start | bytes 294920 | tf_op jit(solution)/shard_map/ppermute | solution.py:17
  77.1 7.0 %collective-permute-start.21 = (bf16[2,64,384]{2,1,0:T(8,128)(2,1)S(1)}, bf16[2,64,384]{2,1,0:T(8,128)(2,1)S(1)}, u32[]{:S(2)}, u32[]{:S(2)}) collective-permute-start(bf16[2,64,384]{2,1,0:T(8,128)(2,1)S(1)} %get-tuple-element.55), channel_id=1, source_target_pairs={{0,8},{4,12},{8,0},{12,4},{16,24},{20,28},{24,16},{28,20},{1,9},{5... | collective-permute-start | bytes 294920 | tf_op jit(solution)/shard_map/ppermute | solution.py:17
  87.0 13.4 %collective-permute-start.22 = (bf16[64,1152]{1,0:T(8,128)(2,1)S(1)}, bf16[64,1152]{1,0:T(8,128)(2,1)S(1)}, u32[]{:S(2)}, u32[]{:S(2)}) collective-permute-start(bf16[64,1152]{1,0:T(8,128)(2,1)S(1)} %get-tuple-element.57), channel_id=1, source_target_pairs={{0,16},{4,20},{8,24},{12,28},{16,0},{20,4},{24,8},{28,12},{1,17},{... | collective-permute-start | bytes 442376 | tf_op jit(solution)/shard_map/ppermute | solution.py:17
  90.8 9.6 %collective-permute-start.23 = (bf16[64,1152]{1,0:T(8,128)(2,1)S(1)}, bf16[64,1152]{1,0:T(8,128)(2,1)S(1)}, u32[]{:S(2)}, u32[]{:S(2)}) collective-permute-start(bf16[64,1152]{1,0:T(8,128)(2,1)S(1)} %get-tuple-element.58), channel_id=1, source_target_pairs={{0,24},{4,28},{8,16},{12,20},{16,8},{20,12},{24,0},{28,4},{1,25},{... | collective-permute-start | bytes 442376 | tf_op jit(solution)/shard_map/ppermute | solution.py:17
  91.2 10.1 %collective-permute-start.24 = (bf16[64,1152]{1,0:T(8,128)(2,1)S(1)}, bf16[64,1152]{1,0:T(8,128)(2,1)S(1)}, u32[]{:S(2)}, u32[]{:S(2)}) collective-permute-start(bf16[64,1152]{1,0:T(8,128)(2,1)S(1)} %get-tuple-element.59), channel_id=1, source_target_pairs={{0,8},{4,12},{8,0},{12,4},{16,24},{20,28},{24,16},{28,20},{1,9},{5... | collective-permute-start | bytes 442376 | tf_op jit(solution)/shard_map/ppermute | solution.py:17
  91.4 4.1 %collective-permute-start.25 = (bf16[64,384]{1,0:T(8,128)(2,1)S(1)}, bf16[64,384]{1,0:T(8,128)(2,1)S(1)}, u32[]{:S(2)}, u32[]{:S(2)}) collective-permute-start(bf16[64,384]{1,0:T(8,128)(2,1)S(1)} %get-tuple-element.61), channel_id=1, source_target_pairs={{0,4},{4,0},{8,12},{12,8},{16,20},{20,16},{24,28},{28,24},{1,5},{5... | collective-permute-start | bytes 147464 | tf_op jit(solution)/shard_map/ppermute | solution.py:17
